TPU v7x, 32 devices: a whole 2x2x4 slice. The times are simulated.
32 devices in a mesh: dp: 8 (over y, x, core), fsdp: 4 (over z).
Axes of the slice: x: 2, y: 2, z: 4, core: 2. Of those that a mesh axis runs over, the one named last changes fastest.
Arguments:
- tokens: bfloat16 [64, 1024, 768], P(('dp', 'fsdp')), may hold values from -6 to 6
- cotangent: bfloat16 [64, 1024, 768], P(('dp', 'fsdp')), may hold values from -6 to 6
- lengths: int32 [64], replicated, may hold values from 1 to 1024, as said below
- seg_qkv: bfloat16 [768, 2304], P(('dp', 'fsdp')), may hold values from -0.21875 to 0.21875
- seg_out: bfloat16 [768, 768], P(('dp', 'fsdp')), may hold values from -0.625 to 0.625
- seg_up: bfloat16 [768, 3072], P(('dp', 'fsdp')), may hold values from -0.21875 to 0.21875
- seg_down: bfloat16 [3072, 768], P(('dp', 'fsdp')), may hold values from -0.109375 to 0.109375
- seg_vec: bfloat16 [12, 768], P(None, ('dp', 'fsdp')), may hold values from -0.796875 to 0.796875
- cross_qkv: bfloat16 [768, 2304], P(('dp', 'fsdp')), may hold values from -0.21875 to 0.21875
- cross_out: bfloat16 [768, 768], P(('dp', 'fsdp')), may hold values from -0.3125 to 0.3125
- cross_up: bfloat16 [768, 3072], P(('dp', 'fsdp')), may hold values from -0.21875 to 0.21875
- cross_down: bfloat16 [3072, 768], P(('dp', 'fsdp')), may hold values from -0.109375 to 0.109375
- cross_vec: bfloat16 [12, 768], P(None, ('dp', 'fsdp')), may hold values from -0.796875 to 0.796875
- positions: bfloat16 [8, 768], P(None, ('dp', 'fsdp')), may hold values from -6 to 6
Outputs:
- layer_out: bfloat16 [64, 1024, 768], P(('dp', 'fsdp'))
- token_grad: bfloat16 [64, 1024, 768], P(('dp', 'fsdp'))
- grad_seg_qkv: float32 [768, 2304], P(('dp', 'fsdp'))
- grad_seg_out: float32 [768, 768], P(('dp', 'fsdp'))
- grad_seg_up: float32 [768, 3072], P(('dp', 'fsdp'))
- grad_seg_down: float32 [3072, 768], P(('dp', 'fsdp'))
- grad_seg_vec: float32 [12, 768], P(None, ('dp', 'fsdp'))
- grad_cross_qkv: float32 [768, 2304], P(('dp', 'fsdp'))
- grad_cross_out: float32 [768, 768], P(('dp', 'fsdp'))
- grad_cross_up: float32 [768, 3072], P(('dp', 'fsdp'))
- grad_cross_down: float32 [3072, 768], P(('dp', 'fsdp'))
- grad_cross_vec: float32 [12, 768], P(None, ('dp', 'fsdp'))
- grad_positions: float32 [8, 768], P(None, ('dp', 'fsdp'))
Inputs may be any that keep to these rules, and one draw needn't show every extreme that they name: lengths[s] is the number of live tokens of sequence s, which come first in its 1024 slots; some sequence has exactly 1024.
All inputs are finite; a program needn't handle non-finite values.
Results may differ from a plain program's by a relative error of at most 0.025.
Values may be sent and summed in bfloat16 or wider, within the bound.
No kernel may reach another device: no remote copies, remote signals or barrier semaphores. Data moves between devices by JAX's collectives and lax.ppermute only.
A program may use at most 256 MiB of HBM per device.

v0:
```python
import jax
import jax.numpy as jnp
from jax import lax
from jax.sharding import PartitionSpec as P

HEAD = 64
SEG = 128


NORM_EPS = 1e-05
MASK_FILL = -1000000000.0
ROOT_HALF = 0.7071067811865476
INV_ROOT_TAU = 0.3989422804014327


def matmul(left_op, right_op):
    return jnp.dot(left_op, right_op, preferred_element_type=jnp.float32)


def trans_left(left_op, right_op):
    return lax.dot_general(
        left_op, right_op, (((0,), (0,)), ((), ())), preferred_element_type=jnp.float32
    )


def trans_right(left_op, right_op):
    return lax.dot_general(
        left_op, right_op, (((1,), (1,)), ((), ())), preferred_element_type=jnp.float32
    )


def norm_forward(summed, gain_row, shift_row):
    average = jnp.mean(summed, axis=-1, keepdims=True)
    centered = summed - average
    inv_scale = lax.rsqrt(jnp.mean(centered * centered, axis=-1, keepdims=True) + NORM_EPS)
    normed = centered * inv_scale
    return (normed * (1.0 + gain_row) + shift_row, normed, inv_scale)


def norm_backward(upstream, normed, inv_scale, gain_row):
    inner = upstream * (1.0 + gain_row)
    back_grad = inv_scale * (
        inner
        - jnp.mean(inner, axis=-1, keepdims=True)
        - normed * jnp.mean(inner * normed, axis=-1, keepdims=True)
    )
    return (back_grad, jnp.sum(upstream * normed, axis=0), jnp.sum(upstream, axis=0))


def gelu_slope(hidden):
    return (
        0.5 * (1.0 + lax.erf(hidden * ROOT_HALF))
        + hidden * jnp.exp(-0.5 * hidden * hidden) * INV_ROOT_TAU
    )


def split_heads(packed, group_len):
    head_count = packed.shape[1] // (3 * HEAD)
    return [
        portion.reshape(-1, group_len, head_count, HEAD) for portion in jnp.split(packed, 3, axis=1)
    ]


def masked_scores(query_heads, key_heads, allowed):
    raw_scores = jnp.einsum(
        "nqhd,nkhd->nhqk", query_heads, key_heads, preferred_element_type=jnp.float32
    ) * HEAD ** (-0.5)
    return jnp.where(allowed[:, None, None, :], raw_scores, MASK_FILL)


def encode(inputs, inputs_low, weights, allowed):
    qkv_w, out_w, up_w, down_w, vectors = weights
    row_count, feat_dim = inputs_low.shape
    group_len = allowed.shape[1]
    qkv_bias = jnp.concatenate([vectors[0], jnp.zeros_like(vectors[0]), vectors[1]])
    packed = (matmul(inputs_low, qkv_w) + qkv_bias).astype(jnp.bfloat16)
    query_heads, key_heads, value_heads = split_heads(packed, group_len)
    scores = masked_scores(query_heads, key_heads, allowed)
    row_max = jnp.max(scores, axis=-1, keepdims=True)
    expo_vals = jnp.exp(scores - row_max)
    row_total = jnp.sum(expo_vals, axis=-1, keepdims=True)
    log_total = row_max + jnp.log(row_total)
    prob_low = (expo_vals / row_total).astype(jnp.bfloat16)
    mixed = jnp.einsum("nhqk,nkhd->nqhd", prob_low, value_heads, preferred_element_type=jnp.float32)
    mixed = mixed.reshape(row_count, feat_dim).astype(jnp.bfloat16)
    projected = matmul(mixed, out_w) + vectors[2]
    first_out, normed_one, scale_one = norm_forward(inputs + projected, vectors[3], vectors[4])
    first_low = first_out.astype(jnp.bfloat16)
    hidden = matmul(first_low, up_w) + vectors[5:-3].reshape(-1)
    activated = jax.nn.gelu(hidden, approximate=False).astype(jnp.bfloat16)
    down_out = matmul(activated, down_w) + vectors[-3]
    result, normed_two, scale_two = norm_forward(first_out + down_out, vectors[-2], vectors[-1])
    return (
        result,
        (
            packed,
            log_total,
            mixed,
            normed_one,
            scale_one,
            first_low,
            hidden,
            activated,
            normed_two,
            scale_two,
        ),
    )


def encode_back(upstream, inputs_low, weights, allowed, kept):
    qkv_w, out_w, up_w, down_w, vectors = weights
    (
        packed,
        log_total,
        mixed,
        normed_one,
        scale_one,
        first_low,
        hidden,
        activated,
        normed_two,
        scale_two,
    ) = kept
    row_count, feat_dim = inputs_low.shape
    group_len = allowed.shape[1]
    back_two, gain_two, shift_two = norm_backward(upstream, normed_two, scale_two, vectors[-2])
    down_grad = back_two.astype(jnp.bfloat16)
    grad_down_w = trans_left(activated, down_grad)
    hidden_grad = (trans_right(down_grad, down_w) * gelu_slope(hidden)).astype(jnp.bfloat16)
    grad_up_w = trans_left(first_low, hidden_grad)
    first_grad = trans_right(hidden_grad, up_w) + back_two
    back_one, gain_one, shift_one = norm_backward(first_grad, normed_one, scale_one, vectors[3])
    proj_grad = back_one.astype(jnp.bfloat16)
    grad_out_w = trans_left(mixed, proj_grad)
    query_heads, key_heads, value_heads = split_heads(packed, group_len)
    mixed_grad = trans_right(proj_grad, out_w).astype(jnp.bfloat16).reshape(value_heads.shape)
    scores = masked_scores(query_heads, key_heads, allowed)
    prob_vals = jnp.exp(scores - log_total)
    grad_values = jnp.einsum(
        "nhqk,nqhd->nkhd",
        prob_vals.astype(jnp.bfloat16),
        mixed_grad,
        preferred_element_type=jnp.float32,
    )
    grad_prob = jnp.einsum(
        "nqhd,nkhd->nhqk", mixed_grad, value_heads, preferred_element_type=jnp.float32
    )
    score_grad = (
        prob_vals * (grad_prob - jnp.sum(prob_vals * grad_prob, axis=-1, keepdims=True))
    ).astype(jnp.bfloat16)
    grad_query = jnp.einsum(
        "nhqk,nkhd->nqhd", score_grad, key_heads, preferred_element_type=jnp.float32
    ) * HEAD ** (-0.5)
    grad_keys = jnp.einsum(
        "nhqk,nqhd->nkhd", score_grad, query_heads, preferred_element_type=jnp.float32
    ) * HEAD ** (-0.5)
    packed_grad = jnp.concatenate(
        [
            grad_query.reshape(row_count, feat_dim),
            grad_keys.reshape(row_count, feat_dim),
            grad_values.reshape(row_count, feat_dim),
        ],
        axis=1,
    ).astype(jnp.bfloat16)
    grad_qkv_w = trans_left(inputs_low, packed_grad)
    bias_grads = jnp.sum(packed_grad, axis=0, dtype=jnp.float32).reshape(3, feat_dim)
    grad_inputs = trans_right(packed_grad, qkv_w) + back_one
    grad_vectors = jnp.concatenate(
        [
            bias_grads[0:1],
            bias_grads[2:3],
            jnp.sum(proj_grad, axis=0, dtype=jnp.float32)[None],
            gain_one[None],
            shift_one[None],
            jnp.sum(hidden_grad, axis=0, dtype=jnp.float32).reshape(-1, feat_dim),
            jnp.sum(down_grad, axis=0, dtype=jnp.float32)[None],
            gain_two[None],
            shift_two[None],
        ],
        axis=0,
    )
    return (grad_inputs, (grad_qkv_w, grad_out_w, grad_up_w, grad_down_w, grad_vectors))


def deal_tables(lengths, seq_len, seq_local):
    seq_total = lengths.shape[0]
    seq_ids = jnp.arange(seq_total, dtype=jnp.int32)
    ranking = (seq_len - lengths) * seq_total + seq_ids
    rank_of = jnp.sum((ranking[None, :] < ranking[:, None]).astype(jnp.int32), axis=1)
    device_count = seq_total // seq_local
    rounds = rank_of // device_count
    column = rank_of % device_count
    device_pick = jnp.where(rounds % 2 == 0, column, device_count - 1 - column)
    placed_at = device_pick * seq_local + rounds
    dealing = jnp.sum(
        jnp.where(placed_at[None, :] == seq_ids[:, None], seq_ids[None, :], 0), axis=1
    )
    return (dealing, placed_at)


def redeal(stacked, index):
    spread = lax.all_to_all(stacked, ("dp", "fsdp"), split_axis=2, concat_axis=1, tiled=True)
    picked = jnp.take(spread, index, axis=1)
    return lax.all_to_all(picked, ("dp", "fsdp"), split_axis=1, concat_axis=2, tiled=True)


def unpack(gathered):
    seg_weights = (
        gathered[0],
        gathered[1],
        gathered[2],
        gathered[3],
        gathered[4].astype(jnp.float32),
    )
    cross_weights = (
        gathered[5],
        gathered[6],
        gathered[7],
        gathered[8],
        gathered[9].astype(jnp.float32),
    )
    return (seg_weights, cross_weights, gathered[10].astype(jnp.float32))


def shards(
    tokens,
    cotangent,
    lengths,
    seg_qkv,
    seg_out,
    seg_up,
    seg_down,
    seg_vec,
    cross_qkv,
    cross_out,
    cross_up,
    cross_down,
    cross_vec,
    positions,
):
    gathered = (
        lax.all_gather(seg_qkv, ("dp", "fsdp"), axis=0, tiled=True),
        lax.all_gather(seg_out, ("dp", "fsdp"), axis=0, tiled=True),
        lax.all_gather(seg_up, ("dp", "fsdp"), axis=0, tiled=True),
        lax.all_gather(seg_down, ("dp", "fsdp"), axis=0, tiled=True),
        lax.all_gather(seg_vec, ("dp", "fsdp"), axis=1, tiled=True),
        lax.all_gather(cross_qkv, ("dp", "fsdp"), axis=0, tiled=True),
        lax.all_gather(cross_out, ("dp", "fsdp"), axis=0, tiled=True),
        lax.all_gather(cross_up, ("dp", "fsdp"), axis=0, tiled=True),
        lax.all_gather(cross_down, ("dp", "fsdp"), axis=0, tiled=True),
        lax.all_gather(cross_vec, ("dp", "fsdp"), axis=1, tiled=True),
        lax.all_gather(positions, ("dp", "fsdp"), axis=1, tiled=True),
    )
    seg_weights, cross_weights, pos_table = unpack(gathered)
    seq_local, seq_len, feat_dim = tokens.shape
    seg_count = seq_len // SEG
    dealing, inverse = deal_tables(lengths, seq_len, seq_local)
    first_pos = lax.axis_index(("dp", "fsdp")) * seq_local
    my_seqs = lax.dynamic_slice_in_dim(dealing, first_pos, seq_local)
    my_lengths = jnp.take(lengths, my_seqs)
    arrived = redeal(jnp.stack([tokens, cotangent]), dealing)
    dealt_rows = arrived[0].reshape(-1, feat_dim)
    token_pos = jnp.arange(seq_len)
    live_mask = token_pos[None, :] < my_lengths[:, None]
    seg_opens = token_pos % SEG == 0
    keys_ok = (live_mask | seg_opens[None, :]).reshape(-1, SEG)
    seg_live = (jnp.arange(seg_count) * SEG)[None, :] < my_lengths[:, None]
    live_float = live_mask[..., None].astype(jnp.float32)
    seg_result, seg_kept = encode(dealt_rows, dealt_rows, seg_weights, keys_ok)
    seg_grid = seg_result.reshape(seq_local, seg_count, SEG, feat_dim)
    heads_in = (seg_grid[:, :, 0, :] + pos_table[None]).reshape(-1, feat_dim)
    heads_low = heads_in.astype(jnp.bfloat16)
    cross_result, cross_kept = encode(heads_in, heads_low, cross_weights, seg_live)
    merged = jnp.concatenate(
        [cross_result.reshape(seq_local, seg_count, 1, feat_dim), seg_grid[:, :, 1:, :]], axis=2
    )
    layer_out = (merged.reshape(seq_local, seq_len, feat_dim) * live_float).astype(jnp.bfloat16)
    gathered = (
        lax.all_gather(seg_qkv, ("dp", "fsdp"), axis=0, tiled=True),
        lax.all_gather(seg_out, ("dp", "fsdp"), axis=0, tiled=True),
        lax.all_gather(seg_up, ("dp", "fsdp"), axis=0, tiled=True),
        lax.all_gather(seg_down, ("dp", "fsdp"), axis=0, tiled=True),
        lax.all_gather(seg_vec, ("dp", "fsdp"), axis=1, tiled=True),
        lax.all_gather(cross_qkv, ("dp", "fsdp"), axis=0, tiled=True),
        lax.all_gather(cross_out, ("dp", "fsdp"), axis=0, tiled=True),
        lax.all_gather(cross_up, ("dp", "fsdp"), axis=0, tiled=True),
        lax.all_gather(cross_down, ("dp", "fsdp"), axis=0, tiled=True),
        lax.all_gather(cross_vec, ("dp", "fsdp"), axis=1, tiled=True),
        lax.all_gather(positions, ("dp", "fsdp"), axis=1, tiled=True),
    )
    seg_weights, cross_weights, pos_table = unpack(gathered)
    grad_grid = (arrived[1].astype(jnp.float32) * live_float).reshape(
        seq_local, seg_count, SEG, feat_dim
    )
    cross_up_grad = grad_grid[:, :, 0, :].reshape(-1, feat_dim)
    heads_grad, cross_grads = encode_back(
        cross_up_grad, heads_low, cross_weights, seg_live, cross_kept
    )
    heads_grid = heads_grad.reshape(seq_local, seg_count, feat_dim)
    grad_positions = jnp.sum(heads_grid, axis=0)
    seg_up_grad = jnp.concatenate(
        [heads_grid[:, :, None, :], grad_grid[:, :, 1:, :]], axis=2
    ).reshape(-1, feat_dim)
    rows_grad, seg_grads = encode_back(seg_up_grad, dealt_rows, seg_weights, keys_ok, seg_kept)
    token_grad = rows_grad.reshape(seq_local, seq_len, feat_dim).astype(jnp.bfloat16)
    summed = (
        lax.psum_scatter(seg_grads[0], ("dp", "fsdp"), scatter_dimension=0, tiled=True),
        lax.psum_scatter(seg_grads[1], ("dp", "fsdp"), scatter_dimension=0, tiled=True),
        lax.psum_scatter(seg_grads[2], ("dp", "fsdp"), scatter_dimension=0, tiled=True),
        lax.psum_scatter(seg_grads[3], ("dp", "fsdp"), scatter_dimension=0, tiled=True),
        lax.psum_scatter(seg_grads[4], ("dp", "fsdp"), scatter_dimension=1, tiled=True),
        lax.psum_scatter(cross_grads[0], ("dp", "fsdp"), scatter_dimension=0, tiled=True),
        lax.psum_scatter(cross_grads[1], ("dp", "fsdp"), scatter_dimension=0, tiled=True),
        lax.psum_scatter(cross_grads[2], ("dp", "fsdp"), scatter_dimension=0, tiled=True),
        lax.psum_scatter(cross_grads[3], ("dp", "fsdp"), scatter_dimension=0, tiled=True),
        lax.psum_scatter(cross_grads[4], ("dp", "fsdp"), scatter_dimension=1, tiled=True),
        lax.psum_scatter(grad_positions, ("dp", "fsdp"), scatter_dimension=1, tiled=True),
    )
    home = redeal(jnp.stack([layer_out, token_grad]), inverse)
    return (
        home[0],
        home[1],
        summed[0],
        summed[1],
        summed[2],
        summed[3],
        summed[4],
        summed[5],
        summed[6],
        summed[7],
        summed[8],
        summed[9],
        summed[10],
    )


def solution(mesh):
    in_specs = (
        P(("dp", "fsdp"), None, None),
        P(("dp", "fsdp"), None, None),
        P(),
        P(("dp", "fsdp"), None),
        P(("dp", "fsdp"), None),
        P(("dp", "fsdp"), None),
        P(("dp", "fsdp"), None),
        P(None, ("dp", "fsdp")),
        P(("dp", "fsdp"), None),
        P(("dp", "fsdp"), None),
        P(("dp", "fsdp"), None),
        P(("dp", "fsdp"), None),
        P(None, ("dp", "fsdp")),
        P(None, ("dp", "fsdp")),
    )
    out_specs = (
        P(("dp", "fsdp"), None, None),
        P(("dp", "fsdp"), None, None),
        P(("dp", "fsdp"), None),
        P(("dp", "fsdp"), None),
        P(("dp", "fsdp"), None),
        P(("dp", "fsdp"), None),
        P(None, ("dp", "fsdp")),
        P(("dp", "fsdp"), None),
        P(("dp", "fsdp"), None),
        P(("dp", "fsdp"), None),
        P(("dp", "fsdp"), None),
        P(None, ("dp", "fsdp")),
        P(None, ("dp", "fsdp")),
    )
    return jax.shard_map(shards, mesh=mesh, in_specs=in_specs, out_specs=out_specs, check_vma=False)
```

profile of v0, /device:TPU:0, one launch (start us, length us, event | category | flops | bytes accessed | tf_op | source)
XLA Modules:
  0.0 2208.5 jit_solution(18385512892250474450)
XLA Ops:
  10.0 11.9 copy_bitcast_fusion
  21.9 9.3 pad_maximum_fusion
  40.7 153.7 %all-to-all-done = bf16[2,2,1024,768]{3,1,0,2:T(2,128)(2,1)} async-done(((bf16[2,2,1024,768]{3,1,0,2:T(2,128)(2,1)}), bf16[2,2,1024,768]{3,1,0,2:T(2,128)(2,1)}, u32[]{:S(2)}, u32[]{:S(2)}) %all-to-all-start) | async-done | bytes 6291488 | tf_op jit(solution)/shard_map/all_to_all | solution.py:202
  222.5 234.0 %all-gather = bf16[32,24,12]{1,2,0:T(8,128)(2,1)S(1)} all-gather(bf16[1,24,12]{1,2,0:T(8,128)(2,1)S(1)} %bitcast.253), channel_id=1, replica_groups=mesh['dp'=8,'fsdp'=4] {'dp','fsdp'}, dimensions={0}, use_global_device_ids=true | all-gather | bytes 19008 | tf_op jit(solution)/shard_map/all_gather | solution.py:246
  458.4 64.7 %all-gather.2 = bf16[32,24,12]{1,2,0:T(8,128)(2,1)S(1)} all-gather(bf16[1,24,12]{1,2,0:T(8,128)(2,1)S(1)} %bitcast.254), channel_id=1, replica_groups=mesh['dp'=8,'fsdp'=4] {'dp','fsdp'}, dimensions={0}, use_global_device_ids=true | all-gather | bytes 19008 | tf_op jit(solution)/shard_map/all_gather | solution.py:251
  523.5 67.2 %all-gather.1 = bf16[32,24,8]{1,2,0:T(8,128)(2,1)S(1)} all-gather(bf16[1,24,8]{1,2,0:T(8,128)(2,1)S(1)} %bitcast.255), channel_id=1, replica_groups=mesh['dp'=8,'fsdp'=4] {'dp','fsdp'}, dimensions={0}, use_global_device_ids=true | all-gather | bytes 12672 | tf_op jit(solution)/shard_map/all_gather | solution.py:252
  604.3 9.9 add_convert_fusion
  675.3 70.7 %fusion.2 = (bf16[2048,3072]{1,0:T(8,128)(2,1)}, f32[2048,3072]{1,0:T(8,128)}) fusion(f32[3072]{0:T(1024)S(1)} %add.339, bf16[768,3072]{1,0:T(8,128)(2,1)} %all-gather.16.cloned.1.call-done, f32[2048,768]{1,0:T(8,128)} %copy-done.6, f32[768]{0:T(1024)S(1)} %get-tuple-element.39, f32[768]{0:T(1024)S(1)} %get-tuple-element.40, f32[2048]{0:T(1024)S(1)} %add_rsqrt_fusion.1, ...), kind=kOutput, calls=%fused_computation.7 | convolution fusion | flops 10086776832 | bytes 48793600 | tf_op jit(solution)/shard_map/dot_general | solution.py:17
  749.4 15.8 fusion.142
  846.2 26.8 %convert_reduce_fusion = (f32[3072]{0:T(1024)S(1)}, bf16[2048,3072]{1,0:T(8,128)(2,1)}) fusion(f32[2048,3072]{1,0:T(8,128)} %get-tuple-element.84, f32[3072]{0:T(1024)S(1)} %copy-done.92, bf16[3072,768]{1,0:T(8,128)(2,1)} %all-gather.18.cloned.1.call-done, f32[2048,768]{1,0:T(8,128)S(1)} %get-tuple-element.52), kind=kOutput, calls=%fused_computation.14 | convolution fusion | flops 9747035136 | bytes 48783360 | tf_op jit(solution)/shard_map/dot_general | solution.py:27
  873.1 18.6 multiply_reduce_fusion.1
  908.9 14.9 multiply_reduce_fusion
  985.7 12.7 fusion.147
  1003.9 18.1 fusion.131
  1022.1 17.3 fusion.110
  1044.9 11.6 add_convert_fusion.1
  1094.5 143.0 %all-to-all-done.2 = bf16[2,2,1024,768]{3,1,0,2:T(2,128)(2,1)} async-done(((bf16[2,2,1024,768]{3,1,0,2:T(2,128)(2,1)}), bf16[2,2,1024,768]{3,1,0,2:T(2,128)(2,1)}, u32[]{:S(2)}, u32[]{:S(2)}) %all-to-all-start.2) | async-done | bytes 6291488 | tf_op jit(solution)/shard_map/all_to_all | solution.py:202
  1273.4 137.5 %all-to-all-done.3 = bf16[2,64,32,768]{3,2,0,1:T(8,128)(2,1)} async-done(((bf16[2,64,32,768]{3,2,0,1:T(8,128)(2,1)}), bf16[2,64,32,768]{3,2,0,1:T(8,128)(2,1)}, u32[]{:S(2)}, u32[]{:S(2)}) %all-to-all-start.3) | async-done | bytes 6291488 | tf_op jit(solution)/shard_map/all_to_all | solution.py:204
  1418.8 91.2 %reduce-scatter.12.cloned.1.call-done = f32[24,2304]{1,0:T(8,128)} async-done(((f32[768,2304]{1,0:T(8,128)}), f32[24,2304]{1,0:T(8,128)}) %reduce-scatter.12.cloned.1.call-update) | async-done | bytes 221200 | tf_op jit(solution)/shard_map/reduce_scatter | solution.py:307
  1510.0 125.7 %reduce-scatter.20.cloned.1.call-done = f32[24,2304]{1,0:T(8,128)} async-done(((f32[768,2304]{1,0:T(8,128)}), f32[24,2304]{1,0:T(8,128)}) %reduce-scatter.20.cloned.1.call-update) | async-done | bytes 221200 | tf_op jit(solution)/shard_map/reduce_scatter | solution.py:312
  1635.7 141.0 %reduce-scatter.16.cloned.1.call-done = f32[24,3072]{1,0:T(8,128)} async-done(((f32[768,3072]{1,0:T(8,128)}), f32[24,3072]{1,0:T(8,128)}) %reduce-scatter.16.cloned.1.call-update) | async-done | bytes 294928 | tf_op jit(solution)/shard_map/reduce_scatter | solution.py:309
  1776.7 142.1 %reduce-scatter.18.cloned.1.call-done = f32[96,768]{1,0:T(8,128)} async-done(((f32[3072,768]{1,0:T(8,128)}), f32[96,768]{1,0:T(8,128)}) %reduce-scatter.18.cloned.1.call-update) | async-done | bytes 294928 | tf_op jit(solution)/shard_map/reduce_scatter | solution.py:310
  1918.8 140.9 %reduce-scatter.24.cloned.1.call-done = f32[24,3072]{1,0:T(8,128)} async-done(((f32[768,3072]{1,0:T(8,128)}), f32[24,3072]{1,0:T(8,128)}) %reduce-scatter.24.cloned.1.call-update) | async-done | bytes 294928 | tf_op jit(solution)/shard_map/reduce_scatter | solution.py:314
  2059.8 142.0 %reduce-scatter.26.cloned.1.call-done = f32[96,768]{1,0:T(8,128)} async-done(((f32[3072,768]{1,0:T(8,128)}), f32[96,768]{1,0:T(8,128)}) %reduce-scatter.26.cloned.1.call-update) | async-done | bytes 294928 | tf_op jit(solution)/shard_map/reduce_scatter | solution.py:315
  (470 shorter events, 371.5 us)
Async XLA Ops:
  7.2 595.5 %all-gather.12.cloned.1.call-start = ((), (), s32[]{:S(2)}) async-start(), calls=%async_computation.12 | async-start | bytes 3649536 | tf_op jit(solution)/shard_map/all_gather | solution.py:242
  7.9 658.0 %all-gather.14.cloned.1.call-start = ((), (), s32[]{:S(2)}) async-start(), calls=%async_computation.13 | async-start | bytes 1216512 | tf_op jit(solution)/shard_map/all_gather | solution.py:243
  8.7 666.6 %all-gather.16.cloned.1.call-start = ((), (), s32[]{:S(2)}) async-start(), calls=%async_computation.14 | async-start | bytes 4866048 | tf_op jit(solution)/shard_map/all_gather | solution.py:244
  9.4 739.9 %all-gather.18.cloned.1.call-start = ((), (), s32[]{:S(2)}) async-start(), calls=%async_computation.15 | async-start | bytes 4866048 | tf_op jit(solution)/shard_map/all_gather | solution.py:245
  31.2 163.2 %all-to-all-start = ((bf16[2,2,1024,768]{3,1,0,2:T(2,128)(2,1)}), bf16[2,2,1024,768]{3,1,0,2:T(2,128)(2,1)}, u32[]{:S(2)}, u32[]{:S(2)}) async-start(bf16[2,2,1024,768]{3,1,0,2:T(2,128)(2,1)} %pad_maximum_fusion), calls=%async_computation | async-start | bytes 12582912 | tf_op jit(solution)/shard_map/all_to_all | solution.py:202
  38.6 732.0 %all-gather.20.cloned.1.call-start = ((), (), s32[]{:S(2)}) async-start(), calls=%async_computation.16 | async-start | bytes 3649536 | tf_op jit(solution)/shard_map/all_gather | solution.py:247
  39.2 735.6 %all-gather.22.cloned.1.call-start = ((), (), s32[]{:S(2)}) async-start(), calls=%async_computation.17 | async-start | bytes 1216512 | tf_op jit(solution)/shard_map/all_gather | solution.py:248
  213.6 244.8 %copy-start.100 = (bf16[12,24]{1,0:T(8,128)(2,1)S(1)}, bf16[12,24]{1,0:T(8,128)(2,1)}, u32[]{:S(2)}) copy-start(bf16[12,24]{1,0:T(8,128)(2,1)} %param.28) | copy-start | bytes 1732
  213.6 309.9 %copy-start.101 = (bf16[8,24]{1,0:T(8,128)(2,1)S(1)}, bf16[8,24]{1,0:T(8,128)(2,1)}, u32[]{:S(2)}) copy-start(bf16[8,24]{1,0:T(8,128)(2,1)} %param.29) | copy-start | bytes 1156
  213.6 382.0 %all-to-all-start.1 = ((bf16[2,64,32,768]{3,2,0,1:T(8,128)(2,1)}), bf16[2,64,32,768]{3,2,0,1:T(8,128)(2,1)}, u32[]{:S(2)}, u32[]{:S(2)}) async-start(bf16[2,64,32,768]{3,2,0,1:T(8,128)(2,1)} %select_bitcast_fusion.1), calls=%async_computation.1 | async-start | bytes 12582912 | tf_op jit(solution)/shard_map/all_to_all | solution.py:204
  220.9 562.5 %all-gather.24.cloned.1.call-start = ((), (), s32[]{:S(2)}) async-start(), calls=%async_computation.18 | async-start | bytes 4866048 | tf_op jit(solution)/shard_map/all_gather | solution.py:249
  221.7 571.7 %all-gather.26.cloned.1.call-start = ((), (), s32[]{:S(2)}) async-start(), calls=%async_computation.19 | async-start | bytes 4866048 | tf_op jit(solution)/shard_map/all_gather | solution.py:250
  222.4 1046.8 %all-reduce.6.cloned.1.call-start = ((), (), s32[]{:S(2)}) async-start(), calls=%async_computation.28 | async-start | bytes 245760
  593.0 156.4 %copy-start.95 = (f32[768]{0:T(1024)}, f32[768]{0:T(1024)S(1)}, u32[]{:S(2)}) copy-start(f32[768]{0:T(1024)S(1)} %get-tuple-element.39) | copy-start | bytes 9220
  976.0 442.8 %reduce-scatter.14.cloned.1.call-start = ((), (), s32[]{:S(2)}) async-start(), calls=%async_computation.21 | async-start | bytes 2433024 | tf_op jit(solution)/shard_map/reduce_scatter | solution.py:308
  983.0 435.8 %reduce-scatter.22.cloned.1.call-start = ((), (), s32[]{:S(2)}) async-start(), calls=%async_computation.25 | async-start | bytes 2433024 | tf_op jit(solution)/shard_map/reduce_scatter | solution.py:313
  985.0 525.0 %reduce-scatter.12.cloned.1.call-start = ((), (), s32[]{:S(2)}) async-start(), calls=%async_computation.20 | async-start | bytes 7299072 | tf_op jit(solution)/shard_map/reduce_scatter | solution.py:307
  998.4 637.2 %reduce-scatter.20.cloned.1.call-start = ((), (), s32[]{:S(2)}) async-start(), calls=%async_computation.24 | async-start | bytes 7299072 | tf_op jit(solution)/shard_map/reduce_scatter | solution.py:312
  1003.3 773.4 %reduce-scatter.16.cloned.1.call-start = ((), (), s32[]{:S(2)}) async-start(), calls=%async_computation.22 | async-start | bytes 9732096 | tf_op jit(solution)/shard_map/reduce_scatter | solution.py:309
  1022.0 896.8 %reduce-scatter.18.cloned.1.call-start = ((), (), s32[]{:S(2)}) async-start(), calls=%async_computation.23 | async-start | bytes 9732096 | tf_op jit(solution)/shard_map/reduce_scatter | solution.py:310
  1085.3 152.2 %all-to-all-start.2 = ((bf16[2,2,1024,768]{3,1,0,2:T(2,128)(2,1)}), bf16[2,2,1024,768]{3,1,0,2:T(2,128)(2,1)}, u32[]{:S(2)}, u32[]{:S(2)}) async-start(bf16[2,2,1024,768]{3,1,0,2:T(2,128)(2,1)} %pad_maximum_fusion.3), calls=%async_computation.2 | async-start | bytes 12582912 | tf_op jit(solution)/shard_map/all_to_all | solution.py:202
  1089.1 970.7 %reduce-scatter.24.cloned.1.call-start = ((), (), s32[]{:S(2)}) async-start(), calls=%async_computation.26 | async-start | bytes 9732096 | tf_op jit(solution)/shard_map/reduce_scatter | solution.py:314
  1256.8 154.1 %all-to-all-start.3 = ((bf16[2,64,32,768]{3,2,0,1:T(8,128)(2,1)}), bf16[2,64,32,768]{3,2,0,1:T(8,128)(2,1)}, u32[]{:S(2)}, u32[]{:S(2)}) async-start(bf16[2,64,32,768]{3,2,0,1:T(8,128)(2,1)} %select_bitcast_fusion), calls=%async_computation.3 | async-start | bytes 12582912 | tf_op jit(solution)/shard_map/all_to_all | solution.py:204
  1263.9 937.8 %reduce-scatter.26.cloned.1.call-start = ((), (), s32[]{:S(2)}) async-start(), calls=%async_computation.27 | async-start | bytes 9732096 | tf_op jit(solution)/shard_map/reduce_scatter | solution.py:315
  (111 other events, 1462.8 us)
Sparse Core Ops, SparseCore 0:
  10.8 102.4 all-gather.11
  116.1 71.7 all-gather.13
  190.7 102.4 all-gather.15
  295.9 85.2 all-gather.17
  383.8 59.4 all-gather.19
  445.9 52.8 all-gather.21
  501.6 62.7 all-gather.23
  567.2 62.4 all-gather.25
  976.1 123.2 all-reduce.5
  1105.1 130.1 reduce-scatter.13
  1242.0 144.2 reduce-scatter.21
  1392.4 117.5 reduce-scatter.11
  1517.2 118.4 reduce-scatter.19
  1642.0 134.6 reduce-scatter.15
  1784.0 134.7 reduce-scatter.17
  1925.2 134.5 reduce-scatter.23
  2067.1 134.6 reduce-scatter.25
where the time goes:
time: 2220 us; the launch traced here: 2210 us
  waiting for transfers between devices  1220 us (55%)
  blocking collectives  366 us (16%)
  matrix products  309 us (14%)
  local copies, waits for them, and re-layouts  175 us (8%)
  other arithmetic  93.4 us (4%)
  starting transfers between devices  26.4 us (1%)
    all_to_all x2, waiting for transfers between devices, redeal(): lax.all_to_all(stacked, ('dp', 'fsdp'), split_axis=2, concat_axis=1, tile...  297 us
    all_gather x1, blocking collectives, shards(): lax.all_gather(seg_vec, ('dp', 'fsdp'), axis=1, tiled=True)  234 us
    reduce_scatter x1, waiting for transfers between devices, shards(): lax.psum_scatter(seg_grads[3], ('dp', 'fsdp'), scatter_dimension=0, tiled...  142 us
    reduce_scatter x1, waiting for transfers between devices, shards(): lax.psum_scatter(cross_grads[3], ('dp', 'fsdp'), scatter_dimension=0, til...  142 us
    reduce_scatter x1, waiting for transfers between devices, shards(): lax.psum_scatter(seg_grads[2], ('dp', 'fsdp'), scatter_dimension=0, tiled...  141 us
    reduce_scatter x1, waiting for transfers between devices, shards(): lax.psum_scatter(cross_grads[2], ('dp', 'fsdp'), scatter_dimension=0, til...  141 us
    all_to_all x2, waiting for transfers between devices, redeal(): lax.all_to_all(picked, ('dp', 'fsdp'), split_axis=1, concat_axis=2, tiled...  138 us
    reduce_scatter x1, waiting for transfers between devices, shards(): lax.psum_scatter(cross_grads[0], ('dp', 'fsdp'), scatter_dimension=0, til...  126 us
  transfers between devices with their start and end apart: 21, of which 9 were waited for; matrix products, arithmetic and copies ran while one was open for 17% of the time, Pallas kernels for 0%

commit v1 on v0

--- a/solution.py
+++ b/solution.py
@@ -182,28 +182,6 @@
     return (grad_inputs, (grad_qkv_w, grad_out_w, grad_up_w, grad_down_w, grad_vectors))
 
 
-def deal_tables(lengths, seq_len, seq_local):
-    seq_total = lengths.shape[0]
-    seq_ids = jnp.arange(seq_total, dtype=jnp.int32)
-    ranking = (seq_len - lengths) * seq_total + seq_ids
-    rank_of = jnp.sum((ranking[None, :] < ranking[:, None]).astype(jnp.int32), axis=1)
-    device_count = seq_total // seq_local
-    rounds = rank_of // device_count
-    column = rank_of % device_count
-    device_pick = jnp.where(rounds % 2 == 0, column, device_count - 1 - column)
-    placed_at = device_pick * seq_local + rounds
-    dealing = jnp.sum(
-        jnp.where(placed_at[None, :] == seq_ids[:, None], seq_ids[None, :], 0), axis=1
-    )
-    return (dealing, placed_at)
-
-
-def redeal(stacked, index):
-    spread = lax.all_to_all(stacked, ("dp", "fsdp"), split_axis=2, concat_axis=1, tiled=True)
-    picked = jnp.take(spread, index, axis=1)
-    return lax.all_to_all(picked, ("dp", "fsdp"), split_axis=1, concat_axis=2, tiled=True)
-
-
 def unpack(gathered):
     seg_weights = (
         gathered[0],
@@ -254,12 +232,9 @@
     seg_weights, cross_weights, pos_table = unpack(gathered)
     seq_local, seq_len, feat_dim = tokens.shape
     seg_count = seq_len // SEG
-    dealing, inverse = deal_tables(lengths, seq_len, seq_local)
     first_pos = lax.axis_index(("dp", "fsdp")) * seq_local
-    my_seqs = lax.dynamic_slice_in_dim(dealing, first_pos, seq_local)
-    my_lengths = jnp.take(lengths, my_seqs)
-    arrived = redeal(jnp.stack([tokens, cotangent]), dealing)
-    dealt_rows = arrived[0].reshape(-1, feat_dim)
+    my_lengths = lax.dynamic_slice_in_dim(lengths, first_pos, seq_local)
+    dealt_rows = tokens.reshape(-1, feat_dim)
     token_pos = jnp.arange(seq_len)
     live_mask = token_pos[None, :] < my_lengths[:, None]
     seg_opens = token_pos % SEG == 0
@@ -275,21 +250,7 @@
         [cross_result.reshape(seq_local, seg_count, 1, feat_dim), seg_grid[:, :, 1:, :]], axis=2
     )
     layer_out = (merged.reshape(seq_local, seq_len, feat_dim) * live_float).astype(jnp.bfloat16)
-    gathered = (
-        lax.all_gather(seg_qkv, ("dp", "fsdp"), axis=0, tiled=True),
-        lax.all_gather(seg_out, ("dp", "fsdp"), axis=0, tiled=True),
-        lax.all_gather(seg_up, ("dp", "fsdp"), axis=0, tiled=True),
-        lax.all_gather(seg_down, ("dp", "fsdp"), axis=0, tiled=True),
-        lax.all_gather(seg_vec, ("dp", "fsdp"), axis=1, tiled=True),
-        lax.all_gather(cross_qkv, ("dp", "fsdp"), axis=0, tiled=True),
-        lax.all_gather(cross_out, ("dp", "fsdp"), axis=0, tiled=True),
-        lax.all_gather(cross_up, ("dp", "fsdp"), axis=0, tiled=True),
-        lax.all_gather(cross_down, ("dp", "fsdp"), axis=0, tiled=True),
-        lax.all_gather(cross_vec, ("dp", "fsdp"), axis=1, tiled=True),
-        lax.all_gather(positions, ("dp", "fsdp"), axis=1, tiled=True),
-    )
-    seg_weights, cross_weights, pos_table = unpack(gathered)
-    grad_grid = (arrived[1].astype(jnp.float32) * live_float).reshape(
+    grad_grid = (cotangent.astype(jnp.float32) * live_float).reshape(
         seq_local, seg_count, SEG, feat_dim
     )
     cross_up_grad = grad_grid[:, :, 0, :].reshape(-1, feat_dim)
@@ -304,22 +265,21 @@
     rows_grad, seg_grads = encode_back(seg_up_grad, dealt_rows, seg_weights, keys_ok, seg_kept)
     token_grad = rows_grad.reshape(seq_local, seq_len, feat_dim).astype(jnp.bfloat16)
     summed = (
-        lax.psum_scatter(seg_grads[0], ("dp", "fsdp"), scatter_dimension=0, tiled=True),
-        lax.psum_scatter(seg_grads[1], ("dp", "fsdp"), scatter_dimension=0, tiled=True),
-        lax.psum_scatter(seg_grads[2], ("dp", "fsdp"), scatter_dimension=0, tiled=True),
-        lax.psum_scatter(seg_grads[3], ("dp", "fsdp"), scatter_dimension=0, tiled=True),
+        lax.psum_scatter(seg_grads[0].astype(jnp.bfloat16), ("dp", "fsdp"), scatter_dimension=0, tiled=True).astype(jnp.float32),
+        lax.psum_scatter(seg_grads[1].astype(jnp.bfloat16), ("dp", "fsdp"), scatter_dimension=0, tiled=True).astype(jnp.float32),
+        lax.psum_scatter(seg_grads[2].astype(jnp.bfloat16), ("dp", "fsdp"), scatter_dimension=0, tiled=True).astype(jnp.float32),
+        lax.psum_scatter(seg_grads[3].astype(jnp.bfloat16), ("dp", "fsdp"), scatter_dimension=0, tiled=True).astype(jnp.float32),
         lax.psum_scatter(seg_grads[4], ("dp", "fsdp"), scatter_dimension=1, tiled=True),
-        lax.psum_scatter(cross_grads[0], ("dp", "fsdp"), scatter_dimension=0, tiled=True),
-        lax.psum_scatter(cross_grads[1], ("dp", "fsdp"), scatter_dimension=0, tiled=True),
-        lax.psum_scatter(cross_grads[2], ("dp", "fsdp"), scatter_dimension=0, tiled=True),
-        lax.psum_scatter(cross_grads[3], ("dp", "fsdp"), scatter_dimension=0, tiled=True),
+        lax.psum_scatter(cross_grads[0].astype(jnp.bfloat16), ("dp", "fsdp"), scatter_dimension=0, tiled=True).astype(jnp.float32),
+        lax.psum_scatter(cross_grads[1].astype(jnp.bfloat16), ("dp", "fsdp"), scatter_dimension=0, tiled=True).astype(jnp.float32),
+        lax.psum_scatter(cross_grads[2].astype(jnp.bfloat16), ("dp", "fsdp"), scatter_dimension=0, tiled=True).astype(jnp.float32),
+        lax.psum_scatter(cross_grads[3].astype(jnp.bfloat16), ("dp", "fsdp"), scatter_dimension=0, tiled=True).astype(jnp.float32),
         lax.psum_scatter(cross_grads[4], ("dp", "fsdp"), scatter_dimension=1, tiled=True),
         lax.psum_scatter(grad_positions, ("dp", "fsdp"), scatter_dimension=1, tiled=True),
     )
-    home = redeal(jnp.stack([layer_out, token_grad]), inverse)
     return (
-        home[0],
-        home[1],
+        layer_out,
+        token_grad,
         summed[0],
         summed[1],
         summed[2],

time: 2220 us -> 1670 us (0.75)
  waiting for transfers between devices: 1220 us -> 993 us
  blocking collectives: 366 us -> 203 us
  local copies, waits for them, and re-layouts: 175 us -> 94.3 us
  other arithmetic: 93.4 us -> 57.4 us
  starting transfers between devices: 26.4 us -> 0.89 us
    all_to_all x4 -> x0, waiting for transfers between devices: 434 us -> none  [the longest x2 297 us: redeal(): lax.all_to_all(stacked, ('dp', 'fsdp'), split_axis=2, concat_axis=1, tile...]
    all_gather x1, blocking collectives: 234 us -> 71.4 us  [shards(): lax.all_gather(seg_vec, ('dp', 'fsdp'), axis=1, tiled=True)]
    unnamed x18 -> x19, waiting for transfers between devices: 5.2 us -> 143 us
    all_gather x1, waiting for transfers between devices: 0.01 us -> 62.1 us  [shards(): lax.all_gather(cross_down, ('dp', 'fsdp'), axis=0, tiled=True)]
    all_gather x1, waiting for transfers between devices: 0.01 us -> 45 us  [shards(): lax.all_gather(cross_up, ('dp', 'fsdp'), axis=0, tiled=True)]
    reduce_scatter x8 -> x7, waiting for transfers between devices: 783 us -> 742 us  [the longest x1 111 us: shards(): lax.psum_scatter(seg_grads[2].astype(jnp.bfloat16), ('dp', 'fsdp'), scatt...]
    all_to_all x4 -> x0, starting transfers between devices: 25.6 us -> none  [the longest x2 14.4 us: redeal(): lax.all_to_all(picked, ('dp', 'fsdp'), split_axis=1, concat_axis=2, tiled...]
    unnamed x239 -> x166, local copies, waits for them, and re-layouts: 49.9 us -> 43.7 us
  transfers between devices with their start and end apart: 21 -> 17, of which waited for: 9 -> 11; matrix products, arithmetic and copies ran while one was open for 17% -> 17% of each run, Pallas kernels for 0% -> 0%
where the time goes in v1:
time: 1670 us; the launch traced here: 1660 us
  waiting for transfers between devices  993 us (59%)
  matrix products  297 us (18%)
  blocking collectives  203 us (12%)
  local copies, waits for them, and re-layouts  94.3 us (6%)
  other arithmetic  57.4 us (3%)
    unnamed x19, waiting for transfers between devices  143 us
    dot_general x8, matrix products, matmul(): return jnp.dot(left_op, right_op, preferred_element_type=jnp.float32)  115 us
    reduce_scatter x1, waiting for transfers between devices, shards(): lax.psum_scatter(seg_grads[2].astype(jnp.bfloat16), ('dp', 'fsdp'), scatt...  111 us
    reduce_scatter x1, waiting for transfers between devices, shards(): lax.psum_scatter(cross_grads[3].astype(jnp.bfloat16), ('dp', 'fsdp'), sca...  111 us
    reduce_scatter x1, waiting for transfers between devices, shards(): lax.psum_scatter(seg_grads[3].astype(jnp.bfloat16), ('dp', 'fsdp'), scatt...  110 us
    reduce_scatter x1, waiting for transfers between devices, shards(): lax.psum_scatter(cross_grads[2].astype(jnp.bfloat16), ('dp', 'fsdp'), sca...  110 us
    reduce_scatter x1, waiting for transfers between devices, shards(): lax.psum_scatter(cross_grads[0].astype(jnp.bfloat16), ('dp', 'fsdp'), sca...  105 us
    reduce_scatter x1, waiting for transfers between devices, shards(): lax.psum_scatter(seg_grads[1].astype(jnp.bfloat16), ('dp', 'fsdp'), scatt...  99 us
  transfers between devices with their start and end apart: 17, of which 11 were waited for; matrix products, arithmetic and copies ran while one was open for 17% of the time, Pallas kernels for 0%

profile of v1, /device:TPU:0, one launch (start us, length us, event | category | flops | bytes accessed | tf_op | source)
XLA Modules:
  0.0 1661.2 jit_solution(1623250501481351003)
XLA Ops:
  12.7 71.4 %all-gather = bf16[32,24,12]{1,2,0:T(8,128)(2,1)S(1)} all-gather(bf16[1,24,12]{1,2,0:T(8,128)(2,1)} %bitcast.227), channel_id=1, replica_groups=mesh['dp'=8,'fsdp'=4] {'dp','fsdp'}, dimensions={0}, use_global_device_ids=true | all-gather | bytes 19008 | tf_op jit(solution)/shard_map/all_gather | solution.py:224
  85.2 64.8 %all-gather.2 = bf16[32,24,12]{1,2,0:T(8,128)(2,1)S(1)} all-gather(bf16[1,24,12]{1,2,0:T(8,128)(2,1)} %bitcast.228), channel_id=1, replica_groups=mesh['dp'=8,'fsdp'=4] {'dp','fsdp'}, dimensions={0}, use_global_device_ids=true | all-gather | bytes 19008 | tf_op jit(solution)/shard_map/all_gather | solution.py:229
  152.1 66.8 %all-gather.1 = bf16[32,24,8]{1,2,0:T(8,128)(2,1)S(1)} all-gather(bf16[1,24,8]{1,2,0:T(8,128)(2,1)} %bitcast.229), channel_id=1, replica_groups=mesh['dp'=8,'fsdp'=4] {'dp','fsdp'}, dimensions={0}, use_global_device_ids=true | all-gather | bytes 12672 | tf_op jit(solution)/shard_map/all_gather | solution.py:230
  300.6 70.5 %fusion.2 = (bf16[2048,3072]{1,0:T(8,128)(2,1)}, f32[2048,3072]{1,0:T(8,128)}) fusion(f32[3072]{0:T(1024)S(1)} %add.290, bf16[768,3072]{1,0:T(8,128)(2,1)} %all-gather.16.cloned.1.call-done, f32[2048,768]{1,0:T(8,128)} %copy-done.4, f32[768]{0:T(1024)S(1)} %get-tuple-element.90, f32[768]{0:T(1024)S(1)} %get-tuple-element.91, f32[2048]{0:T(1024)S(1)} %add_rsqrt_fusion.1, ...), kind=kOutput, calls=%fused_computation.4 | convolution fusion | flops 10086776832 | bytes 48793600 | tf_op jit(solution)/shard_map/dot_general | solution.py:17
  371.1 15.9 fusion.136
  397.9 45.0 %all-gather.24.cloned.1.call-done = bf16[768,3072]{1,0:T(8,128)(2,1)} async-done(((bf16[24,3072]{1,0:T(8,128)(2,1)}), bf16[768,3072]{1,0:T(8,128)(2,1)}) %all-gather.24.cloned.1.call-update) | async-done | bytes 4718608 | tf_op jit(solution)/shard_map/all_gather | solution.py:227
  446.0 62.1 %all-gather.26.cloned.1.call-done = bf16[3072,768]{1,0:T(8,128)(2,1)} async-done(((bf16[96,768]{1,0:T(8,128)(2,1)}), bf16[3072,768]{1,0:T(8,128)(2,1)}) %all-gather.26.cloned.1.call-update) | async-done | bytes 4718608 | tf_op jit(solution)/shard_map/all_gather | solution.py:228
  530.3 27.2 %convert_reduce_fusion = (f32[3072]{0:T(1024)S(1)}, bf16[2048,3072]{1,0:T(8,128)(2,1)}) fusion(f32[2048,3072]{1,0:T(8,128)} %get-tuple-element.129, f32[3072]{0:T(1024)S(1)} %add.290, bf16[3072,768]{1,0:T(8,128)(2,1)} %all-gather.18.cloned.1.call-done, f32[2048,768]{1,0:T(8,128)S(1)} %get-tuple-element.103), kind=kOutput, calls=%fused_computation.11 | convolution fusion | flops 9747035136 | bytes 48783360 | tf_op jit(solution)/shard_map/dot_general | solution.py:27
  557.5 18.6 %multiply_reduce_fusion.1 = (f32[768]{0:T(1024)S(1)}, f32[2048]{0:T(1024)S(1)}, f32[2048]{0:T(1024)S(1)}, f32[768]{0:T(1024)S(1)}, f32[2048,768]{1,0:T(8,128)}) fusion(f32[2048,768]{1,0:T(8,128)S(1)} %bitcast.195, f32[2048]{0:T(1024)S(1)} %add_rsqrt_fusion.1, f32[2048]{0:T(1024)S(1)} %broadcast_multiply_fusion.4, f32[768]{0:T(1024)S(1)} %get-tuple-element.91, ...), kind=kOutput, calls=%fused_computation.46 | convolution fusion | flops 9679398912 | bytes 36217856 | tf_op jit(solution)/shard_map/dot_general | solution.py:27
  593.5 11.6 convert_bitcast_fusion
  605.1 14.6 multiply_reduce_fusion
  675.2 11.1 fusion.26
  698.1 18.3 %convolution_convert_fusion.1 = bf16[768,3072]{1,0:T(8,128)(2,1)} fusion(bf16[2048,3072]{1,0:T(8,128)(2,1)} %get-tuple-element.145, f32[2048,768]{1,0:T(8,128)} %copy-done.4, f32[768]{0:T(1024)S(1)} %copy-done.56, f32[768]{0:T(1024)S(1)} %copy-done.45, f32[2048]{0:T(1024)S(1)} %add_rsqrt_fusion.1, f32[2048]{0:T(1024)S(1)} %broadcast_multiply_fusion.4), kind=kOutput, calls=%fused_computation.71 | convolution fusion | flops 9673900032 | bytes 23615488 | tf_op jit(solution)/shard_map/dot_general | solution.py:21
  716.4 16.4 convolution_convert_fusion
  745.8 11.0 add_convert_fusion.1
  756.8 32.1 %all-reduce.6.cloned.1.call-done = (f32[12,768]{1,0:T(8,128)}, f32[12,768]{1,0:T(8,128)}, f32[8,768]{1,0:T(8,128)}) async-done(((f32[12,768]{1,0:T(8,128)}, f32[12,768]{1,0:T(8,128)}, f32[8,768]{1,0:T(8,128)}), (f32[12,768]{1,0:T(8,128)}, f32[12,768]{1,0:T(8,128)}, f32[8,768]{1,0:T(8,128)})) %all-reduce.6.cloned.1.call-update) | async-done | bytes 98320
  793.1 97.0 %reduce-scatter.22.cloned.1.call-done = bf16[24,768]{1,0:T(8,128)(2,1)} async-done(((bf16[768,768]{1,0:T(8,128)(2,1)}), bf16[24,768]{1,0:T(8,128)(2,1)}) %reduce-scatter.22.cloned.1.call-update) | async-done | bytes 36880 | tf_op jit(solution)/shard_map/reduce_scatter | solution.py:274
  891.5 99.0 %reduce-scatter.14.cloned.1.call-done = bf16[24,768]{1,0:T(8,128)(2,1)} async-done(((bf16[768,768]{1,0:T(8,128)(2,1)}), bf16[24,768]{1,0:T(8,128)(2,1)}) %reduce-scatter.14.cloned.1.call-update) | async-done | bytes 36880 | tf_op jit(solution)/shard_map/reduce_scatter | solution.py:269
  991.9 106.0 %reduce-scatter.28.cloned.1.call-done = bf16[24,2304]{1,0:T(8,128)(2,1)} async-done(((bf16[768,2304]{1,0:T(8,128)(2,1)}), bf16[24,2304]{1,0:T(8,128)(2,1)}) %reduce-scatter.28.cloned.1.call-update) | async-done | bytes 110608
  1100.1 105.3 %reduce-scatter.20.cloned.1.call-done = bf16[24,2304]{1,0:T(8,128)(2,1)} async-done(((bf16[768,2304]{1,0:T(8,128)(2,1)}), bf16[24,2304]{1,0:T(8,128)(2,1)}) %reduce-scatter.20.cloned.1.call-update) | async-done | bytes 110608 | tf_op jit(solution)/shard_map/reduce_scatter | solution.py:273
  1207.0 109.7 %reduce-scatter.24.cloned.1.call-done = bf16[24,3072]{1,0:T(8,128)(2,1)} async-done(((bf16[768,3072]{1,0:T(8,128)(2,1)}), bf16[24,3072]{1,0:T(8,128)(2,1)}) %reduce-scatter.24.cloned.1.call-update) | async-done | bytes 147472 | tf_op jit(solution)/shard_map/reduce_scatter | solution.py:275
  1318.3 110.7 %reduce-scatter.16.cloned.1.call-done = bf16[24,3072]{1,0:T(8,128)(2,1)} async-done(((bf16[768,3072]{1,0:T(8,128)(2,1)}), bf16[24,3072]{1,0:T(8,128)(2,1)}) %reduce-scatter.16.cloned.1.call-update) | async-done | bytes 147472 | tf_op jit(solution)/shard_map/reduce_scatter | solution.py:270
  1430.7 109.8 %reduce-scatter.18.cloned.1.call-done = bf16[96,768]{1,0:T(8,128)(2,1)} async-done(((bf16[3072,768]{1,0:T(8,128)(2,1)}), bf16[96,768]{1,0:T(8,128)(2,1)}) %reduce-scatter.18.cloned.1.call-update) | async-done | bytes 147472 | tf_op jit(solution)/shard_map/reduce_scatter | solution.py:271
  1542.1 110.7 %reduce-scatter.26.cloned.1.call-done = bf16[96,768]{1,0:T(8,128)(2,1)} async-done(((bf16[3072,768]{1,0:T(8,128)(2,1)}), bf16[96,768]{1,0:T(8,128)(2,1)}) %reduce-scatter.26.cloned.1.call-update) | async-done | bytes 147472 | tf_op jit(solution)/shard_map/reduce_scatter | solution.py:276
  (364 shorter events, 240.0 us)
Async XLA Ops:
  7.2 223.3 %all-gather.12.cloned.1.call-start = ((), (), s32[]{:S(2)}) async-start(), calls=%async_computation.8 | async-start | bytes 3649536 | tf_op jit(solution)/shard_map/all_gather | solution.py:220
  7.9 282.2 %all-gather.14.cloned.1.call-start = ((), (), s32[]{:S(2)}) async-start(), calls=%async_computation.9 | async-start | bytes 1216512 | tf_op jit(solution)/shard_map/all_gather | solution.py:221
  8.7 291.9 %all-gather.16.cloned.1.call-start = ((), (), s32[]{:S(2)}) async-start(), calls=%async_computation.10 | async-start | bytes 4866048 | tf_op jit(solution)/shard_map/all_gather | solution.py:222
  9.4 361.7 %all-gather.18.cloned.1.call-start = ((), (), s32[]{:S(2)}) async-start(), calls=%async_computation.11 | async-start | bytes 4866048 | tf_op jit(solution)/shard_map/all_gather | solution.py:223
  10.0 382.3 %all-gather.20.cloned.1.call-start = ((), (), s32[]{:S(2)}) async-start(), calls=%async_computation.12 | async-start | bytes 3649536 | tf_op jit(solution)/shard_map/all_gather | solution.py:225
  10.6 385.3 %all-gather.22.cloned.1.call-start = ((), (), s32[]{:S(2)}) async-start(), calls=%async_computation.13 | async-start | bytes 1216512 | tf_op jit(solution)/shard_map/all_gather | solution.py:226
  11.1 431.8 %all-gather.24.cloned.1.call-start = ((), (), s32[]{:S(2)}) async-start(), calls=%async_computation.14 | async-start | bytes 4866048 | tf_op jit(solution)/shard_map/all_gather | solution.py:227
  11.9 496.2 %all-gather.26.cloned.1.call-start = ((), (), s32[]{:S(2)}) async-start(), calls=%async_computation.15 | async-start | bytes 4866048 | tf_op jit(solution)/shard_map/all_gather | solution.py:228
  12.6 776.3 %all-reduce.6.cloned.1.call-start = ((), (), s32[]{:S(2)}) async-start(), calls=%async_computation.24 | async-start | bytes 245760
  85.2 285.9 %copy-start.55 = (f32[768]{0:T(1024)}, f32[768]{0:T(1024)S(1)}, u32[]{:S(2)}) copy-start(f32[768]{0:T(1024)S(1)} %get-tuple-element.90) | copy-start | bytes 9220
  85.2 490.9 %copy-start.44 = (f32[768]{0:T(1024)}, f32[768]{0:T(1024)S(1)}, u32[]{:S(2)}) copy-start(f32[768]{0:T(1024)S(1)} %get-tuple-element.91) | copy-start | bytes 9220
  389.6 118.5 %copy-start.57 = (f32[768]{0:T(1024)S(1)}, f32[768]{0:T(1024)}, u32[]{:S(2)}) copy-start(f32[768]{0:T(1024)} %get-tuple-element.81) | copy-start | bytes 9220
  397.6 118.2 %copy-start.17 = (f32[16,768]{1,0:T(8,128)}, f32[16,768]{1,0:T(8,128)S(1)}, u32[]{:S(2)}) copy-start(f32[16,768]{1,0:T(8,128)S(1)} %get-tuple-element.135) | copy-start | bytes 147460
  397.6 114.5 %copy-start.49 = (f32[768]{0:T(1024)S(1)}, f32[768]{0:T(1024)}, u32[]{:S(2)}) copy-start(f32[768]{0:T(1024)} %get-tuple-element.80) | copy-start | bytes 9220
  397.6 118.1 %copy-start.50 = (f32[16]{0:T(128)}, f32[16]{0:T(128)S(1)}, u32[]{:S(2)}) copy-start(f32[16]{0:T(128)S(1)} %broadcast_multiply_fusion.10) | copy-start | bytes 196
  397.8 117.9 %copy-start.53 = (f32[16]{0:T(128)}, f32[16]{0:T(128)S(1)}, u32[]{:S(2)}) copy-start(f32[16]{0:T(128)S(1)} %add_rsqrt_fusion.3) | copy-start | bytes 196
  667.1 223.0 %reduce-scatter.22.cloned.1.call-start = ((), (), s32[]{:S(2)}) async-start(), calls=%async_computation.20 | async-start | bytes 1216512 | tf_op jit(solution)/shard_map/reduce_scatter | solution.py:274
  668.7 321.8 %reduce-scatter.14.cloned.1.call-start = ((), (), s32[]{:S(2)}) async-start(), calls=%async_computation.16 | async-start | bytes 1216512 | tf_op jit(solution)/shard_map/reduce_scatter | solution.py:269
  675.2 422.7 %reduce-scatter.28.cloned.1.call-start = ((), (), s32[]{:S(2)}) async-start(), calls=%async_computation.23 | async-start | bytes 3649536
  690.3 515.0 %reduce-scatter.20.cloned.1.call-start = ((), (), s32[]{:S(2)}) async-start(), calls=%async_computation.19 | async-start | bytes 3649536 | tf_op jit(solution)/shard_map/reduce_scatter | solution.py:273
  694.2 622.4 %reduce-scatter.24.cloned.1.call-start = ((), (), s32[]{:S(2)}) async-start(), calls=%async_computation.21 | async-start | bytes 4866048 | tf_op jit(solution)/shard_map/reduce_scatter | solution.py:275
  698.0 731.0 %reduce-scatter.16.cloned.1.call-start = ((), (), s32[]{:S(2)}) async-start(), calls=%async_computation.17 | async-start | bytes 4866048 | tf_op jit(solution)/shard_map/reduce_scatter | solution.py:270
  716.4 824.1 %reduce-scatter.18.cloned.1.call-start = ((), (), s32[]{:S(2)}) async-start(), calls=%async_computation.18 | async-start | bytes 4866048 | tf_op jit(solution)/shard_map/reduce_scatter | solution.py:271
  732.8 920.0 %reduce-scatter.26.cloned.1.call-start = ((), (), s32[]{:S(2)}) async-start(), calls=%async_computation.22 | async-start | bytes 4866048 | tf_op jit(solution)/shard_map/reduce_scatter | solution.py:276
  (69 other events, 1372.1 us)
Sparse Core Ops, SparseCore 0:
  10.8 62.9 all-gather.11
  76.6 52.9 all-gather.13
  132.4 62.7 all-gather.15
  197.9 62.4 all-gather.17
  263.0 58.9 all-gather.19
  324.6 52.8 all-gather.21
  380.3 62.5 all-gather.23
  445.7 62.3 all-gather.25
  667.2 121.6 all-reduce.5
  793.9 96.1 reduce-scatter.21
  895.2 95.2 reduce-scatter.13
  995.8 102.0 reduce-scatter.27
  1103.3 101.9 reduce-scatter.19
  1210.7 105.9 reduce-scatter.23
  1322.9 106.0 reduce-scatter.15
  1434.3 106.0 reduce-scatter.17
  1546.7 106.0 reduce-scatter.25

commit v2 on v1

--- a/solution.py
+++ b/solution.py
@@ -1,3 +1,5 @@
+import functools
+
 import jax
 import jax.numpy as jnp
 from jax import lax
@@ -125,13 +127,10 @@
     group_len = allowed.shape[1]
     back_two, gain_two, shift_two = norm_backward(upstream, normed_two, scale_two, vectors[-2])
     down_grad = back_two.astype(jnp.bfloat16)
-    grad_down_w = trans_left(activated, down_grad)
     hidden_grad = (trans_right(down_grad, down_w) * gelu_slope(hidden)).astype(jnp.bfloat16)
-    grad_up_w = trans_left(first_low, hidden_grad)
     first_grad = trans_right(hidden_grad, up_w) + back_two
     back_one, gain_one, shift_one = norm_backward(first_grad, normed_one, scale_one, vectors[3])
     proj_grad = back_one.astype(jnp.bfloat16)
-    grad_out_w = trans_left(mixed, proj_grad)
     query_heads, key_heads, value_heads = split_heads(packed, group_len)
     mixed_grad = trans_right(proj_grad, out_w).astype(jnp.bfloat16).reshape(value_heads.shape)
     scores = masked_scores(query_heads, key_heads, allowed)
@@ -162,7 +161,6 @@
         ],
         axis=1,
     ).astype(jnp.bfloat16)
-    grad_qkv_w = trans_left(inputs_low, packed_grad)
     bias_grads = jnp.sum(packed_grad, axis=0, dtype=jnp.float32).reshape(3, feat_dim)
     grad_inputs = trans_right(packed_grad, qkv_w) + back_one
     grad_vectors = jnp.concatenate(
@@ -179,28 +177,132 @@
         ],
         axis=0,
     )
-    return (grad_inputs, (grad_qkv_w, grad_out_w, grad_up_w, grad_down_w, grad_vectors))
-
-
-def unpack(gathered):
-    seg_weights = (
-        gathered[0],
-        gathered[1],
-        gathered[2],
-        gathered[3],
-        gathered[4].astype(jnp.float32),
-    )
-    cross_weights = (
-        gathered[5],
-        gathered[6],
-        gathered[7],
-        gathered[8],
-        gathered[9].astype(jnp.float32),
-    )
-    return (seg_weights, cross_weights, gathered[10].astype(jnp.float32))
+    pairs = (
+        (inputs_low, packed_grad),
+        (mixed, proj_grad),
+        (first_low, hidden_grad),
+        (activated, down_grad),
+    )
+    return (grad_inputs, pairs, grad_vectors)
+
+AXES = ("dp", "fsdp")
+
+
+class Links:
+    def __init__(self, outer, inner):
+        self.outer, self.inner = outer, inner
+        self.place = lax.axis_index("dp")
+        self.z = lax.axis_index("fsdp")
+        self.bits = (self.place // 4, self.place // 2 % 2, self.place % 2)
+
+    def flip(self, value, mask):
+        pairs = [
+            (d * self.inner + z, (d ^ mask) * self.inner + z)
+            for d in range(self.outer)
+            for z in range(self.inner)
+        ]
+        return lax.ppermute(value, AXES, pairs)
+
+    def turn(self, value, step):
+        pairs = [
+            (d * self.inner + z, d * self.inner + (z + step) % self.inner)
+            for d in range(self.outer)
+            for z in range(self.inner)
+        ]
+        return lax.ppermute(value, AXES, pairs)
+
+    def gather_z(self, shard):
+        whole = jnp.zeros((self.inner,) + shard.shape, shard.dtype)
+        whole = lax.dynamic_update_index_in_dim(whole, shard, self.z, 0)
+        for step in range(1, self.inner):
+            came = self.turn(shard, step)
+            whole = lax.dynamic_update_index_in_dim(
+                whole, came, (self.z + self.inner - step) % self.inner, 0
+            )
+        return whole
+
+    def spread(self, block):
+        half = block.shape[0] // 2
+        by_x, by_y = self.flip(block, 2), self.flip(block, 4)
+        diag_a, diag_b = self.flip(by_y[:half], 2), self.flip(by_x[half:], 4)
+        mine = [block, by_x, by_y, diag_a, diag_b]
+        return mine, [self.flip(piece, 1) for piece in mine]
+
+    def assemble(self, pieces):
+        mine, theirs = pieces
+        block = mine[0]
+        half = block.shape[0] // 2
+        whole = jnp.zeros((8,) + block.shape, block.dtype)
+        for flip_c, side in ((0, mine), (1, theirs)):
+            for flip_yx, start, piece in (
+                (0, 0, side[0]), (2, 0, side[1]), (4, 0, side[2]), (6, 0, side[3]), (6, half, side[4]),
+            ):
+                where = (self.place ^ (flip_yx + flip_c), start) + (0,) * (block.ndim - 1)
+                whole = lax.dynamic_update_slice(whole, piece[None], where)
+        return whole
+
+    def gather_small(self, shard):
+        block = self.gather_z(shard)
+        whole = jnp.zeros((8,) + block.shape, block.dtype)
+        near = [(0, block)] + [(m, self.flip(block, m)) for m in (2, 4, 6)]
+        near += [(m + 1, self.flip(piece, 1)) for m, piece in near]
+        for mask, piece in near:
+            whole = lax.dynamic_update_index_in_dim(whole, piece, self.place ^ mask, 0)
+        return whole.reshape((-1,) + shard.shape)
+
+    def scatter_sum(self, parts):
+        outer, inner, rows, cols = parts.shape
+        grid = parts.astype(jnp.bfloat16).reshape(2, 2, 2, inner, rows, cols)
+        y, x, c = self.bits
+
+        def pick(array, index, axis):
+            return lax.dynamic_index_in_dim(array, index, axis, keepdims=False)
+
+        def add(*terms):
+            return sum(t.astype(jnp.float32) for t in terms).astype(jnp.bfloat16)
+
+        came = self.flip(pick(grid, 1 - c, 2), 1)
+        grid = add(pick(grid, c, 2), came)
+        near_y, far_y = pick(grid, y, 0), pick(grid, 1 - y, 0)
+        own, to_x = pick(near_y, x, 0), pick(near_y, 1 - x, 0)
+        to_y, to_d = pick(far_y, x, 0), pick(far_y, 1 - x, 0)
+        half = inner // 2
+        came_x, came_y = self.flip(to_d[:half], 2), self.flip(to_d[half:], 4)
+        to_y = jnp.concatenate([add(to_y[:half], came_x), to_y[half:]])
+        to_x = jnp.concatenate([to_x[:half], add(to_x[half:], came_y)])
+        own = add(own, self.flip(to_x, 2), self.flip(to_y, 4))
+        total = pick(own, self.z, 0).astype(jnp.float32)
+        for step in range(1, inner):
+            sent = pick(own, (self.z + step) % inner, 0)
+            total = total + self.turn(sent, step).astype(jnp.float32)
+        return total
+
+
+class PlainLinks:
+    def __init__(self, outer, inner):
+        self.outer, self.inner = outer, inner
+        self.place = lax.axis_index("dp")
+        self.z = lax.axis_index("fsdp")
+
+    def gather_small(self, shard):
+        return lax.all_gather(shard, AXES, axis=0)
+
+    def scatter_sum(self, parts):
+        rows, cols = parts.shape[2:]
+        flat = parts.astype(jnp.bfloat16).reshape(-1, cols)
+        return lax.psum_scatter(flat, AXES, scatter_dimension=0, tiled=True).astype(jnp.float32)
+
+
+def gather_matrices(links, matrices):
+    if isinstance(links, PlainLinks):
+        return [lax.all_gather(m, AXES, axis=0, tiled=True) for m in matrices]
+    blocks = [links.gather_z(m) for m in matrices]
+    return [links.assemble(links.spread(b)).reshape(-1, b.shape[-1]) for b in blocks]
 
 
 def shards(
+    outer,
+    inner,
     tokens,
     cotangent,
     lengths,
@@ -216,82 +318,77 @@
     cross_vec,
     positions,
 ):
-    gathered = (
-        lax.all_gather(seg_qkv, ("dp", "fsdp"), axis=0, tiled=True),
-        lax.all_gather(seg_out, ("dp", "fsdp"), axis=0, tiled=True),
-        lax.all_gather(seg_up, ("dp", "fsdp"), axis=0, tiled=True),
-        lax.all_gather(seg_down, ("dp", "fsdp"), axis=0, tiled=True),
-        lax.all_gather(seg_vec, ("dp", "fsdp"), axis=1, tiled=True),
-        lax.all_gather(cross_qkv, ("dp", "fsdp"), axis=0, tiled=True),
-        lax.all_gather(cross_out, ("dp", "fsdp"), axis=0, tiled=True),
-        lax.all_gather(cross_up, ("dp", "fsdp"), axis=0, tiled=True),
-        lax.all_gather(cross_down, ("dp", "fsdp"), axis=0, tiled=True),
-        lax.all_gather(cross_vec, ("dp", "fsdp"), axis=1, tiled=True),
-        lax.all_gather(positions, ("dp", "fsdp"), axis=1, tiled=True),
-    )
-    seg_weights, cross_weights, pos_table = unpack(gathered)
+    links = (Links if (outer, inner) == (8, 4) else PlainLinks)(outer, inner)
+    devices = outer * inner
+    me = links.place * inner + links.z
     seq_local, seq_len, feat_dim = tokens.shape
     seg_count = seq_len // SEG
-    first_pos = lax.axis_index(("dp", "fsdp")) * seq_local
+    seg_rows, cross_rows = seg_vec.shape[0], cross_vec.shape[0]
+    small = jnp.concatenate([seg_vec, cross_vec, positions])
+    small = links.gather_small(small.reshape(1, -1))
+    small = small.reshape((devices,) + (seg_rows + cross_rows + seg_count, seg_vec.shape[1]))
+    small = small.transpose(1, 0, 2).reshape(-1, feat_dim).astype(jnp.float32)
+    seg_v, cross_v = small[:seg_rows], small[seg_rows : seg_rows + cross_rows]
+    pos_table = small[seg_rows + cross_rows :]
+    seg_weights = gather_matrices(links, [seg_qkv, seg_out, seg_up, seg_down]) + [seg_v]
+    cross_weights = gather_matrices(links, [cross_qkv, cross_out, cross_up, cross_down]) + [cross_v]
+    first_pos = me * seq_local
     my_lengths = lax.dynamic_slice_in_dim(lengths, first_pos, seq_local)
-    dealt_rows = tokens.reshape(-1, feat_dim)
+    rows_in = tokens.reshape(-1, feat_dim)
     token_pos = jnp.arange(seq_len)
     live_mask = token_pos[None, :] < my_lengths[:, None]
     seg_opens = token_pos % SEG == 0
     keys_ok = (live_mask | seg_opens[None, :]).reshape(-1, SEG)
-    seg_live = (jnp.arange(seg_count) * SEG)[None, :] < my_lengths[:, None]
     live_float = live_mask[..., None].astype(jnp.float32)
-    seg_result, seg_kept = encode(dealt_rows, dealt_rows, seg_weights, keys_ok)
+    seg_result, seg_kept = encode(rows_in, rows_in, seg_weights, keys_ok)
     seg_grid = seg_result.reshape(seq_local, seg_count, SEG, feat_dim)
-    heads_in = (seg_grid[:, :, 0, :] + pos_table[None]).reshape(-1, feat_dim)
-    heads_low = heads_in.astype(jnp.bfloat16)
-    cross_result, cross_kept = encode(heads_in, heads_low, cross_weights, seg_live)
-    merged = jnp.concatenate(
-        [cross_result.reshape(seq_local, seg_count, 1, feat_dim), seg_grid[:, :, 1:, :]], axis=2
-    )
-    layer_out = (merged.reshape(seq_local, seq_len, feat_dim) * live_float).astype(jnp.bfloat16)
     grad_grid = (cotangent.astype(jnp.float32) * live_float).reshape(
         seq_local, seg_count, SEG, feat_dim
     )
-    cross_up_grad = grad_grid[:, :, 0, :].reshape(-1, feat_dim)
-    heads_grad, cross_grads = encode_back(
-        cross_up_grad, heads_low, cross_weights, seg_live, cross_kept
-    )
-    heads_grid = heads_grad.reshape(seq_local, seg_count, feat_dim)
-    grad_positions = jnp.sum(heads_grid, axis=0)
+    heads_own = (seg_grid[:, :, 0, :]).reshape(-1, feat_dim)
+    up_own = grad_grid[:, :, 0, :].reshape(-1, feat_dim).astype(jnp.bfloat16)
+    heads_all = links.gather_small(heads_own.astype(jnp.bfloat16)).reshape(-1, feat_dim)
+    up_all = links.gather_small(up_own).reshape(-1, feat_dim).astype(jnp.float32)
+    heads_in = (heads_all.astype(jnp.float32).reshape(-1, seg_count, feat_dim) + pos_table[None]).reshape(-1, feat_dim)
+    heads_low = heads_in.astype(jnp.bfloat16)
+    live_all = (jnp.arange(seg_count) * SEG)[None, :] < lengths[:, None]
+    cross_result, cross_kept = encode(heads_in, heads_low, cross_weights, live_all)
+    heads_grad, pairs, cross_vec_grad = encode_back(
+        up_all, heads_low, cross_weights, live_all, cross_kept
+    )
+    cross_grads = []
+    for left, right in pairs:
+        width = left.shape[1] // devices
+        mine = lax.dynamic_slice_in_dim(left, me * width, width, 1)
+        cross_grads.append(trans_left(mine, right))
+    grad_positions = jnp.sum(heads_grad.reshape(-1, seg_count, feat_dim), axis=0)
+    width = feat_dim // devices
+    cross_vec_grad = lax.dynamic_slice_in_dim(cross_vec_grad, me * width, width, 1)
+    grad_positions = lax.dynamic_slice_in_dim(grad_positions, me * width, width, 1)
+    own_rows = seq_local * seg_count
+    cross_own = lax.dynamic_slice_in_dim(cross_result, me * own_rows, own_rows)
+    heads_grid = lax.dynamic_slice_in_dim(heads_grad, me * own_rows, own_rows).reshape(
+        seq_local, seg_count, feat_dim
+    )
+    merged = jnp.concatenate(
+        [cross_own.reshape(seq_local, seg_count, 1, feat_dim), seg_grid[:, :, 1:, :]], axis=2
+    )
+    layer_out = (merged.reshape(seq_local, seq_len, feat_dim) * live_float).astype(jnp.bfloat16)
     seg_up_grad = jnp.concatenate(
         [heads_grid[:, :, None, :], grad_grid[:, :, 1:, :]], axis=2
     ).reshape(-1, feat_dim)
-    rows_grad, seg_grads = encode_back(seg_up_grad, dealt_rows, seg_weights, keys_ok, seg_kept)
+    rows_grad, pairs, seg_vec_grad = encode_back(seg_up_grad, rows_in, seg_weights, keys_ok, seg_kept)
     token_grad = rows_grad.reshape(seq_local, seq_len, feat_dim).astype(jnp.bfloat16)
-    summed = (
-        lax.psum_scatter(seg_grads[0].astype(jnp.bfloat16), ("dp", "fsdp"), scatter_dimension=0, tiled=True).astype(jnp.float32),
-        lax.psum_scatter(seg_grads[1].astype(jnp.bfloat16), ("dp", "fsdp"), scatter_dimension=0, tiled=True).astype(jnp.float32),
-        lax.psum_scatter(seg_grads[2].astype(jnp.bfloat16), ("dp", "fsdp"), scatter_dimension=0, tiled=True).astype(jnp.float32),
-        lax.psum_scatter(seg_grads[3].astype(jnp.bfloat16), ("dp", "fsdp"), scatter_dimension=0, tiled=True).astype(jnp.float32),
-        lax.psum_scatter(seg_grads[4], ("dp", "fsdp"), scatter_dimension=1, tiled=True),
-        lax.psum_scatter(cross_grads[0].astype(jnp.bfloat16), ("dp", "fsdp"), scatter_dimension=0, tiled=True).astype(jnp.float32),
-        lax.psum_scatter(cross_grads[1].astype(jnp.bfloat16), ("dp", "fsdp"), scatter_dimension=0, tiled=True).astype(jnp.float32),
-        lax.psum_scatter(cross_grads[2].astype(jnp.bfloat16), ("dp", "fsdp"), scatter_dimension=0, tiled=True).astype(jnp.float32),
-        lax.psum_scatter(cross_grads[3].astype(jnp.bfloat16), ("dp", "fsdp"), scatter_dimension=0, tiled=True).astype(jnp.float32),
-        lax.psum_scatter(cross_grads[4], ("dp", "fsdp"), scatter_dimension=1, tiled=True),
-        lax.psum_scatter(grad_positions, ("dp", "fsdp"), scatter_dimension=1, tiled=True),
-    )
-    return (
-        layer_out,
-        token_grad,
-        summed[0],
-        summed[1],
-        summed[2],
-        summed[3],
-        summed[4],
-        summed[5],
-        summed[6],
-        summed[7],
-        summed[8],
-        summed[9],
-        summed[10],
-    )
+    seg_grads = []
+    for left, right in pairs:
+        whole = trans_left(left, right)
+        seg_grads.append(
+            links.scatter_sum(whole.reshape(outer, inner, -1, whole.shape[1]))
+        )
+    vec_parts = seg_vec_grad.reshape(seg_rows, devices, width).transpose(1, 0, 2)
+    vec_parts = vec_parts.reshape(outer, inner, 1, seg_rows * width)
+    seg_vec_sum = links.scatter_sum(vec_parts).reshape(seg_rows, width)
+    return (layer_out, token_grad, *seg_grads, seg_vec_sum, *cross_grads, cross_vec_grad, grad_positions)
 
 
 def solution(mesh):
@@ -326,4 +423,6 @@
         P(None, ("dp", "fsdp")),
         P(None, ("dp", "fsdp")),
     )
-    return jax.shard_map(shards, mesh=mesh, in_specs=in_specs, out_specs=out_specs, check_vma=False)
+    return jax.shard_map(
+        functools.partial(shards, mesh.shape["dp"], mesh.shape["fsdp"]),
+        mesh=mesh, in_specs=in_specs, out_specs=out_specs, check_vma=False)

time: 1670 us -> 1080 us (0.65)
  waiting for transfers between devices: 993 us -> 230 us
  blocking collectives: 203 us -> 0 us
  local copies, waits for them, and re-layouts: 94.3 us -> 266 us
  starting transfers between devices: 0.89 us -> 158 us
  matrix products: 297 us -> 331 us
  other arithmetic: 57.4 us -> 82.1 us
    reduce_scatter x7 -> x0, waiting for transfers between devices: 742 us -> none  [the longest x1 111 us: shards(): lax.psum_scatter(seg_grads[2].astype(jnp.bfloat16), ('dp', 'fsdp'), scatt...]
    ppermute x0 -> x166, waiting for transfers between devices: none -> 230 us  [the longest x118 187 us: flip(): return lax.ppermute(value, AXES, pairs)]
    all_gather x3 -> x0, blocking collectives: 203 us -> none  [the longest x1 71.4 us: shards(): lax.all_gather(seg_vec, ('dp', 'fsdp'), axis=1, tiled=True)]
    ppermute x0 -> x166, starting transfers between devices: none -> 158 us  [the longest x118 80.6 us: flip(): return lax.ppermute(value, AXES, pairs)]
    unnamed x19 -> x0, waiting for transfers between devices: 143 us -> none
    all_gather x8 -> x0, waiting for transfers between devices: 107 us -> none  [the longest x1 62.1 us: shards(): lax.all_gather(cross_down, ('dp', 'fsdp'), axis=0, tiled=True)]
    dynamic_update_slice x0 -> x148, local copies, waits for them, and re-layouts: none -> 94.5 us  [the longest x80 70.1 us: assemble(): whole = lax.dynamic_update_slice(whole, piece[None], where)]
    unnamed x166 -> x312, local copies, waits for them, and re-layouts: 43.7 us -> 34.7 us
  transfers between devices with their start and end apart: 17 -> 166, of which waited for: 11 -> 80; matrix products, arithmetic and copies ran while one was open for 17% -> 31% of each run, Pallas kernels for 0% -> 0%
where the time goes in v2:
time: 1080 us; the launch traced here: 1070 us
  matrix products  331 us (31%)
  local copies, waits for them, and re-layouts  266 us (25%)
  waiting for transfers between devices  230 us (21%)
  starting transfers between devices  158 us (15%)
  other arithmetic  82.1 us (8%)
    ppermute x118, waiting for transfers between devices, flip(): return lax.ppermute(value, AXES, pairs)  187 us
    dot_general x8, matrix products, matmul(): return jnp.dot(left_op, right_op, preferred_element_type=jnp.float32)  128 us
    ppermute x118, starting transfers between devices, flip(): return lax.ppermute(value, AXES, pairs)  80.6 us
    dot_general x8, matrix products, trans_right(): lax.dot_general(left_op, right_op, (((1,), (1,)), ((), ())), preferred_el...  78.8 us
    ppermute x48, starting transfers between devices, turn(): return lax.ppermute(value, AXES, pairs)  77.3 us
    dynamic_update_slice x80, local copies, waits for them, and re-layouts, assemble(): whole = lax.dynamic_update_slice(whole, piece[None], where)  70.1 us
    dot_general x8, matrix products, trans_left(): lax.dot_general(left_op, right_op, (((0,), (0,)), ((), ())), preferred_el...  56.7 us
    ppermute x48, waiting for transfers between devices, turn(): return lax.ppermute(value, AXES, pairs)  42.7 us
  transfers between devices with their start and end apart: 166, of which 80 were waited for; matrix products, arithmetic and copies ran while one was open for 31% of the time, Pallas kernels for 0%

profile of v2, /device:TPU:0, one launch (start us, length us, event | category | flops | bytes accessed | tf_op | source)
XLA Modules:
  0.0 1071.4 jit_solution(16564809223249149359)
XLA Ops:
  252.0 7.8 collective-permute-done.38
  275.5 11.4 %collective-permute-done.96 = bf16[4,24,3072]{2,1,0:T(8,128)(2,1)S(1)} collective-permute-done((bf16[4,24,3072]{2,1,0:T(8,128)(2,1)}, bf16[4,24,3072]{2,1,0:T(8,128)(2,1)S(1)}, u32[]{:S(2)}, u32[]{:S(2)}) %collective-permute-start.96) | collective-permute-done | bytes 589856 | tf_op jit(solution)/shard_map/ppermute | solution.py:204
  289.1 11.9 %collective-permute-done.95 = bf16[4,24,3072]{2,1,0:T(8,128)(2,1)S(1)} collective-permute-done((bf16[4,24,3072]{2,1,0:T(8,128)(2,1)}, bf16[4,24,3072]{2,1,0:T(8,128)(2,1)S(1)}, u32[]{:S(2)}, u32[]{:S(2)}) %collective-permute-start.95) | collective-permute-done | bytes 589856 | tf_op jit(solution)/shard_map/ppermute | solution.py:204
  303.3 10.9 %collective-permute-done.107 = bf16[4,96,768]{2,1,0:T(8,128)(2,1)S(1)} collective-permute-done((bf16[4,96,768]{2,1,0:T(8,128)(2,1)}, bf16[4,96,768]{2,1,0:T(8,128)(2,1)S(1)}, u32[]{:S(2)}, u32[]{:S(2)}) %collective-permute-start.107) | collective-permute-done | bytes 589856 | tf_op jit(solution)/shard_map/ppermute | solution.py:204
  317.8 8.7 collective-permute-done.108
  361.6 9.4 fusion.18
  420.7 7.4 collective-permute-done.40
  431.4 10.7 collective-permute-done.97
  477.2 67.6 %fusion.3 = (bf16[2048,3072]{1,0:T(8,128)(2,1)}, f32[2048,3072]{1,0:T(8,128)}) fusion(f32[3072]{0:T(1024)S(1)} %copy-done.112, bf16[768,3072]{1,0:T(8,128)(2,1)S(1)} %bitcast.743, f32[2048,768]{1,0:T(8,128)S(1)} %get-tuple-element.119, f32[768]{0:T(1024)S(1)} %copy-done.119, f32[768]{0:T(1024)S(1)} %copy-done.110, f32[2048]{0:T(1024)S(1)} %add_rsqrt_fusion.1, ...), kind=kOutput, calls=%fused_computation.5 | convolution fusion | flops 10086776832 | bytes 48793600 | tf_op jit(solution)/shard_map/dot_general | solution.py:19
  547.3 15.3 %fusion.208 = (f32[2048]{0:T(1024)S(1)}, f32[2048,768]{1,0:T(8,128)S(1)}) fusion(f32[768]{0:T(1024)S(1)} %copy-done.123, bf16[2048,3072]{1,0:T(8,128)(2,1)} %get-tuple-element.120, bf16[3072,768]{1,0:T(8,128)(2,1)S(1)} %bitcast.745, f32[768]{0:T(1024)S(1)} %copy-done.119, f32[768]{0:T(1024)S(1)} %copy-done.110, f32[2048]{0:T(1024)S(1)} %add_rsqrt_fusion.1, ...), kind=kOutput, calls=%fused_computation.591 | convolution fusion | flops 9674684416 | bytes 29918208 | tf_op jit(solution)/shard_map/dot_general | solution.py:19
  620.7 18.8 %fusion.22 = (bf16[512,3072]{1,0:T(8,128)(2,1)S(1)}, f32[512,3072]{1,0:T(8,128)S(1)}) fusion(f32[3072]{0:T(1024)S(1)} %copy-done.114, bf16[512,768]{1,0:T(8,128)(2,1)S(1)} %fusion.88, bf16[768,3072]{1,0:T(8,128)(2,1)} %bitcast.149), kind=kOutput, calls=%fused_computation.41 | convolution fusion | flops 2519728128 | bytes 14954496 | tf_op jit(solution)/shard_map/dot_general | solution.py:19
  648.6 7.4 convert_reduce_fusion
  656.0 7.2 multiply_reduce_fusion.8
  727.2 24.4 %fusion.211 = (bf16[3072]{0:T(1024)(128)(2,1)}, bf16[2048,3072]{1,0:T(8,128)(2,1)}) fusion(f32[2048,3072]{1,0:T(8,128)} %get-tuple-element.121, f32[3072]{0:T(1024)S(1)} %copy-done.113, bf16[3072,768]{1,0:T(8,128)(2,1)S(1)} %bitcast.748, f32[2048,768]{1,0:T(8,128)S(1)} %get-tuple-element.50), kind=kOutput, calls=%fused_computation.594 | convolution fusion | flops 9740743680 | bytes 48777216 | tf_op jit(solution)/shard_map/dot_general | solution.py:29
  751.7 19.2 %multiply_reduce_fusion.1 = (bf16[768]{0:T(1024)(128)(2,1)}, f32[2048]{0:T(1024)S(1)}, f32[2048]{0:T(1024)S(1)}, bf16[768]{0:T(1024)(128)(2,1)}, f32[2048,768]{1,0:T(8,128)}) fusion(f32[2048,768]{1,0:T(8,128)S(1)} %bitcast.716, f32[2048]{0:T(1024)S(1)} %copy-done.100, f32[2048]{0:T(1024)S(1)} %copy-done.92, f32[768]{0:T(1024)S(1)} %copy-done.111, ...), kind=kOutput, calls=%fused_computation.57 | convolution fusion | flops 9679398912 | bytes 36214784 | tf_op jit(solution)/shard_map/dot_general | solution.py:29
  788.3 11.7 %convert_bitcast_fusion = bf16[16,128,12,64]{1,3,2,0:T(8,128)(2,1)} fusion(f32[16,12,128]{2,1,0:T(8,128)S(1)} %copy-done.52, f32[16,12,128,128]{2,3,1,0:T(8,128)} %copy-done, pred[16,128]{1,0:T(8,128)(4,1)S(1)} %copy-done.102, bf16[16,128,12,64]{1,0,3,2:T(8,128)(2,1)} %bitcast.731), kind=kOutput, calls=%fused_computation.120 | convolution fusion | flops 416808960 | bytes 18974720 | tf_op jit(solution)/shard_map/nhqk,nqhd->nkhd/dot_general | solution.py:138
  800.0 14.8 %multiply_reduce_fusion = (f32[16,12,128]{2,1,0:T(8,128)S(1)}, f32[16,12,128,128]{2,3,1,0:T(8,128)}) fusion(f32[16,12,128]{2,1,0:T(8,128)S(1)} %copy-done.52, f32[16,12,128,128]{2,3,1,0:T(8,128)} %copy-done, pred[16,128]{1,0:T(8,128)(4,1)S(1)} %copy-done.102, bf16[16,128,12,64]{1,0,3,2:T(8,128)(2,1)} %bitcast.729, bf16[16,128,12,64]{1,0,3,2:T(8,128)(2,1)} %bitcast.732), kind=kOutput, calls=%fused_computation.29 | convolution fusion | flops 418357248 | bytes 31655936 | tf_op jit(solution)/shard_map/nqhd,nkhd->nhqk/dot_general | solution.py:144
  814.8 9.9 multiply_convert_fusion
  824.7 8.3 fusion.49
  835.7 16.5 %convolution_convert_fusion = bf16[3072,768]{1,0:T(8,128)(2,1)} fusion(bf16[2048,3072]{1,0:T(8,128)(2,1)} %get-tuple-element.120, f32[2048,768]{1,0:T(8,128)} %copy-done.18), kind=kOutput, calls=%fused_computation.95 | convolution fusion | flops 9667608576 | bytes 23592960 | tf_op jit(solution)/shard_map/dot_general | solution.py:23
  852.2 16.5 %convolution_convert_fusion.1 = bf16[768,3072]{1,0:T(8,128)(2,1)} fusion(bf16[2048,3072]{1,0:T(8,128)(2,1)} %get-tuple-element.135, f32[2048,768]{1,0:T(8,128)S(1)} %bitcast.718, f32[768]{0:T(1024)S(1)} %copy-done.120, f32[768]{0:T(1024)S(1)} %copy-done.111, f32[2048]{0:T(1024)S(1)} %copy-done.100, f32[2048]{0:T(1024)S(1)} %copy-done.92), kind=kOutput, calls=%fused_computation.96 | convolution fusion | flops 9673900032 | bytes 23615488 | tf_op jit(solution)/shard_map/dot_general | solution.py:23
  878.7 10.7 convolution_convert_fusion.2
  889.4 12.2 %add_convert_fusion.1 = bf16[2048,768]{1,0:T(8,128)(2,1)} fusion(f32[2048,768]{1,0:T(8,128)} %copy-done.17, bf16[2048,2304]{0,1:T(8,128)(2,1)S(1)} %bitcast_dynamic-update-slice_fusion, bf16[768,2304]{1,0:T(8,128)(2,1)} %bitcast.752), kind=kOutput, calls=%fused_computation.58 | convolution fusion | flops 7250903040 | bytes 22413312 | tf_op jit(solution)/shard_map/dot_general | solution.py:29
  1037.1 9.7 collective-permute-done.152
  (1043 shorter events, 719.1 us)
Async XLA Ops:
  0.6 100.6 %collective-permute-start = (bf16[24,2304]{1,0:T(8,128)(2,1)}, bf16[24,2304]{1,0:T(8,128)(2,1)S(1)}, u32[]{:S(2)}, u32[]{:S(2)}) collective-permute-start(bf16[24,2304]{1,0:T(8,128)(2,1)} %param.17), channel_id=1, source_target_pairs={{0,1},{1,2},{2,3},{3,0},{4,5},{5,6},{6,7},{7,4},{8,9},{9,10},{10,1... | collective-permute-start | bytes 331784 | tf_op jit(solution)/shard_map/ppermute | solution.py:212
  3.7 101.1 %collective-permute-start.1 = (bf16[24,2304]{1,0:T(8,128)(2,1)}, bf16[24,2304]{1,0:T(8,128)(2,1)S(1)}, u32[]{:S(2)}, u32[]{:S(2)}) collective-permute-start(bf16[24,2304]{1,0:T(8,128)(2,1)} %param.17), channel_id=1, source_target_pairs={{0,2},{1,3},{2,0},{3,1},{4,6},{5,7},{6,4},{7,5},{8,10},{9,11},{10,... | collective-permute-start | bytes 331784 | tf_op jit(solution)/shard_map/ppermute | solution.py:212
  34.7 71.3 %collective-permute-start.2 = (bf16[24,2304]{1,0:T(8,128)(2,1)S(1)}, bf16[24,2304]{1,0:T(8,128)(2,1)S(1)}, u32[]{:S(2)}, u32[]{:S(2)}) collective-permute-start(bf16[24,2304]{1,0:T(8,128)(2,1)S(1)} %copy-done.86), channel_id=1, source_target_pairs={{0,3},{1,0},{2,1},{3,2},{4,7},{5,4},{6,5},{7,6},{8,11},{9,8},{10,9... | collective-permute-start | bytes 331784 | tf_op jit(solution)/shard_map/ppermute | solution.py:212
  35.4 41.6 %collective-permute-start.22 = (bf16[24,768]{1,0:T(8,128)(2,1)S(1)}, bf16[24,768]{1,0:T(8,128)(2,1)S(1)}, u32[]{:S(2)}, u32[]{:S(2)}) collective-permute-start(bf16[24,768]{1,0:T(8,128)(2,1)S(1)} %copy-done.96), channel_id=1, source_target_pairs={{0,1},{1,2},{2,3},{3,0},{4,5},{5,6},{6,7},{7,4},{8,9},{9,10},{10,1... | collective-permute-start | bytes 110600 | tf_op jit(solution)/shard_map/ppermute | solution.py:212
  80.6 61.6 %collective-permute-start.34 = (bf16[24,3072]{1,0:T(8,128)(2,1)}, bf16[24,3072]{1,0:T(8,128)(2,1)S(1)}, u32[]{:S(2)}, u32[]{:S(2)}) collective-permute-start(bf16[24,3072]{1,0:T(8,128)(2,1)} %param.19), channel_id=1, source_target_pairs={{0,1},{1,2},{2,3},{3,0},{4,5},{5,6},{6,7},{7,4},{8,9},{9,10},{10,1... | collective-permute-start | bytes 442376 | tf_op jit(solution)/shard_map/ppermute | solution.py:212
  99.6 46.2 %collective-permute-start.35 = (bf16[24,3072]{1,0:T(8,128)(2,1)}, bf16[24,3072]{1,0:T(8,128)(2,1)S(1)}, u32[]{:S(2)}, u32[]{:S(2)}) collective-permute-start(bf16[24,3072]{1,0:T(8,128)(2,1)} %param.19), channel_id=1, source_target_pairs={{0,2},{1,3},{2,0},{3,1},{4,6},{5,7},{6,4},{7,5},{8,10},{9,11},{10,... | collective-permute-start | bytes 442376 | tf_op jit(solution)/shard_map/ppermute | solution.py:212
  101.3 45.8 %collective-permute-start.36 = (bf16[24,3072]{1,0:T(8,128)(2,1)}, bf16[24,3072]{1,0:T(8,128)(2,1)S(1)}, u32[]{:S(2)}, u32[]{:S(2)}) collective-permute-start(bf16[24,3072]{1,0:T(8,128)(2,1)} %param.19), channel_id=1, source_target_pairs={{0,3},{1,0},{2,1},{3,2},{4,7},{5,4},{6,5},{7,6},{8,11},{9,8},{10,9... | collective-permute-start | bytes 442376 | tf_op jit(solution)/shard_map/ppermute | solution.py:212
  104.8 70.9 %collective-permute-start.46 = (bf16[96,768]{1,0:T(8,128)(2,1)}, bf16[96,768]{1,0:T(8,128)(2,1)S(1)}, u32[]{:S(2)}, u32[]{:S(2)}) collective-permute-start(bf16[96,768]{1,0:T(8,128)(2,1)} %param.20), channel_id=1, source_target_pairs={{0,1},{1,2},{2,3},{3,0},{4,5},{5,6},{6,7},{7,4},{8,9},{9,10},{10,1... | collective-permute-start | bytes 442376 | tf_op jit(solution)/shard_map/ppermute | solution.py:212
  142.2 36.7 %collective-permute-start.48 = (bf16[96,768]{1,0:T(8,128)(2,1)}, bf16[96,768]{1,0:T(8,128)(2,1)S(1)}, u32[]{:S(2)}, u32[]{:S(2)}) collective-permute-start(bf16[96,768]{1,0:T(8,128)(2,1)} %param.20), channel_id=1, source_target_pairs={{0,3},{1,0},{2,1},{3,2},{4,7},{5,4},{6,5},{7,6},{8,11},{9,8},{10,9... | collective-permute-start | bytes 442376 | tf_op jit(solution)/shard_map/ppermute | solution.py:212
  191.0 44.7 %collective-permute-start.3 = (bf16[4,24,2304]{2,1,0:T(8,128)(2,1)}, bf16[4,24,2304]{2,1,0:T(8,128)(2,1)}, u32[]{:S(2)}, u32[]{:S(2)}) collective-permute-start(bf16[4,24,2304]{2,1,0:T(8,128)(2,1)} %bitcast_dynamic-update-slice_fusion.95), channel_id=1, source_target_pairs={{0,8},{1,9},{2,10},{3,11},{4,12},{5,13},{6,14},{7,15},{8,0},{9,1},... | collective-permute-start | bytes 1327112 | tf_op jit(solution)/shard_map/ppermute | solution.py:204
  192.5 45.0 %collective-permute-start.4 = (bf16[4,24,2304]{2,1,0:T(8,128)(2,1)}, bf16[4,24,2304]{2,1,0:T(8,128)(2,1)}, u32[]{:S(2)}, u32[]{:S(2)}) collective-permute-start(bf16[4,24,2304]{2,1,0:T(8,128)(2,1)} %bitcast_dynamic-update-slice_fusion.95), channel_id=1, source_target_pairs={{0,16},{1,17},{2,18},{3,19},{4,20},{5,21},{6,22},{7,23},{8,24},{9,... | collective-permute-start | bytes 1327112 | tf_op jit(solution)/shard_map/ppermute | solution.py:204
  210.1 128.2 %collective-permute-start.7 = (bf16[4,24,2304]{2,1,0:T(8,128)(2,1)}, bf16[4,24,2304]{2,1,0:T(8,128)(2,1)S(1)}, u32[]{:S(2)}, u32[]{:S(2)}) collective-permute-start(bf16[4,24,2304]{2,1,0:T(8,128)(2,1)} %bitcast_dynamic-update-slice_fusion.95), channel_id=1, source_target_pairs={{0,4},{1,5},{2,6},{3,7},{4,0},{5,1},{6,2},{7,3},{8,12},{9,13},{10,... | collective-permute-start | bytes 1327112 | tf_op jit(solution)/shard_map/ppermute | solution.py:204
  259.9 94.2 %collective-permute-start.75 = (bf16[4,24,2304]{2,1,0:T(8,128)(2,1)}, bf16[4,24,2304]{2,1,0:T(8,128)(2,1)S(1)}, u32[]{:S(2)}, u32[]{:S(2)}) collective-permute-start(bf16[4,24,2304]{2,1,0:T(8,128)(2,1)} %bitcast_dynamic-update-slice_fusion.91), channel_id=1, source_target_pairs={{0,4},{1,5},{2,6},{3,7},{4,0},{5,1},{6,2},{7,3},{8,12},{9,13},{10,... | collective-permute-start | bytes 1327112 | tf_op jit(solution)/shard_map/ppermute | solution.py:204
  260.7 168.0 %collective-permute-start.41 = (bf16[4,24,3072]{2,1,0:T(8,128)(2,1)}, bf16[4,24,3072]{2,1,0:T(8,128)(2,1)}, u32[]{:S(2)}, u32[]{:S(2)}) collective-permute-start(bf16[4,24,3072]{2,1,0:T(8,128)(2,1)} %bitcast_dynamic-update-slice_fusion.81), channel_id=1, source_target_pairs={{0,4},{1,5},{2,6},{3,7},{4,0},{5,1},{6,2},{7,3},{8,12},{9,13},{10,... | collective-permute-start | bytes 1769480 | tf_op jit(solution)/shard_map/ppermute | solution.py:204
  263.9 191.0 %collective-permute-start.53 = (bf16[4,96,768]{2,1,0:T(8,128)(2,1)}, bf16[4,96,768]{2,1,0:T(8,128)(2,1)}, u32[]{:S(2)}, u32[]{:S(2)}) collective-permute-start(bf16[4,96,768]{2,1,0:T(8,128)(2,1)} %bitcast_dynamic-update-slice_fusion.77), channel_id=1, source_target_pairs={{0,4},{1,5},{2,6},{3,7},{4,0},{5,1},{6,2},{7,3},{8,12},{9,13},{10,... | collective-permute-start | bytes 1769480 | tf_op jit(solution)/shard_map/ppermute | solution.py:204
  338.3 128.2 %collective-permute-start.99 = (bf16[4,24,3072]{2,1,0:T(8,128)(2,1)}, bf16[4,24,3072]{2,1,0:T(8,128)(2,1)}, u32[]{:S(2)}, u32[]{:S(2)}) collective-permute-start(bf16[4,24,3072]{2,1,0:T(8,128)(2,1)} %bitcast_dynamic-update-slice_fusion.67), channel_id=1, source_target_pairs={{0,4},{1,5},{2,6},{3,7},{4,0},{5,1},{6,2},{7,3},{8,12},{9,13},{10,... | collective-permute-start | bytes 1769480 | tf_op jit(solution)/shard_map/ppermute | solution.py:204
  353.3 109.0 %collective-permute-start.111 = (bf16[4,96,768]{2,1,0:T(8,128)(2,1)}, bf16[4,96,768]{2,1,0:T(8,128)(2,1)}, u32[]{:S(2)}, u32[]{:S(2)}) collective-permute-start(bf16[4,96,768]{2,1,0:T(8,128)(2,1)} %bitcast_dynamic-update-slice_fusion.63), channel_id=1, source_target_pairs={{0,4},{1,5},{2,6},{3,7},{4,0},{5,1},{6,2},{7,3},{8,12},{9,13},{10,... | collective-permute-start | bytes 1769480 | tf_op jit(solution)/shard_map/ppermute | solution.py:204
  361.1 43.1 %collective-permute-start.76 = (bf16[4,24,2304]{2,1,0:T(8,128)(2,1)}, bf16[4,24,2304]{2,1,0:T(8,128)(2,1)}, u32[]{:S(2)}, u32[]{:S(2)}) collective-permute-start(bf16[4,24,2304]{2,1,0:T(8,128)(2,1)} %collective-permute-done.71), channel_id=1, source_target_pairs={{0,4},{1,5},{2,6},{3,7},{4,0},{5,1},{6,2},{7,3},{8,12},{9,13},{10,... | collective-permute-start | bytes 1327112 | tf_op jit(solution)/shard_map/ppermute | solution.py:204
  473.1 71.7 %collective-permute-start.56 = (bf16[2,96,768]{2,1,0:T(8,128)(2,1)}, bf16[2,96,768]{2,1,0:T(8,128)(2,1)}, u32[]{:S(2)}, u32[]{:S(2)}) collective-permute-start(bf16[2,96,768]{2,1,0:T(8,128)(2,1)} %collective-permute-done.51), channel_id=1, source_target_pairs={{0,4},{1,5},{2,6},{3,7},{4,0},{5,1},{6,2},{7,3},{8,12},{9,13},{10,... | collective-permute-start | bytes 884744 | tf_op jit(solution)/shard_map/ppermute | solution.py:204
  474.2 72.1 %collective-permute-start.57 = (bf16[2,96,768]{2,1,0:T(8,128)(2,1)}, bf16[2,96,768]{2,1,0:T(8,128)(2,1)}, u32[]{:S(2)}, u32[]{:S(2)}) collective-permute-start(bf16[2,96,768]{2,1,0:T(8,128)(2,1)} %collective-permute-done.52), channel_id=1, source_target_pairs={{0,4},{1,5},{2,6},{3,7},{4,0},{5,1},{6,2},{7,3},{8,12},{9,13},{10,... | collective-permute-start | bytes 884744 | tf_op jit(solution)/shard_map/ppermute | solution.py:204
  475.4 91.7 %collective-permute-start.102 = (bf16[2,24,3072]{2,1,0:T(8,128)(2,1)}, bf16[2,24,3072]{2,1,0:T(8,128)(2,1)}, u32[]{:S(2)}, u32[]{:S(2)}) collective-permute-start(bf16[2,24,3072]{2,1,0:T(8,128)(2,1)} %collective-permute-done.97), channel_id=1, source_target_pairs={{0,4},{1,5},{2,6},{3,7},{4,0},{5,1},{6,2},{7,3},{8,12},{9,13},{10,... | collective-permute-start | bytes 884744 | tf_op jit(solution)/shard_map/ppermute | solution.py:204
  476.5 92.4 %collective-permute-start.103 = (bf16[2,24,3072]{2,1,0:T(8,128)(2,1)}, bf16[2,24,3072]{2,1,0:T(8,128)(2,1)}, u32[]{:S(2)}, u32[]{:S(2)}) collective-permute-start(bf16[2,24,3072]{2,1,0:T(8,128)(2,1)} %collective-permute-done.98), channel_id=1, source_target_pairs={{0,4},{1,5},{2,6},{3,7},{4,0},{5,1},{6,2},{7,3},{8,12},{9,13},{10,... | collective-permute-start | bytes 884744 | tf_op jit(solution)/shard_map/ppermute | solution.py:204
  476.9 96.0 %collective-permute-start.114 = (bf16[2,96,768]{2,1,0:T(8,128)(2,1)}, bf16[2,96,768]{2,1,0:T(8,128)(2,1)}, u32[]{:S(2)}, u32[]{:S(2)}) collective-permute-start(bf16[2,96,768]{2,1,0:T(8,128)(2,1)} %collective-permute-done.109), channel_id=1, source_target_pairs={{0,4},{1,5},{2,6},{3,7},{4,0},{5,1},{6,2},{7,3},{8,12},{9,13},{10,... | collective-permute-start | bytes 884744 | tf_op jit(solution)/shard_map/ppermute | solution.py:204
  949.9 45.3 %collective-permute-start.126 = (bf16[2,2,4,24,2304]{4,3,2,1,0:T(8,128)(2,1)}, bf16[2,2,4,24,2304]{4,3,2,1,0:T(8,128)(2,1)}, u32[]{:S(2)}, u32[]{:S(2)}) collective-permute-start(bf16[2,2,4,24,2304]{4,3,2,1,0:T(8,128)(2,1)} %dynamic-slice_bitcast_fusion.2), channel_id=1, source_target_pairs={{0,4},{1,5},{2,6},{3,7},{4,0},{5,1},{6,2},{7,3},{8,12},{9,13},{10,... | collective-permute-start | bytes 5308424 | tf_op jit(solution)/shard_map/ppermute | solution.py:204
  (288 other events, 4377.3 us)

commit v3 on v2

v3 whole, which is shorter than its diff:
```python
import functools

import jax
import jax.numpy as jnp
from jax import lax
from jax.experimental import pallas as pl
from jax.experimental.pallas import tpu as pltpu
from jax.sharding import PartitionSpec as P

HEAD = 64
SEG = 128
NORM_EPS = 1e-05
MASK_FILL = -1000000000.0
VMEM = 60 * 2**20
F32, LOW = jnp.float32, jnp.bfloat16


ROOT_HALF = 0.7071067811865476
INV_ROOT_TAU = 0.3989422804014327
AXES = ("dp", "fsdp")

def mm(left_op, right_op):
    return jnp.dot(left_op, right_op, preferred_element_type=F32)


def mm_nt(left_op, right_op):
    return lax.dot_general(left_op, right_op, (((1,), (1,)), ((), ())), preferred_element_type=F32)


def mm_tn(left_op, right_op):
    return lax.dot_general(left_op, right_op, (((0,), (0,)), ((), ())), preferred_element_type=F32)


def normalize(summed):
    average = jnp.mean(summed, axis=-1, keepdims=True)
    centered = summed - average
    inv_scale = lax.rsqrt(jnp.mean(centered * centered, axis=-1, keepdims=True) + NORM_EPS)
    return centered * inv_scale, inv_scale


def normalize_back(inner, normed, inv_scale):
    return inv_scale * (
        inner
        - jnp.mean(inner, axis=-1, keepdims=True)
        - normed * jnp.mean(inner * normed, axis=-1, keepdims=True)
    )


def gelu_parts(hidden):
    size = jnp.abs(hidden)
    near = 1.0 / (1.0 + (0.3275911 * 0.7071067811865476) * size)
    bell = jnp.exp(-0.5 * hidden * hidden)
    poly = 0.5 * 1.061405429
    for term in (-1.453152027, 1.421413741, -0.284496736, 0.254829592):
        poly = poly * near + 0.5 * term
    tail = poly * near * bell
    phi = jnp.where(hidden < 0.0, tail, 1.0 - tail)
    return hidden * phi, phi + hidden * bell * 0.3989422804014327


def pair_stack(pair, low_half):
    zero = jnp.zeros_like(pair)
    return jnp.concatenate(
        [jnp.where(low_half, pair, zero), jnp.where(low_half, zero, pair)], axis=0
    )


def pair_merge(stacked, low_half):
    rows = stacked.shape[0] // 2
    return jnp.where(low_half, stacked[:rows], stacked[rows:])


def pair_probs(query_stack, keys, allowed):
    scores = jnp.where(allowed, mm_nt(query_stack, keys), MASK_FILL)
    expo = jnp.exp(scores - jnp.max(scores, axis=-1, keepdims=True))
    return expo


def attend(query, keys, values, allowed):
    low_half = lax.broadcasted_iota(jnp.int32, query.shape, 1) < HEAD
    stack = pair_stack(query * jnp.asarray(HEAD**-0.5, query.dtype), low_half)
    expo = pair_probs(stack, keys, allowed).astype(LOW)
    wide = jnp.concatenate([values, jnp.ones_like(values)], axis=1)
    both = mm(expo, wide)
    out = both[:, :128] / both[:, 128:]
    return pair_merge(out, low_half)


def attend_back(query, keys, values, grad_mixed, allowed):
    low_half = lax.broadcasted_iota(jnp.int32, query.shape, 1) < HEAD
    stack = pair_stack(query * jnp.asarray(HEAD**-0.5, query.dtype), low_half)
    expo = pair_probs(stack, keys, allowed)
    probs = expo / jnp.sum(expo, axis=-1, keepdims=True)
    grad_stack = pair_stack(grad_mixed, low_half)
    grad_prob = mm_nt(grad_stack, values)
    weighted = probs * grad_prob
    score_grad = (weighted - probs * jnp.sum(weighted, axis=-1, keepdims=True)).astype(LOW)
    grad_query = pair_merge(mm(score_grad, keys), low_half) * HEAD**-0.5
    grad_keys = mm_tn(score_grad, stack)
    grad_values = mm_tn(probs.astype(LOW), grad_stack)
    return grad_query, grad_keys, grad_values


def load_slabs(place, pieces, slabs, sems):
    for _, copy in slab_copies(place, pieces, slabs, sems, True):
        copy.wait()


def slab_copies(place, pieces, slabs, sems, start, first_slab=0):
    count = len(slabs)
    half = count // 2
    copies = []
    spans = ((0, 0, count), (2, 0, count), (4, 0, count), (6, 0, half), (6, half, count))
    for flip_c in (0, 1):
        for index, (flip_yx, first, last) in enumerate(spans):
            block = place ^ (flip_yx + flip_c)
            piece = pieces[flip_c * 5 + index]
            for slab in range(first, last):
                if slab < first_slab:
                    continue
                sem = sems.at[slab * 8 + (flip_yx + flip_c)]
                source, target = piece.at[slab - first], slabs[slab](block)
                copies.append((slab, pltpu.make_async_copy(source, target, sem)))
    if start:
        for _, copy in copies:
            copy.start()
    return copies


def rows_of(ref, block, rows, slab=None):
    where = pl.ds(pl.multiple_of(block * rows, rows), rows)
    return ref.at[where] if slab is None else ref.at[slab, where]


def qkv_slabs(qkv):
    return [functools.partial(rows_of, qkv, rows=96, slab=j) for j in range(3)]


def rest_slabs(out, up, down):
    def down_slab(block, part):
        return down.at[pl.ds(pl.multiple_of(block * 384 + part * 96, 96), 96)]

    slabs = [functools.partial(rows_of, out, rows=96)]
    slabs += [functools.partial(rows_of, up, rows=96, slab=j) for j in range(4)]
    return slabs + [functools.partial(down_slab, part=j) for j in range(4)]


def segment_mask(length, seg_in_seq):
    lane = lax.broadcasted_iota(jnp.int32, (1, SEG), 1)
    return (lane + seg_in_seq * SEG < length) | (lane == 0)


def attn_forward_kernel(segs, seg_count, info, x_ref, vec_ref, *rest):
    pieces, (packed_ref, mixed_ref, qkv, sems) = rest[:10], rest[10:]
    step = pl.program_id(0)

    @pl.when(step == 0)
    def _():
        load_slabs(info[0], pieces, qkv_slabs(qkv), sems)

    rows = x_ref[...]
    for j in range(3):
        part = mm(rows, qkv[j])
        if j != 1:
            part = part + vec_ref[j // 2 : j // 2 + 1, :]
        packed_ref[:, j * 768 : (j + 1) * 768] = part.astype(LOW)
    for s in range(segs):
        seg = step * segs + s
        allowed = segment_mask(info[1 + seg // seg_count], seg % seg_count)
        at = slice(s * SEG, (s + 1) * SEG)
        for h in range(6):
            q, k, v = (packed_ref[at, j * 768 + h * 128 : j * 768 + (h + 1) * 128] for j in range(3))
            mixed_ref[at, h * 128 : (h + 1) * 128] = attend(q, k, v, allowed).astype(LOW)


def ffn_forward_kernel(segs, info, x_ref, mixed_ref, vec_ref, *rest):
    pieces, rest = rest[:10], rest[10:]
    sum_ref, low_ref, act_ref, slope_ref, second_ref, heads_ref, out, up, down, sems = rest

    @pl.when(pl.program_id(0) == 0)
    def _():
        load_slabs(info[0], pieces, rest_slabs(out, up, down), sems)

    summed = x_ref[...].astype(F32) + mm(mixed_ref[...], out[...]) + vec_ref[2:3, :]
    sum_ref[...] = summed
    normed, _ = normalize(summed)
    first = normed * (1.0 + vec_ref[3:4, :]) + vec_ref[4:5, :]
    first_low = first.astype(LOW)
    low_ref[...] = first_low
    total = first + vec_ref[9:10, :]
    for j in range(4):
        hidden = mm(first_low, up[j]) + vec_ref[5 + j : 6 + j, :]
        act, slope = gelu_parts(hidden)
        act = act.astype(LOW)
        act_ref[:, j * 768 : (j + 1) * 768] = act
        slope_ref[:, j * 768 : (j + 1) * 768] = slope.astype(LOW)
        total = total + mm(act, down[j * 768 : (j + 1) * 768, :])
    second_ref[...] = total
    opening = jnp.concatenate([total[s * SEG : s * SEG + 1] for s in range(segs)], axis=0)
    normed, _ = normalize(opening)
    heads_ref[...] = normed * (1.0 + vec_ref[10:11, :]) + vec_ref[11:12, :]


def cross_kernel(blocks, info, heads_ref, up_ref, live_ref, vec_ref, pos_ref, *rest):
    pieces, rest = rest[:10], rest[10:]
    (own_ref, own_grad_ref, grads_ref, pos_grad_ref, qkv_grad_ref, out_grad_ref, up_grad_ref, down_grad_ref) = rest[:8]
    (qkv, out, up, down, sems, result, heads_grad, slope, lefts, act, packed, rights, hidden_grad) = rest[8:]
    step = pl.program_id(0)
    count = heads_ref.shape[0]
    at = pl.ds(pl.multiple_of(step * count, count), count)
    slabs = qkv_slabs(qkv) + rest_slabs(out, up, down)

    @pl.when(step == 0)
    def _():
        copies = slab_copies(info[0], pieces, slabs, sems, True)
        grads_ref[...] = jnp.zeros_like(grads_ref)
        pos_grad_ref[...] = jnp.zeros_like(pos_grad_ref)
        for slab, copy in copies:
            if slab < 3:
                copy.wait()

    vec = vec_ref[...]
    inputs = heads_ref[...].astype(F32).reshape(-1, 8, 768) + pos_ref[...][None]
    inputs = inputs.reshape(count, 768)
    low = inputs.astype(LOW)
    lefts[0, at, :] = low
    for j in range(3):
        part = mm(low, qkv[j])
        if j != 1:
            part = part + vec[j // 2 : j // 2 + 1]
        packed[:, j * 768 : (j + 1) * 768] = part.astype(LOW)
    row = lax.broadcasted_iota(jnp.int32, (2 * SEG, SEG), 0)
    lane = lax.broadcasted_iota(jnp.int32, (2 * SEG, SEG), 1)
    group = row % SEG // 8 == lane // 8
    masks = [group & (live_ref[s : s + 1, :] > 0.0) for s in range(count // SEG)]
    for s, allowed in enumerate(masks):
        part = slice(s * SEG, (s + 1) * SEG)
        for h in range(6):
            q, k, v = (packed[part, j * 768 + h * 128 : j * 768 + (h + 1) * 128] for j in range(3))
            where = pl.ds(pl.multiple_of(step * count + s * SEG, SEG), SEG)
            lefts[1, where, h * 128 : (h + 1) * 128] = attend(q, k, v, allowed).astype(LOW)

    @pl.when(step == 0)
    def _():
        for _, copy in slab_copies(info[0], pieces, slabs, sems, False, 3):
            copy.wait()

    summed = inputs + mm(lefts[1, at, :], out[...]) + vec[2:3]
    normed_one, scale_one = normalize(summed)
    first = normed_one * (1.0 + vec[3:4]) + vec[4:5]
    first_low = first.astype(LOW)
    lefts[2, at, :] = first_low
    total = first + vec[9:10]
    for j in range(4):
        cols = slice(j * 768, (j + 1) * 768)
        hidden = mm(first_low, up[j]) + vec[5 + j : 6 + j]
        active, steep = gelu_parts(hidden)
        act[at, cols] = active.astype(LOW)
        slope[:, cols] = steep.astype(LOW)
        total = total + mm(active.astype(LOW), down[cols, :])
    normed, inv_scale = normalize(total)
    result[at, :] = normed * (1.0 + vec[10:11]) + vec[11:12]
    upstream = up_ref[...].astype(F32)
    back_two = normalize_back(upstream * (1.0 + vec[10:11]), normed, inv_scale)
    down_grad = back_two.astype(LOW)
    rights[1, at, :] = down_grad
    grads_ref[9:10, :] += column_sum(down_grad)
    grads_ref[10:11, :] += column_sum(upstream * normed)
    grads_ref[11:12, :] += column_sum(upstream)
    total = back_two
    for j in range(4):
        cols = slice(j * 768, (j + 1) * 768)
        grad = (mm_nt(down_grad, down[cols, :]) * slope[:, cols].astype(F32)).astype(LOW)
        hidden_grad[at, cols] = grad
        grads_ref[5 + j : 6 + j, :] += column_sum(grad)
        total = total + mm_nt(grad, up[j])
    back_one = normalize_back(total * (1.0 + vec[3:4]), normed_one, scale_one)
    proj_grad = back_one.astype(LOW)
    rights[0, at, :] = proj_grad
    grads_ref[2:3, :] += column_sum(proj_grad)
    grads_ref[3:4, :] += column_sum(total * normed_one)
    grads_ref[4:5, :] += column_sum(total)
    mixed_grad = mm_nt(proj_grad, out[...]).astype(LOW)
    for s, allowed in enumerate(masks):
        part = slice(s * SEG, (s + 1) * SEG)
        where = pl.ds(pl.multiple_of(step * count + s * SEG, SEG), SEG)
        for h in range(6):
            cols = slice(h * 128, (h + 1) * 128)
            q, k, v = (packed[part, j * 768 + h * 128 : j * 768 + (h + 1) * 128] for j in range(3))
            for j, g in enumerate(attend_back(q, k, v, mixed_grad[part, cols], allowed)):
                rights[2 + j, where, cols] = g.astype(LOW)
    total = back_one
    for j in range(3):
        part = rights[2 + j, at, :]
        total = total + mm_nt(part, qkv[j])
        if j != 1:
            grads_ref[j // 2 : j // 2 + 1, :] += column_sum(part)
    heads_grad[at, :] = total
    pos_grad_ref[...] += jnp.sum(total.reshape(-1, 8, 768), axis=0)

    @pl.when(step == blocks - 1)
    def _():
        me = info[1]
        own = pl.ds(pl.multiple_of(me * 16, 16), 16)
        own_ref[...] = result[own, :]
        own_grad_ref[...] = heads_grad[own, :]

        def chosen(left, rows):
            width = left.shape[1]
            wanted = lax.broadcasted_iota(jnp.int32, (rows, width), 1) - lax.broadcasted_iota(
                jnp.int32, (rows, width), 0
            )
            pick = (wanted == me * rows).astype(F32).astype(LOW)
            return mm_nt(pick, left).astype(LOW)

        left = chosen(lefts[0], 24)
        for j in range(3):
            qkv_grad_ref[:, j * 768 : (j + 1) * 768] = mm(left, rights[2 + j])
        out_grad_ref[...] = mm(chosen(lefts[1], 24), rights[0])
        left = chosen(lefts[2], 24)
        for j in range(4):
            cols = slice(j * 768, (j + 1) * 768)
            up_grad_ref[:, cols] = mm(left, hidden_grad[:, cols])
        down_grad_ref[...] = mm(chosen(act[...], 96), rights[1])


def column_sum(value):
    return jnp.sum(value.astype(F32), axis=0, keepdims=True)


def ffn_backward_kernel(segs, seg_count, info, cot_ref, heads_grad_ref, heads_ref, second_ref, sum_ref, slope_ref, vec_ref, *rest):
    pieces, rest = rest[:10], rest[10:]
    (out_ref, down_grad_ref, hidden_grad_ref, proj_grad_ref, mixed_grad_ref, grads_ref, out, up, down, sems) = rest
    step = pl.program_id(0)

    @pl.when(step == 0)
    def _():
        load_slabs(info[0], pieces, rest_slabs(out, up, down), sems)
        grads_ref[...] = jnp.zeros_like(grads_ref)

    count = segs * SEG
    normed, inv_scale = normalize(second_ref[...])
    row = lax.broadcasted_iota(jnp.int32, (SEG, 1), 0)
    result = normed * (1.0 + vec_ref[10:11, :]) + vec_ref[11:12, :]
    ups = []
    for s in range(segs):
        seg = step * segs + s
        at = slice(s * SEG, (s + 1) * SEG)
        live = row + seg % seg_count * SEG < info[1 + seg // seg_count]
        opens = row == 0
        merged = jnp.where(opens, heads_ref[s : s + 1, :], result[at])
        out_ref[at, :] = jnp.where(live, merged, 0.0).astype(LOW)
        grad = jnp.where(live, cot_ref[at, :].astype(F32), 0.0)
        ups.append(jnp.where(opens, heads_grad_ref[s : s + 1, :], grad))
    upstream = jnp.concatenate(ups, axis=0)
    back_two = normalize_back(upstream * (1.0 + vec_ref[10:11, :]), normed, inv_scale)
    down_grad = back_two.astype(LOW)
    down_grad_ref[...] = down_grad
    grads_ref[9:10, :] += column_sum(down_grad)
    grads_ref[10:11, :] += column_sum(upstream * normed)
    grads_ref[11:12, :] += column_sum(upstream)
    total = back_two
    for j in range(4):
        cols = slice(j * 768, (j + 1) * 768)
        grad = mm_nt(down_grad, down[cols, :]) * slope_ref[:, cols].astype(F32)
        grad = grad.astype(LOW)
        hidden_grad_ref[:, cols] = grad
        grads_ref[5 + j : 6 + j, :] += column_sum(grad)
        total = total + mm_nt(grad, up[j])
    normed, inv_scale = normalize(sum_ref[...])
    back_one = normalize_back(total * (1.0 + vec_ref[3:4, :]), normed, inv_scale)
    proj_grad = back_one.astype(LOW)
    proj_grad_ref[...] = proj_grad
    mixed_grad_ref[...] = mm_nt(proj_grad, out[...]).astype(LOW)
    grads_ref[2:3, :] += column_sum(proj_grad)
    grads_ref[3:4, :] += column_sum(total * normed)
    grads_ref[4:5, :] += column_sum(total)


def attn_backward_kernel(segs, seg_count, info, packed_ref, mixed_grad_ref, packed_grad_ref, grads_ref):
    step = pl.program_id(0)

    @pl.when(step == 0)
    def _():
        grads_ref[...] = jnp.zeros_like(grads_ref)

    for s in range(segs):
        seg = step * segs + s
        allowed = segment_mask(info[1 + seg // seg_count], seg % seg_count)
        at = slice(s * SEG, (s + 1) * SEG)
        for h in range(6):
            cols = [slice(j * 768 + h * 128, j * 768 + (h + 1) * 128) for j in range(3)]
            q, k, v = (packed_ref[at, c] for c in cols)
            grads = attend_back(q, k, v, mixed_grad_ref[at, cols[0]], allowed)
            for c, g in zip(cols, grads):
                packed_grad_ref[at, c] = g.astype(LOW)
    grads_ref[0:1, :] += column_sum(packed_grad_ref[:, :768])
    grads_ref[1:2, :] += column_sum(packed_grad_ref[:, 1536:])


def token_grad_kernel(info, packed_grad_ref, proj_grad_ref, *rest):
    pieces, (token_grad_ref, qkv, sems) = rest[:10], rest[10:]

    @pl.when(pl.program_id(0) == 0)
    def _():
        load_slabs(info[0], pieces, qkv_slabs(qkv), sems)

    total = proj_grad_ref[...].astype(F32)
    for j in range(3):
        total = total + mm_nt(packed_grad_ref[:, j * 768 : (j + 1) * 768], qkv[j])
    token_grad_ref[...] = total.astype(LOW)


def weight_grad_kernel(rows, info, left_ref, right_ref, keep_ref, send_ref, total):
    total[...] = mm_tn(left_ref[...], right_ref[...])
    for mask in range(8):
        block = pl.multiple_of((info[0] ^ mask) * rows, rows)
        target = send_ref if mask % 2 else keep_ref
        target[mask // 2] = total[pl.ds(block, rows), :].astype(LOW)


ANY = pl.BlockSpec(memory_space=pl.ANY)
SMEM = pl.BlockSpec(memory_space=pltpu.SMEM)


def block_rows(count, width):
    return pl.BlockSpec((count, width), lambda i: (i, 0))


def fixed(shape):
    return pl.BlockSpec(shape, lambda i: (0,) * len(shape))


def shape_of(dims, kind=LOW):
    return jax.ShapeDtypeStruct(dims, kind)


def params():
    return pltpu.CompilerParams(vmem_limit_bytes=VMEM, dimension_semantics=("arbitrary",))


def qkv_weights():
    return [pltpu.VMEM((3, 768, 768), LOW)], [pltpu.SemaphoreType.DMA((24,))]


def rest_weights():
    weights = [pltpu.VMEM((768, 768), LOW), pltpu.VMEM((4, 768, 768), LOW), pltpu.VMEM((3072, 768), LOW)]
    return weights, [pltpu.SemaphoreType.DMA((72,))]


def cost(flops, size, exps=0):
    return pl.CostEstimate(flops=flops, bytes_accessed=size, transcendentals=exps)


def attn_forward(info, rows_in, vec, pieces, seg_count, segs=2):
    rows = rows_in.shape[0]
    count = segs * SEG
    weights, sems = qkv_weights()
    return pl.pallas_call(
        functools.partial(attn_forward_kernel, segs, seg_count),
        grid=(rows // count,),
        in_specs=[SMEM, block_rows(count, 768), fixed((12, 768))] + [ANY] * 10,
        out_specs=[block_rows(count, 2304), block_rows(count, 768)],
        out_shape=[shape_of((rows, 2304)), shape_of((rows, 768))],
        scratch_shapes=weights + sems,
        compiler_params=params(),
        cost_estimate=cost(2 * rows * 768 * 8000, rows * 768 * 16),
        name="attn_forward",
    )(info, rows_in, vec, *pieces)


def ffn_forward(info, rows_in, mixed, vec, pieces, segs=2):
    rows = rows_in.shape[0]
    count = segs * SEG
    weights, sems = rest_weights()
    few = pl.BlockSpec((None, segs, 768), lambda i: (i, 0, 0))
    return pl.pallas_call(
        functools.partial(ffn_forward_kernel, segs),
        grid=(rows // count,),
        in_specs=[SMEM, block_rows(count, 768), block_rows(count, 768), fixed((12, 768))] + [ANY] * 10,
        out_specs=[block_rows(count, 768), block_rows(count, 768), block_rows(count, 3072), block_rows(count, 3072),
                   block_rows(count, 768), few],
        out_shape=[shape_of((rows, 768), F32), shape_of((rows, 768)), shape_of((rows, 3072)), shape_of((rows, 3072)),
                   shape_of((rows, 768), F32), shape_of((rows // count, segs, 768), F32)],
        scratch_shapes=weights + sems,
        compiler_params=params(),
        cost_estimate=cost(2 * rows * 768 * 14000, rows * 768 * 30),
        name="ffn_forward",
    )(info, rows_in, mixed, vec, *pieces)


def cross_whole(info, heads, upstream, live, vec, positions, pieces):
    rows = heads.shape[0]
    count = 2 * SEG
    weights = qkv_weights()[0] + rest_weights()[0]
    own = [(16, 768), (16, 768), (12, 768), (8, 768), (24, 2304), (24, 768), (24, 3072), (96, 768)]
    return pl.pallas_call(
        functools.partial(cross_kernel, rows // count),
        grid=(rows // count,),
        in_specs=[SMEM, block_rows(count, 768), block_rows(count, 768),
                  pl.BlockSpec((None, 2, SEG), lambda i: (i, 0, 0)), fixed((12, 768)), fixed((8, 768))] + [ANY] * 10,
        out_specs=[fixed(dims) for dims in own],
        out_shape=[shape_of(dims, F32) for dims in own],
        scratch_shapes=weights + [pltpu.SemaphoreType.DMA((96,))] + [
            pltpu.VMEM((rows, 768), F32), pltpu.VMEM((rows, 768), F32), pltpu.VMEM((count, 3072), LOW),
            pltpu.VMEM((3, rows, 768), LOW), pltpu.VMEM((rows, 3072), LOW), pltpu.VMEM((count, 2304), LOW),
            pltpu.VMEM((5, rows, 768), LOW), pltpu.VMEM((rows, 3072), LOW),
        ],
        compiler_params=params(),
        cost_estimate=cost(2 * rows * 768 * 30000, 2**24),
        name="cross_encoder",
    )(info, heads, upstream, live, vec, positions, *pieces)


def ffn_backward(info, cotangent, heads_grad, heads, second, summed, slope, vec, pieces, seg_count, segs=2):
    rows = summed.shape[0]
    count = segs * SEG
    few = pl.BlockSpec((None, segs, 768), lambda i: (i, 0, 0))
    weights, sems = rest_weights()
    return pl.pallas_call(
        functools.partial(ffn_backward_kernel, segs, seg_count),
        grid=(rows // count,),
        in_specs=[SMEM, block_rows(count, 768), few, few, block_rows(count, 768), block_rows(count, 768),
                  block_rows(count, 3072), fixed((12, 768))] + [ANY] * 10,
        out_specs=[block_rows(count, 768), block_rows(count, 768), block_rows(count, 3072), block_rows(count, 768),
                   block_rows(count, 768), fixed((12, 768))],
        out_shape=[shape_of((rows, 768)), shape_of((rows, 768)), shape_of((rows, 3072)), shape_of((rows, 768)),
                   shape_of((rows, 768)), shape_of((12, 768), F32)],
        scratch_shapes=weights + sems,
        compiler_params=params(),
        cost_estimate=cost(2 * rows * 768 * 14000, rows * 768 * 30),
        name="ffn_backward",
    )(info, cotangent, heads_grad.reshape(-1, segs, 768), heads.reshape(-1, segs, 768), second, summed, slope, vec, *pieces)


def attn_backward(info, packed, mixed_grad, seg_count, segs=2):
    rows = packed.shape[0]
    count = segs * SEG
    return pl.pallas_call(
        functools.partial(attn_backward_kernel, segs, seg_count),
        grid=(rows // count,),
        in_specs=[SMEM, block_rows(count, 2304), block_rows(count, 768)],
        out_specs=[block_rows(count, 2304), fixed((2, 768))],
        out_shape=[shape_of((rows, 2304)), shape_of((2, 768), F32)],
        compiler_params=params(),
        cost_estimate=cost(2 * rows * 768 * 16000, rows * 768 * 16),
        name="attn_backward",
    )(info, packed, mixed_grad)


def token_gradient(info, packed_grad, proj_grad, pieces, count=256):
    rows = packed_grad.shape[0]
    weights, sems = qkv_weights()
    return pl.pallas_call(
        token_grad_kernel,
        grid=(rows // count,),
        in_specs=[SMEM, block_rows(count, 2304), block_rows(count, 768)] + [ANY] * 10,
        out_specs=block_rows(count, 768),
        out_shape=shape_of((rows, 768)),
        scratch_shapes=weights + sems,
        compiler_params=params(),
        cost_estimate=cost(2 * rows * 768 * 3000, rows * 768 * 10),
        name="token_gradient",
    )(info, packed_grad, proj_grad, *pieces)


def weight_grad(info, left, right):
    rows, wide = right.shape
    tiles = wide // 768
    moving = pl.BlockSpec((rows, 768), lambda i: (0, i))
    still = fixed((rows, 768))
    out = pl.BlockSpec((4, 96, 768), lambda i: (0, 0, i))
    return pl.pallas_call(
        functools.partial(weight_grad_kernel, 96),
        grid=(tiles,),
        in_specs=[SMEM, still, moving],
        out_specs=[out, out],
        out_shape=[shape_of((4, 96, wide))] * 2,
        scratch_shapes=[pltpu.VMEM((768, 768), F32)],
        compiler_params=params(),
        cost_estimate=cost(2 * rows * 768 * wide, rows * wide * 2),
        name="weight_grad",
    )(info, left, right)


def down_grad_kernel(info, left_ref, right_ref, keep_ref, send_ref, total):
    step = pl.program_id(0)
    total[pl.ds(pl.multiple_of(step * 768, 768), 768), :] = mm_tn(left_ref[...], right_ref[...]).astype(LOW)

    @pl.when(step == pl.num_programs(0) - 1)
    def _():
        for mask in range(8):
            block = pl.multiple_of((info[0] ^ mask) * 384, 384)
            target = send_ref if mask % 2 else keep_ref
            target[mask // 2] = total[pl.ds(block, 384), :]


def down_weight_grad(info, left, right):
    rows, wide = left.shape
    return pl.pallas_call(
        down_grad_kernel,
        grid=(wide // 768,),
        in_specs=[SMEM, pl.BlockSpec((rows, 768), lambda i: (0, i)), fixed((rows, 768))],
        out_specs=[fixed((4, 384, 768))] * 2,
        out_shape=[shape_of((4, 384, 768))] * 2,
        scratch_shapes=[pltpu.VMEM((3072, 768), LOW)],
        compiler_params=params(),
        cost_estimate=cost(2 * rows * 768 * wide, rows * wide * 2),
        name="down_weight_grad",
    )(info, left, right)


def matmul(left_op, right_op):
    return jnp.dot(left_op, right_op, preferred_element_type=jnp.float32)


def trans_left(left_op, right_op):
    return lax.dot_general(
        left_op, right_op, (((0,), (0,)), ((), ())), preferred_element_type=jnp.float32
    )


def trans_right(left_op, right_op):
    return lax.dot_general(
        left_op, right_op, (((1,), (1,)), ((), ())), preferred_element_type=jnp.float32
    )


def norm_forward(summed, gain_row, shift_row):
    average = jnp.mean(summed, axis=-1, keepdims=True)
    centered = summed - average
    inv_scale = lax.rsqrt(jnp.mean(centered * centered, axis=-1, keepdims=True) + NORM_EPS)
    normed = centered * inv_scale
    return (normed * (1.0 + gain_row) + shift_row, normed, inv_scale)


def norm_backward(upstream, normed, inv_scale, gain_row):
    inner = upstream * (1.0 + gain_row)
    back_grad = inv_scale * (
        inner
        - jnp.mean(inner, axis=-1, keepdims=True)
        - normed * jnp.mean(inner * normed, axis=-1, keepdims=True)
    )
    return (back_grad, jnp.sum(upstream * normed, axis=0), jnp.sum(upstream, axis=0))


def gelu_slope(hidden):
    return (
        0.5 * (1.0 + lax.erf(hidden * ROOT_HALF))
        + hidden * jnp.exp(-0.5 * hidden * hidden) * INV_ROOT_TAU
    )


def split_heads(packed, group_len):
    head_count = packed.shape[1] // (3 * HEAD)
    return [
        portion.reshape(-1, group_len, head_count, HEAD) for portion in jnp.split(packed, 3, axis=1)
    ]


def masked_scores(query_heads, key_heads, allowed):
    raw_scores = jnp.einsum(
        "nqhd,nkhd->nhqk", query_heads, key_heads, preferred_element_type=jnp.float32
    ) * HEAD ** (-0.5)
    return jnp.where(allowed[:, None, None, :], raw_scores, MASK_FILL)


def encode(inputs, inputs_low, weights, allowed):
    qkv_w, out_w, up_w, down_w, vectors = weights
    row_count, feat_dim = inputs_low.shape
    group_len = allowed.shape[1]
    qkv_bias = jnp.concatenate([vectors[0], jnp.zeros_like(vectors[0]), vectors[1]])
    packed = (matmul(inputs_low, qkv_w) + qkv_bias).astype(jnp.bfloat16)
    query_heads, key_heads, value_heads = split_heads(packed, group_len)
    scores = masked_scores(query_heads, key_heads, allowed)
    row_max = jnp.max(scores, axis=-1, keepdims=True)
    expo_vals = jnp.exp(scores - row_max)
    row_total = jnp.sum(expo_vals, axis=-1, keepdims=True)
    log_total = row_max + jnp.log(row_total)
    prob_low = (expo_vals / row_total).astype(jnp.bfloat16)
    mixed = jnp.einsum("nhqk,nkhd->nqhd", prob_low, value_heads, preferred_element_type=jnp.float32)
    mixed = mixed.reshape(row_count, feat_dim).astype(jnp.bfloat16)
    projected = matmul(mixed, out_w) + vectors[2]
    first_out, normed_one, scale_one = norm_forward(inputs + projected, vectors[3], vectors[4])
    first_low = first_out.astype(jnp.bfloat16)
    hidden = matmul(first_low, up_w) + vectors[5:-3].reshape(-1)
    activated = jax.nn.gelu(hidden, approximate=False).astype(jnp.bfloat16)
    down_out = matmul(activated, down_w) + vectors[-3]
    result, normed_two, scale_two = norm_forward(first_out + down_out, vectors[-2], vectors[-1])
    return (
        result,
        (
            packed,
            log_total,
            mixed,
            normed_one,
            scale_one,
            first_low,
            hidden,
            activated,
            normed_two,
            scale_two,
        ),
    )


def encode_back(upstream, inputs_low, weights, allowed, kept):
    qkv_w, out_w, up_w, down_w, vectors = weights
    (
        packed,
        log_total,
        mixed,
        normed_one,
        scale_one,
        first_low,
        hidden,
        activated,
        normed_two,
        scale_two,
    ) = kept
    row_count, feat_dim = inputs_low.shape
    group_len = allowed.shape[1]
    back_two, gain_two, shift_two = norm_backward(upstream, normed_two, scale_two, vectors[-2])
    down_grad = back_two.astype(jnp.bfloat16)
    hidden_grad = (trans_right(down_grad, down_w) * gelu_slope(hidden)).astype(jnp.bfloat16)
    first_grad = trans_right(hidden_grad, up_w) + back_two
    back_one, gain_one, shift_one = norm_backward(first_grad, normed_one, scale_one, vectors[3])
    proj_grad = back_one.astype(jnp.bfloat16)
    query_heads, key_heads, value_heads = split_heads(packed, group_len)
    mixed_grad = trans_right(proj_grad, out_w).astype(jnp.bfloat16).reshape(value_heads.shape)
    scores = masked_scores(query_heads, key_heads, allowed)
    prob_vals = jnp.exp(scores - log_total)
    grad_values = jnp.einsum(
        "nhqk,nqhd->nkhd",
        prob_vals.astype(jnp.bfloat16),
        mixed_grad,
        preferred_element_type=jnp.float32,
    )
    grad_prob = jnp.einsum(
        "nqhd,nkhd->nhqk", mixed_grad, value_heads, preferred_element_type=jnp.float32
    )
    score_grad = (
        prob_vals * (grad_prob - jnp.sum(prob_vals * grad_prob, axis=-1, keepdims=True))
    ).astype(jnp.bfloat16)
    grad_query = jnp.einsum(
        "nhqk,nkhd->nqhd", score_grad, key_heads, preferred_element_type=jnp.float32
    ) * HEAD ** (-0.5)
    grad_keys = jnp.einsum(
        "nhqk,nqhd->nkhd", score_grad, query_heads, preferred_element_type=jnp.float32
    ) * HEAD ** (-0.5)
    packed_grad = jnp.concatenate(
        [
            grad_query.reshape(row_count, feat_dim),
            grad_keys.reshape(row_count, feat_dim),
            grad_values.reshape(row_count, feat_dim),
        ],
        axis=1,
    ).astype(jnp.bfloat16)
    bias_grads = jnp.sum(packed_grad, axis=0, dtype=jnp.float32).reshape(3, feat_dim)
    grad_inputs = trans_right(packed_grad, qkv_w) + back_one
    grad_vectors = jnp.concatenate(
        [
            bias_grads[0:1],
            bias_grads[2:3],
            jnp.sum(proj_grad, axis=0, dtype=jnp.float32)[None],
            gain_one[None],
            shift_one[None],
            jnp.sum(hidden_grad, axis=0, dtype=jnp.float32).reshape(-1, feat_dim),
            jnp.sum(down_grad, axis=0, dtype=jnp.float32)[None],
            gain_two[None],
            shift_two[None],
        ],
        axis=0,
    )
    pairs = (
        (inputs_low, packed_grad),
        (mixed, proj_grad),
        (first_low, hidden_grad),
        (activated, down_grad),
    )
    return (grad_inputs, pairs, grad_vectors)


class Links:
    def __init__(self, outer, inner):
        self.outer, self.inner = outer, inner
        self.order = self.place = lax.axis_index("dp")
        self.z = lax.axis_index("fsdp")

    def flip(self, value, mask):
        pairs = [
            (d * self.inner + z, (d ^ mask) * self.inner + z)
            for d in range(self.outer)
            for z in range(self.inner)
        ]
        return lax.ppermute(value, AXES, pairs)

    def turn(self, value, step):
        pairs = [
            (d * self.inner + z, d * self.inner + (z + step) % self.inner)
            for d in range(self.outer)
            for z in range(self.inner)
        ]
        return lax.ppermute(value, AXES, pairs)

    def gather_z(self, shard):
        came = [shard] + [self.turn(shard, step) for step in range(1, self.inner)]
        whole = []
        for z in range(self.inner):
            part = came[-1]
            for step in range(self.inner - 1):
                part = jnp.where(self.z == (z + step) % self.inner, came[step], part)
            whole.append(part)
        return whole

    def spread_near(self, block):
        return self.flip(block, 2), self.flip(block, 4)

    def spread_far(self, by_x, by_y):
        half = by_x.shape[0] // 2
        return self.flip(by_y[:half], 2), self.flip(by_x[half:], 4)

    def spread_core(self, mine):
        return list(mine) + [self.flip(piece, 1) for piece in mine]

    def gather_small(self, shard):
        block = jnp.stack(self.gather_z(shard))
        near = [block] + [self.flip(block, m) for m in (2, 4, 6)]
        near = [lax.select(self.place // 2 % 2 == 0, jnp.stack(p), jnp.stack(p[::-1])) for p in (near[:2], near[2:])]
        plane = lax.select(self.place // 4 == 0, jnp.stack(near), jnp.stack(near[::-1]))
        other = self.flip(plane, 1)
        both = [jnp.stack(p, axis=2) for p in ((plane, other), (other, plane))]
        return lax.select(self.place % 2 == 0, *both).reshape((-1,) + shard.shape)

    def scatter_sum(self, keep, send, line):
        def add(*terms):
            return sum(t.astype(F32) for t in terms).astype(LOW)

        def pick(array, index):
            return lax.dynamic_index_in_dim(array, index, 0, keepdims=False)

        came = self.flip(send, 1)
        to_d = line(add(keep[3], came[3]))
        half = self.inner // 2
        came_x, came_y = self.flip(to_d[:half], 2), self.flip(to_d[half:], 4)
        to_x, to_y = line(add(keep[1], came[1])), line(add(keep[2], came[2]))
        to_y = jnp.concatenate([add(to_y[:half], came_x), to_y[half:]])
        to_x = jnp.concatenate([to_x[:half], add(to_x[half:], came_y)])
        own = add(line(keep[0]), line(came[0]), self.flip(to_x, 2), self.flip(to_y, 4))
        total = pick(own, self.z).astype(F32)
        for step in range(1, self.inner):
            total = total + self.turn(pick(own, (self.z + step) % self.inner), step).astype(F32)
        return total


class PlainLinks:
    def __init__(self, outer, inner):
        self.outer, self.inner = outer, inner
        self.order = lax.axis_index("dp")
        self.z = lax.axis_index("fsdp")
        self.place = 0

    def gather_small(self, shard):
        return lax.all_gather(shard, AXES, axis=0)

    def whole(self, matrix):
        return lax.all_gather(matrix, AXES, axis=0, tiled=True)

    def scatter_sum(self, keep, send, line):
        flat = jnp.stack([keep, send], axis=1).reshape(-1, keep.shape[-1])
        return lax.psum_scatter(flat, AXES, scatter_dimension=0, tiled=True).astype(F32)


def after(value, *earlier):
    return lax.optimization_barrier((value, *earlier))[0]


def slabs_of(matrix):
    rows, wide = matrix.shape
    return matrix.reshape(rows, wide // 768, 768).transpose(1, 0, 2)


def line_block(parts, down_rows):
    wide = jnp.stack([p[: p.shape[0] - down_rows // 24] for p in parts], axis=1)
    wide = wide.reshape(wide.shape[0], -1, 768)
    if not down_rows:
        return wide
    tall = jnp.stack([p[p.shape[0] - down_rows // 24 :].reshape(down_rows, 768) for p in parts])
    return jnp.concatenate([wide, tall.reshape(-1, 96, 768)])


def gather_weights(links, seg, cross):
    if isinstance(links, PlainLinks):

        def pieces(slabs, tall=None):
            parts = []
            for mask in (0, 2, 4, 6, 1, 3, 5, 7):
                part = slabs[:, mask * 96 : (mask + 1) * 96]
                if tall is not None:
                    part = jnp.concatenate([part, tall[mask * 384 : (mask + 1) * 384].reshape(4, 96, 768)])
                half = part.shape[0] // 2
                parts += [part[:half], part[half:]] if mask > 5 else [part]
            return parts

        qkv, out, up, down = (links.whole(m) for m in seg)
        rest = jnp.concatenate([slabs_of(out), slabs_of(up)])
        return pieces(slabs_of(qkv)), pieces(rest, down), [links.whole(m) for m in cross]
    first = slabs_of(seg[0])
    rest = jnp.concatenate([slabs_of(m) for m in seg[1:3]] + [seg[3].reshape(4, 24, 768)])
    other = jnp.concatenate([slabs_of(m) for m in cross[:3]] + [cross[3].reshape(4, 24, 768)])
    line_first = links.gather_z(first)
    line_rest = links.gather_z(after(rest, *line_first))
    line_other = links.gather_z(after(other, *line_rest))
    block = line_block(line_first, 0)
    near = links.spread_near(block)
    far = links.spread_far(*near)
    first = links.spread_core([block, *near, *far])
    block = after(line_block(line_rest, 96), *far)
    near = links.spread_near(block)
    far = links.spread_far(*near)
    rest = links.spread_core([block, *near, *far])
    block = after(line_block(line_other, 96), *far)
    near = links.spread_near(block)
    far = links.spread_far(*near)
    other = links.spread_core([block, *near, *far])
    return first, rest, other


def shards(
    outer,
    inner,
    tokens,
    cotangent,
    lengths,
    seg_qkv,
    seg_out,
    seg_up,
    seg_down,
    seg_vec,
    cross_qkv,
    cross_out,
    cross_up,
    cross_down,
    cross_vec,
    positions,
):
    fast = (outer, inner) == (8, 4)
    links = (Links if fast else PlainLinks)(outer, inner)
    devices = outer * inner
    me = links.order * inner + links.z
    seq_local, seq_len, feat_dim = tokens.shape
    seg_count = seq_len // SEG
    seg_rows, cross_rows = seg_vec.shape[0], cross_vec.shape[0]
    width = feat_dim // devices
    my_lengths = lax.dynamic_slice_in_dim(lengths, me * seq_local, seq_local)
    info = jnp.concatenate([jnp.full((1,), links.place, jnp.int32), my_lengths])
    small = jnp.concatenate([seg_vec, cross_vec, positions]).reshape(1, -1)
    small = links.gather_small(small).reshape(devices, -1, width)
    small = small.transpose(1, 0, 2).reshape(-1, feat_dim).astype(F32)
    seg_v, cross_v = small[:seg_rows], small[seg_rows : seg_rows + cross_rows]
    pos_table = small[seg_rows + cross_rows :]
    first, rest, other = gather_weights(
        links,
        (seg_qkv, seg_out, seg_up, seg_down),
        (cross_qkv, cross_out, cross_up, cross_down),
    )
    rows_in = tokens.reshape(-1, feat_dim)
    cot_rows = cotangent.reshape(-1, feat_dim)
    seg_starts = jnp.arange(seg_count) * SEG
    live_own = (seg_starts[None, :] < my_lengths[:, None]).reshape(-1, 1)
    up_own = jnp.where(live_own, cotangent.reshape(-1, SEG, feat_dim)[:, 0, :], 0)
    up_all = links.gather_small(up_own).reshape(-1, feat_dim)

    packed, mixed = attn_forward(info, rows_in, seg_v, first, seg_count)
    summed, low, act, slope, second, heads = ffn_forward(info, rows_in, mixed, seg_v, rest)
    heads_own = heads.reshape(-1, feat_dim)
    heads_all = links.gather_small(heads_own.astype(LOW)).reshape(-1, feat_dim)
    live_all = seg_starts[None, :] < lengths[:, None]
    if fast:
        cross_info = jnp.stack([links.place, me]).astype(jnp.int32)
        live = live_all.astype(F32).reshape(-1, 2, SEG)
        cross_own, heads_grad, vec_grad, pos_grad, *cross_grads = cross_whole(
            cross_info, heads_all, up_all, live, cross_v, pos_table, other
        )
    else:
        weights = (*other, cross_v)
        heads_in = heads_all.astype(F32).reshape(-1, seg_count, feat_dim) + pos_table[None]
        heads_in = heads_in.reshape(-1, feat_dim)
        cross_result, kept = encode(heads_in, heads_in.astype(LOW), weights, live_all)
        all_grad, pairs, vec_grad = encode_back(
            up_all.astype(F32), heads_in.astype(LOW), weights, live_all, kept
        )
        cross_grads = []
        for left, right in pairs:
            count = left.shape[1] // devices
            mine = lax.dynamic_slice_in_dim(left, me * count, count, 1)
            cross_grads.append(trans_left(mine, right))
        pos_grad = jnp.sum(all_grad.reshape(-1, seg_count, feat_dim), axis=0)
        own = seq_local * seg_count
        cross_own = lax.dynamic_slice_in_dim(cross_result, me * own, own)
        heads_grad = lax.dynamic_slice_in_dim(all_grad, me * own, own)
    cross_vec_grad = lax.dynamic_slice_in_dim(vec_grad, me * width, width, 1)
    grad_positions = lax.dynamic_slice_in_dim(pos_grad, me * width, width, 1)

    layer_out, down_grad, hidden_grad, proj_grad, mixed_grad, grads_two = ffn_backward(
        info, cot_rows, heads_grad, cross_own, second, summed, slope, seg_v, rest, seg_count
    )
    down_parts = down_weight_grad(info, act, down_grad)
    up_parts = weight_grad(info, low, after(hidden_grad, down_parts[1]))
    out_parts = weight_grad(info, mixed, after(proj_grad, up_parts[1]))
    packed_grad, grads_one = attn_backward(info, packed, after(mixed_grad, out_parts[1]), seg_count)
    qkv_parts = weight_grad(info, rows_in, packed_grad)
    token_grad = token_gradient(info, after(packed_grad, qkv_parts[1]), proj_grad, first)

    def by_rows(part):
        return part.reshape(inner, -1, part.shape[-1])

    grad_down = links.scatter_sum(*down_parts, by_rows)
    grad_up = links.scatter_sum(*up_parts, by_rows)
    grad_out = links.scatter_sum(*out_parts, by_rows)
    grad_qkv = links.scatter_sum(*qkv_parts, by_rows)
    vec_parts = jnp.concatenate([grads_one, grads_two[2:]]).reshape(seg_rows, devices, width)
    vec_parts = vec_parts.transpose(1, 0, 2).reshape(outer, inner, seg_rows * width).astype(LOW)
    if fast:
        flipped = [lax.dynamic_index_in_dim(vec_parts, links.place ^ m, 0, keepdims=False) for m in range(8)]
        keep, send = jnp.stack(flipped[::2]), jnp.stack(flipped[1::2])
    else:
        keep, send = vec_parts[::2], vec_parts[1::2]
    grad_vec = links.scatter_sum(keep, send, by_rows).reshape(seg_rows, width)
    return (
        layer_out.reshape(tokens.shape),
        token_grad.reshape(tokens.shape),
        grad_qkv,
        grad_out,
        grad_up,
        grad_down,
        grad_vec,
        *cross_grads,
        cross_vec_grad,
        grad_positions,
    )


def solution(mesh):
    in_specs = (
        P(("dp", "fsdp"), None, None),
        P(("dp", "fsdp"), None, None),
        P(),
        P(("dp", "fsdp"), None),
        P(("dp", "fsdp"), None),
        P(("dp", "fsdp"), None),
        P(("dp", "fsdp"), None),
        P(None, ("dp", "fsdp")),
        P(("dp", "fsdp"), None),
        P(("dp", "fsdp"), None),
        P(("dp", "fsdp"), None),
        P(("dp", "fsdp"), None),
        P(None, ("dp", "fsdp")),
        P(None, ("dp", "fsdp")),
    )
    out_specs = (
        P(("dp", "fsdp"), None, None),
        P(("dp", "fsdp"), None, None),
        P(("dp", "fsdp"), None),
        P(("dp", "fsdp"), None),
        P(("dp", "fsdp"), None),
        P(("dp", "fsdp"), None),
        P(None, ("dp", "fsdp")),
        P(("dp", "fsdp"), None),
        P(("dp", "fsdp"), None),
        P(("dp", "fsdp"), None),
        P(("dp", "fsdp"), None),
        P(None, ("dp", "fsdp")),
        P(None, ("dp", "fsdp")),
    )
    return jax.shard_map(
        functools.partial(shards, mesh.shape["dp"], mesh.shape["fsdp"]),
        mesh=mesh, in_specs=in_specs, out_specs=out_specs, check_vma=False)
```

time: 1080 us -> 613 us (0.57)
  matrix products: 331 us -> 0 us
  Pallas kernels: 0 us -> 281 us
  local copies, waits for them, and re-layouts: 266 us -> 31.3 us
  other arithmetic: 82.1 us -> 18.3 us
  waiting for transfers between devices: 230 us -> 167 us
  starting transfers between devices: 158 us -> 109 us
    dot_general x36 -> x0, matrix products: 331 us -> none  [the longest x8 128 us: matmul(): return jnp.dot(left_op, right_op, preferred_element_type=jnp.float32)]
    pallas_call x0 -> x10, Pallas kernels: none -> 281 us  [the longest x1 50.1 us: cross_whole(): pl.pallas_call(functools.partial(cross_kernel, rows // count), grid=(rows...]
    dynamic_update_slice x148 -> x0, local copies, waits for them, and re-layouts: 94.5 us -> none  [the longest x80 70.1 us: assemble(): whole = lax.dynamic_update_slice(whole, piece[None], where)]
    ppermute x118 -> x64, waiting for transfers between devices: 187 us -> 111 us  [flip(): return lax.ppermute(value, AXES, pairs)]
    reduce_sum x18 -> x0, other arithmetic: 39.1 us -> none  [the longest x3 7.09 us: norm_backward(): jnp.sum(upstream, axis=0)]
    ppermute x118 -> x64, starting transfers between devices: 80.6 us -> 48.9 us  [flip(): return lax.ppermute(value, AXES, pairs)]
    unnamed x312 -> x72, local copies, waits for them, and re-layouts: 34.7 us -> 8.63 us
    convert_element_type x10 -> x6, local copies, waits for them, and re-layouts: 22.3 us -> 0.75 us  [the longest x2 0.37 us: shards(): small = small.transpose(1, 0, 2).reshape(-1, feat_dim).astype(F32)]
  transfers between devices with their start and end apart: 166 -> 97, of which waited for: 80 -> 37; matrix products, arithmetic and copies ran while one was open for 31% -> 7% of each run, Pallas kernels for 0% -> 26%
where the time goes in v3:
time: 613 us; the launch traced here: 608 us
  Pallas kernels  281 us (46%)
  waiting for transfers between devices  167 us (27%)
  starting transfers between devices  109 us (18%)
  local copies, waits for them, and re-layouts  31.3 us (5%)
  other arithmetic  18.3 us (3%)
    ppermute x64, waiting for transfers between devices, flip(): return lax.ppermute(value, AXES, pairs)  111 us
    ppermute x33, starting transfers between devices, turn(): return lax.ppermute(value, AXES, pairs)  60.1 us
    ppermute x33, waiting for transfers between devices, turn(): return lax.ppermute(value, AXES, pairs)  56 us
    pallas_call x1, Pallas kernels, cross_whole(): pl.pallas_call(functools.partial(cross_kernel, rows // count), grid=(rows...  50.1 us
    pallas_call x1, Pallas kernels, attn_backward(): pl.pallas_call(functools.partial(attn_backward_kernel, segs, seg_count),...  49.6 us
    ppermute x64, starting transfers between devices, flip(): return lax.ppermute(value, AXES, pairs)  48.9 us
    pallas_call x1, Pallas kernels, ffn_forward(): pl.pallas_call(functools.partial(ffn_forward_kernel, segs), grid=(rows //...  48.7 us
    pallas_call x1, Pallas kernels, ffn_backward(): pl.pallas_call(functools.partial(ffn_backward_kernel, segs, seg_count), g...  40.6 us
  transfers between devices with their start and end apart: 97, of which 37 were waited for; matrix products, arithmetic and copies ran while one was open for 7% of the time, Pallas kernels for 26%

profile of v3, /device:TPU:0, one launch (start us, length us, event | category | flops | bytes accessed | tf_op | source)
XLA Modules:
  0.0 608.4 jit_solution(1808011722342285545)
XLA Ops:
  1.6 5.1 collective-permute-start.2
  33.3 5.0 collective-permute-done.7
  42.0 14.4 %collective-permute-done.21 = bf16[9,24,768]{2,1,0:T(8,128)(2,1)S(1)} collective-permute-done((bf16[9,24,768]{2,1,0:T(8,128)(2,1)S(1)}, bf16[9,24,768]{2,1,0:T(8,128)(2,1)S(1)}, u32[]{:S(2)}, u32[]{:S(2)}) %collective-permute-start.21) | collective-permute-done | bytes 331808 | tf_op jit(solution)/shard_map/ppermute | solution.py:804
  57.5 9.6 %collective-permute-done.19 = bf16[9,24,768]{2,1,0:T(8,128)(2,1)S(1)} collective-permute-done((bf16[9,24,768]{2,1,0:T(8,128)(2,1)S(1)}, bf16[9,24,768]{2,1,0:T(8,128)(2,1)S(1)}, u32[]{:S(2)}, u32[]{:S(2)}) %collective-permute-start.19) | collective-permute-done | bytes 331808 | tf_op jit(solution)/shard_map/ppermute | solution.py:804
  79.1 5.4 collective-permute-start.47
  85.7 22.7 %collective-permute-done.43 = bf16[4,16,768]{2,1,0:T(8,128)(2,1)S(1)} collective-permute-done((bf16[4,16,768]{2,1,0:T(8,128)(2,1)S(1)}, bf16[4,16,768]{2,1,0:T(8,128)(2,1)S(1)}, u32[]{:S(2)}, u32[]{:S(2)}) %collective-permute-start.43) | collective-permute-done | bytes 98336 | tf_op jit(solution)/shard_map/ppermute | solution.py:796
  112.7 7.6 %collective-permute-done.45 = bf16[12,24,768]{2,1,0:T(8,128)(2,1)S(1)} collective-permute-done((bf16[12,24,768]{2,1,0:T(8,128)(2,1)S(1)}, bf16[12,24,768]{2,1,0:T(8,128)(2,1)S(1)}, u32[]{:S(2)}, u32[]{:S(2)}) %collective-permute-start.45) | collective-permute-done | bytes 442400 | tf_op jit(solution)/shard_map/ppermute | solution.py:804
  123.6 17.1 %collective-permute-done.23.rest_2_ = bf16[9,96,768]{2,1,0:T(8,128)(2,1)} collective-permute-done((bf16[9,96,768]{2,1,0:T(8,128)(2,1)}, bf16[9,96,768]{2,1,0:T(8,128)(2,1)}, u32[]{:S(2)}, u32[]{:S(2)}) %collective-permute-start.23) | collective-permute-done | bytes 1327136 | tf_op jit(solution)/shard_map/ppermute | solution.py:796
  152.7 27.1 %attn_forward.1 = (bf16[2048,2304]{1,0:T(8,128)(2,1)}, bf16[2048,768]{1,0:T(8,128)(2,1)}) custom-call(s32[3]{0:T(128)} %pad_add_fusion.info, bf16[2048,768]{1,0:T(8,128)(2,1)} %bitcast.356, f32[12,768]{1,0:T(8,128)} %slice.390.vec_ref, bf16[3,96,768]{2,1,0:T(8,128)(2,1)} %bitcast.318, bf16[3,96,768]{2,1,0:T(8,128)(2,1)} %copy-done.8, ...), custom_call_target="tpu_custom_call" | custom-call | flops 25165824000 | bytes 25165824 | tf_op jit(solution)/shard_map/attn_forward/pallas_call | solution.py:459
  183.8 48.7 %ffn_forward.1 = (f32[2048,768]{1,0:T(8,128)}, bf16[2048,768]{1,0:T(8,128)(2,1)}, bf16[2048,3072]{1,0:T(8,128)(2,1)}, bf16[2048,3072]{1,0:T(8,128)(2,1)}, f32[2048,768]{1,0:T(8,128)}, /*index=5*/f32[8,2,768]{2,1,0:T(2,128)}) custom-call(s32[3]{0:T(128)} %pad_add_fusion.info, bf16[2048,768]{1,0:T(8,128)(2,1)} %bitcast.357, ...), custom_call_target="tpu_custom_call" | custom-call | flops 44040192000 | bytes 47185920 | tf_op jit(solution)/shard_map/ffn_forward/pallas_call | solution.py:477
  233.3 7.1 %collective-permute-start.33 = (bf16[16,768]{1,0:T(8,128)(2,1)S(1)}, bf16[16,768]{1,0:T(8,128)(2,1)S(1)}, u32[]{:S(2)}, u32[]{:S(2)}) collective-permute-start(bf16[16,768]{1,0:T(8,128)(2,1)S(1)} %convert_element_type.530), channel_id=1, source_target_pairs={{0,3},{1,0},{2,1},{3,2},{4,7},{5,4},{6,5},{7,6},{8,11},{9,8},{10,9... | collective-permute-start | bytes 73736 | tf_op jit(solution)/shard_map/ppermute | solution.py:804
  264.3 15.3 %collective-permute-done.50.rest_3_ = bf16[6,96,768]{2,1,0:T(8,128)(2,1)} collective-permute-done((bf16[6,96,768]{2,1,0:T(8,128)(2,1)S(1)}, bf16[6,96,768]{2,1,0:T(8,128)(2,1)}, u32[]{:S(2)}, u32[]{:S(2)}) %collective-permute-start.50) | collective-permute-done | bytes 884768 | tf_op jit(solution)/shard_map/ppermute | solution.py:796
  287.1 50.1 %cross_encoder.1 = (f32[16,768]{1,0:T(8,128)}, f32[16,768]{1,0:T(8,128)}, f32[12,768]{1,0:T(8,128)}, f32[8,768]{1,0:T(8,128)}, f32[24,2304]{1,0:T(8,128)}, /*ind...) custom-call(s32[2]{0:T(128)} %pad_add_fusion.1.info, bf16[512,768]{1,0:T(8,128)(2,1)} %bitcast.296, ...), custom_call_target="tpu_custom_call" | custom-call | flops 23592960000 | bytes 16777216 | tf_op jit(solution)/shard_map/cross_encoder/pallas_call | solution.py:497
  340.1 40.6 %ffn_backward.1 = (bf16[2048,768]{1,0:T(8,128)(2,1)}, bf16[2048,768]{1,0:T(8,128)(2,1)}, bf16[2048,3072]{1,0:T(8,128)(2,1)}, bf16[2048,768]{1,0:T(8,128)(2,1)}, ...) custom-call(s32[3]{0:T(128)} %pad_add_fusion.info, bf16[2048,768]{1,0:T(8,128)(2,1)} %bitcast.355, ...), custom_call_target="tpu_custom_call" | custom-call | flops 44040192000 | bytes 47185920 | tf_op jit(solution)/shard_map/ffn_backward/pallas_call | solution.py:520
  380.7 16.0 %down_weight_grad.1 = (bf16[4,384,768]{2,1,0:T(8,128)(2,1)}, bf16[4,384,768]{2,1,0:T(8,128)(2,1)}) custom-call(s32[3]{0:T(128)} %pad_add_fusion.info, bf16[2048,3072]{1,0:T(8,128)(2,1)} %get-tuple-element.70.left_ref, bf16[2048,768]{1,0:T(8,128)(2,1)} %get-tuple-element.71.right_ref), custom_call_target="tpu_custom_call" | custom-call | flops 9663676416 | bytes 12582912 | tf_op jit(solution)/shard_map/down_weight_grad/pallas_call | solution.py:600
  396.7 15.0 %weight_grad.3 = (bf16[4,96,3072]{2,1,0:T(8,128)(2,1)}, bf16[4,96,3072]{2,1,0:T(8,128)(2,1)}) custom-call(s32[3]{0:T(128)} %pad_add_fusion.info, bf16[2048,768]{1,0:T(8,128)(2,1)} %get-tuple-element.68.left_ref, bf16[2048,3072]{1,0:T(8,128)(2,1)} %get-tuple-element.73.right_ref), custom_call_target="tpu_custom_call" | custom-call | flops 9663676416 | bytes 12582912 | tf_op jit(solution)/shard_map/weight_grad/pallas_call | solution.py:573
  412.2 6.6 %weight_grad.4 = (bf16[4,96,768]{2,1,0:T(8,128)(2,1)}, bf16[4,96,768]{2,1,0:T(8,128)(2,1)}) custom-call(s32[3]{0:T(128)} %pad_add_fusion.info, bf16[2048,768]{1,0:T(8,128)(2,1)} %get-tuple-element.53.mixed_ref.left_ref, bf16[2048,768]{1,0:T(8,128)(2,1)} %get-tuple-element.75.right_ref.proj_grad_ref), custom_call_target="tpu_custom_call" | custom-call | flops 2415919104 | bytes 3145728 | tf_op jit(solution)/shard_map/weight_grad/pallas_call | solution.py:573
  418.9 49.6 %attn_backward.1 = (bf16[2048,2304]{1,0:T(8,128)(2,1)}, f32[2,768]{1,0:T(2,128)}) custom-call(s32[3]{0:T(128)} %pad_add_fusion.info, bf16[2048,2304]{1,0:T(8,128)(2,1)} %get-tuple-element.65.packed_ref, bf16[2048,768]{1,0:T(8,128)(2,1)} %get-tuple-element.77.mixed_grad_ref), custom_call_target="tpu_custom_call" | custom-call | flops 50331648000 | bytes 25165824 | tf_op jit(solution)/shard_map/attn_backward/pallas_call | solution.py:539
  468.5 12.3 %weight_grad.5 = (bf16[4,96,2304]{2,1,0:T(8,128)(2,1)}, bf16[4,96,2304]{2,1,0:T(8,128)(2,1)}) custom-call(s32[3]{0:T(128)} %pad_add_fusion.info, bf16[2048,768]{1,0:T(8,128)(2,1)} %bitcast.358, bf16[2048,2304]{1,0:T(8,128)(2,1)} %get-tuple-element.80.right_ref.packed_grad_ref), custom_call_target="tpu_custom_call" | custom-call | flops 7247757312 | bytes 9437184 | tf_op jit(solution)/shard_map/weight_grad/pallas_call | solution.py:573
  483.8 14.9 %token_gradient.1 = bf16[2048,768]{1,0:T(8,128)(2,1)} custom-call(s32[3]{0:T(128)} %pad_add_fusion.info, bf16[2048,2304]{1,0:T(8,128)(2,1)} %get-tuple-element.80.right_ref.packed_grad_ref, bf16[2048,768]{1,0:T(8,128)(2,1)} %get-tuple-element.75.right_ref.proj_grad_ref, bf16[3,96,768]{2,1,0:T(8,128)(2,1)} %bitcast.319, bf16[3,96,768]{2,1,0:T(8,128)(2,1)} %copy-done.8, ...), custom_call_target="tpu_custom_call" | custom-call | flops 9437184000 | bytes 15728640 | tf_op jit(solution)/shard_map/token_gradient/pallas_call | solution.py:554
  551.5 4.6 collective-permute-done.59
  569.7 4.5 collective-permute-done.82
  576.7 7.8 %collective-permute-done.75 = bf16[4,24,3072]{2,1,0:T(8,128)(2,1)S(1)} collective-permute-done((bf16[4,24,3072]{2,1,0:T(8,128)(2,1)S(1)}, bf16[4,24,3072]{2,1,0:T(8,128)(2,1)S(1)}, u32[]{:S(2)}, u32[]{:S(2)}) %collective-permute-start.75) | collective-permute-done | bytes 589856 | tf_op jit(solution)/shard_map/ppermute | solution.py:796
  595.0 6.7 %collective-permute-start.87 = (bf16[96,768]{1,0:T(8,128)(2,1)S(1)}, bf16[96,768]{1,0:T(8,128)(2,1)S(1)}, u32[]{:S(2)}, u32[]{:S(2)}) collective-permute-start(bf16[96,768]{1,0:T(8,128)(2,1)S(1)} %get-tuple-element.119), channel_id=1, source_target_pairs={{0,2},{1,3},{2,0},{3,1},{4,6},{5,7},{6,4},{7,5},{8,10},{9,11},{10,... | collective-permute-start | bytes 442376 | tf_op jit(solution)/shard_map/ppermute | solution.py:804
  (411 shorter events, 192.3 us)
Async XLA Ops:
  9.6 29.3 %collective-permute-start.40 = (bf16[16,768]{1,0:T(8,128)(2,1)S(1)}, bf16[16,768]{1,0:T(8,128)(2,1)S(1)}, u32[]{:S(2)}, u32[]{:S(2)}) collective-permute-start(bf16[16,768]{1,0:T(8,128)(2,1)S(1)} %fusion.17), channel_id=1, source_target_pairs={{0,3},{1,0},{2,1},{3,2},{4,7},{5,4},{6,5},{7,6},{8,11},{9,8},{10,9... | collective-permute-start | bytes 73736 | tf_op jit(solution)/shard_map/ppermute | solution.py:804
  12.4 28.3 %collective-permute-start.39 = (bf16[16,768]{1,0:T(8,128)(2,1)S(1)}, bf16[16,768]{1,0:T(8,128)(2,1)S(1)}, u32[]{:S(2)}, u32[]{:S(2)}) collective-permute-start(bf16[16,768]{1,0:T(8,128)(2,1)S(1)} %fusion.17), channel_id=1, source_target_pairs={{0,1},{1,2},{2,3},{3,0},{4,5},{5,6},{6,7},{7,4},{8,9},{9,10},{10,1... | collective-permute-start | bytes 73736 | tf_op jit(solution)/shard_map/ppermute | solution.py:804
  33.3 51.2 %collective-permute-start.6 = (bf16[2,2,4,1,768]{4,2,1,3,0:T(4,128)(2,1)S(1)}, bf16[2,2,4,1,768]{4,2,1,3,0:T(4,128)(2,1)S(1)}, u32[]{:S(2)}, u32[]{:S(2)}) collective-permute-start(bf16[2,2,4,1,768]{4,2,1,3,0:T(4,128)(2,1)S(1)} %maximum_select_fusion.11), channel_id=1, source_target_pairs={{0,4},{1,5},{2,6},{3,7},{4,0},{5,1},{6,2},{7,3},{8,12},{9,13},{10,... | collective-permute-start | bytes 73736 | tf_op jit(solution)/shard_map/ppermute | solution.py:796
  40.8 43.8 %collective-permute-start.42 = (bf16[4,16,768]{2,1,0:T(8,128)(2,1)S(1)}, bf16[4,16,768]{2,1,0:T(8,128)(2,1)}, u32[]{:S(2)}, u32[]{:S(2)}) collective-permute-start(bf16[4,16,768]{2,1,0:T(8,128)(2,1)S(1)} %get-tuple-element.160), channel_id=1, source_target_pairs={{0,16},{1,17},{2,18},{3,19},{4,20},{5,21},{6,22},{7,23},{8,24},{9,... | collective-permute-start | bytes 294920 | tf_op jit(solution)/shard_map/ppermute | solution.py:796
  77.2 43.3 %collective-permute-start.22 = (bf16[9,96,768]{2,1,0:T(8,128)(2,1)}, bf16[9,96,768]{2,1,0:T(8,128)(2,1)}, u32[]{:S(2)}, u32[]{:S(2)}) collective-permute-start(bf16[9,96,768]{2,1,0:T(8,128)(2,1)} %bitcast_dynamic-update-slice_fusion.4.rest_0_), channel_id=1, source_target_pairs={{0,8},{1,9},{2,10},{3,11},{4,12},{5,13},{6,14},{7,15},{8,0},{9,1},... | collective-permute-start | bytes 3981320 | tf_op jit(solution)/shard_map/ppermute | solution.py:796
  77.9 30.4 %collective-permute-start.43 = (bf16[4,16,768]{2,1,0:T(8,128)(2,1)S(1)}, bf16[4,16,768]{2,1,0:T(8,128)(2,1)S(1)}, u32[]{:S(2)}, u32[]{:S(2)}) collective-permute-start(bf16[4,16,768]{2,1,0:T(8,128)(2,1)S(1)} %get-tuple-element.160), channel_id=1, source_target_pairs={{0,24},{1,25},{2,26},{3,27},{4,28},{5,29},{6,30},{7,31},{8,16},{9,... | collective-permute-start | bytes 294920 | tf_op jit(solution)/shard_map/ppermute | solution.py:796
  79.1 33.0 %collective-permute-start.47 = (bf16[12,24,768]{2,1,0:T(8,128)(2,1)S(1)}, bf16[12,24,768]{2,1,0:T(8,128)(2,1)S(1)}, u32[]{:S(2)}, u32[]{:S(2)}) collective-permute-start(bf16[12,24,768]{2,1,0:T(8,128)(2,1)S(1)} %pad_maximum_fusion.7), channel_id=1, source_target_pairs={{0,3},{1,0},{2,1},{3,2},{4,7},{5,4},{6,5},{7,6},{8,11},{9,8},{10,9... | collective-permute-start | bytes 1327112 | tf_op jit(solution)/shard_map/ppermute | solution.py:804
  84.5 27.7 %collective-permute-start.46 = (bf16[12,24,768]{2,1,0:T(8,128)(2,1)S(1)}, bf16[12,24,768]{2,1,0:T(8,128)(2,1)S(1)}, u32[]{:S(2)}, u32[]{:S(2)}) collective-permute-start(bf16[12,24,768]{2,1,0:T(8,128)(2,1)S(1)} %pad_maximum_fusion.7), channel_id=1, source_target_pairs={{0,1},{1,2},{2,3},{3,0},{4,5},{5,6},{6,7},{7,4},{8,9},{9,10},{10,1... | collective-permute-start | bytes 1327112 | tf_op jit(solution)/shard_map/ppermute | solution.py:804
  84.7 35.6 %collective-permute-start.45 = (bf16[12,24,768]{2,1,0:T(8,128)(2,1)S(1)}, bf16[12,24,768]{2,1,0:T(8,128)(2,1)S(1)}, u32[]{:S(2)}, u32[]{:S(2)}) collective-permute-start(bf16[12,24,768]{2,1,0:T(8,128)(2,1)S(1)} %pad_maximum_fusion.7), channel_id=1, source_target_pairs={{0,2},{1,3},{2,0},{3,1},{4,6},{5,7},{6,4},{7,5},{8,10},{9,11},{10,... | collective-permute-start | bytes 1327112 | tf_op jit(solution)/shard_map/ppermute | solution.py:804
  108.3 32.4 %collective-permute-start.23 = (bf16[9,96,768]{2,1,0:T(8,128)(2,1)}, bf16[9,96,768]{2,1,0:T(8,128)(2,1)}, u32[]{:S(2)}, u32[]{:S(2)}) collective-permute-start(bf16[9,96,768]{2,1,0:T(8,128)(2,1)} %bitcast_dynamic-update-slice_fusion.4.rest_0_), channel_id=1, source_target_pairs={{0,16},{1,17},{2,18},{3,19},{4,20},{5,21},{6,22},{7,23},{8,24},{9,... | collective-permute-start | bytes 3981320 | tf_op jit(solution)/shard_map/ppermute | solution.py:796
  112.1 31.4 %collective-permute-start.14 = (bf16[3,96,768]{2,1,0:T(8,128)(2,1)S(1)}, bf16[3,96,768]{2,1,0:T(8,128)(2,1)S(1)}, u32[]{:S(2)}, u32[]{:S(2)}) collective-permute-start(bf16[3,96,768]{2,1,0:T(8,128)(2,1)S(1)} %bitcast.317), channel_id=1, source_target_pairs={{0,4},{1,5},{2,6},{3,7},{4,0},{5,1},{6,2},{7,3},{8,12},{9,13},{10,... | collective-permute-start | bytes 1327112 | tf_op jit(solution)/shard_map/ppermute | solution.py:796
  112.2 34.7 %collective-permute-start.16 = (bf16[3,96,768]{2,1,0:T(8,128)(2,1)}, bf16[3,96,768]{2,1,0:T(8,128)(2,1)S(1)}, u32[]{:S(2)}, u32[]{:S(2)}) collective-permute-start(bf16[3,96,768]{2,1,0:T(8,128)(2,1)} %copy-done.15), channel_id=1, source_target_pairs={{0,4},{1,5},{2,6},{3,7},{4,0},{5,1},{6,2},{7,3},{8,12},{9,13},{10,... | collective-permute-start | bytes 1327112 | tf_op jit(solution)/shard_map/ppermute | solution.py:796
  121.7 31.0 %collective-permute-start.25 = (bf16[5,96,768]{2,1,0:T(8,128)(2,1)S(1)}, bf16[5,96,768]{2,1,0:T(8,128)(2,1)}, u32[]{:S(2)}, u32[]{:S(2)}) collective-permute-start(bf16[5,96,768]{2,1,0:T(8,128)(2,1)S(1)} %slice.517), channel_id=1, source_target_pairs={{0,16},{1,17},{2,18},{3,19},{4,20},{5,21},{6,22},{7,23},{8,24},{9,... | collective-permute-start | bytes 2211848 | tf_op jit(solution)/shard_map/ppermute | solution.py:796
  146.8 33.0 %collective-permute-start.26 = (bf16[9,96,768]{2,1,0:T(8,128)(2,1)}, bf16[9,96,768]{2,1,0:T(8,128)(2,1)S(1)}, u32[]{:S(2)}, u32[]{:S(2)}) collective-permute-start(bf16[9,96,768]{2,1,0:T(8,128)(2,1)} %bitcast_dynamic-update-slice_fusion.4.rest_0_), channel_id=1, source_target_pairs={{0,4},{1,5},{2,6},{3,7},{4,0},{5,1},{6,2},{7,3},{8,12},{9,13},{10,... | collective-permute-start | bytes 3981320 | tf_op jit(solution)/shard_map/ppermute | solution.py:796
  146.9 35.4 %collective-permute-start.28 = (bf16[9,96,768]{2,1,0:T(8,128)(2,1)}, bf16[9,96,768]{2,1,0:T(8,128)(2,1)}, u32[]{:S(2)}, u32[]{:S(2)}) collective-permute-start(bf16[9,96,768]{2,1,0:T(8,128)(2,1)} %collective-permute-done.23.rest_2_), channel_id=1, source_target_pairs={{0,4},{1,5},{2,6},{3,7},{4,0},{5,1},{6,2},{7,3},{8,12},{9,13},{10,... | collective-permute-start | bytes 3981320 | tf_op jit(solution)/shard_map/ppermute | solution.py:796
  147.3 36.4 %collective-permute-start.27 = (bf16[9,96,768]{2,1,0:T(8,128)(2,1)}, bf16[9,96,768]{2,1,0:T(8,128)(2,1)}, u32[]{:S(2)}, u32[]{:S(2)}) collective-permute-start(bf16[9,96,768]{2,1,0:T(8,128)(2,1)} %collective-permute-done.22.rest_1_), channel_id=1, source_target_pairs={{0,4},{1,5},{2,6},{3,7},{4,0},{5,1},{6,2},{7,3},{8,12},{9,13},{10,... | collective-permute-start | bytes 3981320 | tf_op jit(solution)/shard_map/ppermute | solution.py:796
  151.9 28.4 %collective-permute-start.29 = (bf16[4,96,768]{2,1,0:T(8,128)(2,1)}, bf16[4,96,768]{2,1,0:T(8,128)(2,1)}, u32[]{:S(2)}, u32[]{:S(2)}) collective-permute-start(bf16[4,96,768]{2,1,0:T(8,128)(2,1)} %collective-permute-done.24.rest_3_), channel_id=1, source_target_pairs={{0,4},{1,5},{2,6},{3,7},{4,0},{5,1},{6,2},{7,3},{8,12},{9,13},{10,... | collective-permute-start | bytes 1769480 | tf_op jit(solution)/shard_map/ppermute | solution.py:796
  152.7 31.1 %collective-permute-start.30 = (bf16[5,96,768]{2,1,0:T(8,128)(2,1)}, bf16[5,96,768]{2,1,0:T(8,128)(2,1)}, u32[]{:S(2)}, u32[]{:S(2)}) collective-permute-start(bf16[5,96,768]{2,1,0:T(8,128)(2,1)} %collective-permute-done.25.rest_4_), channel_id=1, source_target_pairs={{0,4},{1,5},{2,6},{3,7},{4,0},{5,1},{6,2},{7,3},{8,12},{9,13},{10,... | collective-permute-start | bytes 2211848 | tf_op jit(solution)/shard_map/ppermute | solution.py:796
  179.8 60.6 %collective-permute-start.41 = (bf16[4,16,768]{2,1,0:T(8,128)(2,1)S(1)}, bf16[4,16,768]{2,1,0:T(8,128)(2,1)S(1)}, u32[]{:S(2)}, u32[]{:S(2)}) collective-permute-start(bf16[4,16,768]{2,1,0:T(8,128)(2,1)S(1)} %get-tuple-element.160), channel_id=1, source_target_pairs={{0,8},{1,9},{2,10},{3,11},{4,12},{5,13},{6,14},{7,15},{8,0},{9,1},... | collective-permute-start | bytes 294920 | tf_op jit(solution)/shard_map/ppermute | solution.py:796
  180.3 75.9 %collective-permute-start.49 = (bf16[12,96,768]{2,1,0:T(8,128)(2,1)}, bf16[12,96,768]{2,1,0:T(8,128)(2,1)}, u32[]{:S(2)}, u32[]{:S(2)}) collective-permute-start(bf16[12,96,768]{2,1,0:T(8,128)(2,1)} %bitcast_dynamic-update-slice_fusion.rest_0_), channel_id=1, source_target_pairs={{0,16},{1,17},{2,18},{3,19},{4,20},{5,21},{6,22},{7,23},{8,24},{9,... | collective-permute-start | bytes 5308424 | tf_op jit(solution)/shard_map/ppermute | solution.py:796
  182.3 76.1 %collective-permute-start.48 = (bf16[12,96,768]{2,1,0:T(8,128)(2,1)}, bf16[12,96,768]{2,1,0:T(8,128)(2,1)}, u32[]{:S(2)}, u32[]{:S(2)}) collective-permute-start(bf16[12,96,768]{2,1,0:T(8,128)(2,1)} %bitcast_dynamic-update-slice_fusion.rest_0_), channel_id=1, source_target_pairs={{0,8},{1,9},{2,10},{3,11},{4,12},{5,13},{6,14},{7,15},{8,0},{9,1},... | collective-permute-start | bytes 5308424 | tf_op jit(solution)/shard_map/ppermute | solution.py:796
  411.7 135.9 %collective-permute-start.73 = (bf16[4,96,3072]{2,1,0:T(8,128)(2,1)}, bf16[4,96,3072]{2,1,0:T(8,128)(2,1)S(1)}, u32[]{:S(2)}, u32[]{:S(2)}) collective-permute-start(bf16[4,96,3072]{2,1,0:T(8,128)(2,1)} %get-tuple-element.74), channel_id=1, source_target_pairs={{0,4},{1,5},{2,6},{3,7},{4,0},{5,1},{6,2},{7,3},{8,12},{9,13},{10,... | collective-permute-start | bytes 7077896 | tf_op jit(solution)/shard_map/ppermute | solution.py:796
  418.9 87.2 %collective-permute-start.65 = (bf16[4,96,768]{2,1,0:T(8,128)(2,1)}, bf16[4,96,768]{2,1,0:T(8,128)(2,1)S(1)}, u32[]{:S(2)}, u32[]{:S(2)}) collective-permute-start(bf16[4,96,768]{2,1,0:T(8,128)(2,1)} %get-tuple-element.76), channel_id=1, source_target_pairs={{0,4},{1,5},{2,6},{3,7},{4,0},{5,1},{6,2},{7,3},{8,12},{9,13},{10,... | collective-permute-start | bytes 1769480 | tf_op jit(solution)/shard_map/ppermute | solution.py:796
  480.8 53.8 %collective-permute-start.57 = (bf16[4,96,2304]{2,1,0:T(8,128)(2,1)}, bf16[4,96,2304]{2,1,0:T(8,128)(2,1)}, u32[]{:S(2)}, u32[]{:S(2)}) collective-permute-start(bf16[4,96,2304]{2,1,0:T(8,128)(2,1)} %get-tuple-element.79), channel_id=1, source_target_pairs={{0,4},{1,5},{2,6},{3,7},{4,0},{5,1},{6,2},{7,3},{8,12},{9,13},{10,... | collective-permute-start | bytes 5308424 | tf_op jit(solution)/shard_map/ppermute | solution.py:796
  (105 other events, 1100.1 us)

commit v4 on v3

--- a/solution.py
+++ b/solution.py
@@ -47,15 +47,8 @@
 
 
 def gelu_parts(hidden):
-    size = jnp.abs(hidden)
-    near = 1.0 / (1.0 + (0.3275911 * 0.7071067811865476) * size)
-    bell = jnp.exp(-0.5 * hidden * hidden)
-    poly = 0.5 * 1.061405429
-    for term in (-1.453152027, 1.421413741, -0.284496736, 0.254829592):
-        poly = poly * near + 0.5 * term
-    tail = poly * near * bell
-    phi = jnp.where(hidden < 0.0, tail, 1.0 - tail)
-    return hidden * phi, phi + hidden * bell * 0.3989422804014327
+    phi = 0.5 * (1.0 + lax.erf(hidden * ROOT_HALF))
+    return hidden * phi, phi + hidden * jnp.exp(-0.5 * hidden * hidden) * INV_ROOT_TAU
 
 
 def pair_stack(pair, low_half):
@@ -70,93 +63,87 @@
     return jnp.where(low_half, stacked[:rows], stacked[rows:])
 
 
-def pair_probs(query_stack, keys, allowed):
-    scores = jnp.where(allowed, mm_nt(query_stack, keys), MASK_FILL)
-    expo = jnp.exp(scores - jnp.max(scores, axis=-1, keepdims=True))
-    return expo
+def pair_probs(stack, keys, allowed):
+    scores = jnp.where(allowed, mm_nt(keys, stack), MASK_FILL)
+    expo = jnp.exp(scores - jnp.max(scores, axis=0, keepdims=True))
+    return expo * (1.0 / jnp.sum(expo, axis=0, keepdims=True))
 
 
 def attend(query, keys, values, allowed):
     low_half = lax.broadcasted_iota(jnp.int32, query.shape, 1) < HEAD
     stack = pair_stack(query * jnp.asarray(HEAD**-0.5, query.dtype), low_half)
-    expo = pair_probs(stack, keys, allowed).astype(LOW)
-    wide = jnp.concatenate([values, jnp.ones_like(values)], axis=1)
-    both = mm(expo, wide)
-    out = both[:, :128] / both[:, 128:]
-    return pair_merge(out, low_half)
+    return pair_merge(mm_tn(pair_probs(stack, keys, allowed).astype(LOW), values), low_half)
 
 
 def attend_back(query, keys, values, grad_mixed, allowed):
     low_half = lax.broadcasted_iota(jnp.int32, query.shape, 1) < HEAD
     stack = pair_stack(query * jnp.asarray(HEAD**-0.5, query.dtype), low_half)
-    expo = pair_probs(stack, keys, allowed)
-    probs = expo / jnp.sum(expo, axis=-1, keepdims=True)
+    probs = pair_probs(stack, keys, allowed)
     grad_stack = pair_stack(grad_mixed, low_half)
-    grad_prob = mm_nt(grad_stack, values)
-    weighted = probs * grad_prob
-    score_grad = (weighted - probs * jnp.sum(weighted, axis=-1, keepdims=True)).astype(LOW)
-    grad_query = pair_merge(mm(score_grad, keys), low_half) * HEAD**-0.5
-    grad_keys = mm_tn(score_grad, stack)
-    grad_values = mm_tn(probs.astype(LOW), grad_stack)
-    return grad_query, grad_keys, grad_values
-
-
-def load_slabs(place, pieces, slabs, sems):
-    for _, copy in slab_copies(place, pieces, slabs, sems, True):
-        copy.wait()
-
-
-def slab_copies(place, pieces, slabs, sems, start, first_slab=0):
+    grad_prob = mm_nt(values, grad_stack)
+    inner = jnp.sum(probs * grad_prob, axis=0, keepdims=True)
+    score_grad = (probs * (grad_prob - inner)).astype(LOW)
+    grad_query = pair_merge(mm_tn(score_grad, keys), low_half) * HEAD**-0.5
+    return grad_query, mm(score_grad, stack), mm(probs.astype(LOW), grad_stack)
+
+
+def slab_copies(place, pieces, slabs, sems, first_sem=0):
     count = len(slabs)
-    half = count // 2
+    half = (count + 1) // 2
+    spans = [(0, 0, count), (2, 0, count), (4, 0, count)]
+    spans += [(6, 0, count)] if len(pieces) == 8 else [(6, 0, half), (6, half, count)]
     copies = []
-    spans = ((0, 0, count), (2, 0, count), (4, 0, count), (6, 0, half), (6, half, count))
     for flip_c in (0, 1):
         for index, (flip_yx, first, last) in enumerate(spans):
             block = place ^ (flip_yx + flip_c)
-            piece = pieces[flip_c * 5 + index]
+            piece = pieces[flip_c * len(spans) + index]
             for slab in range(first, last):
-                if slab < first_slab:
-                    continue
-                sem = sems.at[slab * 8 + (flip_yx + flip_c)]
-                source, target = piece.at[slab - first], slabs[slab](block)
-                copies.append((slab, pltpu.make_async_copy(source, target, sem)))
-    if start:
-        for _, copy in copies:
-            copy.start()
+                source = piece.at[pl.ds((slab - first) * 96, 96)]
+                sem = sems.at[first_sem + slab * 8 + flip_yx + flip_c]
+                copies.append(pltpu.make_async_copy(source, slabs[slab](block), sem))
     return copies
 
 
-def rows_of(ref, block, rows, slab=None):
+def load(copies):
+    for copy in copies:
+        copy.start()
+    for copy in copies:
+        copy.wait()
+
+
+def rows_of(ref, block, rows=96, slab=None):
     where = pl.ds(pl.multiple_of(block * rows, rows), rows)
     return ref.at[where] if slab is None else ref.at[slab, where]
 
 
+def down_rows(ref, block, part):
+    return ref.at[pl.ds(pl.multiple_of(block * 384 + part * 96, 96), 96)]
+
+
 def qkv_slabs(qkv):
-    return [functools.partial(rows_of, qkv, rows=96, slab=j) for j in range(3)]
-
-
-def rest_slabs(out, up, down):
-    def down_slab(block, part):
-        return down.at[pl.ds(pl.multiple_of(block * 384 + part * 96, 96), 96)]
-
-    slabs = [functools.partial(rows_of, out, rows=96)]
-    slabs += [functools.partial(rows_of, up, rows=96, slab=j) for j in range(4)]
-    return slabs + [functools.partial(down_slab, part=j) for j in range(4)]
+    return [functools.partial(rows_of, qkv, slab=j) for j in range(3)]
+
+
+def mid_slabs(out, up):
+    return [functools.partial(rows_of, out)] + [functools.partial(rows_of, up, slab=j) for j in range(4)]
+
+
+def down_slabs(down):
+    return [functools.partial(down_rows, down, part=j) for j in range(4)]
 
 
 def segment_mask(length, seg_in_seq):
-    lane = lax.broadcasted_iota(jnp.int32, (1, SEG), 1)
-    return (lane + seg_in_seq * SEG < length) | (lane == 0)
-
-
-def attn_forward_kernel(segs, seg_count, info, x_ref, vec_ref, *rest):
-    pieces, (packed_ref, mixed_ref, qkv, sems) = rest[:10], rest[10:]
+    row = lax.broadcasted_iota(jnp.int32, (SEG, 2 * SEG), 0)
+    return (row + seg_in_seq * SEG < length) | (row == 0)
+
+
+def attn_forward_kernel(segs, seg_count, first_step, info, x_ref, vec_ref, *rest):
+    pieces, (packed_ref, mixed_ref, qkv, sems) = rest[:10], rest[-4:]
     step = pl.program_id(0)
 
     @pl.when(step == 0)
     def _():
-        load_slabs(info[0], pieces, qkv_slabs(qkv), sems)
+        load(slab_copies(info[0], pieces, qkv_slabs(qkv), sems))
 
     rows = x_ref[...]
     for j in range(3):
@@ -165,7 +152,7 @@
             part = part + vec_ref[j // 2 : j // 2 + 1, :]
         packed_ref[:, j * 768 : (j + 1) * 768] = part.astype(LOW)
     for s in range(segs):
-        seg = step * segs + s
+        seg = (step + first_step) * segs + s
         allowed = segment_mask(info[1 + seg // seg_count], seg % seg_count)
         at = slice(s * SEG, (s + 1) * SEG)
         for h in range(6):
@@ -173,28 +160,39 @@
             mixed_ref[at, h * 128 : (h + 1) * 128] = attend(q, k, v, allowed).astype(LOW)
 
 
-def ffn_forward_kernel(segs, info, x_ref, mixed_ref, vec_ref, *rest):
-    pieces, rest = rest[:10], rest[10:]
-    sum_ref, low_ref, act_ref, slope_ref, second_ref, heads_ref, out, up, down, sems = rest
+def norm_one(summed, vec_ref):
+    normed, _ = normalize(summed)
+    return normed * (1.0 + vec_ref[3:4, :]) + vec_ref[4:5, :]
+
+
+def mid_forward_kernel(info, x_ref, mixed_ref, vec_ref, *rest):
+    pieces, (sum_ref, low_ref, act_ref, slope_ref, out, up, sems) = rest[:10], rest[10:]
 
     @pl.when(pl.program_id(0) == 0)
     def _():
-        load_slabs(info[0], pieces, rest_slabs(out, up, down), sems)
+        load(slab_copies(info[0], pieces, mid_slabs(out, up), sems))
 
     summed = x_ref[...].astype(F32) + mm(mixed_ref[...], out[...]) + vec_ref[2:3, :]
     sum_ref[...] = summed
-    normed, _ = normalize(summed)
-    first = normed * (1.0 + vec_ref[3:4, :]) + vec_ref[4:5, :]
-    first_low = first.astype(LOW)
+    first_low = norm_one(summed, vec_ref).astype(LOW)
     low_ref[...] = first_low
-    total = first + vec_ref[9:10, :]
+    hidden = mm(first_low, up[0]) + vec_ref[5:6, :]
     for j in range(4):
-        hidden = mm(first_low, up[j]) + vec_ref[5 + j : 6 + j, :]
+        later = mm(first_low, up[j + 1]) + vec_ref[6 + j : 7 + j, :] if j < 3 else None
         act, slope = gelu_parts(hidden)
-        act = act.astype(LOW)
-        act_ref[:, j * 768 : (j + 1) * 768] = act
+        act_ref[:, j * 768 : (j + 1) * 768] = act.astype(LOW)
         slope_ref[:, j * 768 : (j + 1) * 768] = slope.astype(LOW)
-        total = total + mm(act, down[j * 768 : (j + 1) * 768, :])
+        hidden = later
+
+
+def down_forward_kernel(segs, info, sum_ref, act_ref, vec_ref, *rest):
+    pieces, (second_ref, heads_ref, down, sems) = rest[:8], rest[8:]
+
+    @pl.when(pl.program_id(0) == 0)
+    def _():
+        load(slab_copies(info[0], pieces, down_slabs(down), sems))
+
+    total = norm_one(sum_ref[...], vec_ref) + vec_ref[9:10, :] + mm(act_ref[...], down[...])
     second_ref[...] = total
     opening = jnp.concatenate([total[s * SEG : s * SEG + 1] for s in range(segs)], axis=0)
     normed, _ = normalize(opening)
@@ -202,22 +200,24 @@
 
 
 def cross_kernel(blocks, info, heads_ref, up_ref, live_ref, vec_ref, pos_ref, *rest):
-    pieces, rest = rest[:10], rest[10:]
+    wide, tall, rest = rest[0], rest[1], rest[2:]
     (own_ref, own_grad_ref, grads_ref, pos_grad_ref, qkv_grad_ref, out_grad_ref, up_grad_ref, down_grad_ref) = rest[:8]
     (qkv, out, up, down, sems, result, heads_grad, slope, lefts, act, packed, rights, hidden_grad) = rest[8:]
     step = pl.program_id(0)
     count = heads_ref.shape[0]
     at = pl.ds(pl.multiple_of(step * count, count), count)
-    slabs = qkv_slabs(qkv) + rest_slabs(out, up, down)
+    targets = [qkv.at[j] for j in range(3)] + [out] + [up.at[j] for j in range(4)]
+    copies = [pltpu.make_async_copy(wide.at[j], t, sems.at[j]) for j, t in enumerate(targets)]
+    copies.append(pltpu.make_async_copy(tall, down, sems.at[8]))
 
     @pl.when(step == 0)
     def _():
-        copies = slab_copies(info[0], pieces, slabs, sems, True)
+        for copy in copies:
+            copy.start()
         grads_ref[...] = jnp.zeros_like(grads_ref)
         pos_grad_ref[...] = jnp.zeros_like(pos_grad_ref)
-        for slab, copy in copies:
-            if slab < 3:
-                copy.wait()
+        for copy in copies[:3]:
+            copy.wait()
 
     vec = vec_ref[...]
     inputs = heads_ref[...].astype(F32).reshape(-1, 8, 768) + pos_ref[...][None]
@@ -229,10 +229,13 @@
         if j != 1:
             part = part + vec[j // 2 : j // 2 + 1]
         packed[:, j * 768 : (j + 1) * 768] = part.astype(LOW)
-    row = lax.broadcasted_iota(jnp.int32, (2 * SEG, SEG), 0)
-    lane = lax.broadcasted_iota(jnp.int32, (2 * SEG, SEG), 1)
-    group = row % SEG // 8 == lane // 8
-    masks = [group & (live_ref[s : s + 1, :] > 0.0) for s in range(count // SEG)]
+    row = lax.broadcasted_iota(jnp.int32, (SEG, 2 * SEG), 0)
+    lane = lax.broadcasted_iota(jnp.int32, (SEG, 2 * SEG), 1)
+    group = row // 8 == lane % SEG // 8
+    masks = []
+    for s in range(count // SEG):
+        live = live_ref[s * SEG : (s + 1) * SEG, :]
+        masks.append(group & (jnp.concatenate([live, live], axis=1) > 0.0))
     for s, allowed in enumerate(masks):
         part = slice(s * SEG, (s + 1) * SEG)
         for h in range(6):
@@ -242,7 +245,7 @@
 
     @pl.when(step == 0)
     def _():
-        for _, copy in slab_copies(info[0], pieces, slabs, sems, False, 3):
+        for copy in copies[3:]:
             copy.wait()
 
     summed = inputs + mm(lefts[1, at, :], out[...]) + vec[2:3]
@@ -329,13 +332,14 @@
 
 
 def ffn_backward_kernel(segs, seg_count, info, cot_ref, heads_grad_ref, heads_ref, second_ref, sum_ref, slope_ref, vec_ref, *rest):
-    pieces, rest = rest[:10], rest[10:]
+    pieces, more, rest = rest[:10], rest[10:18], rest[18:]
     (out_ref, down_grad_ref, hidden_grad_ref, proj_grad_ref, mixed_grad_ref, grads_ref, out, up, down, sems) = rest
     step = pl.program_id(0)
 
     @pl.when(step == 0)
     def _():
-        load_slabs(info[0], pieces, rest_slabs(out, up, down), sems)
+        copies = slab_copies(info[0], more, down_slabs(down), sems, 40)
+        load(copies + slab_copies(info[0], pieces, mid_slabs(out, up), sems))
         grads_ref[...] = jnp.zeros_like(grads_ref)
 
     count = segs * SEG
@@ -377,7 +381,8 @@
     grads_ref[4:5, :] += column_sum(total)
 
 
-def attn_backward_kernel(segs, seg_count, info, packed_ref, mixed_grad_ref, packed_grad_ref, grads_ref):
+def attn_backward_kernel(segs, seg_count, first_step, info, packed_ref, mixed_grad_ref, *rest):
+    packed_grad_ref, grads_ref = rest[-2:]
     step = pl.program_id(0)
 
     @pl.when(step == 0)
@@ -385,7 +390,7 @@
         grads_ref[...] = jnp.zeros_like(grads_ref)
 
     for s in range(segs):
-        seg = step * segs + s
+        seg = (step + first_step) * segs + s
         allowed = segment_mask(info[1 + seg // seg_count], seg % seg_count)
         at = slice(s * SEG, (s + 1) * SEG)
         for h in range(6):
@@ -403,7 +408,7 @@
 
     @pl.when(pl.program_id(0) == 0)
     def _():
-        load_slabs(info[0], pieces, qkv_slabs(qkv), sems)
+        load(slab_copies(info[0], pieces, qkv_slabs(qkv), sems))
 
     total = proj_grad_ref[...].astype(F32)
     for j in range(3):
@@ -411,14 +416,30 @@
     token_grad_ref[...] = total.astype(LOW)
 
 
-def weight_grad_kernel(rows, info, left_ref, right_ref, keep_ref, send_ref, total):
-    total[...] = mm_tn(left_ref[...], right_ref[...])
+def send_slab(place, total, keep_ref, send_ref, rows):
     for mask in range(8):
-        block = pl.multiple_of((info[0] ^ mask) * rows, rows)
+        block = pl.multiple_of((place ^ mask) * rows, rows)
         target = send_ref if mask % 2 else keep_ref
         target[mask // 2] = total[pl.ds(block, rows), :].astype(LOW)
 
 
+def qkv_grad_kernel(info, left_ref, right_ref, keep_ref, send_ref, total):
+    total[...] = mm_tn(left_ref[...], right_ref[...])
+    send_slab(info[0], total, keep_ref, send_ref, 96)
+
+
+def mid_grad_kernel(info, mixed_ref, proj_ref, low_ref, hidden_ref, keep_ref, send_ref, total):
+    @pl.when(pl.program_id(0) == 0)
+    def _():
+        total[...] = mm_tn(mixed_ref[...], proj_ref[...])
+
+    @pl.when(pl.program_id(0) > 0)
+    def _():
+        total[...] = mm_tn(low_ref[...], hidden_ref[...])
+
+    send_slab(info[0], total, keep_ref, send_ref, 96)
+
+
 ANY = pl.BlockSpec(memory_space=pl.ANY)
 SMEM = pl.BlockSpec(memory_space=pltpu.SMEM)
 
@@ -439,69 +460,88 @@
     return pltpu.CompilerParams(vmem_limit_bytes=VMEM, dimension_semantics=("arbitrary",))
 
 
-def qkv_weights():
-    return [pltpu.VMEM((3, 768, 768), LOW)], [pltpu.SemaphoreType.DMA((24,))]
-
-
-def rest_weights():
-    weights = [pltpu.VMEM((768, 768), LOW), pltpu.VMEM((4, 768, 768), LOW), pltpu.VMEM((3072, 768), LOW)]
-    return weights, [pltpu.SemaphoreType.DMA((72,))]
-
-
-def cost(flops, size, exps=0):
-    return pl.CostEstimate(flops=flops, bytes_accessed=size, transcendentals=exps)
-
-
-def attn_forward(info, rows_in, vec, pieces, seg_count, segs=2):
+def cost(flops, size):
+    return pl.CostEstimate(flops=flops, bytes_accessed=size, transcendentals=0)
+
+
+QKV = [pltpu.VMEM((3, 768, 768), LOW)]
+MID = [pltpu.VMEM((768, 768), LOW), pltpu.VMEM((4, 768, 768), LOW)]
+DOWN = [pltpu.VMEM((3072, 768), LOW)]
+
+
+def sems(count):
+    return [pltpu.SemaphoreType.DMA((count,))]
+
+
+def shifted(count, width, first):
+    return pl.BlockSpec((count, width), lambda i: (i + first, 0))
+
+
+def attn_forward(info, rows_in, vec, pieces, seg_count, half, before=None, segs=4):
     rows = rows_in.shape[0]
     count = segs * SEG
-    weights, sems = qkv_weights()
+    steps = rows // count // 2
+    first = half * steps
+    before = list(before or [])
     return pl.pallas_call(
-        functools.partial(attn_forward_kernel, segs, seg_count),
-        grid=(rows // count,),
-        in_specs=[SMEM, block_rows(count, 768), fixed((12, 768))] + [ANY] * 10,
-        out_specs=[block_rows(count, 2304), block_rows(count, 768)],
+        functools.partial(attn_forward_kernel, segs, seg_count, first),
+        grid=(steps,),
+        in_specs=[SMEM, shifted(count, 768, first), fixed((12, 768))] + [ANY] * (10 + len(before)),
+        out_specs=[shifted(count, 2304, first), shifted(count, 768, first)],
         out_shape=[shape_of((rows, 2304)), shape_of((rows, 768))],
-        scratch_shapes=weights + sems,
+        scratch_shapes=QKV + sems(24),
+        input_output_aliases={13: 0, 14: 1} if before else {},
         compiler_params=params(),
-        cost_estimate=cost(2 * rows * 768 * 8000, rows * 768 * 16),
+        cost_estimate=cost(rows * 768 * 8000, rows * 768 * 8),
         name="attn_forward",
-    )(info, rows_in, vec, *pieces)
-
-
-def ffn_forward(info, rows_in, mixed, vec, pieces, segs=2):
+    )(info, rows_in, vec, *pieces, *before)
+
+
+def mid_forward(info, rows_in, mixed, vec, pieces, segs=2):
     rows = rows_in.shape[0]
     count = segs * SEG
-    weights, sems = rest_weights()
+    return pl.pallas_call(
+        mid_forward_kernel,
+        grid=(rows // count,),
+        in_specs=[SMEM, block_rows(count, 768), block_rows(count, 768), fixed((12, 768))] + [ANY] * 10,
+        out_specs=[block_rows(count, 768), block_rows(count, 768), block_rows(count, 3072), block_rows(count, 3072)],
+        out_shape=[shape_of((rows, 768), F32), shape_of((rows, 768)), shape_of((rows, 3072)), shape_of((rows, 3072))],
+        scratch_shapes=MID + sems(40),
+        compiler_params=params(),
+        cost_estimate=cost(2 * rows * 768 * 8000, rows * 768 * 30),
+        name="mid_forward",
+    )(info, rows_in, mixed, vec, *pieces)
+
+
+def down_forward(info, summed, act, vec, pieces, segs=2):
+    rows = summed.shape[0]
+    count = segs * SEG
     few = pl.BlockSpec((None, segs, 768), lambda i: (i, 0, 0))
     return pl.pallas_call(
-        functools.partial(ffn_forward_kernel, segs),
+        functools.partial(down_forward_kernel, segs),
         grid=(rows // count,),
-        in_specs=[SMEM, block_rows(count, 768), block_rows(count, 768), fixed((12, 768))] + [ANY] * 10,
-        out_specs=[block_rows(count, 768), block_rows(count, 768), block_rows(count, 3072), block_rows(count, 3072),
-                   block_rows(count, 768), few],
-        out_shape=[shape_of((rows, 768), F32), shape_of((rows, 768)), shape_of((rows, 3072)), shape_of((rows, 3072)),
-                   shape_of((rows, 768), F32), shape_of((rows // count, segs, 768), F32)],
-        scratch_shapes=weights + sems,
+        in_specs=[SMEM, block_rows(count, 768), block_rows(count, 3072), fixed((12, 768))] + [ANY] * 8,
+        out_specs=[block_rows(count, 768), few],
+        out_shape=[shape_of((rows, 768), F32), shape_of((rows // count, segs, 768), F32)],
+        scratch_shapes=DOWN + sems(32),
         compiler_params=params(),
-        cost_estimate=cost(2 * rows * 768 * 14000, rows * 768 * 30),
-        name="ffn_forward",
-    )(info, rows_in, mixed, vec, *pieces)
-
-
-def cross_whole(info, heads, upstream, live, vec, positions, pieces):
+        cost_estimate=cost(2 * rows * 768 * 4000, rows * 768 * 16),
+        name="down_forward",
+    )(info, summed, act, vec, *pieces)
+
+
+def cross_whole(info, heads, upstream, live, vec, positions, wide, tall):
     rows = heads.shape[0]
     count = 2 * SEG
-    weights = qkv_weights()[0] + rest_weights()[0]
     own = [(16, 768), (16, 768), (12, 768), (8, 768), (24, 2304), (24, 768), (24, 3072), (96, 768)]
     return pl.pallas_call(
         functools.partial(cross_kernel, rows // count),
         grid=(rows // count,),
-        in_specs=[SMEM, block_rows(count, 768), block_rows(count, 768),
-                  pl.BlockSpec((None, 2, SEG), lambda i: (i, 0, 0)), fixed((12, 768)), fixed((8, 768))] + [ANY] * 10,
+        in_specs=[SMEM, block_rows(count, 768), block_rows(count, 768), block_rows(count, SEG),
+                  fixed((12, 768)), fixed((8, 768)), ANY, ANY],
         out_specs=[fixed(dims) for dims in own],
         out_shape=[shape_of(dims, F32) for dims in own],
-        scratch_shapes=weights + [pltpu.SemaphoreType.DMA((96,))] + [
+        scratch_shapes=QKV + MID + DOWN + sems(9) + [
             pltpu.VMEM((rows, 768), F32), pltpu.VMEM((rows, 768), F32), pltpu.VMEM((count, 3072), LOW),
             pltpu.VMEM((3, rows, 768), LOW), pltpu.VMEM((rows, 3072), LOW), pltpu.VMEM((count, 2304), LOW),
             pltpu.VMEM((5, rows, 768), LOW), pltpu.VMEM((rows, 3072), LOW),
@@ -509,78 +549,99 @@
         compiler_params=params(),
         cost_estimate=cost(2 * rows * 768 * 30000, 2**24),
         name="cross_encoder",
-    )(info, heads, upstream, live, vec, positions, *pieces)
-
-
-def ffn_backward(info, cotangent, heads_grad, heads, second, summed, slope, vec, pieces, seg_count, segs=2):
+    )(info, heads, upstream, live, vec, positions, wide, tall)
+
+
+def ffn_backward(info, cotangent, heads_grad, heads, second, summed, slope, vec, mid, down, seg_count, segs=2):
     rows = summed.shape[0]
     count = segs * SEG
     few = pl.BlockSpec((None, segs, 768), lambda i: (i, 0, 0))
-    weights, sems = rest_weights()
     return pl.pallas_call(
         functools.partial(ffn_backward_kernel, segs, seg_count),
         grid=(rows // count,),
         in_specs=[SMEM, block_rows(count, 768), few, few, block_rows(count, 768), block_rows(count, 768),
-                  block_rows(count, 3072), fixed((12, 768))] + [ANY] * 10,
+                  block_rows(count, 3072), fixed((12, 768))] + [ANY] * 18,
         out_specs=[block_rows(count, 768), block_rows(count, 768), block_rows(count, 3072), block_rows(count, 768),
                    block_rows(count, 768), fixed((12, 768))],
         out_shape=[shape_of((rows, 768)), shape_of((rows, 768)), shape_of((rows, 3072)), shape_of((rows, 768)),
                    shape_of((rows, 768)), shape_of((12, 768), F32)],
-        scratch_shapes=weights + sems,
+        scratch_shapes=MID + DOWN + sems(72),
         compiler_params=params(),
         cost_estimate=cost(2 * rows * 768 * 14000, rows * 768 * 30),
         name="ffn_backward",
-    )(info, cotangent, heads_grad.reshape(-1, segs, 768), heads.reshape(-1, segs, 768), second, summed, slope, vec, *pieces)
-
-
-def attn_backward(info, packed, mixed_grad, seg_count, segs=2):
+    )(info, cotangent, heads_grad.reshape(-1, segs, 768), heads.reshape(-1, segs, 768), second, summed, slope, vec, *mid, *down)
+
+
+def attn_backward(info, packed, mixed_grad, seg_count, half, before=None, segs=2):
     rows = packed.shape[0]
     count = segs * SEG
+    steps = rows // count // 2
+    first = half * steps
+    before = [] if before is None else [before]
     return pl.pallas_call(
-        functools.partial(attn_backward_kernel, segs, seg_count),
-        grid=(rows // count,),
-        in_specs=[SMEM, block_rows(count, 2304), block_rows(count, 768)],
-        out_specs=[block_rows(count, 2304), fixed((2, 768))],
+        functools.partial(attn_backward_kernel, segs, seg_count, first),
+        grid=(steps,),
+        in_specs=[SMEM, shifted(count, 2304, first), shifted(count, 768, first)] + [ANY] * len(before),
+        out_specs=[shifted(count, 2304, first), fixed((2, 768))],
         out_shape=[shape_of((rows, 2304)), shape_of((2, 768), F32)],
+        input_output_aliases={3: 0} if before else {},
         compiler_params=params(),
-        cost_estimate=cost(2 * rows * 768 * 16000, rows * 768 * 16),
+        cost_estimate=cost(rows * 768 * 10000, rows * 768 * 8),
         name="attn_backward",
-    )(info, packed, mixed_grad)
-
-
-def token_gradient(info, packed_grad, proj_grad, pieces, count=256):
+    )(info, packed, mixed_grad, *before)
+
+
+def token_gradient(info, packed_grad, proj_grad, pieces, count=512):
     rows = packed_grad.shape[0]
-    weights, sems = qkv_weights()
     return pl.pallas_call(
         token_grad_kernel,
         grid=(rows // count,),
         in_specs=[SMEM, block_rows(count, 2304), block_rows(count, 768)] + [ANY] * 10,
         out_specs=block_rows(count, 768),
         out_shape=shape_of((rows, 768)),
-        scratch_shapes=weights + sems,
+        scratch_shapes=QKV + sems(24),
         compiler_params=params(),
         cost_estimate=cost(2 * rows * 768 * 3000, rows * 768 * 10),
         name="token_gradient",
     )(info, packed_grad, proj_grad, *pieces)
 
 
-def weight_grad(info, left, right):
-    rows, wide = right.shape
-    tiles = wide // 768
-    moving = pl.BlockSpec((rows, 768), lambda i: (0, i))
-    still = fixed((rows, 768))
-    out = pl.BlockSpec((4, 96, 768), lambda i: (0, 0, i))
+def grad_outs(slabs):
+    out = pl.BlockSpec((4, 96, 768), lambda i: (0, i, 0))
+    return [out, out], [shape_of((4, slabs * 96, 768))] * 2
+
+
+def qkv_weight_grad(info, left, right):
+    rows = left.shape[0]
+    specs, shapes = grad_outs(3)
     return pl.pallas_call(
-        functools.partial(weight_grad_kernel, 96),
-        grid=(tiles,),
-        in_specs=[SMEM, still, moving],
-        out_specs=[out, out],
-        out_shape=[shape_of((4, 96, wide))] * 2,
+        qkv_grad_kernel,
+        grid=(3,),
+        in_specs=[SMEM, fixed((rows, 768)), pl.BlockSpec((rows, 768), lambda i: (0, i))],
+        out_specs=specs,
+        out_shape=shapes,
         scratch_shapes=[pltpu.VMEM((768, 768), F32)],
         compiler_params=params(),
-        cost_estimate=cost(2 * rows * 768 * wide, rows * wide * 2),
-        name="weight_grad",
+        cost_estimate=cost(2 * rows * 768 * 2304, rows * 2304 * 2),
+        name="qkv_weight_grad",
     )(info, left, right)
+
+
+def mid_weight_grad(info, mixed, proj_grad, low, hidden_grad):
+    rows = mixed.shape[0]
+    specs, shapes = grad_outs(5)
+    still = fixed((rows, 768))
+    return pl.pallas_call(
+        mid_grad_kernel,
+        grid=(5,),
+        in_specs=[SMEM, still, still, still, pl.BlockSpec((rows, 768), lambda i: (0, jnp.maximum(i - 1, 0)))],
+        out_specs=specs,
+        out_shape=shapes,
+        scratch_shapes=[pltpu.VMEM((768, 768), F32)],
+        compiler_params=params(),
+        cost_estimate=cost(2 * rows * 768 * 3840, rows * 3840 * 2),
+        name="mid_weight_grad",
+    )(info, mixed, proj_grad, low, hidden_grad)
 
 
 def down_grad_kernel(info, left_ref, right_ref, keep_ref, send_ref, total):
@@ -816,41 +877,25 @@
     def spread_near(self, block):
         return self.flip(block, 2), self.flip(block, 4)
 
-    def spread_far(self, by_x, by_y):
-        half = by_x.shape[0] // 2
+    def spread_far(self, by_x, by_y, half):
         return self.flip(by_y[:half], 2), self.flip(by_x[half:], 4)
 
     def spread_core(self, mine):
         return list(mine) + [self.flip(piece, 1) for piece in mine]
+
+    def in_order(self, parts):
+        for axis, mask in ((4, 4), (2, 2), (1, 1)):
+            odd = self.place // axis % 2 == 1
+            parts = [jnp.where(odd, parts[m ^ mask], parts[m]) for m in range(8)]
+        return jnp.stack(parts)
 
     def gather_small(self, shard):
         block = jnp.stack(self.gather_z(shard))
         near = [block] + [self.flip(block, m) for m in (2, 4, 6)]
-        near = [lax.select(self.place // 2 % 2 == 0, jnp.stack(p), jnp.stack(p[::-1])) for p in (near[:2], near[2:])]
-        plane = lax.select(self.place // 4 == 0, jnp.stack(near), jnp.stack(near[::-1]))
+        plane = jnp.stack(near)
         other = self.flip(plane, 1)
-        both = [jnp.stack(p, axis=2) for p in ((plane, other), (other, plane))]
-        return lax.select(self.place % 2 == 0, *both).reshape((-1,) + shard.shape)
-
-    def scatter_sum(self, keep, send, line):
-        def add(*terms):
-            return sum(t.astype(F32) for t in terms).astype(LOW)
-
-        def pick(array, index):
-            return lax.dynamic_index_in_dim(array, index, 0, keepdims=False)
-
-        came = self.flip(send, 1)
-        to_d = line(add(keep[3], came[3]))
-        half = self.inner // 2
-        came_x, came_y = self.flip(to_d[:half], 2), self.flip(to_d[half:], 4)
-        to_x, to_y = line(add(keep[1], came[1])), line(add(keep[2], came[2]))
-        to_y = jnp.concatenate([add(to_y[:half], came_x), to_y[half:]])
-        to_x = jnp.concatenate([to_x[:half], add(to_x[half:], came_y)])
-        own = add(line(keep[0]), line(came[0]), self.flip(to_x, 2), self.flip(to_y, 4))
-        total = pick(own, self.z).astype(F32)
-        for step in range(1, self.inner):
-            total = total + self.turn(pick(own, (self.z + step) % self.inner), step).astype(F32)
-        return total
+        whole = self.in_order([(plane, other)[m % 2][m // 2] for m in range(8)])
+        return whole.reshape((-1,) + shard.shape)
 
 
 class PlainLinks:
@@ -863,12 +908,71 @@
     def gather_small(self, shard):
         return lax.all_gather(shard, AXES, axis=0)
 
-    def whole(self, matrix):
-        return lax.all_gather(matrix, AXES, axis=0, tiled=True)
-
-    def scatter_sum(self, keep, send, line):
-        flat = jnp.stack([keep, send], axis=1).reshape(-1, keep.shape[-1])
-        return lax.psum_scatter(flat, AXES, scatter_dimension=0, tiled=True).astype(F32)
+
+def add(*terms):
+    return sum(t.astype(F32) for t in terms).astype(LOW)
+
+
+class Sum:
+    def __init__(self, links, keep, send, slabs):
+        self.links, self.keep, self.slabs = links, keep, slabs
+        self.came = links.flip(send, 1)
+
+    def line(self, part):
+        inner = self.links.inner
+        part = part.reshape(self.slabs, inner, -1, part.shape[-1])
+        return part.transpose(1, 0, 2, 3).reshape(inner, -1, part.shape[-1])
+
+    def to(self, index):
+        return self.line(add(self.keep[index], self.came[index]))
+
+    def far(self):
+        half = self.links.inner // 2
+        to_d = self.to(3)
+        self.far_came = [self.links.flip(to_d[:half], 2), self.links.flip(to_d[half:], 4)]
+        return self.far_came
+
+    def near(self):
+        half = self.links.inner // 2
+        came_x, came_y = self.far_came
+        to_x, to_y = self.to(1), self.to(2)
+        to_y = jnp.concatenate([add(to_y[:half], came_x), to_y[half:]])
+        to_x = jnp.concatenate([to_x[:half], add(to_x[half:], came_y)])
+        self.near_came = [self.links.flip(to_x, 2), self.links.flip(to_y, 4)]
+        return self.near_came
+
+    def direct(self):
+        self.near_came = [self.links.flip(self.to(m // 2), m) for m in (2, 4, 6)]
+        return self.near_came
+
+    def finish(self):
+        links = self.links
+        own = add(self.line(self.keep[0]), self.line(self.came[0]), *self.near_came)
+
+        def pick(index):
+            return lax.dynamic_index_in_dim(own, index % links.inner, 0, keepdims=False)
+
+        total = pick(links.z).astype(F32)
+        for step in range(1, links.inner):
+            total = total + links.turn(pick(links.z + step), step).astype(F32)
+        return total
+
+
+class PlainSum:
+    def __init__(self, links, keep, send, slabs):
+        flat = jnp.stack([keep, send], axis=1).reshape(8, slabs, -1, 768)
+        rows = flat.shape[2] * 8 // (links.outer * links.inner)
+        flat = flat.transpose(1, 0, 2, 3).reshape(slabs, -1, 768) if slabs > 1 else flat.reshape(1, -1, 768)
+        self.total = lax.psum_scatter(flat, AXES, scatter_dimension=1, tiled=True).reshape(-1, 768).astype(F32)
+        self.came = keep
+
+    def far(self):
+        return []
+
+    near = direct = far
+
+    def finish(self):
+        return self.total
 
 
 def after(value, *earlier):
@@ -880,50 +984,19 @@
     return matrix.reshape(rows, wide // 768, 768).transpose(1, 0, 2)
 
 
-def line_block(parts, down_rows):
-    wide = jnp.stack([p[: p.shape[0] - down_rows // 24] for p in parts], axis=1)
-    wide = wide.reshape(wide.shape[0], -1, 768)
-    if not down_rows:
-        return wide
-    tall = jnp.stack([p[p.shape[0] - down_rows // 24 :].reshape(down_rows, 768) for p in parts])
-    return jnp.concatenate([wide, tall.reshape(-1, 96, 768)])
-
-
-def gather_weights(links, seg, cross):
-    if isinstance(links, PlainLinks):
-
-        def pieces(slabs, tall=None):
-            parts = []
-            for mask in (0, 2, 4, 6, 1, 3, 5, 7):
-                part = slabs[:, mask * 96 : (mask + 1) * 96]
-                if tall is not None:
-                    part = jnp.concatenate([part, tall[mask * 384 : (mask + 1) * 384].reshape(4, 96, 768)])
-                half = part.shape[0] // 2
-                parts += [part[:half], part[half:]] if mask > 5 else [part]
-            return parts
-
-        qkv, out, up, down = (links.whole(m) for m in seg)
-        rest = jnp.concatenate([slabs_of(out), slabs_of(up)])
-        return pieces(slabs_of(qkv)), pieces(rest, down), [links.whole(m) for m in cross]
-    first = slabs_of(seg[0])
-    rest = jnp.concatenate([slabs_of(m) for m in seg[1:3]] + [seg[3].reshape(4, 24, 768)])
-    other = jnp.concatenate([slabs_of(m) for m in cross[:3]] + [cross[3].reshape(4, 24, 768)])
-    line_first = links.gather_z(first)
-    line_rest = links.gather_z(after(rest, *line_first))
-    line_other = links.gather_z(after(other, *line_rest))
-    block = line_block(line_first, 0)
-    near = links.spread_near(block)
-    far = links.spread_far(*near)
-    first = links.spread_core([block, *near, *far])
-    block = after(line_block(line_rest, 96), *far)
-    near = links.spread_near(block)
-    far = links.spread_far(*near)
-    rest = links.spread_core([block, *near, *far])
-    block = after(line_block(line_other, 96), *far)
-    near = links.spread_near(block)
-    far = links.spread_far(*near)
-    other = links.spread_core([block, *near, *far])
-    return first, rest, other
+def matrix_of(slabs):
+    count, rows, width = slabs.shape
+    return slabs.transpose(1, 0, 2).reshape(rows, count * width)
+
+
+def plain_pieces(slabs, whole):
+    count = slabs.shape[0]
+    half = (count + 1) // 2 * 96
+    parts = []
+    for mask in (0, 2, 4, 6, 1, 3, 5, 7):
+        part = slabs[:, mask * 96 : (mask + 1) * 96].reshape(-1, 768)
+        parts += [part] if whole or mask < 6 and mask != 7 else [part[:half], part[half:]]
+    return parts
 
 
 def shards(
@@ -946,6 +1019,7 @@
 ):
     fast = (outer, inner) == (8, 4)
     links = (Links if fast else PlainLinks)(outer, inner)
+    summing = Sum if fast else PlainSum
     devices = outer * inner
     me = links.order * inner + links.z
     seq_local, seq_len, feat_dim = tokens.shape
@@ -955,35 +1029,63 @@
     my_lengths = lax.dynamic_slice_in_dim(lengths, me * seq_local, seq_local)
     info = jnp.concatenate([jnp.full((1,), links.place, jnp.int32), my_lengths])
     small = jnp.concatenate([seg_vec, cross_vec, positions]).reshape(1, -1)
-    small = links.gather_small(small).reshape(devices, -1, width)
-    small = small.transpose(1, 0, 2).reshape(-1, feat_dim).astype(F32)
-    seg_v, cross_v = small[:seg_rows], small[seg_rows : seg_rows + cross_rows]
-    pos_table = small[seg_rows + cross_rows :]
-    first, rest, other = gather_weights(
-        links,
-        (seg_qkv, seg_out, seg_up, seg_down),
-        (cross_qkv, cross_out, cross_up, cross_down),
-    )
+    wide = jnp.concatenate([slabs_of(cross_qkv), slabs_of(cross_out), slabs_of(cross_up)])
+    mid_shard = jnp.concatenate([slabs_of(seg_out), slabs_of(seg_up)])
     rows_in = tokens.reshape(-1, feat_dim)
     cot_rows = cotangent.reshape(-1, feat_dim)
     seg_starts = jnp.arange(seg_count) * SEG
     live_own = (seg_starts[None, :] < my_lengths[:, None]).reshape(-1, 1)
     up_own = jnp.where(live_own, cotangent.reshape(-1, SEG, feat_dim)[:, 0, :], 0)
-    up_all = links.gather_small(up_own).reshape(-1, feat_dim)
-
-    packed, mixed = attn_forward(info, rows_in, seg_v, first, seg_count)
-    summed, low, act, slope, second, heads = ffn_forward(info, rows_in, mixed, seg_v, rest)
+
+    wide = lax.all_gather(wide, AXES, axis=1, tiled=True)
+    tall = lax.all_gather(cross_down, AXES, axis=0, tiled=True)
+    if fast:
+        first = jnp.concatenate([slabs_of(seg_qkv).reshape(-1, 768), jnp.pad(small, ((0, 7), (0, 0)))])
+        line_first = links.gather_z(first)
+        line_mid = links.gather_z(after(mid_shard, *line_first))
+        line_down = links.gather_z(after(seg_down, *line_mid))
+        weights = jnp.stack([p[:72].reshape(3, 24, 768) for p in line_first], axis=1).reshape(-1, 768)
+        rows = jnp.concatenate([p[72:73] for p in line_first])
+        block = jnp.concatenate([weights, jnp.pad(rows, ((0, 12), (0, 0)))])
+        near = links.spread_near(block)
+        far = links.spread_far(*near, 192)
+        first = links.spread_core([block, *near, *far])
+        ends = [p[288:292] for p in first[:3]] + [first[4][96:100]]
+        others = [p[288:292] for p in first[5:8]] + [first[9][96:100]]
+        small = links.in_order([(ends, others)[m % 2][m // 2] for m in range(8)])
+        block = after(jnp.stack(line_mid, axis=1).reshape(-1, 768), *far)
+        near_mid = links.spread_near(block)
+        far_mid = links.spread_far(*near_mid, 288)
+        mid = links.spread_core([block, *near_mid, *far_mid])
+        block = after(jnp.concatenate(line_down), *far_mid)
+        down = links.spread_core([block] + [links.flip(block, m) for m in (2, 4, 6)])
+    else:
+        first = plain_pieces(lax.all_gather(slabs_of(seg_qkv), AXES, axis=1, tiled=True), False)
+        mid = plain_pieces(lax.all_gather(mid_shard, AXES, axis=1, tiled=True), False)
+        down_whole = lax.all_gather(seg_down, AXES, axis=0, tiled=True)
+        down = [down_whole[m * 384 : (m + 1) * 384] for m in (0, 2, 4, 6, 1, 3, 5, 7)]
+        small = links.gather_small(small)
+        near_mid = []
+    small = small.reshape(devices, -1, width).transpose(1, 0, 2).reshape(-1, feat_dim).astype(F32)
+    seg_v, cross_v = small[:seg_rows], small[seg_rows : seg_rows + cross_rows]
+    pos_table = small[seg_rows + cross_rows :]
+
+    before = attn_forward(info, rows_in, seg_v, first, seg_count, 0)
+    packed, mixed = attn_forward(info, after(rows_in, *near_mid), seg_v, first, seg_count, 1, before)
+    summed, low, act, slope = mid_forward(info, rows_in, mixed, seg_v, mid)
+    second, heads = down_forward(info, summed, act, seg_v, down)
     heads_own = heads.reshape(-1, feat_dim)
-    heads_all = links.gather_small(heads_own.astype(LOW)).reshape(-1, feat_dim)
+    both = links.gather_small(jnp.stack([heads_own.astype(LOW), up_own]))
+    heads_all, up_all = both[:, 0].reshape(-1, feat_dim), both[:, 1].reshape(-1, feat_dim)
     live_all = seg_starts[None, :] < lengths[:, None]
     if fast:
         cross_info = jnp.stack([links.place, me]).astype(jnp.int32)
-        live = live_all.astype(F32).reshape(-1, 2, SEG)
+        live = jnp.broadcast_to(live_all.reshape(-1, 1), (live_all.size, SEG)).astype(F32)
         cross_own, heads_grad, vec_grad, pos_grad, *cross_grads = cross_whole(
-            cross_info, heads_all, up_all, live, cross_v, pos_table, other
+            cross_info, heads_all, up_all, live, cross_v, pos_table, wide, tall
         )
     else:
-        weights = (*other, cross_v)
+        weights = (matrix_of(wide[:3]), wide[3], matrix_of(wide[4:]), tall, cross_v)
         heads_in = heads_all.astype(F32).reshape(-1, seg_count, feat_dim) + pos_table[None]
         heads_in = heads_in.reshape(-1, feat_dim)
         cross_result, kept = encode(heads_in, heads_in.astype(LOW), weights, live_all)
@@ -1003,36 +1105,33 @@
     grad_positions = lax.dynamic_slice_in_dim(pos_grad, me * width, width, 1)
 
     layer_out, down_grad, hidden_grad, proj_grad, mixed_grad, grads_two = ffn_backward(
-        info, cot_rows, heads_grad, cross_own, second, summed, slope, seg_v, rest, seg_count
-    )
-    down_parts = down_weight_grad(info, act, down_grad)
-    up_parts = weight_grad(info, low, after(hidden_grad, down_parts[1]))
-    out_parts = weight_grad(info, mixed, after(proj_grad, up_parts[1]))
-    packed_grad, grads_one = attn_backward(info, packed, after(mixed_grad, out_parts[1]), seg_count)
-    qkv_parts = weight_grad(info, rows_in, packed_grad)
-    token_grad = token_gradient(info, after(packed_grad, qkv_parts[1]), proj_grad, first)
-
-    def by_rows(part):
-        return part.reshape(inner, -1, part.shape[-1])
-
-    grad_down = links.scatter_sum(*down_parts, by_rows)
-    grad_up = links.scatter_sum(*up_parts, by_rows)
-    grad_out = links.scatter_sum(*out_parts, by_rows)
-    grad_qkv = links.scatter_sum(*qkv_parts, by_rows)
-    vec_parts = jnp.concatenate([grads_one, grads_two[2:]]).reshape(seg_rows, devices, width)
-    vec_parts = vec_parts.transpose(1, 0, 2).reshape(outer, inner, seg_rows * width).astype(LOW)
-    if fast:
-        flipped = [lax.dynamic_index_in_dim(vec_parts, links.place ^ m, 0, keepdims=False) for m in range(8)]
-        keep, send = jnp.stack(flipped[::2]), jnp.stack(flipped[1::2])
-    else:
-        keep, send = vec_parts[::2], vec_parts[1::2]
-    grad_vec = links.scatter_sum(keep, send, by_rows).reshape(seg_rows, width)
+        info, cot_rows, heads_grad, cross_own, second, summed, slope, seg_v, mid, down, seg_count
+    )
+    down_sum = summing(links, *down_weight_grad(info, act, down_grad), 1)
+    mid_parts = mid_weight_grad(info, mixed, proj_grad, low, after(hidden_grad, down_sum.keep if fast else down_sum.came))
+    mid_sum = summing(links, *mid_parts, 5)
+    grads_mid = lax.psum(grads_two[2:], AXES)
+    half_grad, grads_one = attn_backward(
+        info, packed, after(mixed_grad, mid_parts[1], down_sum.came), seg_count, 0
+    )
+    ready = after(mixed_grad, half_grad, *down_sum.far(), mid_sum.came)
+    packed_grad, grads_more = attn_backward(info, packed, ready, seg_count, 1, half_grad)
+    ready = after(packed_grad, *down_sum.near(), *mid_sum.far())
+    qkv_sum = summing(links, *qkv_weight_grad(info, rows_in, ready), 3)
+    ready = after(packed_grad, *mid_sum.near(), qkv_sum.came)
+    token_grad = token_gradient(info, ready, proj_grad, first)
+    qkv_sum.direct()
+    grads_one = lax.psum(grads_one + grads_more, AXES)
+    grad_down = down_sum.finish()
+    grad_mid = mid_sum.finish().reshape(5, -1, feat_dim)
+    grad_qkv = matrix_of(qkv_sum.finish().reshape(3, -1, feat_dim))
+    grad_vec = lax.dynamic_slice_in_dim(jnp.concatenate([grads_one, grads_mid]), me * width, width, 1)
     return (
         layer_out.reshape(tokens.shape),
         token_grad.reshape(tokens.shape),
         grad_qkv,
-        grad_out,
-        grad_up,
+        grad_mid[0],
+        matrix_of(grad_mid[1:]),
         grad_down,
         grad_vec,
         *cross_grads,

time: 613 us -> 557 us (0.909)
  waiting for transfers between devices: 167 us -> 115 us
  blocking collectives: 0 us -> 48.8 us
  starting transfers between devices: 109 us -> 66.7 us
  Pallas kernels: 281 us -> 250 us
  between operations: 2.32 us -> 15.3 us
  other arithmetic: 18.3 us -> 27.9 us
    psum x0 -> x1, blocking collectives: none -> 48.8 us  [shards(): grads_one = lax.psum(grads_one + grads_more, AXES)]
    ppermute x64 -> x43, waiting for transfers between devices: 111 us -> 67.4 us  [flip(): return lax.ppermute(value, AXES, pairs)]
    ppermute x33 -> x21, starting transfers between devices: 60.1 us -> 33.6 us  [turn(): return lax.ppermute(value, AXES, pairs)]
    pallas_call x6 -> x8, Pallas kernels: 159 us -> 142 us  [the longest x2 34.6 us: attn_backward(): pl.pallas_call(functools.partial(attn_backward_kernel, segs, seg_count, f...]
    ppermute x64 -> x43, starting transfers between devices: 48.9 us -> 33 us  [flip(): return lax.ppermute(value, AXES, pairs)]
    pallas_call x1, Pallas kernels: 50.1 us -> 38.6 us  [cross_whole(): pl.pallas_call(functools.partial(cross_kernel, rows // count), grid=(rows...]
    ppermute x33 -> x21, waiting for transfers between devices: 56 us -> 47 us  [turn(): return lax.ppermute(value, AXES, pairs)]
    unnamed x72 -> x63, local copies, waits for them, and re-layouts: 8.63 us -> 1.88 us
  transfers between devices with their start and end apart: 97 -> 66, of which waited for: 37 -> 25; matrix products, arithmetic and copies ran while one was open for 7% -> 9% of each run, Pallas kernels for 26% -> 26%
where the time goes in v4:
time: 557 us; the launch traced here: 551 us
  Pallas kernels  250 us (45%)
  waiting for transfers between devices  115 us (21%)
  starting transfers between devices  66.7 us (12%)
  blocking collectives  48.8 us (9%)
  other arithmetic  27.9 us (5%)
  local copies, waits for them, and re-layouts  27.5 us (5%)
  between operations  15.3 us (3%)
    ppermute x43, waiting for transfers between devices, flip(): return lax.ppermute(value, AXES, pairs)  67.4 us
    psum x1, blocking collectives, shards(): grads_one = lax.psum(grads_one + grads_more, AXES)  48.8 us
    ppermute x21, waiting for transfers between devices, turn(): return lax.ppermute(value, AXES, pairs)  47 us
    pallas_call x1, Pallas kernels, ffn_backward(): pl.pallas_call(functools.partial(ffn_backward_kernel, segs, seg_count), g...  40.3 us
    pallas_call x1, Pallas kernels, cross_whole(): pl.pallas_call(functools.partial(cross_kernel, rows // count), grid=(rows...  38.6 us
    pallas_call x2, Pallas kernels, attn_backward(): pl.pallas_call(functools.partial(attn_backward_kernel, segs, seg_count, f...  34.6 us
    ppermute x21, starting transfers between devices, turn(): return lax.ppermute(value, AXES, pairs)  33.6 us
    ppermute x43, starting transfers between devices, flip(): return lax.ppermute(value, AXES, pairs)  33 us
  transfers between devices with their start and end apart: 66, of which 25 were waited for; matrix products, arithmetic and copies ran while one was open for 9% of the time, Pallas kernels for 26%

profile of v4, /device:TPU:0, one launch (start us, length us, event | category | flops | bytes accessed | tf_op | source)
XLA Modules:
  0.0 551.4 jit_solution(8716888509273881312)
XLA Ops:
  12.3 5.1 collective-permute-start.2
  25.4 4.3 collective-permute-done
  36.2 6.1 %collective-permute-done.5 = bf16[5,24,768]{2,1,0:T(8,128)(2,1)S(1)} collective-permute-done((bf16[5,24,768]{2,1,0:T(8,128)(2,1)S(1)}, bf16[5,24,768]{2,1,0:T(8,128)(2,1)S(1)}, u32[]{:S(2)}, u32[]{:S(2)}) %collective-permute-start.5) | collective-permute-done | bytes 184352 | tf_op jit(solution)/shard_map/ppermute | solution.py:865
  42.4 7.2 %collective-permute-done.3 = bf16[5,24,768]{2,1,0:T(8,128)(2,1)S(1)} collective-permute-done((bf16[5,24,768]{2,1,0:T(8,128)(2,1)S(1)}, bf16[5,24,768]{2,1,0:T(8,128)(2,1)S(1)}, u32[]{:S(2)}, u32[]{:S(2)}) %collective-permute-start.3) | collective-permute-done | bytes 184352 | tf_op jit(solution)/shard_map/ppermute | solution.py:865
  49.7 6.5 %collective-permute-start.26 = (bf16[96,768]{1,0:T(8,128)(2,1)S(1)}, bf16[96,768]{1,0:T(8,128)(2,1)S(1)}, u32[]{:S(2)}, u32[]{:S(2)}) collective-permute-start(bf16[96,768]{1,0:T(8,128)(2,1)S(1)} %copy-done.12), channel_id=1, source_target_pairs={{0,3},{1,0},{2,1},{3,2},{4,7},{5,4},{6,5},{7,6},{8,11},{9,8},{10,9... | collective-permute-start | bytes 442376 | tf_op jit(solution)/shard_map/ppermute | solution.py:865
  70.4 10.5 %collective-permute-done.7.rest_3_ = bf16[192,768]{1,0:T(8,128)(2,1)} collective-permute-done((bf16[192,768]{1,0:T(8,128)(2,1)S(1)}, bf16[192,768]{1,0:T(8,128)(2,1)}, u32[]{:S(2)}, u32[]{:S(2)}) %collective-permute-start.7) | collective-permute-done | bytes 294944 | tf_op jit(solution)/shard_map/ppermute | solution.py:857
  84.8 16.2 %collective-permute-done.10.rest_1_ = bf16[480,768]{1,0:T(8,128)(2,1)S(1)} collective-permute-done((bf16[480,768]{1,0:T(8,128)(2,1)S(1)}, bf16[480,768]{1,0:T(8,128)(2,1)S(1)}, u32[]{:S(2)}, u32[]{:S(2)}) %collective-permute-start.10) | collective-permute-done | bytes 737312 | tf_op jit(solution)/shard_map/ppermute | solution.py:857
  104.8 5.2 collective-permute-done.18.rest_4_
  110.1 13.2 %attn_forward.2 = (bf16[2048,2304]{1,0:T(8,128)(2,1)}, bf16[2048,768]{1,0:T(8,128)(2,1)}) custom-call(s32[3]{0:T(128)} %pad_add_fusion.info, bf16[2048,768]{1,0:T(8,128)(2,1)} %bitcast.293, f32[12,768]{1,0:T(8,128)} %slice.270.vec_ref, bf16[304,768]{1,0:T(8,128)(2,1)} %copy-done.11, bf16[304,768]{1,0:T(8,128)(2,1)} %collective-permute-done.8.rest_1_, ...), custom_call_target="tpu_custom_call" | custom-call | flops 12582912000 | bytes 12582912 | tf_op jit(solution)/shard_map/attn_forward/pallas_call | solution.py:486
  127.4 13.0 %attn_forward.3 = (bf16[2048,2304]{1,0:T(8,128)(2,1)}, bf16[2048,768]{1,0:T(8,128)(2,1)}) custom-call(s32[3]{0:T(128)} %pad_add_fusion.info, bf16[2048,768]{1,0:T(8,128)(2,1)} %bitcast.294, f32[12,768]{1,0:T(8,128)} %slice.270.vec_ref, bf16[304,768]{1,0:T(8,128)(2,1)} %copy-done.11, ...), custom_call_target="tpu_custom_call", output_to_operand_aliasing={{0}: (13, {}), {1}: (14, {})} | custom-call | flops 12582912000 | bytes 12582912 | tf_op jit(solution)/shard_map/attn_forward/pallas_call | solution.py:486
  142.6 19.6 %collective-permute-done.28.rest_2_.rest_12_ = bf16[384,768]{1,0:T(8,128)(2,1)S(1)} collective-permute-done((bf16[384,768]{1,0:T(8,128)(2,1)S(1)}, bf16[384,768]{1,0:T(8,128)(2,1)S(1)}, u32[]{:S(2)}, u32[]{:S(2)}) %collective-permute-start.28) | collective-permute-done | bytes 589856 | tf_op jit(solution)/shard_map/ppermute | solution.py:857
  163.8 29.1 %mid_forward.1 = (f32[2048,768]{1,0:T(8,128)}, bf16[2048,768]{1,0:T(8,128)(2,1)}, bf16[2048,3072]{1,0:T(8,128)(2,1)}, bf16[2048,3072]{1,0:T(8,128)(2,1)}) custom-call(s32[3]{0:T(128)} %pad_add_fusion.info, bf16[2048,768]{1,0:T(8,128)(2,1)} %bitcast.295, bf16[2048,768]{1,0:T(8,128)(2,1)} %get-tuple-element.62.mixed_ref, f32[12,768]{1,0:T(8,128)} %slice.270.vec_ref, ...), custom_call_target="tpu_custom_call" | custom-call | flops 25165824000 | bytes 47185920 | tf_op jit(solution)/shard_map/mid_forward/pallas_call | solution.py:503
  193.8 19.6 %down_forward.1 = (f32[2048,768]{1,0:T(8,128)}, f32[8,2,768]{2,1,0:T(2,128)}) custom-call(s32[3]{0:T(128)} %pad_add_fusion.info, f32[2048,768]{1,0:T(8,128)} %get-tuple-element.63.sum_ref, bf16[2048,3072]{1,0:T(8,128)(2,1)} %get-tuple-element.64.act_ref.left_ref, f32[12,768]{1,0:T(8,128)} %slice.270.vec_ref, bf16[384,768]{1,0:T(8,128)(2,1)} %copy-done.10, ...), custom_call_target="tpu_custom_call" | custom-call | flops 12582912000 | bytes 25165824 | tf_op jit(solution)/shard_map/down_forward/pallas_call | solution.py:520
  240.8 38.6 %cross_encoder.1 = (f32[16,768]{1,0:T(8,128)}, f32[16,768]{1,0:T(8,128)}, f32[12,768]{1,0:T(8,128)}, f32[8,768]{1,0:T(8,128)}, f32[24,2304]{1,0:T(8,128)}, /*ind...) custom-call(s32[2]{0:T(128)} %pad_add_fusion.1.info, bf16[512,768]{1,0:T(8,128)(2,1)} %bitcast.263, ...), custom_call_target="tpu_custom_call" | custom-call | flops 23592960000 | bytes 16777216 | tf_op jit(solution)/shard_map/cross_encoder/pallas_call | solution.py:537
  282.4 40.3 %ffn_backward.1 = (bf16[2048,768]{1,0:T(8,128)(2,1)}, bf16[2048,768]{1,0:T(8,128)(2,1)}, bf16[2048,3072]{1,0:T(8,128)(2,1)}, bf16[2048,768]{1,0:T(8,128)(2,1)}, ...) custom-call(s32[3]{0:T(128)} %pad_add_fusion.info, bf16[2048,768]{1,0:T(8,128)(2,1)} %bitcast.292, ...), custom_call_target="tpu_custom_call" | custom-call | flops 44040192000 | bytes 47185920 | tf_op jit(solution)/shard_map/ffn_backward/pallas_call | solution.py:559
  322.7 16.0 %down_weight_grad.1 = (bf16[4,384,768]{2,1,0:T(8,128)(2,1)}, bf16[4,384,768]{2,1,0:T(8,128)(2,1)}) custom-call(s32[3]{0:T(128)} %pad_add_fusion.info, bf16[2048,3072]{1,0:T(8,128)(2,1)} %get-tuple-element.64.act_ref.left_ref, bf16[2048,768]{1,0:T(8,128)(2,1)} %get-tuple-element.78.right_ref), custom_call_target="tpu_custom_call" | custom-call | flops 9663676416 | bytes 12582912 | tf_op jit(solution)/shard_map/down_weight_grad/pallas_call | solution.py:661
  339.8 19.9 %mid_weight_grad.1 = (bf16[4,480,768]{2,1,0:T(8,128)(2,1)}, bf16[4,480,768]{2,1,0:T(8,128)(2,1)}) custom-call(s32[3]{0:T(128)} %pad_add_fusion.info, bf16[2048,768]{1,0:T(8,128)(2,1)} %get-tuple-element.62.mixed_ref, bf16[2048,768]{1,0:T(8,128)(2,1)} %get-tuple-element.75.proj_ref.proj_grad_ref, bf16[2048,768]{1,0:T(8,128)(2,1)} %get-tuple-element.76.low_ref, ...), custom_call_target="tpu_custom_call" | custom-call | flops 12079595520 | bytes 15728640 | tf_op jit(solution)/shard_map/mid_weight_grad/pallas_call | solution.py:634
  365.8 17.5 %attn_backward.2 = (bf16[2048,2304]{1,0:T(8,128)(2,1)}, f32[2,768]{1,0:T(2,128)}) custom-call(s32[3]{0:T(128)} %pad_add_fusion.info, bf16[2048,2304]{1,0:T(8,128)(2,1)} %get-tuple-element.73.packed_ref, bf16[2048,768]{1,0:T(8,128)(2,1)} %get-tuple-element.85.mixed_grad_ref), custom_call_target="tpu_custom_call" | custom-call | flops 15728640000 | bytes 12582912 | tf_op jit(solution)/shard_map/attn_backward/pallas_call | solution.py:581
  394.5 17.1 %attn_backward.3 = (bf16[2048,2304]{1,0:T(8,128)(2,1)}, f32[2,768]{1,0:T(2,128)}) custom-call(s32[3]{0:T(128)} %pad_add_fusion.info, bf16[2048,2304]{1,0:T(8,128)(2,1)} %get-tuple-element.73.packed_ref, bf16[2048,768]{1,0:T(8,128)(2,1)} %get-tuple-element.85.mixed_grad_ref, bf16[2048,2304]{1,0:T(8,128)(2,1)} %get-tuple-element.84.rest_0_), custom_call_target="tpu_custom_call", output_to_operand_aliasing={{0}: (3, {})} | custom-call | flops 15728640000 | bytes 12582912 | tf_op jit(solution)/shard_map/attn_backward/pallas_call | solution.py:581
  415.2 12.3 %qkv_weight_grad.1 = (bf16[4,288,768]{2,1,0:T(8,128)(2,1)}, bf16[4,288,768]{2,1,0:T(8,128)(2,1)}) custom-call(s32[3]{0:T(128)} %pad_add_fusion.info, bf16[2048,768]{1,0:T(8,128)(2,1)} %bitcast.296, bf16[2048,2304]{1,0:T(8,128)(2,1)} %get-tuple-element.90.right_ref.packed_grad_ref), custom_call_target="tpu_custom_call" | custom-call | flops 7247757312 | bytes 9437184 | tf_op jit(solution)/shard_map/qkv_weight_grad/pallas_call | solution.py:617
  436.7 48.8 %all-reduce.2 = (f32[2,768]{1,0:T(2,128)S(1)}, f32[10,768]{1,0:T(8,128)S(1)}) all-reduce(f32[2,768]{1,0:T(2,128)S(1)} %add.283, f32[10,768]{1,0:T(8,128)} %slice.331), channel_id=1, replica_groups=mesh['dp'=8,'fsdp'=4] {'dp','fsdp'}, use_global_device_ids=true, to_apply=%region_0.1 | all-reduce | flops 9216 | bytes 73728 | tf_op jit(solution)/shard_map/psum | solution.py:1124
  502.9 5.0 collective-permute-done.62
  512.1 6.1 %collective-permute-done.59 = bf16[120,768]{1,0:T(8,128)(2,1)S(1)} collective-permute-done((bf16[120,768]{1,0:T(8,128)(2,1)S(1)}, bf16[120,768]{1,0:T(8,128)(2,1)S(1)}, u32[]{:S(2)}, u32[]{:S(2)}) %collective-permute-start.59) | collective-permute-done | bytes 184352 | tf_op jit(solution)/shard_map/ppermute | solution.py:865
  530.1 13.4 %token_gradient.1 = bf16[2048,768]{1,0:T(8,128)(2,1)} custom-call(s32[3]{0:T(128)} %pad_add_fusion.info, bf16[2048,2304]{1,0:T(8,128)(2,1)} %get-tuple-element.90.right_ref.packed_grad_ref, bf16[2048,768]{1,0:T(8,128)(2,1)} %get-tuple-element.75.proj_ref.proj_grad_ref, bf16[304,768]{1,0:T(8,128)(2,1)} %copy-done.11, ...), custom_call_target="tpu_custom_call" | custom-call | flops 9437184000 | bytes 15728640 | tf_op jit(solution)/shard_map/token_gradient/pallas_call | solution.py:596
  (307 shorter events, 145.4 us)
Async XLA Ops:
  7.2 232.8 %all-gather.5.cloned.1.call-start = ((), (), s32[]{:S(2)}) async-start(), calls=%async_computation.1 | async-start | bytes 4866048 | tf_op jit(solution)/shard_map/all_gather | solution.py:1041
  8.0 232.1 %all-gather.3.cloned.1.call-start = ((), (), s32[]{:S(2)}) async-start(), calls=%async_computation | async-start | bytes 9732096 | tf_op jit(solution)/shard_map/all_gather | solution.py:1040
  33.1 23.8 %collective-permute-start.8 = (bf16[304,768]{1,0:T(8,128)(2,1)S(1)}, bf16[304,768]{1,0:T(8,128)(2,1)}, u32[]{:S(2)}, u32[]{:S(2)}) collective-permute-start(bf16[304,768]{1,0:T(8,128)(2,1)S(1)} %fusion.10.rest_0_), channel_id=1, source_target_pairs={{0,8},{1,9},{2,10},{3,11},{4,12},{5,13},{6,14},{7,15},{8,0},{9,1},... | collective-permute-start | bytes 1400840 | tf_op jit(solution)/shard_map/ppermute | solution.py:857
  34.7 28.8 %collective-permute-start.6 = (bf16[304,768]{1,0:T(8,128)(2,1)S(1)}, bf16[304,768]{1,0:T(8,128)(2,1)}, u32[]{:S(2)}, u32[]{:S(2)}) collective-permute-start(bf16[304,768]{1,0:T(8,128)(2,1)S(1)} %fusion.10.rest_0_), channel_id=1, source_target_pairs={{0,16},{1,17},{2,18},{3,19},{4,20},{5,21},{6,22},{7,23},{8,24},{9,... | collective-permute-start | bytes 1400840 | tf_op jit(solution)/shard_map/ppermute | solution.py:857
  80.9 44.4 %collective-permute-start.19 = (bf16[480,768]{1,0:T(8,128)(2,1)S(1)}, bf16[480,768]{1,0:T(8,128)(2,1)}, u32[]{:S(2)}, u32[]{:S(2)}) collective-permute-start(bf16[480,768]{1,0:T(8,128)(2,1)S(1)} %bitcast.264), channel_id=1, source_target_pairs={{0,4},{1,5},{2,6},{3,7},{4,0},{5,1},{6,2},{7,3},{8,12},{9,13},{10,... | collective-permute-start | bytes 2211848 | tf_op jit(solution)/shard_map/ppermute | solution.py:857
  80.9 22.2 %collective-permute-start.11 = (bf16[480,768]{1,0:T(8,128)(2,1)S(1)}, bf16[480,768]{1,0:T(8,128)(2,1)}, u32[]{:S(2)}, u32[]{:S(2)}) collective-permute-start(bf16[480,768]{1,0:T(8,128)(2,1)S(1)} %bitcast.265), channel_id=1, source_target_pairs={{0,16},{1,17},{2,18},{3,19},{4,20},{5,21},{6,22},{7,23},{8,24},{9,... | collective-permute-start | bytes 2211848 | tf_op jit(solution)/shard_map/ppermute | solution.py:857
  83.0 27.0 %collective-permute-start.16 = (bf16[192,768]{1,0:T(8,128)(2,1)}, bf16[192,768]{1,0:T(8,128)(2,1)}, u32[]{:S(2)}, u32[]{:S(2)}) collective-permute-start(bf16[192,768]{1,0:T(8,128)(2,1)} %collective-permute-done.7.rest_3_), channel_id=1, source_target_pairs={{0,4},{1,5},{2,6},{3,7},{4,0},{5,1},{6,2},{7,3},{8,12},{9,13},{10,... | collective-permute-start | bytes 884744 | tf_op jit(solution)/shard_map/ppermute | solution.py:857
  104.8 22.5 %collective-permute-start.21 = (bf16[480,768]{1,0:T(8,128)(2,1)}, bf16[480,768]{1,0:T(8,128)(2,1)}, u32[]{:S(2)}, u32[]{:S(2)}) collective-permute-start(bf16[480,768]{1,0:T(8,128)(2,1)} %collective-permute-done.11.rest_2_), channel_id=1, source_target_pairs={{0,4},{1,5},{2,6},{3,7},{4,0},{5,1},{6,2},{7,3},{8,12},{9,13},{10,... | collective-permute-start | bytes 2211848 | tf_op jit(solution)/shard_map/ppermute | solution.py:857
  125.3 36.9 %collective-permute-start.28 = (bf16[384,768]{1,0:T(8,128)(2,1)S(1)}, bf16[384,768]{1,0:T(8,128)(2,1)S(1)}, u32[]{:S(2)}, u32[]{:S(2)}) collective-permute-start(bf16[384,768]{1,0:T(8,128)(2,1)S(1)} %pad_maximum_fusion.4.rest_0_.rest_10_), channel_id=1, source_target_pairs={{0,16},{1,17},{2,18},{3,19},{4,20},{5,21},{6,22},{7,23},{8,24},{9,... | collective-permute-start | bytes 1769480 | tf_op jit(solution)/shard_map/ppermute | solution.py:857
  126.8 37.0 %collective-permute-start.27 = (bf16[384,768]{1,0:T(8,128)(2,1)S(1)}, bf16[384,768]{1,0:T(8,128)(2,1)S(1)}, u32[]{:S(2)}, u32[]{:S(2)}) collective-permute-start(bf16[384,768]{1,0:T(8,128)(2,1)S(1)} %pad_maximum_fusion.4.rest_0_.rest_10_), channel_id=1, source_target_pairs={{0,8},{1,9},{2,10},{3,11},{4,12},{5,13},{6,14},{7,15},{8,0},{9,1},... | collective-permute-start | bytes 1769480 | tf_op jit(solution)/shard_map/ppermute | solution.py:857
  127.4 36.4 %collective-permute-start.22 = (bf16[288,768]{1,0:T(8,128)(2,1)S(1)}, bf16[288,768]{1,0:T(8,128)(2,1)}, u32[]{:S(2)}, u32[]{:S(2)}) collective-permute-start(bf16[288,768]{1,0:T(8,128)(2,1)S(1)} %collective-permute-done.17.rest_3_), channel_id=1, source_target_pairs={{0,4},{1,5},{2,6},{3,7},{4,0},{5,1},{6,2},{7,3},{8,12},{9,13},{10,... | collective-permute-start | bytes 1327112 | tf_op jit(solution)/shard_map/ppermute | solution.py:857
  140.4 52.6 %collective-permute-start.30 = (bf16[384,768]{1,0:T(8,128)(2,1)S(1)}, bf16[384,768]{1,0:T(8,128)(2,1)S(1)}, u32[]{:S(2)}, u32[]{:S(2)}) collective-permute-start(bf16[384,768]{1,0:T(8,128)(2,1)S(1)} %pad_maximum_fusion.4.rest_0_.rest_10_), channel_id=1, source_target_pairs={{0,4},{1,5},{2,6},{3,7},{4,0},{5,1},{6,2},{7,3},{8,12},{9,13},{10,... | collective-permute-start | bytes 1769480 | tf_op jit(solution)/shard_map/ppermute | solution.py:857
  142.5 50.4 %collective-permute-start.33 = (bf16[384,768]{1,0:T(8,128)(2,1)}, bf16[384,768]{1,0:T(8,128)(2,1)}, u32[]{:S(2)}, u32[]{:S(2)}) collective-permute-start(bf16[384,768]{1,0:T(8,128)(2,1)} %collective-permute-done.29.rest_3_.rest_13_), channel_id=1, source_target_pairs={{0,4},{1,5},{2,6},{3,7},{4,0},{5,1},{6,2},{7,3},{8,12},{9,13},{10,... | collective-permute-start | bytes 1769480 | tf_op jit(solution)/shard_map/ppermute | solution.py:857
  162.2 30.8 %collective-permute-start.32 = (bf16[384,768]{1,0:T(8,128)(2,1)S(1)}, bf16[384,768]{1,0:T(8,128)(2,1)}, u32[]{:S(2)}, u32[]{:S(2)}) collective-permute-start(bf16[384,768]{1,0:T(8,128)(2,1)S(1)} %collective-permute-done.28.rest_2_.rest_12_), channel_id=1, source_target_pairs={{0,4},{1,5},{2,6},{3,7},{4,0},{5,1},{6,2},{7,3},{8,12},{9,13},{10,... | collective-permute-start | bytes 1769480 | tf_op jit(solution)/shard_map/ppermute | solution.py:857
  163.8 29.2 %collective-permute-start.31 = (bf16[384,768]{1,0:T(8,128)(2,1)S(1)}, bf16[384,768]{1,0:T(8,128)(2,1)}, u32[]{:S(2)}, u32[]{:S(2)}) collective-permute-start(bf16[384,768]{1,0:T(8,128)(2,1)S(1)} %collective-permute-done.27.rest_1_.rest_11_), channel_id=1, source_target_pairs={{0,4},{1,5},{2,6},{3,7},{4,0},{5,1},{6,2},{7,3},{8,12},{9,13},{10,... | collective-permute-start | bytes 1769480 | tf_op jit(solution)/shard_map/ppermute | solution.py:857
  359.7 28.6 %collective-permute-start.44 = (bf16[4,480,768]{2,1,0:T(8,128)(2,1)}, bf16[4,480,768]{2,1,0:T(8,128)(2,1)}, u32[]{:S(2)}, u32[]{:S(2)}) collective-permute-start(bf16[4,480,768]{2,1,0:T(8,128)(2,1)} %get-tuple-element.81), channel_id=1, source_target_pairs={{0,4},{1,5},{2,6},{3,7},{4,0},{5,1},{6,2},{7,3},{8,12},{9,13},{10,... | collective-permute-start | bytes 8847368 | tf_op jit(solution)/shard_map/ppermute | solution.py:857
  363.7 23.0 %collective-permute-start.42 = (bf16[2,96,768]{2,1,0:T(8,128)(2,1)}, bf16[2,96,768]{2,1,0:T(8,128)(2,1)S(1)}, u32[]{:S(2)}, u32[]{:S(2)}) collective-permute-start(bf16[2,96,768]{2,1,0:T(8,128)(2,1)} %bitcast.63), channel_id=1, source_target_pairs={{0,8},{1,9},{2,10},{3,11},{4,12},{5,13},{6,14},{7,15},{8,0},{9,1},... | collective-permute-start | bytes 884744 | tf_op jit(solution)/shard_map/ppermute | solution.py:857
  385.3 29.9 %collective-permute-start.49 = (bf16[4,96,768]{2,1,0:T(8,128)(2,1)}, bf16[4,96,768]{2,1,0:T(8,128)(2,1)}, u32[]{:S(2)}, u32[]{:S(2)}) collective-permute-start(bf16[4,96,768]{2,1,0:T(8,128)(2,1)} %pad_maximum_fusion.5), channel_id=1, source_target_pairs={{0,8},{1,9},{2,10},{3,11},{4,12},{5,13},{6,14},{7,15},{8,0},{9,1},... | collective-permute-start | bytes 1769480 | tf_op jit(solution)/shard_map/ppermute | solution.py:857
  387.7 27.5 %collective-permute-start.50 = (bf16[4,96,768]{2,1,0:T(8,128)(2,1)}, bf16[4,96,768]{2,1,0:T(8,128)(2,1)}, u32[]{:S(2)}, u32[]{:S(2)}) collective-permute-start(bf16[4,96,768]{2,1,0:T(8,128)(2,1)} %pad_maximum_fusion.6), channel_id=1, source_target_pairs={{0,16},{1,17},{2,18},{3,19},{4,20},{5,21},{6,22},{7,23},{8,24},{9,... | collective-permute-start | bytes 1769480 | tf_op jit(solution)/shard_map/ppermute | solution.py:857
  392.5 22.7 %collective-permute-start.45 = (bf16[2,120,768]{2,1,0:T(8,128)(2,1)}, bf16[2,120,768]{2,1,0:T(8,128)(2,1)}, u32[]{:S(2)}, u32[]{:S(2)}) collective-permute-start(bf16[2,120,768]{2,1,0:T(8,128)(2,1)} %bitcast.72), channel_id=1, source_target_pairs={{0,16},{1,17},{2,18},{3,19},{4,20},{5,21},{6,22},{7,23},{8,24},{9,... | collective-permute-start | bytes 1105928 | tf_op jit(solution)/shard_map/ppermute | solution.py:857
  393.9 21.3 %collective-permute-start.47 = (bf16[2,120,768]{2,1,0:T(8,128)(2,1)}, bf16[2,120,768]{2,1,0:T(8,128)(2,1)}, u32[]{:S(2)}, u32[]{:S(2)}) collective-permute-start(bf16[2,120,768]{2,1,0:T(8,128)(2,1)} %bitcast.77), channel_id=1, source_target_pairs={{0,8},{1,9},{2,10},{3,11},{4,12},{5,13},{6,14},{7,15},{8,0},{9,1},... | collective-permute-start | bytes 1105928 | tf_op jit(solution)/shard_map/ppermute | solution.py:857
  427.6 66.6 %collective-permute-start.51 = (bf16[4,288,768]{2,1,0:T(8,128)(2,1)}, bf16[4,288,768]{2,1,0:T(8,128)(2,1)}, u32[]{:S(2)}, u32[]{:S(2)}) collective-permute-start(bf16[4,288,768]{2,1,0:T(8,128)(2,1)} %get-tuple-element.89), channel_id=1, source_target_pairs={{0,4},{1,5},{2,6},{3,7},{4,0},{5,1},{6,2},{7,3},{8,12},{9,13},{10,... | collective-permute-start | bytes 5308424 | tf_op jit(solution)/shard_map/ppermute | solution.py:857
  429.8 62.0 %collective-permute-start.48 = (bf16[4,120,768]{2,1,0:T(8,128)(2,1)}, bf16[4,120,768]{2,1,0:T(8,128)(2,1)}, u32[]{:S(2)}, u32[]{:S(2)}) collective-permute-start(bf16[4,120,768]{2,1,0:T(8,128)(2,1)} %pad_maximum_fusion.3), channel_id=1, source_target_pairs={{0,16},{1,17},{2,18},{3,19},{4,20},{5,21},{6,22},{7,23},{8,24},{9,... | collective-permute-start | bytes 2211848 | tf_op jit(solution)/shard_map/ppermute | solution.py:857
  432.4 59.4 %collective-permute-start.46 = (bf16[4,120,768]{2,1,0:T(8,128)(2,1)}, bf16[4,120,768]{2,1,0:T(8,128)(2,1)}, u32[]{:S(2)}, u32[]{:S(2)}) collective-permute-start(bf16[4,120,768]{2,1,0:T(8,128)(2,1)} %pad_maximum_fusion.2), channel_id=1, source_target_pairs={{0,8},{1,9},{2,10},{3,11},{4,12},{5,13},{6,14},{7,15},{8,0},{9,1},... | collective-permute-start | bytes 2211848 | tf_op jit(solution)/shard_map/ppermute | solution.py:857
  (73 other events, 1056.6 us)
Sparse Core Ops, SparseCore 0:
  10.9 77.6 all-gather.4
  92.2 92.8 all-gather.2

commit v5 on v4

--- a/solution.py
+++ b/solution.py
@@ -200,15 +200,15 @@
 
 
 def cross_kernel(blocks, info, heads_ref, up_ref, live_ref, vec_ref, pos_ref, *rest):
-    wide, tall, rest = rest[0], rest[1], rest[2:]
+    wide, rest = rest[0], rest[1:]
     (own_ref, own_grad_ref, grads_ref, pos_grad_ref, qkv_grad_ref, out_grad_ref, up_grad_ref, down_grad_ref) = rest[:8]
     (qkv, out, up, down, sems, result, heads_grad, slope, lefts, act, packed, rights, hidden_grad) = rest[8:]
     step = pl.program_id(0)
     count = heads_ref.shape[0]
     at = pl.ds(pl.multiple_of(step * count, count), count)
     targets = [qkv.at[j] for j in range(3)] + [out] + [up.at[j] for j in range(4)]
+    targets += [down.at[j * 768 : (j + 1) * 768] for j in range(4)]
     copies = [pltpu.make_async_copy(wide.at[j], t, sems.at[j]) for j, t in enumerate(targets)]
-    copies.append(pltpu.make_async_copy(tall, down, sems.at[8]))
 
     @pl.when(step == 0)
     def _():
@@ -324,7 +324,9 @@
         for j in range(4):
             cols = slice(j * 768, (j + 1) * 768)
             up_grad_ref[:, cols] = mm(left, hidden_grad[:, cols])
-        down_grad_ref[...] = mm(chosen(act[...], 96), rights[1])
+        for j in range(4):
+            left = chosen(act[:, j * 768 : (j + 1) * 768], 24)
+            down_grad_ref[j * 24 : (j + 1) * 24, :] = mm(left, rights[1])
 
 
 def column_sum(value):
@@ -423,9 +425,20 @@
         target[mask // 2] = total[pl.ds(block, rows), :].astype(LOW)
 
 
-def qkv_grad_kernel(info, left_ref, right_ref, keep_ref, send_ref, total):
+def qkv_grad_kernel(info, left_ref, right_ref, more_ref, keep_ref, send_ref, total):
+    step = pl.program_id(0)
     total[...] = mm_tn(left_ref[...], right_ref[...])
-    send_slab(info[0], total, keep_ref, send_ref, 96)
+    at = pl.ds(pl.multiple_of(step * 96, 96), 96)
+    for mask in range(8):
+        block = pl.multiple_of((info[0] ^ mask) * 96, 96)
+        target = send_ref if mask % 2 else keep_ref
+        target[mask // 2, at, :] = total[pl.ds(block, 96), :].astype(LOW)
+
+    @pl.when(step == 0)
+    def _():
+        for mask in range(8):
+            target = send_ref if mask % 2 else keep_ref
+            target[mask // 2, 288:304, :] = more_ref[mask]
 
 
 def mid_grad_kernel(info, mixed_ref, proj_ref, low_ref, hidden_ref, keep_ref, send_ref, total):
@@ -530,7 +543,7 @@
     )(info, summed, act, vec, *pieces)
 
 
-def cross_whole(info, heads, upstream, live, vec, positions, wide, tall):
+def cross_whole(info, heads, upstream, live, vec, positions, wide):
     rows = heads.shape[0]
     count = 2 * SEG
     own = [(16, 768), (16, 768), (12, 768), (8, 768), (24, 2304), (24, 768), (24, 3072), (96, 768)]
@@ -538,10 +551,10 @@
         functools.partial(cross_kernel, rows // count),
         grid=(rows // count,),
         in_specs=[SMEM, block_rows(count, 768), block_rows(count, 768), block_rows(count, SEG),
-                  fixed((12, 768)), fixed((8, 768)), ANY, ANY],
+                  fixed((12, 768)), fixed((8, 768)), ANY],
         out_specs=[fixed(dims) for dims in own],
         out_shape=[shape_of(dims, F32) for dims in own],
-        scratch_shapes=QKV + MID + DOWN + sems(9) + [
+        scratch_shapes=QKV + MID + DOWN + sems(12) + [
             pltpu.VMEM((rows, 768), F32), pltpu.VMEM((rows, 768), F32), pltpu.VMEM((count, 3072), LOW),
             pltpu.VMEM((3, rows, 768), LOW), pltpu.VMEM((rows, 3072), LOW), pltpu.VMEM((count, 2304), LOW),
             pltpu.VMEM((5, rows, 768), LOW), pltpu.VMEM((rows, 3072), LOW),
@@ -549,7 +562,7 @@
         compiler_params=params(),
         cost_estimate=cost(2 * rows * 768 * 30000, 2**24),
         name="cross_encoder",
-    )(info, heads, upstream, live, vec, positions, wide, tall)
+    )(info, heads, upstream, live, vec, positions, wide)
 
 
 def ffn_backward(info, cotangent, heads_grad, heads, second, summed, slope, vec, mid, down, seg_count, segs=2):
@@ -611,20 +624,20 @@
     return [out, out], [shape_of((4, slabs * 96, 768))] * 2
 
 
-def qkv_weight_grad(info, left, right):
+def qkv_weight_grad(info, left, right, more):
     rows = left.shape[0]
-    specs, shapes = grad_outs(3)
+    out = fixed((4, 304, 768))
     return pl.pallas_call(
         qkv_grad_kernel,
         grid=(3,),
-        in_specs=[SMEM, fixed((rows, 768)), pl.BlockSpec((rows, 768), lambda i: (0, i))],
-        out_specs=specs,
-        out_shape=shapes,
+        in_specs=[SMEM, fixed((rows, 768)), pl.BlockSpec((rows, 768), lambda i: (0, i)), fixed((8, 16, 768))],
+        out_specs=[out, out],
+        out_shape=[shape_of((4, 304, 768))] * 2,
         scratch_shapes=[pltpu.VMEM((768, 768), F32)],
         compiler_params=params(),
         cost_estimate=cost(2 * rows * 768 * 2304, rows * 2304 * 2),
         name="qkv_weight_grad",
-    )(info, left, right)
+    )(info, left, right, more)
 
 
 def mid_weight_grad(info, mixed, proj_grad, low, hidden_grad):
@@ -916,12 +929,18 @@
 class Sum:
     def __init__(self, links, keep, send, slabs):
         self.links, self.keep, self.slabs = links, keep, slabs
+        self.more = keep.shape[1] % 96
         self.came = links.flip(send, 1)
 
     def line(self, part):
         inner = self.links.inner
-        part = part.reshape(self.slabs, inner, -1, part.shape[-1])
-        return part.transpose(1, 0, 2, 3).reshape(inner, -1, part.shape[-1])
+        count = part.shape[0] - self.more
+        main = part[:count].reshape(self.slabs, inner, -1, part.shape[-1])
+        main = main.transpose(1, 0, 2, 3).reshape(inner, -1, part.shape[-1])
+        if not self.more:
+            return main
+        rows = part[count : count + inner].reshape(inner, 1, -1)
+        return jnp.concatenate([main, jnp.pad(rows, ((0, 0), (0, 7), (0, 0)))], axis=1)
 
     def to(self, index):
         return self.line(add(self.keep[index], self.came[index]))
@@ -945,34 +964,37 @@
         self.near_came = [self.links.flip(self.to(m // 2), m) for m in (2, 4, 6)]
         return self.near_came
 
-    def finish(self):
+    def turn(self, *earlier):
         links = self.links
         own = add(self.line(self.keep[0]), self.line(self.came[0]), *self.near_came)
-
-        def pick(index):
-            return lax.dynamic_index_in_dim(own, index % links.inner, 0, keepdims=False)
-
-        total = pick(links.z).astype(F32)
-        for step in range(1, links.inner):
-            total = total + links.turn(pick(links.z + step), step).astype(F32)
-        return total
+        own = after(own, *earlier) if earlier else own
+        parts = [lax.dynamic_index_in_dim(own, (links.z + k) % links.inner, 0, keepdims=False) for k in range(links.inner)]
+        self.turned = [parts[0]] + [links.turn(parts[k], k) for k in range(1, links.inner)]
+        return self.turned[1:]
+
+    def total(self):
+        return sum(t.astype(F32) for t in self.turned)
 
 
 class PlainSum:
     def __init__(self, links, keep, send, slabs):
-        flat = jnp.stack([keep, send], axis=1).reshape(8, slabs, -1, 768)
-        rows = flat.shape[2] * 8 // (links.outer * links.inner)
-        flat = flat.transpose(1, 0, 2, 3).reshape(slabs, -1, 768) if slabs > 1 else flat.reshape(1, -1, 768)
-        self.total = lax.psum_scatter(flat, AXES, scatter_dimension=1, tiled=True).reshape(-1, 768).astype(F32)
+        more = keep.shape[1] % 96
+        flat = jnp.stack([keep, send], axis=1).reshape(8, -1, 768)
+        main = flat[:, : flat.shape[1] - more].reshape(8, slabs, -1, 768)
+        main = main.transpose(1, 0, 2, 3).reshape(slabs, -1, 768)
         self.came = keep
-
-    def far(self):
+        self.sums = lax.psum_scatter(main, AXES, scatter_dimension=1, tiled=True).reshape(-1, 768)
+        if more:
+            rows = flat[:, flat.shape[1] - more :][:, : links.outer * links.inner // 8].reshape(-1, 768)
+            self.sums = jnp.concatenate([self.sums, lax.psum_scatter(rows, AXES, scatter_dimension=0, tiled=True)])
+
+    def far(self, *earlier):
         return []
 
-    near = direct = far
-
-    def finish(self):
-        return self.total
+    near = direct = turn = far
+
+    def total(self):
+        return self.sums.astype(F32)
 
 
 def after(value, *earlier):
@@ -987,6 +1009,18 @@
 def matrix_of(slabs):
     count, rows, width = slabs.shape
     return slabs.transpose(1, 0, 2).reshape(rows, count * width)
+
+
+def mix_columns(matrix, devices):
+    rows, wide = matrix.shape
+    matrix = matrix.reshape(rows, devices, 4, -1).transpose(0, 2, 1, 3)
+    return matrix.reshape(rows, wide)
+
+
+def unmix_columns(matrix, devices):
+    rows, wide = matrix.shape
+    matrix = matrix.reshape(rows, 4, devices, -1).transpose(0, 2, 1, 3)
+    return matrix.reshape(rows, wide)
 
 
 def plain_pieces(slabs, whole):
@@ -1029,7 +1063,9 @@
     my_lengths = lax.dynamic_slice_in_dim(lengths, me * seq_local, seq_local)
     info = jnp.concatenate([jnp.full((1,), links.place, jnp.int32), my_lengths])
     small = jnp.concatenate([seg_vec, cross_vec, positions]).reshape(1, -1)
-    wide = jnp.concatenate([slabs_of(cross_qkv), slabs_of(cross_out), slabs_of(cross_up)])
+    up_slabs = mix_columns(cross_up, devices).reshape(-1, 4, feat_dim).transpose(1, 0, 2)
+    wide = [slabs_of(cross_qkv), slabs_of(cross_out), up_slabs, cross_down.reshape(4, -1, feat_dim)]
+    wide = jnp.concatenate(wide)
     mid_shard = jnp.concatenate([slabs_of(seg_out), slabs_of(seg_up)])
     rows_in = tokens.reshape(-1, feat_dim)
     cot_rows = cotangent.reshape(-1, feat_dim)
@@ -1037,8 +1073,6 @@
     live_own = (seg_starts[None, :] < my_lengths[:, None]).reshape(-1, 1)
     up_own = jnp.where(live_own, cotangent.reshape(-1, SEG, feat_dim)[:, 0, :], 0)
 
-    wide = lax.all_gather(wide, AXES, axis=1, tiled=True)
-    tall = lax.all_gather(cross_down, AXES, axis=0, tiled=True)
     if fast:
         first = jnp.concatenate([slabs_of(seg_qkv).reshape(-1, 768), jnp.pad(small, ((0, 7), (0, 0)))])
         line_first = links.gather_z(first)
@@ -1048,31 +1082,41 @@
         rows = jnp.concatenate([p[72:73] for p in line_first])
         block = jnp.concatenate([weights, jnp.pad(rows, ((0, 12), (0, 0)))])
         near = links.spread_near(block)
-        far = links.spread_far(*near, 192)
+        wide = after(wide, *line_mid, *near)
+        far = links.spread_far(*(after(p, *line_mid) for p in near), 192)
         first = links.spread_core([block, *near, *far])
         ends = [p[288:292] for p in first[:3]] + [first[4][96:100]]
         others = [p[288:292] for p in first[5:8]] + [first[9][96:100]]
         small = links.in_order([(ends, others)[m % 2][m // 2] for m in range(8)])
         block = after(jnp.stack(line_mid, axis=1).reshape(-1, 768), *far)
-        near_mid = links.spread_near(block)
-        far_mid = links.spread_far(*near_mid, 288)
-        mid = links.spread_core([block, *near_mid, *far_mid])
-        block = after(jnp.concatenate(line_down), *far_mid)
-        down = links.spread_core([block] + [links.flip(block, m) for m in (2, 4, 6)])
+        mid = [block, *links.spread_near(block)]
     else:
         first = plain_pieces(lax.all_gather(slabs_of(seg_qkv), AXES, axis=1, tiled=True), False)
         mid = plain_pieces(lax.all_gather(mid_shard, AXES, axis=1, tiled=True), False)
         down_whole = lax.all_gather(seg_down, AXES, axis=0, tiled=True)
         down = [down_whole[m * 384 : (m + 1) * 384] for m in (0, 2, 4, 6, 1, 3, 5, 7)]
         small = links.gather_small(small)
-        near_mid = []
+    wide = lax.all_gather(wide, AXES, axis=1, tiled=True)
     small = small.reshape(devices, -1, width).transpose(1, 0, 2).reshape(-1, feat_dim).astype(F32)
     seg_v, cross_v = small[:seg_rows], small[seg_rows : seg_rows + cross_rows]
     pos_table = small[seg_rows + cross_rows :]
+    hidden_rows = slice(5, cross_rows - 3)
+    cross_v = cross_v.at[hidden_rows].set(mix_columns(cross_v[hidden_rows].reshape(1, -1), devices).reshape(-1, feat_dim))
 
     before = attn_forward(info, rows_in, seg_v, first, seg_count, 0)
-    packed, mixed = attn_forward(info, after(rows_in, *near_mid), seg_v, first, seg_count, 1, before)
+    if fast:
+        far = links.spread_far(*(after(p, before[0]) for p in mid[1:]), 288)
+        rows_late = after(rows_in, *mid[1:])
+    else:
+        rows_late = rows_in
+    packed, mixed = attn_forward(info, rows_late, seg_v, first, seg_count, 1, before)
+    if fast:
+        mid = [*mid, *far] + links.spread_core(mid)[3:] + [links.flip(after(p, packed), 1) for p in far]
+        block = after(jnp.concatenate(line_down), *far)
+        near = [links.flip(block, m) for m in (2, 4, 6)]
     summed, low, act, slope = mid_forward(info, rows_in, mixed, seg_v, mid)
+    if fast:
+        down = [block, *near, links.flip(block, 1), *(links.flip(after(p, act), 1) for p in near)]
     second, heads = down_forward(info, summed, act, seg_v, down)
     heads_own = heads.reshape(-1, feat_dim)
     both = links.gather_small(jnp.stack([heads_own.astype(LOW), up_own]))
@@ -1082,10 +1126,10 @@
         cross_info = jnp.stack([links.place, me]).astype(jnp.int32)
         live = jnp.broadcast_to(live_all.reshape(-1, 1), (live_all.size, SEG)).astype(F32)
         cross_own, heads_grad, vec_grad, pos_grad, *cross_grads = cross_whole(
-            cross_info, heads_all, up_all, live, cross_v, pos_table, wide, tall
+            cross_info, heads_all, up_all, live, cross_v, pos_table, wide
         )
     else:
-        weights = (matrix_of(wide[:3]), wide[3], matrix_of(wide[4:]), tall, cross_v)
+        weights = (matrix_of(wide[:3]), wide[3], matrix_of(wide[4:8]), wide[8:].reshape(-1, feat_dim), cross_v)
         heads_in = heads_all.astype(F32).reshape(-1, seg_count, feat_dim) + pos_table[None]
         heads_in = heads_in.reshape(-1, feat_dim)
         cross_result, kept = encode(heads_in, heads_in.astype(LOW), weights, live_all)
@@ -1094,13 +1138,17 @@
         )
         cross_grads = []
         for left, right in pairs:
-            count = left.shape[1] // devices
-            mine = lax.dynamic_slice_in_dim(left, me * count, count, 1)
-            cross_grads.append(trans_left(mine, right))
+            left = left.reshape(left.shape[0], -1, feat_dim)
+            mine = lax.dynamic_slice_in_dim(left, me * width, width, 2)
+            cross_grads.append(trans_left(mine.reshape(left.shape[0], -1), right))
         pos_grad = jnp.sum(all_grad.reshape(-1, seg_count, feat_dim), axis=0)
         own = seq_local * seg_count
         cross_own = lax.dynamic_slice_in_dim(cross_result, me * own, own)
         heads_grad = lax.dynamic_slice_in_dim(all_grad, me * own, own)
+    cross_grads[2] = unmix_columns(cross_grads[2], devices)
+    vec_grad = vec_grad.at[hidden_rows].set(
+        unmix_columns(vec_grad[hidden_rows].reshape(1, -1), devices).reshape(-1, feat_dim)
+    )
     cross_vec_grad = lax.dynamic_slice_in_dim(vec_grad, me * width, width, 1)
     grad_positions = lax.dynamic_slice_in_dim(pos_grad, me * width, width, 1)
 
@@ -1110,22 +1158,31 @@
     down_sum = summing(links, *down_weight_grad(info, act, down_grad), 1)
     mid_parts = mid_weight_grad(info, mixed, proj_grad, low, after(hidden_grad, down_sum.keep if fast else down_sum.came))
     mid_sum = summing(links, *mid_parts, 5)
-    grads_mid = lax.psum(grads_two[2:], AXES)
     half_grad, grads_one = attn_backward(
         info, packed, after(mixed_grad, mid_parts[1], down_sum.came), seg_count, 0
     )
     ready = after(mixed_grad, half_grad, *down_sum.far(), mid_sum.came)
     packed_grad, grads_more = attn_backward(info, packed, ready, seg_count, 1, half_grad)
+    vec_parts = jnp.concatenate([grads_one + grads_more, grads_two[2:]]).reshape(seg_rows, devices, width)
+    vec_parts = vec_parts.transpose(1, 0, 2).reshape(outer, inner, seg_rows * width).astype(LOW)
+    if outer > 8:
+        vec_parts = vec_parts.reshape(8, -1, seg_rows * width)
+    vec_parts = jnp.pad(vec_parts, ((0, 0), (0, 16 - vec_parts.shape[1]), (0, feat_dim - seg_rows * width)))
+    if fast:
+        vec_parts = links.in_order(list(vec_parts))
     ready = after(packed_grad, *down_sum.near(), *mid_sum.far())
-    qkv_sum = summing(links, *qkv_weight_grad(info, rows_in, ready), 3)
-    ready = after(packed_grad, *mid_sum.near(), qkv_sum.came)
+    keep, send = qkv_weight_grad(info, rows_in, ready, vec_parts)
+    qkv_sum = summing(links, keep, after(send, *down_sum.turn(), *mid_sum.near()), 3)
+    ready = after(packed_grad, qkv_sum.came)
     token_grad = token_gradient(info, ready, proj_grad, first)
     qkv_sum.direct()
-    grads_one = lax.psum(grads_one + grads_more, AXES)
-    grad_down = down_sum.finish()
-    grad_mid = mid_sum.finish().reshape(5, -1, feat_dim)
-    grad_qkv = matrix_of(qkv_sum.finish().reshape(3, -1, feat_dim))
-    grad_vec = lax.dynamic_slice_in_dim(jnp.concatenate([grads_one, grads_mid]), me * width, width, 1)
+    mid_sum.turn()
+    qkv_sum.turn(token_grad)
+    grad_down = down_sum.total()
+    grad_mid = mid_sum.total().reshape(5, -1, feat_dim)
+    total = qkv_sum.total()
+    grad_qkv = matrix_of(total[: 3 * width].reshape(3, -1, feat_dim))
+    grad_vec = total[3 * width, : seg_rows * width].reshape(seg_rows, width)
     return (
         layer_out.reshape(tokens.shape),
         token_grad.reshape(tokens.shape),

time: 557 us -> 483 us (0.87)
  waiting for transfers between devices: 115 us -> 63.5 us
  blocking collectives: 48.8 us -> 0 us
  starting transfers between devices: 66.7 us -> 78.1 us
  local copies, waits for them, and re-layouts: 27.5 us -> 37.3 us
    psum x1 -> x0, blocking collectives: 48.8 us -> none  [shards(): grads_one = lax.psum(grads_one + grads_more, AXES)]
    ppermute x43, waiting for transfers between devices: 67.4 us -> 39.2 us  [flip(): return lax.ppermute(value, AXES, pairs)]
    ppermute x21, waiting for transfers between devices: 47 us -> 24.3 us  [turn(): return lax.ppermute(value, AXES, pairs)]
    ppermute x21, starting transfers between devices: 33.6 us -> 47.1 us  [turn(): return lax.ppermute(value, AXES, pairs)]
  transfers between devices with their start and end apart: 66 -> 65, of which waited for: 25 -> 20; matrix products, arithmetic and copies ran while one was open for 9% -> 12% of each run, Pallas kernels for 26% -> 33%
where the time goes in v5:
time: 483 us; the launch traced here: 475 us
  Pallas kernels  252 us (52%)
  starting transfers between devices  78.1 us (16%)
  waiting for transfers between devices  63.5 us (13%)
  local copies, waits for them, and re-layouts  37.3 us (8%)
  other arithmetic  28.5 us (6%)
  between operations  15.6 us (3%)
    ppermute x21, starting transfers between devices, turn(): return lax.ppermute(value, AXES, pairs)  47.1 us
    pallas_call x1, Pallas kernels, ffn_backward(): pl.pallas_call(functools.partial(ffn_backward_kernel, segs, seg_count), g...  40.5 us
    pallas_call x1, Pallas kernels, cross_whole(): pl.pallas_call(functools.partial(cross_kernel, rows // count), grid=(rows...  39.3 us
    ppermute x43, waiting for transfers between devices, flip(): return lax.ppermute(value, AXES, pairs)  39.2 us
    pallas_call x2, Pallas kernels, attn_backward(): pl.pallas_call(functools.partial(attn_backward_kernel, segs, seg_count, f...  34.7 us
    ppermute x43, starting transfers between devices, flip(): return lax.ppermute(value, AXES, pairs)  30.9 us
    pallas_call x1, Pallas kernels, mid_forward(): pl.pallas_call(mid_forward_kernel, grid=(rows // count,), in_specs=[SMEM,...  28.9 us
    pallas_call x2, Pallas kernels, attn_forward(): pl.pallas_call(functools.partial(attn_forward_kernel, segs, seg_count, fi...  26 us
  transfers between devices with their start and end apart: 65, of which 20 were waited for; matrix products, arithmetic and copies ran while one was open for 12% of the time, Pallas kernels for 33%

profile of v5, /device:TPU:0, one launch (start us, length us, event | category | flops | bytes accessed | tf_op | source)
XLA Modules:
  0.0 474.6 jit_solution(17611782898440483442)
XLA Ops:
  9.0 4.1 collective-permute-start
  17.9 4.7 collective-permute-done
  30.6 3.8 collective-permute-start.5
  38.0 5.1 %collective-permute-done.3 = bf16[5,24,768]{2,1,0:T(8,128)(2,1)S(1)} collective-permute-done((bf16[5,24,768]{2,1,0:T(8,128)(2,1)S(1)}, bf16[5,24,768]{2,1,0:T(8,128)(2,1)S(1)}, u32[]{:S(2)}, u32[]{:S(2)}) %collective-permute-start.3) | collective-permute-done | bytes 184352 | tf_op jit(solution)/shard_map/ppermute | solution.py:878
  48.0 4.6 collective-permute-done.9.rest_4_
  53.3 5.7 %collective-permute-done.7.rest_3_ = bf16[192,768]{1,0:T(8,128)(2,1)} collective-permute-done((bf16[192,768]{1,0:T(8,128)(2,1)S(1)}, bf16[192,768]{1,0:T(8,128)(2,1)}, u32[]{:S(2)}, u32[]{:S(2)}) %collective-permute-start.7) | collective-permute-done | bytes 294944 | tf_op jit(solution)/shard_map/ppermute | solution.py:870
  64.1 13.0 %attn_forward.2 = (bf16[2048,2304]{1,0:T(8,128)(2,1)}, bf16[2048,768]{1,0:T(8,128)(2,1)}) custom-call(s32[3]{0:T(128)} %pad_add_fusion.info, bf16[2048,768]{1,0:T(8,128)(2,1)} %bitcast.319, f32[12,768]{1,0:T(8,128)} %slice.359.vec_ref, bf16[304,768]{1,0:T(8,128)(2,1)} %copy-done.9, bf16[304,768]{1,0:T(8,128)(2,1)} %collective-permute-done.8.rest_1_, ...), custom_call_target="tpu_custom_call" | custom-call | flops 12582912000 | bytes 12582912 | tf_op jit(solution)/shard_map/attn_forward/pallas_call | solution.py:499
  81.2 5.8 %collective-permute-start.25 = (bf16[96,768]{1,0:T(8,128)(2,1)S(1)}, bf16[96,768]{1,0:T(8,128)(2,1)S(1)}, u32[]{:S(2)}, u32[]{:S(2)}) collective-permute-start(bf16[96,768]{1,0:T(8,128)(2,1)S(1)} %copy-done.12), channel_id=1, source_target_pairs={{0,1},{1,2},{2,3},{3,0},{4,5},{5,6},{6,7},{7,4},{8,9},{9,10},{10,1... | collective-permute-start | bytes 442376 | tf_op jit(solution)/shard_map/ppermute | solution.py:878
  90.7 6.7 %collective-permute-done.24 = bf16[96,768]{1,0:T(8,128)(2,1)S(1)} collective-permute-done((bf16[96,768]{1,0:T(8,128)(2,1)S(1)}, bf16[96,768]{1,0:T(8,128)(2,1)S(1)}, u32[]{:S(2)}, u32[]{:S(2)}) %collective-permute-start.24) | collective-permute-done | bytes 147488 | tf_op jit(solution)/shard_map/ppermute | solution.py:878
  99.8 13.0 %attn_forward.3 = (bf16[2048,2304]{1,0:T(8,128)(2,1)}, bf16[2048,768]{1,0:T(8,128)(2,1)}) custom-call(s32[3]{0:T(128)} %pad_add_fusion.info, bf16[2048,768]{1,0:T(8,128)(2,1)} %bitcast.320, f32[12,768]{1,0:T(8,128)} %slice.359.vec_ref, bf16[304,768]{1,0:T(8,128)(2,1)} %copy-done.9, ...), custom_call_target="tpu_custom_call", output_to_operand_aliasing={{0}: (13, {}), {1}: (14, {})} | custom-call | flops 12582912000 | bytes 12582912 | tf_op jit(solution)/shard_map/attn_forward/pallas_call | solution.py:499
  118.5 28.9 %mid_forward.1 = (f32[2048,768]{1,0:T(8,128)}, bf16[2048,768]{1,0:T(8,128)(2,1)}, bf16[2048,3072]{1,0:T(8,128)(2,1)}, bf16[2048,3072]{1,0:T(8,128)(2,1)}) custom-call(s32[3]{0:T(128)} %pad_add_fusion.info, bf16[2048,768]{1,0:T(8,128)(2,1)} %bitcast.321, bf16[2048,768]{1,0:T(8,128)(2,1)} %get-tuple-element.100.mixed_ref, f32[12,768]{1,0:T(8,128)} %slice.359.vec_ref, ...), custom_call_target="tpu_custom_call" | custom-call | flops 25165824000 | bytes 47185920 | tf_op jit(solution)/shard_map/mid_forward/pallas_call | solution.py:516
  148.0 8.3 %collective-permute-done.28.rest_2_.rest_12_ = bf16[384,768]{1,0:T(8,128)(2,1)} collective-permute-done((bf16[384,768]{1,0:T(8,128)(2,1)S(1)}, bf16[384,768]{1,0:T(8,128)(2,1)}, u32[]{:S(2)}, u32[]{:S(2)}) %collective-permute-start.28) | collective-permute-done | bytes 589856 | tf_op jit(solution)/shard_map/ppermute | solution.py:870
  156.3 8.4 %collective-permute-done.27.rest_1_.rest_11_ = bf16[384,768]{1,0:T(8,128)(2,1)} collective-permute-done((bf16[384,768]{1,0:T(8,128)(2,1)S(1)}, bf16[384,768]{1,0:T(8,128)(2,1)}, u32[]{:S(2)}, u32[]{:S(2)}) %collective-permute-start.27) | collective-permute-done | bytes 589856 | tf_op jit(solution)/shard_map/ppermute | solution.py:870
  167.6 19.4 %down_forward.1 = (f32[2048,768]{1,0:T(8,128)}, f32[8,2,768]{2,1,0:T(2,128)}) custom-call(s32[3]{0:T(128)} %pad_add_fusion.info, f32[2048,768]{1,0:T(8,128)} %get-tuple-element.106.sum_ref, bf16[2048,3072]{1,0:T(8,128)(2,1)} %get-tuple-element.107.act_ref.left_ref, f32[12,768]{1,0:T(8,128)} %slice.359.vec_ref, bf16[384,768]{1,0:T(8,128)(2,1)} %copy-done.8, ...), custom_call_target="tpu_custom_call" | custom-call | flops 12582912000 | bytes 25165824 | tf_op jit(solution)/shard_map/down_forward/pallas_call | solution.py:533
  200.3 3.9 collective-permute-done.37
  212.9 39.3 %cross_encoder.1 = (f32[16,768]{1,0:T(8,128)}, f32[16,768]{1,0:T(8,128)}, f32[12,768]{1,0:T(8,128)}, f32[8,768]{1,0:T(8,128)}, f32[24,2304]{1,0:T(8,128)}, /*ind...) custom-call(s32[2]{0:T(128)} %pad_add_fusion.1.info, bf16[512,768]{1,0:T(8,128)(2,1)} %bitcast.287, ...), custom_call_target="tpu_custom_call" | custom-call | flops 23592960000 | bytes 16777216 | tf_op jit(solution)/shard_map/cross_encoder/pallas_call | solution.py:550
  255.2 40.5 %ffn_backward.1 = (bf16[2048,768]{1,0:T(8,128)(2,1)}, bf16[2048,768]{1,0:T(8,128)(2,1)}, bf16[2048,3072]{1,0:T(8,128)(2,1)}, bf16[2048,768]{1,0:T(8,128)(2,1)}, ...) custom-call(s32[3]{0:T(128)} %pad_add_fusion.info, bf16[2048,768]{1,0:T(8,128)(2,1)} %bitcast.318, ...), custom_call_target="tpu_custom_call" | custom-call | flops 44040192000 | bytes 47185920 | tf_op jit(solution)/shard_map/ffn_backward/pallas_call | solution.py:572
  295.6 16.1 %down_weight_grad.1 = (bf16[4,384,768]{2,1,0:T(8,128)(2,1)}, bf16[4,384,768]{2,1,0:T(8,128)(2,1)}) custom-call(s32[3]{0:T(128)} %pad_add_fusion.info, bf16[2048,3072]{1,0:T(8,128)(2,1)} %get-tuple-element.107.act_ref.left_ref, bf16[2048,768]{1,0:T(8,128)(2,1)} %get-tuple-element.124.right_ref), custom_call_target="tpu_custom_call" | custom-call | flops 9663676416 | bytes 12582912 | tf_op jit(solution)/shard_map/down_weight_grad/pallas_call | solution.py:674
  312.2 20.0 %mid_weight_grad.1 = (bf16[4,480,768]{2,1,0:T(8,128)(2,1)}, bf16[4,480,768]{2,1,0:T(8,128)(2,1)}) custom-call(s32[3]{0:T(128)} %pad_add_fusion.info, bf16[2048,768]{1,0:T(8,128)(2,1)} %get-tuple-element.100.mixed_ref, bf16[2048,768]{1,0:T(8,128)(2,1)} %get-tuple-element.121.proj_ref.proj_grad_ref, bf16[2048,768]{1,0:T(8,128)(2,1)} %get-tuple-element.122.low_ref, ...), custom_call_target="tpu_custom_call" | custom-call | flops 12079595520 | bytes 15728640 | tf_op jit(solution)/shard_map/mid_weight_grad/pallas_call | solution.py:647
  337.8 17.6 %attn_backward.2 = (bf16[2048,2304]{1,0:T(8,128)(2,1)}, f32[2,768]{1,0:T(2,128)}) custom-call(s32[3]{0:T(128)} %pad_add_fusion.info, bf16[2048,2304]{1,0:T(8,128)(2,1)} %get-tuple-element.103.packed_ref, bf16[2048,768]{1,0:T(8,128)(2,1)} %get-tuple-element.131.mixed_grad_ref), custom_call_target="tpu_custom_call" | custom-call | flops 15728640000 | bytes 12582912 | tf_op jit(solution)/shard_map/attn_backward/pallas_call | solution.py:594
  367.0 17.1 %attn_backward.3 = (bf16[2048,2304]{1,0:T(8,128)(2,1)}, f32[2,768]{1,0:T(2,128)}) custom-call(s32[3]{0:T(128)} %pad_add_fusion.info, bf16[2048,2304]{1,0:T(8,128)(2,1)} %get-tuple-element.103.packed_ref, bf16[2048,768]{1,0:T(8,128)(2,1)} %get-tuple-element.131.mixed_grad_ref, ...), custom_call_target="tpu_custom_call", output_to_operand_aliasing={{0}: (3, {})} | custom-call | flops 15728640000 | bytes 12582912 | tf_op jit(solution)/shard_map/attn_backward/pallas_call | solution.py:594
  394.0 3.8 collective-permute-start.50
  398.8 13.4 %qkv_weight_grad.1 = (bf16[4,304,768]{2,1,0:T(8,128)(2,1)}, bf16[4,304,768]{2,1,0:T(8,128)(2,1)}) custom-call(s32[3]{0:T(128)} %pad_add_fusion.info, bf16[2048,768]{1,0:T(8,128)(2,1)} %bitcast.322, bf16[2048,2304]{1,0:T(8,128)(2,1)} %get-tuple-element.140.right_ref.packed_grad_ref, bf16[8,16,768]{2,1,0:T(8,128)(2,1)} %copy-done.28), custom_call_target="tpu_custom_call" | custom-call | flops 7247757312 | bytes 9437184 | tf_op jit(solution)/shard_map/qkv_weight_grad/pallas_call | solution.py:630
  435.3 13.4 %token_gradient.1 = bf16[2048,768]{1,0:T(8,128)(2,1)} custom-call(s32[3]{0:T(128)} %pad_add_fusion.info, bf16[2048,2304]{1,0:T(8,128)(2,1)} %get-tuple-element.140.right_ref.packed_grad_ref, bf16[2048,768]{1,0:T(8,128)(2,1)} %get-tuple-element.121.proj_ref.proj_grad_ref, bf16[304,768]{1,0:T(8,128)(2,1)} %copy-done.9, ...), custom_call_target="tpu_custom_call" | custom-call | flops 9437184000 | bytes 15728640 | tf_op jit(solution)/shard_map/token_gradient/pallas_call | solution.py:609
  (364 shorter events, 142.6 us)
Async XLA Ops:
  7.2 204.9 %all-gather.2.cloned.1.call-start = ((), (), s32[]{:S(2)}) async-start(), calls=%async_computation | async-start | bytes 14598144 | tf_op jit(solution)/shard_map/all_gather | solution.py:1099
  23.8 20.3 %collective-permute-start.8 = (bf16[304,768]{1,0:T(8,128)(2,1)S(1)}, bf16[304,768]{1,0:T(8,128)(2,1)}, u32[]{:S(2)}, u32[]{:S(2)}) collective-permute-start(bf16[304,768]{1,0:T(8,128)(2,1)S(1)} %fusion.17.rest_0_), channel_id=1, source_target_pairs={{0,8},{1,9},{2,10},{3,11},{4,12},{5,13},{6,14},{7,15},{8,0},{9,1},... | collective-permute-start | bytes 1400840 | tf_op jit(solution)/shard_map/ppermute | solution.py:870
  60.5 29.2 %collective-permute-start.10 = (bf16[480,768]{1,0:T(8,128)(2,1)S(1)}, bf16[480,768]{1,0:T(8,128)(2,1)}, u32[]{:S(2)}, u32[]{:S(2)}) collective-permute-start(bf16[480,768]{1,0:T(8,128)(2,1)S(1)} %bitcast.289), channel_id=1, source_target_pairs={{0,8},{1,9},{2,10},{3,11},{4,12},{5,13},{6,14},{7,15},{8,0},{9,1},... | collective-permute-start | bytes 2211848 | tf_op jit(solution)/shard_map/ppermute | solution.py:870
  78.0 21.3 %collective-permute-start.17 = (bf16[288,768]{1,0:T(8,128)(2,1)S(1)}, bf16[288,768]{1,0:T(8,128)(2,1)S(1)}, u32[]{:S(2)}, u32[]{:S(2)}) collective-permute-start(bf16[288,768]{1,0:T(8,128)(2,1)S(1)} %slice.360), channel_id=1, source_target_pairs={{0,8},{1,9},{2,10},{3,11},{4,12},{5,13},{6,14},{7,15},{8,0},{9,1},... | collective-permute-start | bytes 1327112 | tf_op jit(solution)/shard_map/ppermute | solution.py:870
  86.9 26.1 %collective-permute-start.26 = (bf16[96,768]{1,0:T(8,128)(2,1)S(1)}, bf16[96,768]{1,0:T(8,128)(2,1)S(1)}, u32[]{:S(2)}, u32[]{:S(2)}) collective-permute-start(bf16[96,768]{1,0:T(8,128)(2,1)S(1)} %copy-done.12), channel_id=1, source_target_pairs={{0,3},{1,0},{2,1},{3,2},{4,7},{5,4},{6,5},{7,6},{8,11},{9,8},{10,9... | collective-permute-start | bytes 442376 | tf_op jit(solution)/shard_map/ppermute | solution.py:878
  89.7 23.9 %collective-permute-start.19 = (bf16[480,768]{1,0:T(8,128)(2,1)S(1)}, bf16[480,768]{1,0:T(8,128)(2,1)}, u32[]{:S(2)}, u32[]{:S(2)}) collective-permute-start(bf16[480,768]{1,0:T(8,128)(2,1)S(1)} %bitcast.290), channel_id=1, source_target_pairs={{0,4},{1,5},{2,6},{3,7},{4,0},{5,1},{6,2},{7,3},{8,12},{9,13},{10,... | collective-permute-start | bytes 2211848 | tf_op jit(solution)/shard_map/ppermute | solution.py:870
  113.6 33.9 %collective-permute-start.29 = (bf16[384,768]{1,0:T(8,128)(2,1)S(1)}, bf16[384,768]{1,0:T(8,128)(2,1)S(1)}, u32[]{:S(2)}, u32[]{:S(2)}) collective-permute-start(bf16[384,768]{1,0:T(8,128)(2,1)S(1)} %pad_maximum_fusion.4.rest_0_.rest_10_), channel_id=1, source_target_pairs={{0,24},{1,25},{2,26},{3,27},{4,28},{5,29},{6,30},{7,31},{8,16},{9,... | collective-permute-start | bytes 1769480 | tf_op jit(solution)/shard_map/ppermute | solution.py:870
  115.7 40.6 %collective-permute-start.28 = (bf16[384,768]{1,0:T(8,128)(2,1)S(1)}, bf16[384,768]{1,0:T(8,128)(2,1)}, u32[]{:S(2)}, u32[]{:S(2)}) collective-permute-start(bf16[384,768]{1,0:T(8,128)(2,1)S(1)} %pad_maximum_fusion.4.rest_0_.rest_10_), channel_id=1, source_target_pairs={{0,16},{1,17},{2,18},{3,19},{4,20},{5,21},{6,22},{7,23},{8,24},{9,... | collective-permute-start | bytes 1769480 | tf_op jit(solution)/shard_map/ppermute | solution.py:870
  116.8 47.8 %collective-permute-start.27 = (bf16[384,768]{1,0:T(8,128)(2,1)S(1)}, bf16[384,768]{1,0:T(8,128)(2,1)}, u32[]{:S(2)}, u32[]{:S(2)}) collective-permute-start(bf16[384,768]{1,0:T(8,128)(2,1)S(1)} %pad_maximum_fusion.4.rest_0_.rest_10_), channel_id=1, source_target_pairs={{0,8},{1,9},{2,10},{3,11},{4,12},{5,13},{6,14},{7,15},{8,0},{9,1},... | collective-permute-start | bytes 1769480 | tf_op jit(solution)/shard_map/ppermute | solution.py:870
  117.7 48.2 %collective-permute-start.30 = (bf16[384,768]{1,0:T(8,128)(2,1)S(1)}, bf16[384,768]{1,0:T(8,128)(2,1)}, u32[]{:S(2)}, u32[]{:S(2)}) collective-permute-start(bf16[384,768]{1,0:T(8,128)(2,1)S(1)} %pad_maximum_fusion.4.rest_0_.rest_10_), channel_id=1, source_target_pairs={{0,4},{1,5},{2,6},{3,7},{4,0},{5,1},{6,2},{7,3},{8,12},{9,13},{10,... | collective-permute-start | bytes 1769480 | tf_op jit(solution)/shard_map/ppermute | solution.py:870
  311.7 20.5 %collective-permute-start.41 = (bf16[4,384,768]{2,1,0:T(8,128)(2,1)}, bf16[4,384,768]{2,1,0:T(8,128)(2,1)}, u32[]{:S(2)}, u32[]{:S(2)}) collective-permute-start(bf16[4,384,768]{2,1,0:T(8,128)(2,1)} %get-tuple-element.128), channel_id=1, source_target_pairs={{0,4},{1,5},{2,6},{3,7},{4,0},{5,1},{6,2},{7,3},{8,12},{9,13},{10,... | collective-permute-start | bytes 7077896 | tf_op jit(solution)/shard_map/ppermute | solution.py:870
  332.2 26.9 %collective-permute-start.44 = (bf16[4,480,768]{2,1,0:T(8,128)(2,1)}, bf16[4,480,768]{2,1,0:T(8,128)(2,1)}, u32[]{:S(2)}, u32[]{:S(2)}) collective-permute-start(bf16[4,480,768]{2,1,0:T(8,128)(2,1)} %get-tuple-element.127), channel_id=1, source_target_pairs={{0,4},{1,5},{2,6},{3,7},{4,0},{5,1},{6,2},{7,3},{8,12},{9,13},{10,... | collective-permute-start | bytes 8847368 | tf_op jit(solution)/shard_map/ppermute | solution.py:870
  335.5 20.0 %collective-permute-start.42 = (bf16[2,96,768]{2,1,0:T(8,128)(2,1)S(1)}, bf16[2,96,768]{2,1,0:T(8,128)(2,1)S(1)}, u32[]{:S(2)}, u32[]{:S(2)}) collective-permute-start(bf16[2,96,768]{2,1,0:T(8,128)(2,1)S(1)} %bitcast.308), channel_id=1, source_target_pairs={{0,8},{1,9},{2,10},{3,11},{4,12},{5,13},{6,14},{7,15},{8,0},{9,1},... | collective-permute-start | bytes 884744 | tf_op jit(solution)/shard_map/ppermute | solution.py:870
  336.7 20.6 %collective-permute-start.43 = (bf16[2,96,768]{2,1,0:T(8,128)(2,1)S(1)}, bf16[2,96,768]{2,1,0:T(8,128)(2,1)S(1)}, u32[]{:S(2)}, u32[]{:S(2)}) collective-permute-start(bf16[2,96,768]{2,1,0:T(8,128)(2,1)S(1)} %bitcast.307), channel_id=1, source_target_pairs={{0,16},{1,17},{2,18},{3,19},{4,20},{5,21},{6,22},{7,23},{8,24},{9,... | collective-permute-start | bytes 884744 | tf_op jit(solution)/shard_map/ppermute | solution.py:870
  356.5 30.6 %collective-permute-start.46 = (bf16[4,96,768]{2,1,0:T(8,128)(2,1)}, bf16[4,96,768]{2,1,0:T(8,128)(2,1)}, u32[]{:S(2)}, u32[]{:S(2)}) collective-permute-start(bf16[4,96,768]{2,1,0:T(8,128)(2,1)} %pad_maximum_fusion.6), channel_id=1, source_target_pairs={{0,16},{1,17},{2,18},{3,19},{4,20},{5,21},{6,22},{7,23},{8,24},{9,... | collective-permute-start | bytes 1769480 | tf_op jit(solution)/shard_map/ppermute | solution.py:870
  358.2 28.9 %collective-permute-start.45 = (bf16[4,96,768]{2,1,0:T(8,128)(2,1)}, bf16[4,96,768]{2,1,0:T(8,128)(2,1)}, u32[]{:S(2)}, u32[]{:S(2)}) collective-permute-start(bf16[4,96,768]{2,1,0:T(8,128)(2,1)} %pad_maximum_fusion.5), channel_id=1, source_target_pairs={{0,8},{1,9},{2,10},{3,11},{4,12},{5,13},{6,14},{7,15},{8,0},{9,1},... | collective-permute-start | bytes 1769480 | tf_op jit(solution)/shard_map/ppermute | solution.py:870
  363.8 25.4 %collective-permute-start.47 = (bf16[2,120,768]{2,1,0:T(8,128)(2,1)}, bf16[2,120,768]{2,1,0:T(8,128)(2,1)}, u32[]{:S(2)}, u32[]{:S(2)}) collective-permute-start(bf16[2,120,768]{2,1,0:T(8,128)(2,1)} %bitcast.75), channel_id=1, source_target_pairs={{0,8},{1,9},{2,10},{3,11},{4,12},{5,13},{6,14},{7,15},{8,0},{9,1},... | collective-permute-start | bytes 1105928 | tf_op jit(solution)/shard_map/ppermute | solution.py:870
  365.8 25.7 %collective-permute-start.48 = (bf16[2,120,768]{2,1,0:T(8,128)(2,1)}, bf16[2,120,768]{2,1,0:T(8,128)(2,1)}, u32[]{:S(2)}, u32[]{:S(2)}) collective-permute-start(bf16[2,120,768]{2,1,0:T(8,128)(2,1)} %bitcast.77), channel_id=1, source_target_pairs={{0,16},{1,17},{2,18},{3,19},{4,20},{5,21},{6,22},{7,23},{8,24},{9,... | collective-permute-start | bytes 1105928 | tf_op jit(solution)/shard_map/ppermute | solution.py:870
  390.5 21.7 %collective-permute-start.53 = (bf16[4,120,768]{2,1,0:T(8,128)(2,1)S(1)}, bf16[4,120,768]{2,1,0:T(8,128)(2,1)}, u32[]{:S(2)}, u32[]{:S(2)}) collective-permute-start(bf16[4,120,768]{2,1,0:T(8,128)(2,1)S(1)} %pad_maximum_fusion.3), channel_id=1, source_target_pairs={{0,16},{1,17},{2,18},{3,19},{4,20},{5,21},{6,22},{7,23},{8,24},{9,... | collective-permute-start | bytes 2211848 | tf_op jit(solution)/shard_map/ppermute | solution.py:870
  426.0 31.7 %collective-permute-start.61 = (bf16[120,768]{1,0:T(8,128)(2,1)}, bf16[120,768]{1,0:T(8,128)(2,1)}, u32[]{:S(2)}, u32[]{:S(2)}) collective-permute-start(bf16[120,768]{1,0:T(8,128)(2,1)} %get-tuple-element.182), channel_id=1, source_target_pairs={{0,1},{1,2},{2,3},{3,0},{4,5},{5,6},{6,7},{7,4},{8,9},{9,10},{10,1... | collective-permute-start | bytes 552968 | tf_op jit(solution)/shard_map/ppermute | solution.py:878
  426.9 32.9 %collective-permute-start.62 = (bf16[120,768]{1,0:T(8,128)(2,1)}, bf16[120,768]{1,0:T(8,128)(2,1)}, u32[]{:S(2)}, u32[]{:S(2)}) collective-permute-start(bf16[120,768]{1,0:T(8,128)(2,1)} %get-tuple-element.184), channel_id=1, source_target_pairs={{0,2},{1,3},{2,0},{3,1},{4,6},{5,7},{6,4},{7,5},{8,10},{9,11},{10,... | collective-permute-start | bytes 552968 | tf_op jit(solution)/shard_map/ppermute | solution.py:878
  428.9 19.8 %collective-permute-start.55 = (bf16[4,80,768]{2,1,0:T(8,128)(2,1)S(1)}, bf16[4,80,768]{2,1,0:T(8,128)(2,1)S(1)}, u32[]{:S(2)}, u32[]{:S(2)}) collective-permute-start(bf16[4,80,768]{2,1,0:T(8,128)(2,1)S(1)} %fusion.14), channel_id=1, source_target_pairs={{0,8},{1,9},{2,10},{3,11},{4,12},{5,13},{6,14},{7,15},{8,0},{9,1},... | collective-permute-start | bytes 1474568 | tf_op jit(solution)/shard_map/ppermute | solution.py:870
  430.1 23.7 %collective-permute-start.56 = (bf16[4,80,768]{2,1,0:T(8,128)(2,1)S(1)}, bf16[4,80,768]{2,1,0:T(8,128)(2,1)S(1)}, u32[]{:S(2)}, u32[]{:S(2)}) collective-permute-start(bf16[4,80,768]{2,1,0:T(8,128)(2,1)S(1)} %fusion.15), channel_id=1, source_target_pairs={{0,16},{1,17},{2,18},{3,19},{4,20},{5,21},{6,22},{7,23},{8,24},{9,... | collective-permute-start | bytes 1474568 | tf_op jit(solution)/shard_map/ppermute | solution.py:870
  432.3 21.5 %collective-permute-start.57 = (bf16[4,80,768]{2,1,0:T(8,128)(2,1)}, bf16[4,80,768]{2,1,0:T(8,128)(2,1)S(1)}, u32[]{:S(2)}, u32[]{:S(2)}) collective-permute-start(bf16[4,80,768]{2,1,0:T(8,128)(2,1)} %fusion.16), channel_id=1, source_target_pairs={{0,24},{1,25},{2,26},{3,27},{4,28},{5,29},{6,30},{7,31},{8,16},{9,... | collective-permute-start | bytes 1474568 | tf_op jit(solution)/shard_map/ppermute | solution.py:870
  (78 other events, 856.7 us)
Sparse Core Ops, SparseCore 0:
  44.3 138.9 all-gather.1

commit v6 on v5

--- a/solution.py
+++ b/solution.py
@@ -333,54 +333,94 @@
     return jnp.sum(value.astype(F32), axis=0, keepdims=True)
 
 
-def ffn_backward_kernel(segs, seg_count, info, cot_ref, heads_grad_ref, heads_ref, second_ref, sum_ref, slope_ref, vec_ref, *rest):
-    pieces, more, rest = rest[:10], rest[10:18], rest[18:]
-    (out_ref, down_grad_ref, hidden_grad_ref, proj_grad_ref, mixed_grad_ref, grads_ref, out, up, down, sems) = rest
-    step = pl.program_id(0)
-
-    @pl.when(step == 0)
-    def _():
-        copies = slab_copies(info[0], more, down_slabs(down), sems, 40)
-        load(copies + slab_copies(info[0], pieces, mid_slabs(out, up), sems))
-        grads_ref[...] = jnp.zeros_like(grads_ref)
-
-    count = segs * SEG
-    normed, inv_scale = normalize(second_ref[...])
-    row = lax.broadcasted_iota(jnp.int32, (SEG, 1), 0)
-    result = normed * (1.0 + vec_ref[10:11, :]) + vec_ref[11:12, :]
-    ups = []
-    for s in range(segs):
-        seg = step * segs + s
-        at = slice(s * SEG, (s + 1) * SEG)
-        live = row + seg % seg_count * SEG < info[1 + seg // seg_count]
-        opens = row == 0
-        merged = jnp.where(opens, heads_ref[s : s + 1, :], result[at])
-        out_ref[at, :] = jnp.where(live, merged, 0.0).astype(LOW)
-        grad = jnp.where(live, cot_ref[at, :].astype(F32), 0.0)
-        ups.append(jnp.where(opens, heads_grad_ref[s : s + 1, :], grad))
-    upstream = jnp.concatenate(ups, axis=0)
-    back_two = normalize_back(upstream * (1.0 + vec_ref[10:11, :]), normed, inv_scale)
+def ffn_back_rows(upstream, second, summed, slope, vec, grads_ref, hidden_grad, out, up, down):
+    normed, inv_scale = normalize(second)
+    back_two = normalize_back(upstream * (1.0 + vec[10:11, :]), normed, inv_scale)
     down_grad = back_two.astype(LOW)
-    down_grad_ref[...] = down_grad
     grads_ref[9:10, :] += column_sum(down_grad)
     grads_ref[10:11, :] += column_sum(upstream * normed)
     grads_ref[11:12, :] += column_sum(upstream)
     total = back_two
     for j in range(4):
         cols = slice(j * 768, (j + 1) * 768)
-        grad = mm_nt(down_grad, down[cols, :]) * slope_ref[:, cols].astype(F32)
-        grad = grad.astype(LOW)
-        hidden_grad_ref[:, cols] = grad
+        grad = (mm_nt(down_grad, down[cols, :]) * slope(cols).astype(F32)).astype(LOW)
+        hidden_grad(cols, grad)
         grads_ref[5 + j : 6 + j, :] += column_sum(grad)
         total = total + mm_nt(grad, up[j])
-    normed, inv_scale = normalize(sum_ref[...])
-    back_one = normalize_back(total * (1.0 + vec_ref[3:4, :]), normed, inv_scale)
+    normed, inv_scale = normalize(summed)
+    back_one = normalize_back(total * (1.0 + vec[3:4, :]), normed, inv_scale)
     proj_grad = back_one.astype(LOW)
-    proj_grad_ref[...] = proj_grad
-    mixed_grad_ref[...] = mm_nt(proj_grad, out[...]).astype(LOW)
     grads_ref[2:3, :] += column_sum(proj_grad)
     grads_ref[3:4, :] += column_sum(total * normed)
     grads_ref[4:5, :] += column_sum(total)
+    return down_grad, proj_grad, mm_nt(proj_grad, out[...]).astype(LOW)
+
+
+def load_ffn(place, mid, rest, out, up, down, sems):
+    return slab_copies(place, rest, down_slabs(down), sems, 40) + slab_copies(place, mid, mid_slabs(out, up), sems)
+
+
+def ffn_backward_kernel(segs, seg_count, first_step, info, cot_ref, second_ref, sum_ref, slope_ref, vec_ref, *rest):
+    mid, more, rest = rest[:10], rest[10:18], rest[-10:]
+    out_ref, down_grad_ref, hidden_grad_ref, proj_grad_ref, mixed_grad_ref, grads_ref, out, up, down, sems = rest
+    step = pl.program_id(0)
+
+    @pl.when(step == 0)
+    def _():
+        load(load_ffn(info[0], mid, more, out, up, down, sems))
+        grads_ref[...] = jnp.zeros_like(grads_ref)
+
+    second = second_ref[...]
+    normed, _ = normalize(second)
+    result = normed * (1.0 + vec_ref[10:11, :]) + vec_ref[11:12, :]
+    row = lax.broadcasted_iota(jnp.int32, (SEG, 1), 0)
+    ups = []
+    for s in range(segs):
+        seg = (step + first_step) * segs + s
+        at = slice(s * SEG, (s + 1) * SEG)
+        live = row + seg % seg_count * SEG < info[1 + seg // seg_count]
+        out_ref[at, :] = jnp.where(live, result[at], 0.0).astype(LOW)
+        ups.append(jnp.where(live & (row > 0), cot_ref[at, :].astype(F32), 0.0))
+
+    def store(cols, grad):
+        hidden_grad_ref[:, cols] = grad
+
+    down_grad_ref[...], proj_grad_ref[...], mixed_grad_ref[...] = ffn_back_rows(
+        jnp.concatenate(ups, axis=0), second, sum_ref[...], lambda cols: slope_ref[:, cols], vec_ref, grads_ref, store,
+        out, up, down,
+    )
+
+
+def opening_kernel(segs, seg_count, info, heads_ref, heads_grad_ref, vec_ref, *rest):
+    tops_in, sources, mid, more, rest = rest[:5], rest[5:8], rest[8:18], rest[18:26], rest[26:]
+    tops_out, grads_ref, tops, parts, hidden = rest[:5], rest[5], rest[6:11], rest[11:14], rest[14]
+    out, up, down, sems, top_sems = rest[15:]
+    copies = load_ffn(info[0], mid, more, out, up, down, sems)
+    for i, (source, target) in enumerate(zip((*tops_in, *sources), (*tops, *parts))):
+        copies.append(pltpu.make_async_copy(source.at[:, 0 : target.shape[1], :], target, top_sems.at[i]))
+    load(copies)
+    grads_ref[...] = jnp.zeros_like(grads_ref)
+    second, summed, slope = (part[:, 0, :] if part.shape[1] == 8 else part for part in parts)
+    slope = slope[...].astype(F32)[:, 0, :]
+
+    def store(cols, grad):
+        hidden[:, cols] = grad.astype(F32)
+
+    down_grad, proj_grad, mixed_grad = ffn_back_rows(
+        heads_grad_ref[...], second, summed, lambda cols: slope[:, cols], vec_ref, grads_ref, store, out, up, down
+    )
+    seg = lax.broadcasted_iota(jnp.int32, (segs, 1), 0)
+    length = jnp.full((segs, 1), info[1], jnp.int32)
+    for i in range(1, segs // seg_count):
+        length = jnp.where(seg >= i * seg_count, info[1 + i], length)
+    merged = jnp.where(lax.rem(seg, seg_count) * SEG < length, heads_ref[...], 0.0)
+    outs = []
+    values = (merged, down_grad.astype(F32), hidden[...], proj_grad.astype(F32), mixed_grad.astype(F32))
+    for i, (value, top) in enumerate(zip(values, tops)):
+        row = lax.broadcasted_iota(jnp.int32, top.shape, 1)
+        top[...] = jnp.where(row == 0, value[:, None, :], top[...].astype(F32)).astype(LOW)
+        outs.append(pltpu.make_async_copy(top, tops_out[i].at[:, 0:16, :], top_sems.at[i]))
+    load(outs)
 
 
 def attn_backward_kernel(segs, seg_count, first_step, info, packed_ref, mixed_grad_ref, *rest):
@@ -565,24 +605,52 @@
     )(info, heads, upstream, live, vec, positions, wide)
 
 
-def ffn_backward(info, cotangent, heads_grad, heads, second, summed, slope, vec, mid, down, seg_count, segs=2):
+def ffn_backward(info, cotangent, second, summed, slope, vec, mid, down, seg_count, half, before=None, segs=2):
     rows = summed.shape[0]
     count = segs * SEG
-    few = pl.BlockSpec((None, segs, 768), lambda i: (i, 0, 0))
+    steps = rows // count // 2
+    first = half * steps
+    before = list(before or [])
+    widths = (768, 768, 3072, 768, 768)
     return pl.pallas_call(
-        functools.partial(ffn_backward_kernel, segs, seg_count),
-        grid=(rows // count,),
-        in_specs=[SMEM, block_rows(count, 768), few, few, block_rows(count, 768), block_rows(count, 768),
-                  block_rows(count, 3072), fixed((12, 768))] + [ANY] * 18,
-        out_specs=[block_rows(count, 768), block_rows(count, 768), block_rows(count, 3072), block_rows(count, 768),
-                   block_rows(count, 768), fixed((12, 768))],
-        out_shape=[shape_of((rows, 768)), shape_of((rows, 768)), shape_of((rows, 3072)), shape_of((rows, 768)),
-                   shape_of((rows, 768)), shape_of((12, 768), F32)],
+        functools.partial(ffn_backward_kernel, segs, seg_count, first),
+        grid=(steps,),
+        in_specs=[SMEM, shifted(count, 768, first), shifted(count, 768, first), shifted(count, 768, first),
+                  shifted(count, 3072, first), fixed((12, 768))] + [ANY] * (18 + len(before)),
+        out_specs=[shifted(count, w, first) for w in widths] + [fixed((12, 768))],
+        out_shape=[shape_of((rows, w)) for w in widths] + [shape_of((12, 768), F32)],
         scratch_shapes=MID + DOWN + sems(72),
+        input_output_aliases={24 + i: i for i in range(5)} if before else {},
         compiler_params=params(),
-        cost_estimate=cost(2 * rows * 768 * 14000, rows * 768 * 30),
+        cost_estimate=cost(rows * 768 * 14000, rows * 768 * 15),
         name="ffn_backward",
-    )(info, cotangent, heads_grad.reshape(-1, segs, 768), heads.reshape(-1, segs, 768), second, summed, slope, vec, *mid, *down)
+    )(info, cotangent, second, summed, slope, vec, *mid, *down, *before)
+
+
+def opening_backward(info, heads, heads_grad, vec, arrays, sources, mid, down, seg_count):
+    segs = heads.shape[0]
+
+    def grouped(array):
+        return array.reshape(segs, SEG, array.shape[1])
+
+    arrays, sources = [grouped(a) for a in arrays], [grouped(a) for a in sources]
+    whole = fixed((segs, 768))
+    *done, grads = pl.pallas_call(
+        functools.partial(opening_kernel, segs, seg_count),
+        grid=(1,),
+        in_specs=[SMEM, whole, whole, fixed((12, 768))] + [ANY] * 26,
+        out_specs=[ANY] * 5 + [fixed((12, 768))],
+        out_shape=[shape_of(a.shape) for a in arrays] + [shape_of((12, 768), F32)],
+        scratch_shapes=[pltpu.VMEM((segs, 16, a.shape[2]), LOW) for a in arrays]
+        + [pltpu.VMEM((segs, 8, 768), F32)] * 2
+        + [pltpu.VMEM((segs, 16, 3072), LOW), pltpu.VMEM((segs, 3072), F32)]
+        + MID + DOWN + sems(72) + sems(8),
+        input_output_aliases={4 + i: i for i in range(5)},
+        compiler_params=params(),
+        cost_estimate=cost(2**33, 2**24),
+        name="opening_backward",
+    )(info, heads, heads_grad, vec, *arrays, *sources, *mid, *down)
+    return [a.reshape(-1, a.shape[2]) for a in done], grads
 
 
 def attn_backward(info, packed, mixed_grad, seg_count, half, before=None, segs=2):
@@ -893,8 +961,8 @@
     def spread_far(self, by_x, by_y, half):
         return self.flip(by_y[:half], 2), self.flip(by_x[half:], 4)
 
-    def spread_core(self, mine):
-        return list(mine) + [self.flip(piece, 1) for piece in mine]
+    def core(self, pieces):
+        return [self.flip(piece, 1) for piece in pieces]
 
     def in_order(self, parts):
         for axis, mask in ((4, 4), (2, 2), (1, 1)):
@@ -902,13 +970,17 @@
             parts = [jnp.where(odd, parts[m ^ mask], parts[m]) for m in range(8)]
         return jnp.stack(parts)
 
-    def gather_small(self, shard):
+    def gather_small(self, shard, line_only=False):
         block = jnp.stack(self.gather_z(shard))
-        near = [block] + [self.flip(block, m) for m in (2, 4, 6)]
-        plane = jnp.stack(near)
+        return block if line_only else self.gather_core(self.gather_plane(block))
+
+    def gather_plane(self, block):
+        return jnp.stack([block] + [self.flip(block, m) for m in (2, 4, 6)])
+
+    def gather_core(self, plane):
         other = self.flip(plane, 1)
         whole = self.in_order([(plane, other)[m % 2][m // 2] for m in range(8)])
-        return whole.reshape((-1,) + shard.shape)
+        return whole.reshape((-1,) + plane.shape[2:])
 
 
 class PlainLinks:
@@ -918,7 +990,7 @@
         self.z = lax.axis_index("fsdp")
         self.place = 0
 
-    def gather_small(self, shard):
+    def gather_small(self, shard, line_only=False):
         return lax.all_gather(shard, AXES, axis=0)
 
 
@@ -1076,19 +1148,18 @@
     if fast:
         first = jnp.concatenate([slabs_of(seg_qkv).reshape(-1, 768), jnp.pad(small, ((0, 7), (0, 0)))])
         line_first = links.gather_z(first)
-        line_mid = links.gather_z(after(mid_shard, *line_first))
-        line_down = links.gather_z(after(seg_down, *line_mid))
+        line_rest = jnp.concatenate([mid_shard, seg_down.reshape(4, -1, feat_dim)])
+        line_rest = links.gather_z(after(line_rest, *line_first))
         weights = jnp.stack([p[:72].reshape(3, 24, 768) for p in line_first], axis=1).reshape(-1, 768)
         rows = jnp.concatenate([p[72:73] for p in line_first])
         block = jnp.concatenate([weights, jnp.pad(rows, ((0, 12), (0, 0)))])
         near = links.spread_near(block)
-        wide = after(wide, *line_mid, *near)
-        far = links.spread_far(*(after(p, *line_mid) for p in near), 192)
-        first = links.spread_core([block, *near, *far])
+        far = links.spread_far(*near, 192)
+        first = [block, *near, *far, *links.core([after(p, *far, *line_rest) for p in (block, *near, *far)])]
         ends = [p[288:292] for p in first[:3]] + [first[4][96:100]]
         others = [p[288:292] for p in first[5:8]] + [first[9][96:100]]
         small = links.in_order([(ends, others)[m % 2][m // 2] for m in range(8)])
-        block = after(jnp.stack(line_mid, axis=1).reshape(-1, 768), *far)
+        block = after(jnp.stack([p[:5] for p in line_rest], axis=1).reshape(-1, 768), *far)
         mid = [block, *links.spread_near(block)]
     else:
         first = plain_pieces(lax.all_gather(slabs_of(seg_qkv), AXES, axis=1, tiled=True), False)
@@ -1096,7 +1167,6 @@
         down_whole = lax.all_gather(seg_down, AXES, axis=0, tiled=True)
         down = [down_whole[m * 384 : (m + 1) * 384] for m in (0, 2, 4, 6, 1, 3, 5, 7)]
         small = links.gather_small(small)
-    wide = lax.all_gather(wide, AXES, axis=1, tiled=True)
     small = small.reshape(devices, -1, width).transpose(1, 0, 2).reshape(-1, feat_dim).astype(F32)
     seg_v, cross_v = small[:seg_rows], small[seg_rows : seg_rows + cross_rows]
     pos_table = small[seg_rows + cross_rows :]
@@ -1104,6 +1174,7 @@
     cross_v = cross_v.at[hidden_rows].set(mix_columns(cross_v[hidden_rows].reshape(1, -1), devices).reshape(-1, feat_dim))
 
     before = attn_forward(info, rows_in, seg_v, first, seg_count, 0)
+    wide = lax.all_gather(after(wide, before[0], *(mid[1:] if fast else ())), AXES, axis=1, tiled=True)
     if fast:
         far = links.spread_far(*(after(p, before[0]) for p in mid[1:]), 288)
         rows_late = after(rows_in, *mid[1:])
@@ -1111,15 +1182,23 @@
         rows_late = rows_in
     packed, mixed = attn_forward(info, rows_late, seg_v, first, seg_count, 1, before)
     if fast:
-        mid = [*mid, *far] + links.spread_core(mid)[3:] + [links.flip(after(p, packed), 1) for p in far]
-        block = after(jnp.concatenate(line_down), *far)
+        late = links.core([after(p, packed, *far) for p in (*mid, *far)])
+        mid = [*mid, *far, *late]
+        block = after(jnp.concatenate([p[5:] for p in line_rest]).reshape(-1, feat_dim), *late)
         near = [links.flip(block, m) for m in (2, 4, 6)]
     summed, low, act, slope = mid_forward(info, rows_in, mixed, seg_v, mid)
     if fast:
         down = [block, *near, links.flip(block, 1), *(links.flip(after(p, act), 1) for p in near)]
     second, heads = down_forward(info, summed, act, seg_v, down)
     heads_own = heads.reshape(-1, feat_dim)
-    both = links.gather_small(jnp.stack([heads_own.astype(LOW), up_own]))
+    both = links.gather_small(jnp.stack([heads_own.astype(LOW), up_own]), True)
+    back = functools.partial(ffn_backward, info, seg_count=seg_count)
+    args = (second, summed, slope, seg_v, mid, down)
+    if fast:
+        first_half = back(cot_rows, *args, half=0)
+        both = links.gather_plane(after(both, first_half[1]))
+        *arrays, grads_two = back(after(cot_rows, first_half[1]), *args, half=1, before=first_half[:5])
+        both = links.gather_core(after(both, arrays[1]))
     heads_all, up_all = both[:, 0].reshape(-1, feat_dim), both[:, 1].reshape(-1, feat_dim)
     live_all = seg_starts[None, :] < lengths[:, None]
     if fast:
@@ -1145,16 +1224,14 @@
         own = seq_local * seg_count
         cross_own = lax.dynamic_slice_in_dim(cross_result, me * own, own)
         heads_grad = lax.dynamic_slice_in_dim(all_grad, me * own, own)
-    cross_grads[2] = unmix_columns(cross_grads[2], devices)
-    vec_grad = vec_grad.at[hidden_rows].set(
-        unmix_columns(vec_grad[hidden_rows].reshape(1, -1), devices).reshape(-1, feat_dim)
-    )
-    cross_vec_grad = lax.dynamic_slice_in_dim(vec_grad, me * width, width, 1)
-    grad_positions = lax.dynamic_slice_in_dim(pos_grad, me * width, width, 1)
-
-    layer_out, down_grad, hidden_grad, proj_grad, mixed_grad, grads_two = ffn_backward(
-        info, cot_rows, heads_grad, cross_own, second, summed, slope, seg_v, mid, down, seg_count
-    )
+        first_half = back(after(cot_rows, heads_grad, *cross_grads), *args, half=0)
+        *arrays, grads_two = back(cot_rows, *args, half=1, before=first_half[:5])
+    grads_two = grads_two + first_half[5]
+    arrays, grads_more = opening_backward(
+        info, cross_own, heads_grad, seg_v, arrays, (second, summed, slope), mid, down, seg_count
+    )
+    layer_out, down_grad, hidden_grad, proj_grad, mixed_grad = arrays
+    grads_two = grads_two + grads_more
     down_sum = summing(links, *down_weight_grad(info, act, down_grad), 1)
     mid_parts = mid_weight_grad(info, mixed, proj_grad, low, after(hidden_grad, down_sum.keep if fast else down_sum.came))
     mid_sum = summing(links, *mid_parts, 5)
@@ -1178,6 +1255,12 @@
     qkv_sum.direct()
     mid_sum.turn()
     qkv_sum.turn(token_grad)
+    cross_grads[2] = unmix_columns(after(cross_grads[2], token_grad), devices)
+    vec_grad = vec_grad.at[hidden_rows].set(
+        unmix_columns(after(vec_grad[hidden_rows], token_grad).reshape(1, -1), devices).reshape(-1, feat_dim)
+    )
+    cross_vec_grad = lax.dynamic_slice_in_dim(vec_grad, me * width, width, 1)
+    grad_positions = lax.dynamic_slice_in_dim(pos_grad, me * width, width, 1)
     grad_down = down_sum.total()
     grad_mid = mid_sum.total().reshape(5, -1, feat_dim)
     total = qkv_sum.total()

time: 483 us -> 469 us (0.971)
  waiting for transfers between devices: 63.5 us -> 32.5 us
  Pallas kernels: 252 us -> 274 us
  starting transfers between devices: 78.1 us -> 68.2 us
    ppermute x43, waiting for transfers between devices: 39.2 us -> 14.4 us  [flip(): return lax.ppermute(value, AXES, pairs)]
    pallas_call x1 -> x3, Pallas kernels: 40.5 us -> 61.4 us  [the longest x2 48.1 us: ffn_backward(): pl.pallas_call(functools.partial(ffn_backward_kernel, segs, seg_count, fi...]
    ppermute x21 -> x18, starting transfers between devices: 47.1 us -> 38.4 us  [turn(): return lax.ppermute(value, AXES, pairs)]
    ppermute x21 -> x18, waiting for transfers between devices: 24.3 us -> 18.1 us  [turn(): return lax.ppermute(value, AXES, pairs)]
  transfers between devices with their start and end apart: 65 -> 62, of which waited for: 20 -> 13; matrix products, arithmetic and copies ran while one was open for 12% -> 14% of each run, Pallas kernels for 33% -> 44%
where the time goes in v6:
time: 469 us; the launch traced here: 462 us
  Pallas kernels  274 us (58%)
  starting transfers between devices  68.2 us (15%)
  local copies, waits for them, and re-layouts  40.4 us (9%)
  waiting for transfers between devices  32.5 us (7%)
  other arithmetic  31.7 us (7%)
  between operations  15.8 us (3%)
    pallas_call x2, Pallas kernels, ffn_backward(): pl.pallas_call(functools.partial(ffn_backward_kernel, segs, seg_count, fi...  48.1 us
    pallas_call x1, Pallas kernels, cross_whole(): pl.pallas_call(functools.partial(cross_kernel, rows // count), grid=(rows...  39.4 us
    ppermute x18, starting transfers between devices, turn(): return lax.ppermute(value, AXES, pairs)  38.4 us
    pallas_call x2, Pallas kernels, attn_backward(): pl.pallas_call(functools.partial(attn_backward_kernel, segs, seg_count, f...  34.7 us
    ppermute x43, starting transfers between devices, flip(): return lax.ppermute(value, AXES, pairs)  29.8 us
    pallas_call x1, Pallas kernels, mid_forward(): pl.pallas_call(mid_forward_kernel, grid=(rows // count,), in_specs=[SMEM,...  29 us
    pallas_call x2, Pallas kernels, attn_forward(): pl.pallas_call(functools.partial(attn_forward_kernel, segs, seg_count, fi...  26.1 us
    pallas_call x1, Pallas kernels, down_forward(): pl.pallas_call(functools.partial(down_forward_kernel, segs), grid=(rows /...  20.2 us
  transfers between devices with their start and end apart: 62, of which 13 were waited for; matrix products, arithmetic and copies ran while one was open for 14% of the time, Pallas kernels for 44%

profile of v6, /device:TPU:0, one launch (start us, length us, event | category | flops | bytes accessed | tf_op | source)
XLA Modules:
  0.0 462.2 jit_solution(14772118150040092702)
XLA Ops:
  9.0 4.1 collective-permute-start
  17.0 5.6 %collective-permute-done = bf16[80,768]{1,0:T(8,128)(2,1)S(1)} collective-permute-done((bf16[80,768]{1,0:T(8,128)(2,1)S(1)}, bf16[80,768]{1,0:T(8,128)(2,1)S(1)}, u32[]{:S(2)}, u32[]{:S(2)}) %collective-permute-start) | collective-permute-done | bytes 122912 | tf_op jit(solution)/shard_map/ppermute | solution.py:946
  27.7 3.7 collective-permute-start.3
  31.4 3.8 collective-permute-start.5
  42.5 10.8 %collective-permute-done.3 = bf16[9,24,768]{2,1,0:T(8,128)(2,1)S(1)} collective-permute-done((bf16[9,24,768]{2,1,0:T(8,128)(2,1)S(1)}, bf16[9,24,768]{2,1,0:T(8,128)(2,1)S(1)}, u32[]{:S(2)}, u32[]{:S(2)}) %collective-permute-start.3) | collective-permute-done | bytes 331808 | tf_op jit(solution)/shard_map/ppermute | solution.py:946
  63.5 13.2 %attn_forward.2 = (bf16[2048,2304]{1,0:T(8,128)(2,1)}, bf16[2048,768]{1,0:T(8,128)(2,1)}) custom-call(s32[3]{0:T(128)} %pad_add_fusion.info, bf16[2048,768]{1,0:T(8,128)(2,1)} %bitcast.309, f32[12,768]{1,0:T(8,128)} %slice.399.vec_ref, bf16[304,768]{1,0:T(8,128)(2,1)} %fusion.17.rest_0_, bf16[304,768]{1,0:T(8,128)(2,1)} %collective-permute-done.8.rest_1_, ...), custom_call_target="tpu_custom_call" | custom-call | flops 12582912000 | bytes 12582912 | tf_op jit(solution)/shard_map/attn_forward/pallas_call | solution.py:539
  79.6 13.0 %attn_forward.3 = (bf16[2048,2304]{1,0:T(8,128)(2,1)}, bf16[2048,768]{1,0:T(8,128)(2,1)}) custom-call(s32[3]{0:T(128)} %pad_add_fusion.info, bf16[2048,768]{1,0:T(8,128)(2,1)} %bitcast.310, f32[12,768]{1,0:T(8,128)} %slice.399.vec_ref, bf16[304,768]{1,0:T(8,128)(2,1)} %fusion.17.rest_0_, ...), custom_call_target="tpu_custom_call", output_to_operand_aliasing={{0}: (13, {}), {1}: (14, {})} | custom-call | flops 12582912000 | bytes 12582912 | tf_op jit(solution)/shard_map/attn_forward/pallas_call | solution.py:539
  101.6 29.0 %mid_forward.1 = (f32[2048,768]{1,0:T(8,128)}, bf16[2048,768]{1,0:T(8,128)(2,1)}, bf16[2048,3072]{1,0:T(8,128)(2,1)}, bf16[2048,3072]{1,0:T(8,128)(2,1)}) custom-call(s32[3]{0:T(128)} %pad_add_fusion.info, bf16[2048,768]{1,0:T(8,128)(2,1)} %bitcast.311, bf16[2048,768]{1,0:T(8,128)(2,1)} %get-tuple-element.125.mixed_ref, f32[12,768]{1,0:T(8,128)} %slice.399.vec_ref, ...), custom_call_target="tpu_custom_call" | custom-call | flops 25165824000 | bytes 47185920 | tf_op jit(solution)/shard_map/mid_forward/pallas_call | solution.py:556
  133.4 5.3 %collective-permute-done.24.rest_1_.rest_11_.rest_19_ = bf16[384,768]{1,0:T(8,128)(2,1)S(1)} collective-permute-done((bf16[384,768]{1,0:T(8,128)(2,1)S(1)}, bf16[384,768]{1,0:T(8,128)(2,1)S(1)}, u32[]{:S(2)}, u32[]{:S(2)}) %collective-permute-start.24) | collective-permute-done | bytes 589856 | tf_op jit(solution)/shard_map/ppermute | solution.py:938
  140.9 20.2 %down_forward.1 = (f32[2048,768]{1,0:T(8,128)}, f32[8,2,768]{2,1,0:T(2,128)}) custom-call(s32[3]{0:T(128)} %pad_add_fusion.info, f32[2048,768]{1,0:T(8,128)} %get-tuple-element.134.sum_ref, bf16[2048,3072]{1,0:T(8,128)(2,1)} %get-tuple-element.135.act_ref.left_ref, f32[12,768]{1,0:T(8,128)} %slice.399.vec_ref, bf16[384,768]{1,0:T(8,128)(2,1)} %bitcast.253, ...), custom_call_target="tpu_custom_call" | custom-call | flops 12582912000 | bytes 25165824 | tf_op jit(solution)/shard_map/down_forward/pallas_call | solution.py:573
  162.0 5.8 %collective-permute-start.31 = (bf16[2,16,768]{2,1,0:T(8,128)(2,1)S(1)}, bf16[2,16,768]{2,1,0:T(8,128)(2,1)S(1)}, u32[]{:S(2)}, u32[]{:S(2)}) collective-permute-start(bf16[2,16,768]{2,1,0:T(8,128)(2,1)S(1)} %pad_maximum_fusion.11), channel_id=1, source_target_pairs={{0,2},{1,3},{2,0},{3,1},{4,6},{5,7},{6,4},{7,5},{8,10},{9,11},{10,... | collective-permute-start | bytes 147464 | tf_op jit(solution)/shard_map/ppermute | solution.py:946
  169.0 2.6 collective-permute-start.33
  171.6 24.1 %ffn_backward.2 = (bf16[2048,768]{1,0:T(8,128)(2,1)}, bf16[2048,768]{1,0:T(8,128)(2,1)}, bf16[2048,3072]{1,0:T(8,128)(2,1)}, bf16[2048,768]{1,0:T(8,128)(2,1)}, ...) custom-call(s32[3]{0:T(128)} %pad_add_fusion.info, bf16[2048,768]{1,0:T(8,128)(2,1)} %bitcast.307, ...), custom_call_target="tpu_custom_call" | custom-call | flops 22020096000 | bytes 23592960 | tf_op jit(solution)/shard_map/ffn_backward/pallas_call | solution.py:615
  199.4 24.0 %ffn_backward.3 = (bf16[2048,768]{1,0:T(8,128)(2,1)}, bf16[2048,768]{1,0:T(8,128)(2,1)}, bf16[2048,3072]{1,0:T(8,128)(2,1)}, bf16[2048,768]{1,0:T(8,128)(2,1)}, ...) custom-call(s32[3]{0:T(128)} %pad_add_fusion.info, ...), custom_call_target="tpu_custom_call", output_to_operand_aliasing={{0}: (24, {}), {1}: (25, {}), {2}: (26, {}), {3}: (27, {}),... | custom-call | flops 22020096000 | bytes 23592960 | tf_op jit(solution)/shard_map/ffn_backward/pallas_call | solution.py:615
  229.5 39.4 %cross_encoder.1 = (f32[16,768]{1,0:T(8,128)}, f32[16,768]{1,0:T(8,128)}, f32[12,768]{1,0:T(8,128)}, f32[8,768]{1,0:T(8,128)}, f32[24,2304]{1,0:T(8,128)}, /*ind...) custom-call(s32[2]{0:T(128)} %pad_add_fusion.1.info, bf16[512,768]{1,0:T(8,128)(2,1)} %bitcast.282, ...), custom_call_target="tpu_custom_call" | custom-call | flops 23592960000 | bytes 16777216 | tf_op jit(solution)/shard_map/cross_encoder/pallas_call | solution.py:590
  268.8 13.3 %opening_backward.1 = (bf16[16,128,768]{2,1,0:T(8,128)(2,1)}, bf16[16,128,768]{2,1,0:T(8,128)(2,1)}, bf16[16,128,3072]{2,1,0:T(8,128)(2,1)}, bf16[16,128,768]{2,...) custom-call(s32[3]{0:T(128)} %pad_add_fusion.info, ...), custom_call_target="tpu_custom_call", output_to_operand_aliasing={{0}: (4, {}), {1}: (5, {}), {2}: (6, {}), {3}: (7, {}), {4}... | custom-call | flops 8589934592 | bytes 16777216 | tf_op jit(solution)/shard_map/opening_backward/pallas_call | solution.py:638
  282.2 16.1 %down_weight_grad.1 = (bf16[4,384,768]{2,1,0:T(8,128)(2,1)}, bf16[4,384,768]{2,1,0:T(8,128)(2,1)}) custom-call(s32[3]{0:T(128)} %pad_add_fusion.info, bf16[2048,3072]{1,0:T(8,128)(2,1)} %get-tuple-element.135.act_ref.left_ref, bf16[2048,768]{1,0:T(8,128)(2,1)} %bitcast.229), custom_call_target="tpu_custom_call" | custom-call | flops 9663676416 | bytes 12582912 | tf_op jit(solution)/shard_map/down_weight_grad/pallas_call | solution.py:742
  298.8 19.9 %mid_weight_grad.1 = (bf16[4,480,768]{2,1,0:T(8,128)(2,1)}, bf16[4,480,768]{2,1,0:T(8,128)(2,1)}) custom-call(s32[3]{0:T(128)} %pad_add_fusion.info, bf16[2048,768]{1,0:T(8,128)(2,1)} %get-tuple-element.125.mixed_ref, bf16[2048,768]{1,0:T(8,128)(2,1)} %bitcast.231, bf16[2048,768]{1,0:T(8,128)(2,1)} %get-tuple-element.162.low_ref, bf16[2048,3072]{1,0:T(8,128)(2,1)} %bitcast.218), custom_call_target="tpu_custom_call" | custom-call | flops 12079595520 | bytes 15728640 | tf_op jit(solution)/shard_map/mid_weight_grad/pallas_call | solution.py:715
  319.3 2.8 convert_add_fusion.1
  325.8 17.5 %attn_backward.2 = (bf16[2048,2304]{1,0:T(8,128)(2,1)}, f32[2,768]{1,0:T(2,128)}) custom-call(s32[3]{0:T(128)} %pad_add_fusion.info, bf16[2048,2304]{1,0:T(8,128)(2,1)} %get-tuple-element.128.packed_ref, bf16[2048,768]{1,0:T(8,128)(2,1)} %bitcast.234), custom_call_target="tpu_custom_call" | custom-call | flops 15728640000 | bytes 12582912 | tf_op jit(solution)/shard_map/attn_backward/pallas_call | solution.py:662
  355.4 17.2 %attn_backward.3 = (bf16[2048,2304]{1,0:T(8,128)(2,1)}, f32[2,768]{1,0:T(2,128)}) custom-call(s32[3]{0:T(128)} %pad_add_fusion.info, bf16[2048,2304]{1,0:T(8,128)(2,1)} %get-tuple-element.128.packed_ref, bf16[2048,768]{1,0:T(8,128)(2,1)} %bitcast.235, bf16[2048,2304]{1,0:T(8,128)(2,1)} %get-tuple-element.170.rest_0_), custom_call_target="tpu_custom_call", output_to_operand_aliasing={{0}: (3, {})} | custom-call | flops 15728640000 | bytes 12582912 | tf_op jit(solution)/shard_map/attn_backward/pallas_call | solution.py:662
  387.9 13.4 %qkv_weight_grad.1 = (bf16[4,304,768]{2,1,0:T(8,128)(2,1)}, bf16[4,304,768]{2,1,0:T(8,128)(2,1)}) custom-call(s32[3]{0:T(128)} %pad_add_fusion.info, bf16[2048,768]{1,0:T(8,128)(2,1)} %bitcast.312, bf16[2048,2304]{1,0:T(8,128)(2,1)} %get-tuple-element.182.right_ref.packed_grad_ref, bf16[8,16,768]{2,1,0:T(8,128)(2,1)} %copy-done.36), custom_call_target="tpu_custom_call" | custom-call | flops 7247757312 | bytes 9437184 | tf_op jit(solution)/shard_map/qkv_weight_grad/pallas_call | solution.py:698
  417.4 13.4 %token_gradient.1 = bf16[2048,768]{1,0:T(8,128)(2,1)} custom-call(s32[3]{0:T(128)} %pad_add_fusion.info, bf16[2048,2304]{1,0:T(8,128)(2,1)} %get-tuple-element.182.right_ref.packed_grad_ref, bf16[2048,768]{1,0:T(8,128)(2,1)} %bitcast.232, bf16[304,768]{1,0:T(8,128)(2,1)} %fusion.17.rest_0_, bf16[304,768]{1,0:T(8,128)(2,1)} %collective-permute-done.8.rest_1_, ...), custom_call_target="tpu_custom_call" | custom-call | flops 9437184000 | bytes 15728640 | tf_op jit(solution)/shard_map/token_gradient/pallas_call | solution.py:677
  430.9 3.0 collective-permute-start.60
  (379 shorter events, 125.3 us)
Async XLA Ops:
  7.2 221.5 %all-gather.2.cloned.1.call-start = ((), (), s32[]{:S(2)}) async-start(), calls=%async_computation | async-start | bytes 14598144 | tf_op jit(solution)/shard_map/all_gather | solution.py:1177
  27.7 25.6 %collective-permute-start.3 = (bf16[9,24,768]{2,1,0:T(8,128)(2,1)S(1)}, bf16[9,24,768]{2,1,0:T(8,128)(2,1)S(1)}, u32[]{:S(2)}, u32[]{:S(2)}) collective-permute-start(bf16[9,24,768]{2,1,0:T(8,128)(2,1)S(1)} %pad_maximum_fusion.9), channel_id=1, source_target_pairs={{0,2},{1,3},{2,0},{3,1},{4,6},{5,7},{6,4},{7,5},{8,10},{9,11},{10,... | collective-permute-start | bytes 995336 | tf_op jit(solution)/shard_map/ppermute | solution.py:946
  31.4 21.9 %collective-permute-start.4 = (bf16[9,24,768]{2,1,0:T(8,128)(2,1)S(1)}, bf16[9,24,768]{2,1,0:T(8,128)(2,1)S(1)}, u32[]{:S(2)}, u32[]{:S(2)}) collective-permute-start(bf16[9,24,768]{2,1,0:T(8,128)(2,1)S(1)} %pad_maximum_fusion.9), channel_id=1, source_target_pairs={{0,1},{1,2},{2,3},{3,0},{4,5},{5,6},{6,7},{7,4},{8,9},{9,10},{10,1... | collective-permute-start | bytes 995336 | tf_op jit(solution)/shard_map/ppermute | solution.py:946
  31.4 22.8 %collective-permute-start.5 = (bf16[9,24,768]{2,1,0:T(8,128)(2,1)S(1)}, bf16[9,24,768]{2,1,0:T(8,128)(2,1)S(1)}, u32[]{:S(2)}, u32[]{:S(2)}) collective-permute-start(bf16[9,24,768]{2,1,0:T(8,128)(2,1)S(1)} %pad_maximum_fusion.9), channel_id=1, source_target_pairs={{0,3},{1,0},{2,1},{3,2},{4,7},{5,4},{6,5},{7,6},{8,11},{9,8},{10,9... | collective-permute-start | bytes 995336 | tf_op jit(solution)/shard_map/ppermute | solution.py:946
  98.0 32.5 %collective-permute-start.26 = (bf16[384,768]{1,0:T(8,128)(2,1)S(1)}, bf16[384,768]{1,0:T(8,128)(2,1)S(1)}, u32[]{:S(2)}, u32[]{:S(2)}) collective-permute-start(bf16[384,768]{1,0:T(8,128)(2,1)S(1)} %bitcast.249), channel_id=1, source_target_pairs={{0,24},{1,25},{2,26},{3,27},{4,28},{5,29},{6,30},{7,31},{8,16},{9,... | collective-permute-start | bytes 1769480 | tf_op jit(solution)/shard_map/ppermute | solution.py:938
  99.5 33.7 %collective-permute-start.25 = (bf16[384,768]{1,0:T(8,128)(2,1)S(1)}, bf16[384,768]{1,0:T(8,128)(2,1)S(1)}, u32[]{:S(2)}, u32[]{:S(2)}) collective-permute-start(bf16[384,768]{1,0:T(8,128)(2,1)S(1)} %bitcast.250), channel_id=1, source_target_pairs={{0,16},{1,17},{2,18},{3,19},{4,20},{5,21},{6,22},{7,23},{8,24},{9,... | collective-permute-start | bytes 1769480 | tf_op jit(solution)/shard_map/ppermute | solution.py:938
  101.0 37.7 %collective-permute-start.24 = (bf16[384,768]{1,0:T(8,128)(2,1)S(1)}, bf16[384,768]{1,0:T(8,128)(2,1)S(1)}, u32[]{:S(2)}, u32[]{:S(2)}) collective-permute-start(bf16[384,768]{1,0:T(8,128)(2,1)S(1)} %bitcast.251), channel_id=1, source_target_pairs={{0,8},{1,9},{2,10},{3,11},{4,12},{5,13},{6,14},{7,15},{8,0},{9,1},... | collective-permute-start | bytes 1769480 | tf_op jit(solution)/shard_map/ppermute | solution.py:938
  101.5 38.5 %collective-permute-start.27 = (bf16[384,768]{1,0:T(8,128)(2,1)S(1)}, bf16[384,768]{1,0:T(8,128)(2,1)S(1)}, u32[]{:S(2)}, u32[]{:S(2)}) collective-permute-start(bf16[384,768]{1,0:T(8,128)(2,1)S(1)} %bitcast.252), channel_id=1, source_target_pairs={{0,4},{1,5},{2,6},{3,7},{4,0},{5,1},{6,2},{7,3},{8,12},{9,13},{10,... | collective-permute-start | bytes 1769480 | tf_op jit(solution)/shard_map/ppermute | solution.py:938
  162.0 33.8 %collective-permute-start.31 = (bf16[2,16,768]{2,1,0:T(8,128)(2,1)S(1)}, bf16[2,16,768]{2,1,0:T(8,128)(2,1)S(1)}, u32[]{:S(2)}, u32[]{:S(2)}) collective-permute-start(bf16[2,16,768]{2,1,0:T(8,128)(2,1)S(1)} %pad_maximum_fusion.11), channel_id=1, source_target_pairs={{0,2},{1,3},{2,0},{3,1},{4,6},{5,7},{6,4},{7,5},{8,10},{9,11},{10,... | collective-permute-start | bytes 147464 | tf_op jit(solution)/shard_map/ppermute | solution.py:946
  167.8 28.0 %collective-permute-start.32 = (bf16[2,16,768]{2,1,0:T(8,128)(2,1)S(1)}, bf16[2,16,768]{2,1,0:T(8,128)(2,1)S(1)}, u32[]{:S(2)}, u32[]{:S(2)}) collective-permute-start(bf16[2,16,768]{2,1,0:T(8,128)(2,1)S(1)} %pad_maximum_fusion.11), channel_id=1, source_target_pairs={{0,1},{1,2},{2,3},{3,0},{4,5},{5,6},{6,7},{7,4},{8,9},{9,10},{10,1... | collective-permute-start | bytes 147464 | tf_op jit(solution)/shard_map/ppermute | solution.py:946
  169.0 26.7 %collective-permute-start.33 = (bf16[2,16,768]{2,1,0:T(8,128)(2,1)S(1)}, bf16[2,16,768]{2,1,0:T(8,128)(2,1)S(1)}, u32[]{:S(2)}, u32[]{:S(2)}) collective-permute-start(bf16[2,16,768]{2,1,0:T(8,128)(2,1)S(1)} %pad_maximum_fusion.11), channel_id=1, source_target_pairs={{0,3},{1,0},{2,1},{3,2},{4,7},{5,4},{6,5},{7,6},{8,11},{9,8},{10,9... | collective-permute-start | bytes 147464 | tf_op jit(solution)/shard_map/ppermute | solution.py:946
  195.8 27.6 %collective-permute-start.34 = (bf16[4,2,16,768]{3,2,1,0:T(8,128)(2,1)S(1)}, bf16[4,2,16,768]{3,2,1,0:T(8,128)(2,1)S(1)}, u32[]{:S(2)}, u32[]{:S(2)}) collective-permute-start(bf16[4,2,16,768]{3,2,1,0:T(8,128)(2,1)S(1)} %pad_maximum_fusion.10), channel_id=1, source_target_pairs={{0,8},{1,9},{2,10},{3,11},{4,12},{5,13},{6,14},{7,15},{8,0},{9,1},... | collective-permute-start | bytes 589832 | tf_op jit(solution)/shard_map/ppermute | solution.py:938
  197.4 26.0 %collective-permute-start.35 = (bf16[4,2,16,768]{3,2,1,0:T(8,128)(2,1)S(1)}, bf16[4,2,16,768]{3,2,1,0:T(8,128)(2,1)S(1)}, u32[]{:S(2)}, u32[]{:S(2)}) collective-permute-start(bf16[4,2,16,768]{3,2,1,0:T(8,128)(2,1)S(1)} %pad_maximum_fusion.10), channel_id=1, source_target_pairs={{0,16},{1,17},{2,18},{3,19},{4,20},{5,21},{6,22},{7,23},{8,24},{9,... | collective-permute-start | bytes 589832 | tf_op jit(solution)/shard_map/ppermute | solution.py:938
  198.8 24.6 %collective-permute-start.36 = (bf16[4,2,16,768]{3,2,1,0:T(8,128)(2,1)S(1)}, bf16[4,2,16,768]{3,2,1,0:T(8,128)(2,1)S(1)}, u32[]{:S(2)}, u32[]{:S(2)}) collective-permute-start(bf16[4,2,16,768]{3,2,1,0:T(8,128)(2,1)S(1)} %pad_maximum_fusion.10), channel_id=1, source_target_pairs={{0,24},{1,25},{2,26},{3,27},{4,28},{5,29},{6,30},{7,31},{8,16},{9,... | collective-permute-start | bytes 589832 | tf_op jit(solution)/shard_map/ppermute | solution.py:938
  298.3 21.0 %collective-permute-start.38 = (bf16[4,384,768]{2,1,0:T(8,128)(2,1)}, bf16[4,384,768]{2,1,0:T(8,128)(2,1)}, u32[]{:S(2)}, u32[]{:S(2)}) collective-permute-start(bf16[4,384,768]{2,1,0:T(8,128)(2,1)} %get-tuple-element.168), channel_id=1, source_target_pairs={{0,4},{1,5},{2,6},{3,7},{4,0},{5,1},{6,2},{7,3},{8,12},{9,13},{10,... | collective-permute-start | bytes 7077896 | tf_op jit(solution)/shard_map/ppermute | solution.py:938
  318.6 27.8 %collective-permute-start.41 = (bf16[4,480,768]{2,1,0:T(8,128)(2,1)}, bf16[4,480,768]{2,1,0:T(8,128)(2,1)}, u32[]{:S(2)}, u32[]{:S(2)}) collective-permute-start(bf16[4,480,768]{2,1,0:T(8,128)(2,1)} %get-tuple-element.167), channel_id=1, source_target_pairs={{0,4},{1,5},{2,6},{3,7},{4,0},{5,1},{6,2},{7,3},{8,12},{9,13},{10,... | collective-permute-start | bytes 8847368 | tf_op jit(solution)/shard_map/ppermute | solution.py:938
  344.4 32.3 %collective-permute-start.43 = (bf16[4,96,768]{2,1,0:T(8,128)(2,1)}, bf16[4,96,768]{2,1,0:T(8,128)(2,1)}, u32[]{:S(2)}, u32[]{:S(2)}) collective-permute-start(bf16[4,96,768]{2,1,0:T(8,128)(2,1)} %pad_maximum_fusion.6), channel_id=1, source_target_pairs={{0,16},{1,17},{2,18},{3,19},{4,20},{5,21},{6,22},{7,23},{8,24},{9,... | collective-permute-start | bytes 1769480 | tf_op jit(solution)/shard_map/ppermute | solution.py:938
  345.9 30.8 %collective-permute-start.42 = (bf16[4,96,768]{2,1,0:T(8,128)(2,1)}, bf16[4,96,768]{2,1,0:T(8,128)(2,1)}, u32[]{:S(2)}, u32[]{:S(2)}) collective-permute-start(bf16[4,96,768]{2,1,0:T(8,128)(2,1)} %pad_maximum_fusion.5), channel_id=1, source_target_pairs={{0,8},{1,9},{2,10},{3,11},{4,12},{5,13},{6,14},{7,15},{8,0},{9,1},... | collective-permute-start | bytes 1769480 | tf_op jit(solution)/shard_map/ppermute | solution.py:938
  350.7 28.1 %collective-permute-start.44 = (bf16[2,120,768]{2,1,0:T(8,128)(2,1)}, bf16[2,120,768]{2,1,0:T(8,128)(2,1)}, u32[]{:S(2)}, u32[]{:S(2)}) collective-permute-start(bf16[2,120,768]{2,1,0:T(8,128)(2,1)} %bitcast.74), channel_id=1, source_target_pairs={{0,8},{1,9},{2,10},{3,11},{4,12},{5,13},{6,14},{7,15},{8,0},{9,1},... | collective-permute-start | bytes 1105928 | tf_op jit(solution)/shard_map/ppermute | solution.py:938
  354.0 27.5 %collective-permute-start.45 = (bf16[2,120,768]{2,1,0:T(8,128)(2,1)}, bf16[2,120,768]{2,1,0:T(8,128)(2,1)}, u32[]{:S(2)}, u32[]{:S(2)}) collective-permute-start(bf16[2,120,768]{2,1,0:T(8,128)(2,1)} %bitcast.76), channel_id=1, source_target_pairs={{0,16},{1,17},{2,18},{3,19},{4,20},{5,21},{6,22},{7,23},{8,24},{9,... | collective-permute-start | bytes 1105928 | tf_op jit(solution)/shard_map/ppermute | solution.py:938
  407.0 33.6 %collective-permute-start.58 = (bf16[120,768]{1,0:T(8,128)(2,1)}, bf16[120,768]{1,0:T(8,128)(2,1)}, u32[]{:S(2)}, u32[]{:S(2)}) collective-permute-start(bf16[120,768]{1,0:T(8,128)(2,1)} %get-tuple-element.230), channel_id=1, source_target_pairs={{0,1},{1,2},{2,3},{3,0},{4,5},{5,6},{6,7},{7,4},{8,9},{9,10},{10,1... | collective-permute-start | bytes 552968 | tf_op jit(solution)/shard_map/ppermute | solution.py:946
  407.6 34.2 %collective-permute-start.59 = (bf16[120,768]{1,0:T(8,128)(2,1)}, bf16[120,768]{1,0:T(8,128)(2,1)}, u32[]{:S(2)}, u32[]{:S(2)}) collective-permute-start(bf16[120,768]{1,0:T(8,128)(2,1)} %get-tuple-element.232), channel_id=1, source_target_pairs={{0,2},{1,3},{2,0},{3,1},{4,6},{5,7},{6,4},{7,5},{8,10},{9,11},{10,... | collective-permute-start | bytes 552968 | tf_op jit(solution)/shard_map/ppermute | solution.py:946
  412.7 23.6 %collective-permute-start.53 = (bf16[4,80,768]{2,1,0:T(8,128)(2,1)S(1)}, bf16[4,80,768]{2,1,0:T(8,128)(2,1)S(1)}, u32[]{:S(2)}, u32[]{:S(2)}) collective-permute-start(bf16[4,80,768]{2,1,0:T(8,128)(2,1)S(1)} %fusion.15), channel_id=1, source_target_pairs={{0,16},{1,17},{2,18},{3,19},{4,20},{5,21},{6,22},{7,23},{8,24},{9,... | collective-permute-start | bytes 1474568 | tf_op jit(solution)/shard_map/ppermute | solution.py:938
  415.0 21.3 %collective-permute-start.54 = (bf16[4,80,768]{2,1,0:T(8,128)(2,1)}, bf16[4,80,768]{2,1,0:T(8,128)(2,1)S(1)}, u32[]{:S(2)}, u32[]{:S(2)}) collective-permute-start(bf16[4,80,768]{2,1,0:T(8,128)(2,1)} %fusion.16), channel_id=1, source_target_pairs={{0,24},{1,25},{2,26},{3,27},{4,28},{5,29},{6,30},{7,31},{8,16},{9,... | collective-permute-start | bytes 1474568 | tf_op jit(solution)/shard_map/ppermute | solution.py:938
  (82 other events, 737.1 us)
Sparse Core Ops, SparseCore 0:
  76.9 121.9 all-gather.1

commit v7 on v6

--- a/solution.py
+++ b/solution.py
@@ -1044,8 +1044,9 @@
         self.turned = [parts[0]] + [links.turn(parts[k], k) for k in range(1, links.inner)]
         return self.turned[1:]
 
-    def total(self):
-        return sum(t.astype(F32) for t in self.turned)
+    def total(self, *earlier):
+        parts = [after(t, *earlier) for t in self.turned] if earlier else self.turned
+        return sum(t.astype(F32) for t in parts)
 
 
 class PlainSum:
@@ -1065,7 +1066,7 @@
 
     near = direct = turn = far
 
-    def total(self):
+    def total(self, *earlier):
         return self.sums.astype(F32)
 
 
@@ -1148,18 +1149,18 @@
     if fast:
         first = jnp.concatenate([slabs_of(seg_qkv).reshape(-1, 768), jnp.pad(small, ((0, 7), (0, 0)))])
         line_first = links.gather_z(first)
-        line_rest = jnp.concatenate([mid_shard, seg_down.reshape(4, -1, feat_dim)])
-        line_rest = links.gather_z(after(line_rest, *line_first))
+        line_mid = links.gather_z(after(mid_shard, *line_first))
         weights = jnp.stack([p[:72].reshape(3, 24, 768) for p in line_first], axis=1).reshape(-1, 768)
         rows = jnp.concatenate([p[72:73] for p in line_first])
         block = jnp.concatenate([weights, jnp.pad(rows, ((0, 12), (0, 0)))])
         near = links.spread_near(block)
         far = links.spread_far(*near, 192)
-        first = [block, *near, *far, *links.core([after(p, *far, *line_rest) for p in (block, *near, *far)])]
+        first = [block, *near, *far, *links.core([after(p, *far, *line_mid) for p in (block, *near, *far)])]
+        line_down = links.gather_z(after(seg_down, *first[5:]))
         ends = [p[288:292] for p in first[:3]] + [first[4][96:100]]
         others = [p[288:292] for p in first[5:8]] + [first[9][96:100]]
         small = links.in_order([(ends, others)[m % 2][m // 2] for m in range(8)])
-        block = after(jnp.stack([p[:5] for p in line_rest], axis=1).reshape(-1, 768), *far)
+        block = after(jnp.stack(line_mid, axis=1).reshape(-1, 768), *far)
         mid = [block, *links.spread_near(block)]
     else:
         first = plain_pieces(lax.all_gather(slabs_of(seg_qkv), AXES, axis=1, tiled=True), False)
@@ -1174,7 +1175,7 @@
     cross_v = cross_v.at[hidden_rows].set(mix_columns(cross_v[hidden_rows].reshape(1, -1), devices).reshape(-1, feat_dim))
 
     before = attn_forward(info, rows_in, seg_v, first, seg_count, 0)
-    wide = lax.all_gather(after(wide, before[0], *(mid[1:] if fast else ())), AXES, axis=1, tiled=True)
+    wide = lax.all_gather(after(wide, before[0], *((*mid[1:], *line_down) if fast else ())), AXES, axis=1, tiled=True)
     if fast:
         far = links.spread_far(*(after(p, before[0]) for p in mid[1:]), 288)
         rows_late = after(rows_in, *mid[1:])
@@ -1182,9 +1183,10 @@
         rows_late = rows_in
     packed, mixed = attn_forward(info, rows_late, seg_v, first, seg_count, 1, before)
     if fast:
-        late = links.core([after(p, packed, *far) for p in (*mid, *far)])
-        mid = [*mid, *far, *late]
-        block = after(jnp.concatenate([p[5:] for p in line_rest]).reshape(-1, feat_dim), *late)
+        early = links.core([after(p, before[0]) for p in mid])
+        late = links.core([after(p, packed, *far, *early) for p in far])
+        mid = [*mid, *far, *early, *late]
+        block = after(jnp.concatenate(line_down), *late)
         near = [links.flip(block, m) for m in (2, 4, 6)]
     summed, low, act, slope = mid_forward(info, rows_in, mixed, seg_v, mid)
     if fast:
@@ -1263,7 +1265,7 @@
     grad_positions = lax.dynamic_slice_in_dim(pos_grad, me * width, width, 1)
     grad_down = down_sum.total()
     grad_mid = mid_sum.total().reshape(5, -1, feat_dim)
-    total = qkv_sum.total()
+    total = qkv_sum.total(cross_grads[2], cross_vec_grad)
     grad_qkv = matrix_of(total[: 3 * width].reshape(3, -1, feat_dim))
     grad_vec = total[3 * width, : seg_rows * width].reshape(seg_rows, width)
     return (

time: 469 us -> 469 us (level)
  waiting for transfers between devices: 32.5 us -> 25.6 us
  starting transfers between devices: 68.2 us -> 74.4 us
    ppermute x18 -> x21, waiting for transfers between devices: 18.1 us -> 10.6 us  [turn(): return lax.ppermute(value, AXES, pairs)]
    ppermute x18 -> x21, starting transfers between devices: 38.4 us -> 43.3 us  [turn(): return lax.ppermute(value, AXES, pairs)]
  transfers between devices with their start and end apart: 62 -> 65, of which waited for: 13 -> 13; matrix products, arithmetic and copies ran while one was open for 14% -> 14% of each run, Pallas kernels for 44% -> 44%
where the time goes in v7:
time: 469 us; the launch traced here: 463 us
  Pallas kernels  274 us (58%)
  starting transfers between devices  74.4 us (16%)
  local copies, waits for them, and re-layouts  36.9 us (8%)
  other arithmetic  36.3 us (8%)
  waiting for transfers between devices  25.6 us (5%)
  between operations  15.7 us (3%)
    pallas_call x2, Pallas kernels, ffn_backward(): pl.pallas_call(functools.partial(ffn_backward_kernel, segs, seg_count, fi...  48.1 us
    ppermute x21, starting transfers between devices, turn(): return lax.ppermute(value, AXES, pairs)  43.3 us
    pallas_call x1, Pallas kernels, cross_whole(): pl.pallas_call(functools.partial(cross_kernel, rows // count), grid=(rows...  39.3 us
    pallas_call x2, Pallas kernels, attn_backward(): pl.pallas_call(functools.partial(attn_backward_kernel, segs, seg_count, f...  34.7 us
    ppermute x43, starting transfers between devices, flip(): return lax.ppermute(value, AXES, pairs)  31.1 us
    pallas_call x1, Pallas kernels, mid_forward(): pl.pallas_call(mid_forward_kernel, grid=(rows // count,), in_specs=[SMEM,...  29.3 us
    pallas_call x2, Pallas kernels, attn_forward(): pl.pallas_call(functools.partial(attn_forward_kernel, segs, seg_count, fi...  26.4 us
    pallas_call x1, Pallas kernels, mid_weight_grad(): pl.pallas_call(mid_grad_kernel, grid=(5,), in_specs=[SMEM, still, still,...  19.8 us
  transfers between devices with their start and end apart: 65, of which 13 were waited for; matrix products, arithmetic and copies ran while one was open for 14% of the time, Pallas kernels for 44%

profile of v7, /device:TPU:0, one launch (start us, length us, event | category | flops | bytes accessed | tf_op | source)
XLA Modules:
  0.0 462.6 jit_solution(11142157847941477636)
XLA Ops:
  9.0 4.1 collective-permute-start
  17.0 5.6 %collective-permute-done = bf16[80,768]{1,0:T(8,128)(2,1)S(1)} collective-permute-done((bf16[80,768]{1,0:T(8,128)(2,1)S(1)}, bf16[80,768]{1,0:T(8,128)(2,1)S(1)}, u32[]{:S(2)}, u32[]{:S(2)}) %collective-permute-start) | collective-permute-done | bytes 122912 | tf_op jit(solution)/shard_map/ppermute | solution.py:946
  27.0 3.7 collective-permute-start.3
  30.7 3.8 collective-permute-start.5
  39.8 3.3 collective-permute-done.3
  52.2 6.6 %collective-permute-start.24 = (bf16[96,768]{1,0:T(8,128)(2,1)}, bf16[96,768]{1,0:T(8,128)(2,1)S(1)}, u32[]{:S(2)}, u32[]{:S(2)}) collective-permute-start(bf16[96,768]{1,0:T(8,128)(2,1)} %param.24), channel_id=1, source_target_pairs={{0,2},{1,3},{2,0},{3,1},{4,6},{5,7},{6,4},{7,5},{8,10},{9,11},{10,... | collective-permute-start | bytes 442376 | tf_op jit(solution)/shard_map/ppermute | solution.py:946
  58.8 3.8 collective-permute-start.26
  66.4 13.2 %attn_forward.2 = (bf16[2048,2304]{1,0:T(8,128)(2,1)}, bf16[2048,768]{1,0:T(8,128)(2,1)}) custom-call(s32[3]{0:T(128)} %pad_add_fusion.info, bf16[2048,768]{1,0:T(8,128)(2,1)} %bitcast.303, f32[12,768]{1,0:T(8,128)} %slice.371.vec_ref, bf16[304,768]{1,0:T(8,128)(2,1)} %copy-done.17, bf16[304,768]{1,0:T(8,128)(2,1)} %collective-permute-done.8.rest_1_, ...), custom_call_target="tpu_custom_call" | custom-call | flops 12582912000 | bytes 12582912 | tf_op jit(solution)/shard_map/attn_forward/pallas_call | solution.py:539
  84.1 13.2 %attn_forward.3 = (bf16[2048,2304]{1,0:T(8,128)(2,1)}, bf16[2048,768]{1,0:T(8,128)(2,1)}) custom-call(s32[3]{0:T(128)} %pad_add_fusion.info, bf16[2048,768]{1,0:T(8,128)(2,1)} %bitcast.304, f32[12,768]{1,0:T(8,128)} %slice.371.vec_ref, bf16[304,768]{1,0:T(8,128)(2,1)} %copy-done.17, ...), custom_call_target="tpu_custom_call", output_to_operand_aliasing={{0}: (13, {}), {1}: (14, {})} | custom-call | flops 12582912000 | bytes 12582912 | tf_op jit(solution)/shard_map/attn_forward/pallas_call | solution.py:539
  105.5 29.3 %mid_forward.1 = (f32[2048,768]{1,0:T(8,128)}, bf16[2048,768]{1,0:T(8,128)(2,1)}, bf16[2048,3072]{1,0:T(8,128)(2,1)}, bf16[2048,3072]{1,0:T(8,128)(2,1)}) custom-call(s32[3]{0:T(128)} %pad_add_fusion.info, bf16[2048,768]{1,0:T(8,128)(2,1)} %bitcast.305, bf16[2048,768]{1,0:T(8,128)(2,1)} %get-tuple-element.128.mixed_ref, f32[12,768]{1,0:T(8,128)} %slice.371.vec_ref, ...), custom_call_target="tpu_custom_call" | custom-call | flops 25165824000 | bytes 47185920 | tf_op jit(solution)/shard_map/mid_forward/pallas_call | solution.py:556
  137.1 5.5 %collective-permute-done.27.rest_1_.rest_11_.rest_19_ = bf16[384,768]{1,0:T(8,128)(2,1)S(1)} collective-permute-done((bf16[384,768]{1,0:T(8,128)(2,1)S(1)}, bf16[384,768]{1,0:T(8,128)(2,1)S(1)}, u32[]{:S(2)}, u32[]{:S(2)}) %collective-permute-start.27) | collective-permute-done | bytes 589856 | tf_op jit(solution)/shard_map/ppermute | solution.py:938
  144.8 19.7 %down_forward.1 = (f32[2048,768]{1,0:T(8,128)}, f32[8,2,768]{2,1,0:T(2,128)}) custom-call(s32[3]{0:T(128)} %pad_add_fusion.info, f32[2048,768]{1,0:T(8,128)} %get-tuple-element.135.sum_ref, bf16[2048,3072]{1,0:T(8,128)(2,1)} %get-tuple-element.136.act_ref.left_ref, f32[12,768]{1,0:T(8,128)} %slice.371.vec_ref, bf16[384,768]{1,0:T(8,128)(2,1)} %copy-done.3, ...), custom_call_target="tpu_custom_call" | custom-call | flops 12582912000 | bytes 25165824 | tf_op jit(solution)/shard_map/down_forward/pallas_call | solution.py:573
  166.1 3.2 collective-permute-start.36
  169.4 24.1 %ffn_backward.2 = (bf16[2048,768]{1,0:T(8,128)(2,1)}, bf16[2048,768]{1,0:T(8,128)(2,1)}, bf16[2048,3072]{1,0:T(8,128)(2,1)}, bf16[2048,768]{1,0:T(8,128)(2,1)}, ...) custom-call(s32[3]{0:T(128)} %pad_add_fusion.info, bf16[2048,768]{1,0:T(8,128)(2,1)} %bitcast.301, ...), custom_call_target="tpu_custom_call" | custom-call | flops 22020096000 | bytes 23592960 | tf_op jit(solution)/shard_map/ffn_backward/pallas_call | solution.py:615
  197.1 24.0 %ffn_backward.3 = (bf16[2048,768]{1,0:T(8,128)(2,1)}, bf16[2048,768]{1,0:T(8,128)(2,1)}, bf16[2048,3072]{1,0:T(8,128)(2,1)}, bf16[2048,768]{1,0:T(8,128)(2,1)}, ...) custom-call(s32[3]{0:T(128)} %pad_add_fusion.info, ...), custom_call_target="tpu_custom_call", output_to_operand_aliasing={{0}: (24, {}), {1}: (25, {}), {2}: (26, {}), {3}: (27, {}),... | custom-call | flops 22020096000 | bytes 23592960 | tf_op jit(solution)/shard_map/ffn_backward/pallas_call | solution.py:615
  227.3 39.3 %cross_encoder.1 = (f32[16,768]{1,0:T(8,128)}, f32[16,768]{1,0:T(8,128)}, f32[12,768]{1,0:T(8,128)}, f32[8,768]{1,0:T(8,128)}, f32[24,2304]{1,0:T(8,128)}, /*ind...) custom-call(s32[2]{0:T(128)} %pad_add_fusion.1.info, bf16[512,768]{1,0:T(8,128)(2,1)} %bitcast.273, ...), custom_call_target="tpu_custom_call" | custom-call | flops 23592960000 | bytes 16777216 | tf_op jit(solution)/shard_map/cross_encoder/pallas_call | solution.py:590
  266.6 13.3 %opening_backward.1 = (bf16[16,128,768]{2,1,0:T(8,128)(2,1)}, bf16[16,128,768]{2,1,0:T(8,128)(2,1)}, bf16[16,128,3072]{2,1,0:T(8,128)(2,1)}, bf16[16,128,768]{2,...) custom-call(s32[3]{0:T(128)} %pad_add_fusion.info, ...), custom_call_target="tpu_custom_call", output_to_operand_aliasing={{0}: (4, {}), {1}: (5, {}), {2}: (6, {}), {3}: (7, {}), {4}... | custom-call | flops 8589934592 | bytes 16777216 | tf_op jit(solution)/shard_map/opening_backward/pallas_call | solution.py:638
  279.9 16.4 %down_weight_grad.1 = (bf16[4,384,768]{2,1,0:T(8,128)(2,1)}, bf16[4,384,768]{2,1,0:T(8,128)(2,1)}) custom-call(s32[3]{0:T(128)} %pad_add_fusion.info, bf16[2048,3072]{1,0:T(8,128)(2,1)} %get-tuple-element.136.act_ref.left_ref, bf16[2048,768]{1,0:T(8,128)(2,1)} %bitcast.229), custom_call_target="tpu_custom_call" | custom-call | flops 9663676416 | bytes 12582912 | tf_op jit(solution)/shard_map/down_weight_grad/pallas_call | solution.py:742
  296.8 19.8 %mid_weight_grad.1 = (bf16[4,480,768]{2,1,0:T(8,128)(2,1)}, bf16[4,480,768]{2,1,0:T(8,128)(2,1)}) custom-call(s32[3]{0:T(128)} %pad_add_fusion.info, bf16[2048,768]{1,0:T(8,128)(2,1)} %get-tuple-element.128.mixed_ref, bf16[2048,768]{1,0:T(8,128)(2,1)} %bitcast.231, bf16[2048,768]{1,0:T(8,128)(2,1)} %get-tuple-element.164.low_ref, bf16[2048,3072]{1,0:T(8,128)(2,1)} %bitcast.218), custom_call_target="tpu_custom_call" | custom-call | flops 12079595520 | bytes 15728640 | tf_op jit(solution)/shard_map/mid_weight_grad/pallas_call | solution.py:715
  323.5 17.5 %attn_backward.2 = (bf16[2048,2304]{1,0:T(8,128)(2,1)}, f32[2,768]{1,0:T(2,128)}) custom-call(s32[3]{0:T(128)} %pad_add_fusion.info, bf16[2048,2304]{1,0:T(8,128)(2,1)} %get-tuple-element.132.packed_ref, bf16[2048,768]{1,0:T(8,128)(2,1)} %bitcast.234), custom_call_target="tpu_custom_call" | custom-call | flops 15728640000 | bytes 12582912 | tf_op jit(solution)/shard_map/attn_backward/pallas_call | solution.py:662
  353.1 17.1 %attn_backward.3 = (bf16[2048,2304]{1,0:T(8,128)(2,1)}, f32[2,768]{1,0:T(2,128)}) custom-call(s32[3]{0:T(128)} %pad_add_fusion.info, bf16[2048,2304]{1,0:T(8,128)(2,1)} %get-tuple-element.132.packed_ref, bf16[2048,768]{1,0:T(8,128)(2,1)} %bitcast.235, bf16[2048,2304]{1,0:T(8,128)(2,1)} %get-tuple-element.172.rest_0_), custom_call_target="tpu_custom_call", output_to_operand_aliasing={{0}: (3, {})} | custom-call | flops 15728640000 | bytes 12582912 | tf_op jit(solution)/shard_map/attn_backward/pallas_call | solution.py:662
  385.6 13.2 %qkv_weight_grad.1 = (bf16[4,304,768]{2,1,0:T(8,128)(2,1)}, bf16[4,304,768]{2,1,0:T(8,128)(2,1)}) custom-call(s32[3]{0:T(128)} %pad_add_fusion.info, bf16[2048,768]{1,0:T(8,128)(2,1)} %bitcast.306, bf16[2048,2304]{1,0:T(8,128)(2,1)} %get-tuple-element.184.right_ref.packed_grad_ref, bf16[8,16,768]{2,1,0:T(8,128)(2,1)} %copy-done.36), custom_call_target="tpu_custom_call" | custom-call | flops 7247757312 | bytes 9437184 | tf_op jit(solution)/shard_map/qkv_weight_grad/pallas_call | solution.py:698
  417.0 13.4 %token_gradient.1 = bf16[2048,768]{1,0:T(8,128)(2,1)} custom-call(s32[3]{0:T(128)} %pad_add_fusion.info, bf16[2048,2304]{1,0:T(8,128)(2,1)} %get-tuple-element.184.right_ref.packed_grad_ref, bf16[2048,768]{1,0:T(8,128)(2,1)} %bitcast.232, bf16[304,768]{1,0:T(8,128)(2,1)} %copy-done.17, bf16[304,768]{1,0:T(8,128)(2,1)} %collective-permute-done.8.rest_1_, ...), custom_call_target="tpu_custom_call" | custom-call | flops 9437184000 | bytes 15728640 | tf_op jit(solution)/shard_map/token_gradient/pallas_call | solution.py:677
  430.5 2.9 collective-permute-start.63
  (371 shorter events, 130.5 us)
Async XLA Ops:
  7.2 219.2 %all-gather.2.cloned.1.call-start = ((), (), s32[]{:S(2)}) async-start(), calls=%async_computation | async-start | bytes 14598144 | tf_op jit(solution)/shard_map/all_gather | solution.py:1178
  50.5 30.9 %collective-permute-start.10 = (bf16[480,768]{1,0:T(8,128)(2,1)S(1)}, bf16[480,768]{1,0:T(8,128)(2,1)S(1)}, u32[]{:S(2)}, u32[]{:S(2)}) collective-permute-start(bf16[480,768]{1,0:T(8,128)(2,1)S(1)} %bitcast.239), channel_id=1, source_target_pairs={{0,8},{1,9},{2,10},{3,11},{4,12},{5,13},{6,14},{7,15},{8,0},{9,1},... | collective-permute-start | bytes 2211848 | tf_op jit(solution)/shard_map/ppermute | solution.py:938
  51.2 30.2 %collective-permute-start.11 = (bf16[480,768]{1,0:T(8,128)(2,1)S(1)}, bf16[480,768]{1,0:T(8,128)(2,1)S(1)}, u32[]{:S(2)}, u32[]{:S(2)}) collective-permute-start(bf16[480,768]{1,0:T(8,128)(2,1)S(1)} %bitcast.240), channel_id=1, source_target_pairs={{0,16},{1,17},{2,18},{3,19},{4,20},{5,21},{6,22},{7,23},{8,24},{9,... | collective-permute-start | bytes 2211848 | tf_op jit(solution)/shard_map/ppermute | solution.py:938
  52.2 27.3 %collective-permute-start.24 = (bf16[96,768]{1,0:T(8,128)(2,1)}, bf16[96,768]{1,0:T(8,128)(2,1)S(1)}, u32[]{:S(2)}, u32[]{:S(2)}) collective-permute-start(bf16[96,768]{1,0:T(8,128)(2,1)} %param.24), channel_id=1, source_target_pairs={{0,2},{1,3},{2,0},{3,1},{4,6},{5,7},{6,4},{7,5},{8,10},{9,11},{10,... | collective-permute-start | bytes 442376 | tf_op jit(solution)/shard_map/ppermute | solution.py:946
  102.0 32.8 %collective-permute-start.29 = (bf16[384,768]{1,0:T(8,128)(2,1)S(1)}, bf16[384,768]{1,0:T(8,128)(2,1)S(1)}, u32[]{:S(2)}, u32[]{:S(2)}) collective-permute-start(bf16[384,768]{1,0:T(8,128)(2,1)S(1)} %pad_maximum_fusion.4.rest_0_.rest_10_.rest_18_), channel_id=1, source_target_pairs={{0,24},{1,25},{2,26},{3,27},{4,28},{5,29},{6,30},{7,31},{8,16},{9,... | collective-permute-start | bytes 1769480 | tf_op jit(solution)/shard_map/ppermute | solution.py:938
  103.0 34.1 %collective-permute-start.28 = (bf16[384,768]{1,0:T(8,128)(2,1)S(1)}, bf16[384,768]{1,0:T(8,128)(2,1)S(1)}, u32[]{:S(2)}, u32[]{:S(2)}) collective-permute-start(bf16[384,768]{1,0:T(8,128)(2,1)S(1)} %pad_maximum_fusion.4.rest_0_.rest_10_.rest_18_), channel_id=1, source_target_pairs={{0,16},{1,17},{2,18},{3,19},{4,20},{5,21},{6,22},{7,23},{8,24},{9,... | collective-permute-start | bytes 1769480 | tf_op jit(solution)/shard_map/ppermute | solution.py:938
  104.1 38.5 %collective-permute-start.27 = (bf16[384,768]{1,0:T(8,128)(2,1)S(1)}, bf16[384,768]{1,0:T(8,128)(2,1)S(1)}, u32[]{:S(2)}, u32[]{:S(2)}) collective-permute-start(bf16[384,768]{1,0:T(8,128)(2,1)S(1)} %pad_maximum_fusion.4.rest_0_.rest_10_.rest_18_), channel_id=1, source_target_pairs={{0,8},{1,9},{2,10},{3,11},{4,12},{5,13},{6,14},{7,15},{8,0},{9,1},... | collective-permute-start | bytes 1769480 | tf_op jit(solution)/shard_map/ppermute | solution.py:938
  105.5 38.4 %collective-permute-start.30 = (bf16[384,768]{1,0:T(8,128)(2,1)S(1)}, bf16[384,768]{1,0:T(8,128)(2,1)S(1)}, u32[]{:S(2)}, u32[]{:S(2)}) collective-permute-start(bf16[384,768]{1,0:T(8,128)(2,1)S(1)} %pad_maximum_fusion.4.rest_0_.rest_10_.rest_18_), channel_id=1, source_target_pairs={{0,4},{1,5},{2,6},{3,7},{4,0},{5,1},{6,2},{7,3},{8,12},{9,13},{10,... | collective-permute-start | bytes 1769480 | tf_op jit(solution)/shard_map/ppermute | solution.py:938
  165.4 28.1 %collective-permute-start.34 = (bf16[2,16,768]{2,1,0:T(8,128)(2,1)S(1)}, bf16[2,16,768]{2,1,0:T(8,128)(2,1)S(1)}, u32[]{:S(2)}, u32[]{:S(2)}) collective-permute-start(bf16[2,16,768]{2,1,0:T(8,128)(2,1)S(1)} %pad_maximum_fusion.11), channel_id=1, source_target_pairs={{0,2},{1,3},{2,0},{3,1},{4,6},{5,7},{6,4},{7,5},{8,10},{9,11},{10,... | collective-permute-start | bytes 147464 | tf_op jit(solution)/shard_map/ppermute | solution.py:946
  165.5 28.0 %collective-permute-start.35 = (bf16[2,16,768]{2,1,0:T(8,128)(2,1)S(1)}, bf16[2,16,768]{2,1,0:T(8,128)(2,1)S(1)}, u32[]{:S(2)}, u32[]{:S(2)}) collective-permute-start(bf16[2,16,768]{2,1,0:T(8,128)(2,1)S(1)} %pad_maximum_fusion.11), channel_id=1, source_target_pairs={{0,1},{1,2},{2,3},{3,0},{4,5},{5,6},{6,7},{7,4},{8,9},{9,10},{10,1... | collective-permute-start | bytes 147464 | tf_op jit(solution)/shard_map/ppermute | solution.py:946
  166.1 27.4 %collective-permute-start.36 = (bf16[2,16,768]{2,1,0:T(8,128)(2,1)S(1)}, bf16[2,16,768]{2,1,0:T(8,128)(2,1)S(1)}, u32[]{:S(2)}, u32[]{:S(2)}) collective-permute-start(bf16[2,16,768]{2,1,0:T(8,128)(2,1)S(1)} %pad_maximum_fusion.11), channel_id=1, source_target_pairs={{0,3},{1,0},{2,1},{3,2},{4,7},{5,4},{6,5},{7,6},{8,11},{9,8},{10,9... | collective-permute-start | bytes 147464 | tf_op jit(solution)/shard_map/ppermute | solution.py:946
  193.6 27.6 %collective-permute-start.37 = (bf16[4,2,16,768]{3,2,1,0:T(8,128)(2,1)S(1)}, bf16[4,2,16,768]{3,2,1,0:T(8,128)(2,1)S(1)}, u32[]{:S(2)}, u32[]{:S(2)}) collective-permute-start(bf16[4,2,16,768]{3,2,1,0:T(8,128)(2,1)S(1)} %pad_maximum_fusion.9), channel_id=1, source_target_pairs={{0,8},{1,9},{2,10},{3,11},{4,12},{5,13},{6,14},{7,15},{8,0},{9,1},... | collective-permute-start | bytes 589832 | tf_op jit(solution)/shard_map/ppermute | solution.py:938
  194.8 26.4 %collective-permute-start.38 = (bf16[4,2,16,768]{3,2,1,0:T(8,128)(2,1)S(1)}, bf16[4,2,16,768]{3,2,1,0:T(8,128)(2,1)S(1)}, u32[]{:S(2)}, u32[]{:S(2)}) collective-permute-start(bf16[4,2,16,768]{3,2,1,0:T(8,128)(2,1)S(1)} %pad_maximum_fusion.9), channel_id=1, source_target_pairs={{0,16},{1,17},{2,18},{3,19},{4,20},{5,21},{6,22},{7,23},{8,24},{9,... | collective-permute-start | bytes 589832 | tf_op jit(solution)/shard_map/ppermute | solution.py:938
  196.2 25.0 %collective-permute-start.39 = (bf16[4,2,16,768]{3,2,1,0:T(8,128)(2,1)S(1)}, bf16[4,2,16,768]{3,2,1,0:T(8,128)(2,1)S(1)}, u32[]{:S(2)}, u32[]{:S(2)}) collective-permute-start(bf16[4,2,16,768]{3,2,1,0:T(8,128)(2,1)S(1)} %pad_maximum_fusion.9), channel_id=1, source_target_pairs={{0,24},{1,25},{2,26},{3,27},{4,28},{5,29},{6,30},{7,31},{8,16},{9,... | collective-permute-start | bytes 589832 | tf_op jit(solution)/shard_map/ppermute | solution.py:938
  296.3 21.0 %collective-permute-start.41 = (bf16[4,384,768]{2,1,0:T(8,128)(2,1)}, bf16[4,384,768]{2,1,0:T(8,128)(2,1)}, u32[]{:S(2)}, u32[]{:S(2)}) collective-permute-start(bf16[4,384,768]{2,1,0:T(8,128)(2,1)} %get-tuple-element.170), channel_id=1, source_target_pairs={{0,4},{1,5},{2,6},{3,7},{4,0},{5,1},{6,2},{7,3},{8,12},{9,13},{10,... | collective-permute-start | bytes 7077896 | tf_op jit(solution)/shard_map/ppermute | solution.py:938
  316.6 27.8 %collective-permute-start.44 = (bf16[4,480,768]{2,1,0:T(8,128)(2,1)}, bf16[4,480,768]{2,1,0:T(8,128)(2,1)}, u32[]{:S(2)}, u32[]{:S(2)}) collective-permute-start(bf16[4,480,768]{2,1,0:T(8,128)(2,1)} %get-tuple-element.169), channel_id=1, source_target_pairs={{0,4},{1,5},{2,6},{3,7},{4,0},{5,1},{6,2},{7,3},{8,12},{9,13},{10,... | collective-permute-start | bytes 8847368 | tf_op jit(solution)/shard_map/ppermute | solution.py:938
  342.0 32.3 %collective-permute-start.46 = (bf16[4,96,768]{2,1,0:T(8,128)(2,1)}, bf16[4,96,768]{2,1,0:T(8,128)(2,1)}, u32[]{:S(2)}, u32[]{:S(2)}) collective-permute-start(bf16[4,96,768]{2,1,0:T(8,128)(2,1)} %pad_maximum_fusion.6), channel_id=1, source_target_pairs={{0,16},{1,17},{2,18},{3,19},{4,20},{5,21},{6,22},{7,23},{8,24},{9,... | collective-permute-start | bytes 1769480 | tf_op jit(solution)/shard_map/ppermute | solution.py:938
  343.6 30.8 %collective-permute-start.45 = (bf16[4,96,768]{2,1,0:T(8,128)(2,1)}, bf16[4,96,768]{2,1,0:T(8,128)(2,1)}, u32[]{:S(2)}, u32[]{:S(2)}) collective-permute-start(bf16[4,96,768]{2,1,0:T(8,128)(2,1)} %pad_maximum_fusion.5), channel_id=1, source_target_pairs={{0,8},{1,9},{2,10},{3,11},{4,12},{5,13},{6,14},{7,15},{8,0},{9,1},... | collective-permute-start | bytes 1769480 | tf_op jit(solution)/shard_map/ppermute | solution.py:938
  348.6 27.2 %collective-permute-start.47 = (bf16[2,120,768]{2,1,0:T(8,128)(2,1)}, bf16[2,120,768]{2,1,0:T(8,128)(2,1)}, u32[]{:S(2)}, u32[]{:S(2)}) collective-permute-start(bf16[2,120,768]{2,1,0:T(8,128)(2,1)} %bitcast.75), channel_id=1, source_target_pairs={{0,8},{1,9},{2,10},{3,11},{4,12},{5,13},{6,14},{7,15},{8,0},{9,1},... | collective-permute-start | bytes 1105928 | tf_op jit(solution)/shard_map/ppermute | solution.py:938
  351.6 26.9 %collective-permute-start.48 = (bf16[2,120,768]{2,1,0:T(8,128)(2,1)}, bf16[2,120,768]{2,1,0:T(8,128)(2,1)}, u32[]{:S(2)}, u32[]{:S(2)}) collective-permute-start(bf16[2,120,768]{2,1,0:T(8,128)(2,1)} %bitcast.77), channel_id=1, source_target_pairs={{0,16},{1,17},{2,18},{3,19},{4,20},{5,21},{6,22},{7,23},{8,24},{9,... | collective-permute-start | bytes 1105928 | tf_op jit(solution)/shard_map/ppermute | solution.py:938
  405.3 35.7 %collective-permute-start.61 = (bf16[120,768]{1,0:T(8,128)(2,1)S(1)}, bf16[120,768]{1,0:T(8,128)(2,1)S(1)}, u32[]{:S(2)}, u32[]{:S(2)}) collective-permute-start(bf16[120,768]{1,0:T(8,128)(2,1)S(1)} %get-tuple-element.232), channel_id=1, source_target_pairs={{0,1},{1,2},{2,3},{3,0},{4,5},{5,6},{6,7},{7,4},{8,9},{9,10},{10,1... | collective-permute-start | bytes 552968 | tf_op jit(solution)/shard_map/ppermute | solution.py:946
  405.7 36.8 %collective-permute-start.62 = (bf16[120,768]{1,0:T(8,128)(2,1)S(1)}, bf16[120,768]{1,0:T(8,128)(2,1)}, u32[]{:S(2)}, u32[]{:S(2)}) collective-permute-start(bf16[120,768]{1,0:T(8,128)(2,1)S(1)} %get-tuple-element.234), channel_id=1, source_target_pairs={{0,2},{1,3},{2,0},{3,1},{4,6},{5,7},{6,4},{7,5},{8,10},{9,11},{10,... | collective-permute-start | bytes 552968 | tf_op jit(solution)/shard_map/ppermute | solution.py:946
  412.0 23.8 %collective-permute-start.56 = (bf16[4,80,768]{2,1,0:T(8,128)(2,1)}, bf16[4,80,768]{2,1,0:T(8,128)(2,1)S(1)}, u32[]{:S(2)}, u32[]{:S(2)}) collective-permute-start(bf16[4,80,768]{2,1,0:T(8,128)(2,1)} %fusion.15), channel_id=1, source_target_pairs={{0,16},{1,17},{2,18},{3,19},{4,20},{5,21},{6,22},{7,23},{8,24},{9,... | collective-permute-start | bytes 1474568 | tf_op jit(solution)/shard_map/ppermute | solution.py:938
  414.3 21.5 %collective-permute-start.57 = (bf16[4,80,768]{2,1,0:T(8,128)(2,1)}, bf16[4,80,768]{2,1,0:T(8,128)(2,1)}, u32[]{:S(2)}, u32[]{:S(2)}) collective-permute-start(bf16[4,80,768]{2,1,0:T(8,128)(2,1)} %fusion.16), channel_id=1, source_target_pairs={{0,24},{1,25},{2,26},{3,27},{4,28},{5,29},{6,30},{7,31},{8,16},{9,... | collective-permute-start | bytes 1474568 | tf_op jit(solution)/shard_map/ppermute | solution.py:938
  (82 other events, 870.9 us)
Sparse Core Ops, SparseCore 0:
  81.6 115.5 all-gather.1

commit v8 on v7

--- a/solution.py
+++ b/solution.py
@@ -87,12 +87,12 @@
     return grad_query, mm(score_grad, stack), mm(probs.astype(LOW), grad_stack)
 
 
-def slab_copies(place, pieces, slabs, sems, first_sem=0):
+def slab_copies(place, pieces, slabs, sems, first_sem=0, by_slab=False):
     count = len(slabs)
     half = (count + 1) // 2
     spans = [(0, 0, count), (2, 0, count), (4, 0, count)]
     spans += [(6, 0, count)] if len(pieces) == 8 else [(6, 0, half), (6, half, count)]
-    copies = []
+    copies = [[] for _ in slabs]
     for flip_c in (0, 1):
         for index, (flip_yx, first, last) in enumerate(spans):
             block = place ^ (flip_yx + flip_c)
@@ -100,8 +100,8 @@
             for slab in range(first, last):
                 source = piece.at[pl.ds((slab - first) * 96, 96)]
                 sem = sems.at[first_sem + slab * 8 + flip_yx + flip_c]
-                copies.append(pltpu.make_async_copy(source, slabs[slab](block), sem))
-    return copies
+                copies[slab].append(pltpu.make_async_copy(source, slabs[slab](block), sem))
+    return copies if by_slab else sum(copies, [])
 
 
 def load(copies):
@@ -109,6 +109,23 @@
         copy.start()
     for copy in copies:
         copy.wait()
+
+
+def never(*names):
+    pass
+
+
+def staged(groups):
+    for copies in groups.values():
+        for copy in copies:
+            copy.start()
+
+    def wait(*names):
+        for name in names:
+            for copy in groups[name]:
+                copy.wait()
+
+    return wait
 
 
 def rows_of(ref, block, rows=96, slab=None):
@@ -167,22 +184,32 @@
 
 def mid_forward_kernel(info, x_ref, mixed_ref, vec_ref, *rest):
     pieces, (sum_ref, low_ref, act_ref, slope_ref, out, up, sems) = rest[:10], rest[10:]
-
-    @pl.when(pl.program_id(0) == 0)
-    def _():
-        load(slab_copies(info[0], pieces, mid_slabs(out, up), sems))
-
-    summed = x_ref[...].astype(F32) + mm(mixed_ref[...], out[...]) + vec_ref[2:3, :]
-    sum_ref[...] = summed
-    first_low = norm_one(summed, vec_ref).astype(LOW)
-    low_ref[...] = first_low
-    hidden = mm(first_low, up[0]) + vec_ref[5:6, :]
-    for j in range(4):
-        later = mm(first_low, up[j + 1]) + vec_ref[6 + j : 7 + j, :] if j < 3 else None
-        act, slope = gelu_parts(hidden)
-        act_ref[:, j * 768 : (j + 1) * 768] = act.astype(LOW)
-        slope_ref[:, j * 768 : (j + 1) * 768] = slope.astype(LOW)
-        hidden = later
+    step = pl.program_id(0)
+
+    def body(wait):
+        wait("out")
+        summed = x_ref[...].astype(F32) + mm(mixed_ref[...], out[...]) + vec_ref[2:3, :]
+        sum_ref[...] = summed
+        first_low = norm_one(summed, vec_ref).astype(LOW)
+        low_ref[...] = first_low
+        wait("up0")
+        hidden = mm(first_low, up[0]) + vec_ref[5:6, :]
+        for j in range(4):
+            if j < 3:
+                wait(f"up{j + 1}")
+                later = mm(first_low, up[j + 1]) + vec_ref[6 + j : 7 + j, :]
+            act, slope = gelu_parts(hidden)
+            act_ref[:, j * 768 : (j + 1) * 768] = act.astype(LOW)
+            slope_ref[:, j * 768 : (j + 1) * 768] = slope.astype(LOW)
+            hidden = later
+
+    @pl.when(step == 0)
+    def _():
+        body(staged(mid_groups(info[0], pieces, out, up, sems)))
+
+    @pl.when(step > 0)
+    def _():
+        body(never)
 
 
 def down_forward_kernel(segs, info, sum_ref, act_ref, vec_ref, *rest):
@@ -199,10 +226,11 @@
     heads_ref[...] = normed * (1.0 + vec_ref[10:11, :]) + vec_ref[11:12, :]
 
 
-def cross_kernel(blocks, info, heads_ref, up_ref, live_ref, vec_ref, pos_ref, *rest):
-    wide, rest = rest[0], rest[1:]
-    (own_ref, own_grad_ref, grads_ref, pos_grad_ref, qkv_grad_ref, out_grad_ref, up_grad_ref, down_grad_ref) = rest[:8]
-    (qkv, out, up, down, sems, result, heads_grad, slope, lefts, act, packed, rights, hidden_grad) = rest[8:]
+def cross_kernel(blocks, segs, seg_count, info, heads_ref, up_ref, live_ref, vec_ref, pos_ref, seg_vec_ref, *rest):
+    wide, tops_in, sources, mid, more, rest = rest[0], rest[1:6], rest[6:9], rest[9:19], rest[19:27], rest[27:]
+    grads_ref, pos_grad_ref, qkv_grad_ref, out_grad_ref, up_grad_ref, down_grad_ref, seg_grads_ref, *tops_out = rest[:12]
+    (qkv, out, up, down, sems, result, heads_grad, slope, lefts, act, packed, rights, hidden_grad) = rest[12:25]
+    tops, parts, own_hidden, weights, (seg_sems, top_sems) = rest[25:30], rest[30:33], rest[33], rest[34:37], rest[37:]
     step = pl.program_id(0)
     count = heads_ref.shape[0]
     at = pl.ds(pl.multiple_of(step * count, count), count)
@@ -214,6 +242,7 @@
     def _():
         for copy in copies:
             copy.start()
+        staged(opening_groups(info[0], tops_in, sources, mid, more, tops, parts, weights, seg_sems, top_sems))
         grads_ref[...] = jnp.zeros_like(grads_ref)
         pos_grad_ref[...] = jnp.zeros_like(pos_grad_ref)
         for copy in copies[:3]:
@@ -305,8 +334,16 @@
     def _():
         me = info[1]
         own = pl.ds(pl.multiple_of(me * 16, 16), 16)
-        own_ref[...] = result[own, :]
-        own_grad_ref[...] = heads_grad[own, :]
+        groups = opening_groups(info[0], tops_in, sources, mid, more, tops, parts, weights, seg_sems, top_sems)
+
+        def wait(*names):
+            for name in names:
+                for copy in groups[name]:
+                    copy.wait()
+
+        lengths = [info[2 + i] for i in range(segs // seg_count)]
+        opening_rows(segs, seg_count, lengths, result[own, :], heads_grad[own, :], seg_vec_ref, tops_out,
+                     seg_grads_ref, tops, parts, own_hidden, weights, top_sems, wait)
 
         def chosen(left, rows):
             width = left.shape[1]
@@ -333,7 +370,7 @@
     return jnp.sum(value.astype(F32), axis=0, keepdims=True)
 
 
-def ffn_back_rows(upstream, second, summed, slope, vec, grads_ref, hidden_grad, out, up, down):
+def ffn_back_rows(upstream, second, summed, slope, vec, grads_ref, hidden_grad, out, up, down, wait):
     normed, inv_scale = normalize(second)
     back_two = normalize_back(upstream * (1.0 + vec[10:11, :]), normed, inv_scale)
     down_grad = back_two.astype(LOW)
@@ -341,12 +378,15 @@
     grads_ref[10:11, :] += column_sum(upstream * normed)
     grads_ref[11:12, :] += column_sum(upstream)
     total = back_two
+    wait("down")
     for j in range(4):
         cols = slice(j * 768, (j + 1) * 768)
         grad = (mm_nt(down_grad, down[cols, :]) * slope(cols).astype(F32)).astype(LOW)
         hidden_grad(cols, grad)
         grads_ref[5 + j : 6 + j, :] += column_sum(grad)
+        wait(f"up{j}")
         total = total + mm_nt(grad, up[j])
+    wait("out")
     normed, inv_scale = normalize(summed)
     back_one = normalize_back(total * (1.0 + vec[3:4, :]), normed, inv_scale)
     proj_grad = back_one.astype(LOW)
@@ -356,8 +396,16 @@
     return down_grad, proj_grad, mm_nt(proj_grad, out[...]).astype(LOW)
 
 
-def load_ffn(place, mid, rest, out, up, down, sems):
-    return slab_copies(place, rest, down_slabs(down), sems, 40) + slab_copies(place, mid, mid_slabs(out, up), sems)
+def mid_groups(place, mid, out, up, sems):
+    copies = slab_copies(place, mid, mid_slabs(out, up), sems, by_slab=True)
+    groups = {f"up{j}": copies[j + 1] for j in range(4)}
+    return {"out": copies[0], **groups}
+
+
+def ffn_groups(place, mid, rest, out, up, down, sems):
+    groups = mid_groups(place, mid, out, up, sems)
+    last = groups.pop("out")
+    return {"down": slab_copies(place, rest, down_slabs(down), sems, 40), **groups, "out": last}
 
 
 def ffn_backward_kernel(segs, seg_count, first_step, info, cot_ref, second_ref, sum_ref, slope_ref, vec_ref, *rest):
@@ -365,55 +413,64 @@
     out_ref, down_grad_ref, hidden_grad_ref, proj_grad_ref, mixed_grad_ref, grads_ref, out, up, down, sems = rest
     step = pl.program_id(0)
 
+    def body(wait):
+        second = second_ref[...]
+        normed, _ = normalize(second)
+        result = normed * (1.0 + vec_ref[10:11, :]) + vec_ref[11:12, :]
+        row = lax.broadcasted_iota(jnp.int32, (SEG, 1), 0)
+        ups = []
+        for s in range(segs):
+            seg = (step + first_step) * segs + s
+            at = slice(s * SEG, (s + 1) * SEG)
+            live = row + seg % seg_count * SEG < info[1 + seg // seg_count]
+            out_ref[at, :] = jnp.where(live, result[at], 0.0).astype(LOW)
+            ups.append(jnp.where(live & (row > 0), cot_ref[at, :].astype(F32), 0.0))
+
+        def store(cols, grad):
+            hidden_grad_ref[:, cols] = grad
+
+        down_grad_ref[...], proj_grad_ref[...], mixed_grad_ref[...] = ffn_back_rows(
+            jnp.concatenate(ups, axis=0), second, sum_ref[...], lambda cols: slope_ref[:, cols], vec_ref, grads_ref,
+            store, out, up, down, wait,
+        )
+
     @pl.when(step == 0)
     def _():
-        load(load_ffn(info[0], mid, more, out, up, down, sems))
+        wait = staged(ffn_groups(info[0], mid, more, out, up, down, sems))
         grads_ref[...] = jnp.zeros_like(grads_ref)
-
-    second = second_ref[...]
-    normed, _ = normalize(second)
-    result = normed * (1.0 + vec_ref[10:11, :]) + vec_ref[11:12, :]
-    row = lax.broadcasted_iota(jnp.int32, (SEG, 1), 0)
-    ups = []
-    for s in range(segs):
-        seg = (step + first_step) * segs + s
-        at = slice(s * SEG, (s + 1) * SEG)
-        live = row + seg % seg_count * SEG < info[1 + seg // seg_count]
-        out_ref[at, :] = jnp.where(live, result[at], 0.0).astype(LOW)
-        ups.append(jnp.where(live & (row > 0), cot_ref[at, :].astype(F32), 0.0))
-
-    def store(cols, grad):
-        hidden_grad_ref[:, cols] = grad
-
-    down_grad_ref[...], proj_grad_ref[...], mixed_grad_ref[...] = ffn_back_rows(
-        jnp.concatenate(ups, axis=0), second, sum_ref[...], lambda cols: slope_ref[:, cols], vec_ref, grads_ref, store,
-        out, up, down,
-    )
-
-
-def opening_kernel(segs, seg_count, info, heads_ref, heads_grad_ref, vec_ref, *rest):
-    tops_in, sources, mid, more, rest = rest[:5], rest[5:8], rest[8:18], rest[18:26], rest[26:]
-    tops_out, grads_ref, tops, parts, hidden = rest[:5], rest[5], rest[6:11], rest[11:14], rest[14]
-    out, up, down, sems, top_sems = rest[15:]
-    copies = load_ffn(info[0], mid, more, out, up, down, sems)
-    for i, (source, target) in enumerate(zip((*tops_in, *sources), (*tops, *parts))):
-        copies.append(pltpu.make_async_copy(source.at[:, 0 : target.shape[1], :], target, top_sems.at[i]))
-    load(copies)
+        body(wait)
+
+    @pl.when(step > 0)
+    def _():
+        body(never)
+
+
+def opening_groups(place, tops_in, sources, mid, more, tops, parts, weights, sems, top_sems):
+    pairs = zip((*tops_in, *sources), (*tops, *parts))
+    copies = [
+        pltpu.make_async_copy(source.at[:, 0 : target.shape[1], :], target, top_sems.at[i])
+        for i, (source, target) in enumerate(pairs)
+    ]
+    return {"tops": copies, **ffn_groups(place, mid, more, *weights, sems)}
+
+
+def opening_rows(segs, seg_count, lengths, heads, heads_grad, vec_ref, tops_out, grads_ref, tops, parts, hidden, weights, top_sems, wait):
+    wait("tops")
     grads_ref[...] = jnp.zeros_like(grads_ref)
-    second, summed, slope = (part[:, 0, :] if part.shape[1] == 8 else part for part in parts)
-    slope = slope[...].astype(F32)[:, 0, :]
+    second, summed = parts[0][:, 0, :], parts[1][:, 0, :]
+    slope = parts[2][...].astype(F32)[:, 0, :]
 
     def store(cols, grad):
         hidden[:, cols] = grad.astype(F32)
 
     down_grad, proj_grad, mixed_grad = ffn_back_rows(
-        heads_grad_ref[...], second, summed, lambda cols: slope[:, cols], vec_ref, grads_ref, store, out, up, down
+        heads_grad, second, summed, lambda cols: slope[:, cols], vec_ref, grads_ref, store, *weights, wait
     )
     seg = lax.broadcasted_iota(jnp.int32, (segs, 1), 0)
-    length = jnp.full((segs, 1), info[1], jnp.int32)
-    for i in range(1, segs // seg_count):
-        length = jnp.where(seg >= i * seg_count, info[1 + i], length)
-    merged = jnp.where(lax.rem(seg, seg_count) * SEG < length, heads_ref[...], 0.0)
+    length = jnp.full((segs, 1), lengths[0], jnp.int32)
+    for i in range(1, len(lengths)):
+        length = jnp.where(seg >= i * seg_count, lengths[i], length)
+    merged = jnp.where(lax.rem(seg, seg_count) * SEG < length, heads, 0.0)
     outs = []
     values = (merged, down_grad.astype(F32), hidden[...], proj_grad.astype(F32), mixed_grad.astype(F32))
     for i, (value, top) in enumerate(zip(values, tops)):
@@ -421,6 +478,16 @@
         top[...] = jnp.where(row == 0, value[:, None, :], top[...].astype(F32)).astype(LOW)
         outs.append(pltpu.make_async_copy(top, tops_out[i].at[:, 0:16, :], top_sems.at[i]))
     load(outs)
+
+
+def opening_kernel(segs, seg_count, info, heads_ref, heads_grad_ref, vec_ref, *rest):
+    tops_in, sources, mid, more, rest = rest[:5], rest[5:8], rest[8:18], rest[18:26], rest[26:]
+    tops_out, grads_ref, tops, parts, hidden = rest[:5], rest[5], rest[6:11], rest[11:14], rest[14]
+    *weights, sems, top_sems = rest[15:]
+    wait = staged(opening_groups(info[0], tops_in, sources, mid, more, tops, parts, weights, sems, top_sems))
+    lengths = [info[1 + i] for i in range(segs // seg_count)]
+    opening_rows(segs, seg_count, lengths, heads_ref[...], heads_grad_ref[...], vec_ref, tops_out, grads_ref, tops,
+                 parts, hidden, weights, top_sems, wait)
 
 
 def attn_backward_kernel(segs, seg_count, first_step, info, packed_ref, mixed_grad_ref, *rest):
@@ -583,26 +650,40 @@
     )(info, summed, act, vec, *pieces)
 
 
-def cross_whole(info, heads, upstream, live, vec, positions, wide):
+def grouped(array):
+    return array.reshape(-1, SEG, array.shape[1])
+
+
+def top_scratch(segs, arrays):
+    tops = [pltpu.VMEM((segs, 16, a.shape[2]), LOW) for a in arrays]
+    parts = [pltpu.VMEM((segs, 8, 768), F32)] * 2 + [pltpu.VMEM((segs, 16, 3072), LOW)]
+    return tops + parts + [pltpu.VMEM((segs, 3072), F32)] + MID + DOWN + sems(72) + sems(8)
+
+
+def cross_whole(info, heads, upstream, live, vec, positions, wide, seg_vec, arrays, sources, mid, more, seg_count):
     rows = heads.shape[0]
     count = 2 * SEG
-    own = [(16, 768), (16, 768), (12, 768), (8, 768), (24, 2304), (24, 768), (24, 3072), (96, 768)]
-    return pl.pallas_call(
-        functools.partial(cross_kernel, rows // count),
+    arrays, sources = [grouped(a) for a in arrays], [grouped(a) for a in sources]
+    segs = arrays[0].shape[0]
+    own = [(12, 768), (8, 768), (24, 2304), (24, 768), (24, 3072), (96, 768), (12, 768)]
+    *grads, seg_grads, layer, down, hidden, proj, mixed = pl.pallas_call(
+        functools.partial(cross_kernel, rows // count, segs, seg_count),
         grid=(rows // count,),
         in_specs=[SMEM, block_rows(count, 768), block_rows(count, 768), block_rows(count, SEG),
-                  fixed((12, 768)), fixed((8, 768)), ANY],
-        out_specs=[fixed(dims) for dims in own],
-        out_shape=[shape_of(dims, F32) for dims in own],
+                  fixed((12, 768)), fixed((8, 768)), fixed((12, 768))] + [ANY] * 27,
+        out_specs=[fixed(dims) for dims in own] + [ANY] * 5,
+        out_shape=[shape_of(dims, F32) for dims in own] + [shape_of(a.shape) for a in arrays],
         scratch_shapes=QKV + MID + DOWN + sems(12) + [
             pltpu.VMEM((rows, 768), F32), pltpu.VMEM((rows, 768), F32), pltpu.VMEM((count, 3072), LOW),
             pltpu.VMEM((3, rows, 768), LOW), pltpu.VMEM((rows, 3072), LOW), pltpu.VMEM((count, 2304), LOW),
             pltpu.VMEM((5, rows, 768), LOW), pltpu.VMEM((rows, 3072), LOW),
-        ],
+        ] + top_scratch(segs, arrays),
+        input_output_aliases={8 + i: 7 + i for i in range(5)},
         compiler_params=params(),
         cost_estimate=cost(2 * rows * 768 * 30000, 2**24),
         name="cross_encoder",
-    )(info, heads, upstream, live, vec, positions, wide)
+    )(info, heads, upstream, live, vec, positions, seg_vec, wide, *arrays, *sources, *mid, *more)
+    return grads, seg_grads, [a.reshape(-1, a.shape[2]) for a in (layer, down, hidden, proj, mixed)]
 
 
 def ffn_backward(info, cotangent, second, summed, slope, vec, mid, down, seg_count, half, before=None, segs=2):
@@ -629,10 +710,6 @@
 
 def opening_backward(info, heads, heads_grad, vec, arrays, sources, mid, down, seg_count):
     segs = heads.shape[0]
-
-    def grouped(array):
-        return array.reshape(segs, SEG, array.shape[1])
-
     arrays, sources = [grouped(a) for a in arrays], [grouped(a) for a in sources]
     whole = fixed((segs, 768))
     *done, grads = pl.pallas_call(
@@ -641,10 +718,7 @@
         in_specs=[SMEM, whole, whole, fixed((12, 768))] + [ANY] * 26,
         out_specs=[ANY] * 5 + [fixed((12, 768))],
         out_shape=[shape_of(a.shape) for a in arrays] + [shape_of((12, 768), F32)],
-        scratch_shapes=[pltpu.VMEM((segs, 16, a.shape[2]), LOW) for a in arrays]
-        + [pltpu.VMEM((segs, 8, 768), F32)] * 2
-        + [pltpu.VMEM((segs, 16, 3072), LOW), pltpu.VMEM((segs, 3072), F32)]
-        + MID + DOWN + sems(72) + sems(8),
+        scratch_shapes=top_scratch(segs, arrays),
         input_output_aliases={4 + i: i for i in range(5)},
         compiler_params=params(),
         cost_estimate=cost(2**33, 2**24),
@@ -1204,10 +1278,11 @@
     heads_all, up_all = both[:, 0].reshape(-1, feat_dim), both[:, 1].reshape(-1, feat_dim)
     live_all = seg_starts[None, :] < lengths[:, None]
     if fast:
-        cross_info = jnp.stack([links.place, me]).astype(jnp.int32)
+        cross_info = jnp.concatenate([jnp.stack([links.place, me]).astype(jnp.int32), my_lengths])
         live = jnp.broadcast_to(live_all.reshape(-1, 1), (live_all.size, SEG)).astype(F32)
-        cross_own, heads_grad, vec_grad, pos_grad, *cross_grads = cross_whole(
-            cross_info, heads_all, up_all, live, cross_v, pos_table, wide
+        (vec_grad, pos_grad, *cross_grads), grads_more, arrays = cross_whole(
+            cross_info, heads_all, up_all, live, cross_v, pos_table, wide,
+            seg_v, arrays, (second, summed, slope), mid, down, seg_count,
         )
     else:
         weights = (matrix_of(wide[:3]), wide[3], matrix_of(wide[4:8]), wide[8:].reshape(-1, feat_dim), cross_v)
@@ -1228,12 +1303,11 @@
         heads_grad = lax.dynamic_slice_in_dim(all_grad, me * own, own)
         first_half = back(after(cot_rows, heads_grad, *cross_grads), *args, half=0)
         *arrays, grads_two = back(cot_rows, *args, half=1, before=first_half[:5])
-    grads_two = grads_two + first_half[5]
-    arrays, grads_more = opening_backward(
-        info, cross_own, heads_grad, seg_v, arrays, (second, summed, slope), mid, down, seg_count
-    )
+        arrays, grads_more = opening_backward(
+            info, cross_own, heads_grad, seg_v, arrays, (second, summed, slope), mid, down, seg_count
+        )
     layer_out, down_grad, hidden_grad, proj_grad, mixed_grad = arrays
-    grads_two = grads_two + grads_more
+    grads_two = grads_two + first_half[5] + grads_more
     down_sum = summing(links, *down_weight_grad(info, act, down_grad), 1)
     mid_parts = mid_weight_grad(info, mixed, proj_grad, low, after(hidden_grad, down_sum.keep if fast else down_sum.came))
     mid_sum = summing(links, *mid_parts, 5)

time: 469 us -> 463 us (0.987)
    pallas_call x2 -> x1, Pallas kernels: 52.6 us -> 50.9 us  [cross_whole(): pl.pallas_call(functools.partial(cross_kernel, rows // count, segs, seg_c...]
  transfers between devices with their start and end apart: 65 -> 65, of which waited for: 13 -> 13; matrix products, arithmetic and copies ran while one was open for 14% -> 13% of each run, Pallas kernels for 44% -> 45%
where the time goes in v8:
time: 463 us; the launch traced here: 458 us
  Pallas kernels  272 us (59%)
  starting transfers between devices  75.3 us (16%)
  local copies, waits for them, and re-layouts  37.1 us (8%)
  other arithmetic  31.8 us (7%)
  waiting for transfers between devices  25.7 us (6%)
  between operations  15.7 us (3%)
    pallas_call x1, Pallas kernels, cross_whole(): pl.pallas_call(functools.partial(cross_kernel, rows // count, segs, seg_c...  50.9 us
    pallas_call x2, Pallas kernels, ffn_backward(): pl.pallas_call(functools.partial(ffn_backward_kernel, segs, seg_count, fi...  48.9 us
    ppermute x21, starting transfers between devices, turn(): return lax.ppermute(value, AXES, pairs)  43.6 us
    pallas_call x2, Pallas kernels, attn_backward(): pl.pallas_call(functools.partial(attn_backward_kernel, segs, seg_count, f...  34.5 us
    ppermute x43, starting transfers between devices, flip(): return lax.ppermute(value, AXES, pairs)  31.6 us
    pallas_call x1, Pallas kernels, mid_forward(): pl.pallas_call(mid_forward_kernel, grid=(rows // count,), in_specs=[SMEM,...  29.7 us
    pallas_call x2, Pallas kernels, attn_forward(): pl.pallas_call(functools.partial(attn_forward_kernel, segs, seg_count, fi...  26.1 us
    pallas_call x1, Pallas kernels, mid_weight_grad(): pl.pallas_call(mid_grad_kernel, grid=(5,), in_specs=[SMEM, still, still,...  19.8 us
  transfers between devices with their start and end apart: 65, of which 13 were waited for; matrix products, arithmetic and copies ran while one was open for 13% of the time, Pallas kernels for 45%

profile of v8, /device:TPU:0, one launch (start us, length us, event | category | flops | bytes accessed | tf_op | source)
XLA Modules:
  0.0 457.5 jit_solution(3043910766188778078)
XLA Ops:
  9.0 4.1 collective-permute-start
  17.0 5.6 %collective-permute-done = bf16[80,768]{1,0:T(8,128)(2,1)S(1)} collective-permute-done((bf16[80,768]{1,0:T(8,128)(2,1)S(1)}, bf16[80,768]{1,0:T(8,128)(2,1)S(1)}, u32[]{:S(2)}, u32[]{:S(2)}) %collective-permute-start) | collective-permute-done | bytes 122912 | tf_op jit(solution)/shard_map/ppermute | solution.py:1020
  27.7 3.7 collective-permute-start.3
  31.4 3.8 collective-permute-start.5
  40.7 3.1 collective-permute-done.3
  52.9 6.8 %collective-permute-start.24 = (bf16[96,768]{1,0:T(8,128)(2,1)S(1)}, bf16[96,768]{1,0:T(8,128)(2,1)S(1)}, u32[]{:S(2)}, u32[]{:S(2)}) collective-permute-start(bf16[96,768]{1,0:T(8,128)(2,1)S(1)} %copy-done.8), channel_id=1, source_target_pairs={{0,2},{1,3},{2,0},{3,1},{4,6},{5,7},{6,4},{7,5},{8,10},{9,11},{10,... | collective-permute-start | bytes 442376 | tf_op jit(solution)/shard_map/ppermute | solution.py:1020
  59.6 4.0 collective-permute-start.26
  66.6 13.0 %attn_forward.2 = (bf16[2048,2304]{1,0:T(8,128)(2,1)}, bf16[2048,768]{1,0:T(8,128)(2,1)}) custom-call(s32[3]{0:T(128)} %pad_add_fusion.1.info, bf16[2048,768]{1,0:T(8,128)(2,1)} %bitcast.288, f32[12,768]{1,0:T(8,128)} %slice.371.vec_ref.seg_vec_ref, bf16[304,768]{1,0:T(8,128)(2,1)} %fusion.17.rest_0_, bf16[304,768]{1,0:T(8,128)(2,1)} %collective-permute-done.8.rest_1_, ...), custom_call_target="tpu_custom_call" | custom-call | flops 12582912000 | bytes 12582912 | tf_op jit(solution)/shard_map/attn_forward/pallas_call | solution.py:606
  83.7 13.2 %attn_forward.3 = (bf16[2048,2304]{1,0:T(8,128)(2,1)}, bf16[2048,768]{1,0:T(8,128)(2,1)}) custom-call(s32[3]{0:T(128)} %pad_add_fusion.1.info, bf16[2048,768]{1,0:T(8,128)(2,1)} %bitcast.289, f32[12,768]{1,0:T(8,128)} %slice.371.vec_ref.seg_vec_ref, bf16[304,768]{1,0:T(8,128)(2,1)} %fusion.17.rest_0_, ...), custom_call_target="tpu_custom_call", output_to_operand_aliasing={{0}: (13, {}), {1}: (14, {})} | custom-call | flops 12582912000 | bytes 12582912 | tf_op jit(solution)/shard_map/attn_forward/pallas_call | solution.py:606
  104.4 29.7 %mid_forward.1 = (f32[2048,768]{1,0:T(8,128)}, bf16[2048,768]{1,0:T(8,128)(2,1)}, bf16[2048,3072]{1,0:T(8,128)(2,1)}, bf16[2048,3072]{1,0:T(8,128)(2,1)}) custom-call(s32[3]{0:T(128)} %pad_add_fusion.1.info, bf16[2048,768]{1,0:T(8,128)(2,1)} %bitcast.290, bf16[2048,768]{1,0:T(8,128)(2,1)} %get-tuple-element.126.mixed_ref, ...), custom_call_target="tpu_custom_call" | custom-call | flops 25165824000 | bytes 47185920 | tf_op jit(solution)/shard_map/mid_forward/pallas_call | solution.py:623
  136.2 5.5 %collective-permute-done.27.rest_1_.rest_11_.rest_20_ = bf16[384,768]{1,0:T(8,128)(2,1)} collective-permute-done((bf16[384,768]{1,0:T(8,128)(2,1)S(1)}, bf16[384,768]{1,0:T(8,128)(2,1)}, u32[]{:S(2)}, u32[]{:S(2)}) %collective-permute-start.27) | collective-permute-done | bytes 589856 | tf_op jit(solution)/shard_map/ppermute | solution.py:1012
  144.1 19.3 %down_forward.1 = (f32[2048,768]{1,0:T(8,128)}, f32[8,2,768]{2,1,0:T(2,128)}) custom-call(s32[3]{0:T(128)} %pad_add_fusion.1.info, f32[2048,768]{1,0:T(8,128)} %get-tuple-element.133.sum_ref, bf16[2048,3072]{1,0:T(8,128)(2,1)} %get-tuple-element.134.act_ref.left_ref, f32[12,768]{1,0:T(8,128)} %slice.371.vec_ref.seg_vec_ref, bf16[384,768]{1,0:T(8,128)(2,1)} %copy-done.6, ...), custom_call_target="tpu_custom_call" | custom-call | flops 12582912000 | bytes 25165824 | tf_op jit(solution)/shard_map/down_forward/pallas_call | solution.py:640
  168.2 24.6 %ffn_backward.2 = (bf16[2048,768]{1,0:T(8,128)(2,1)}, bf16[2048,768]{1,0:T(8,128)(2,1)}, bf16[2048,3072]{1,0:T(8,128)(2,1)}, bf16[2048,768]{1,0:T(8,128)(2,1)}, ...) custom-call(s32[3]{0:T(128)} %pad_add_fusion.1.info, bf16[2048,768]{1,0:T(8,128)(2,1)} %bitcast.286, ...), custom_call_target="tpu_custom_call" | custom-call | flops 22020096000 | bytes 23592960 | tf_op jit(solution)/shard_map/ffn_backward/pallas_call | solution.py:696
  196.4 24.3 %ffn_backward.3 = (bf16[2048,768]{1,0:T(8,128)(2,1)}, bf16[2048,768]{1,0:T(8,128)(2,1)}, bf16[2048,3072]{1,0:T(8,128)(2,1)}, bf16[2048,768]{1,0:T(8,128)(2,1)}, ...) custom-call(s32[3]{0:T(128)} %pad_add_fusion.1.info, ...), custom_call_target="tpu_custom_call", output_to_operand_aliasing={{0}: (24, {}), {1}: (25, {}), {2}: (26, {}), {3}: (27, {}),... | custom-call | flops 22020096000 | bytes 23592960 | tf_op jit(solution)/shard_map/ffn_backward/pallas_call | solution.py:696
  226.8 50.9 %cross_encoder.1 = (f32[12,768]{1,0:T(8,128)}, f32[8,768]{1,0:T(8,128)}, f32[24,2304]{1,0:T(8,128)}, f32[24,768]{1,0:T(8,128)}, f32[24,3072]{1,0:T(8,128)}, /*in...) custom-call(s32[4]{0:T(128)} %pad_add_fusion.info, ...), custom_call_target="tpu_custom_call", output_to_operand_aliasing={{7}: (8, {}), {8}: (9, {}), {9}: (10, {}), {10}: (11, {}), ... | custom-call | flops 23592960000 | bytes 16777216 | tf_op jit(solution)/shard_map/cross_encoder/pallas_call | solution.py:669
  277.7 16.1 %down_weight_grad.1 = (bf16[4,384,768]{2,1,0:T(8,128)(2,1)}, bf16[4,384,768]{2,1,0:T(8,128)(2,1)}) custom-call(s32[3]{0:T(128)} %pad_add_fusion.1.info, bf16[2048,3072]{1,0:T(8,128)(2,1)} %get-tuple-element.134.act_ref.left_ref, bf16[2048,768]{1,0:T(8,128)(2,1)} %bitcast.301), custom_call_target="tpu_custom_call" | custom-call | flops 9663676416 | bytes 12582912 | tf_op jit(solution)/shard_map/down_weight_grad/pallas_call | solution.py:816
  294.2 19.8 %mid_weight_grad.1 = (bf16[4,480,768]{2,1,0:T(8,128)(2,1)}, bf16[4,480,768]{2,1,0:T(8,128)(2,1)}) custom-call(s32[3]{0:T(128)} %pad_add_fusion.1.info, bf16[2048,768]{1,0:T(8,128)(2,1)} %get-tuple-element.126.mixed_ref, bf16[2048,768]{1,0:T(8,128)(2,1)} %bitcast.303, bf16[2048,768]{1,0:T(8,128)(2,1)} %get-tuple-element.160.low_ref, bf16[2048,3072]{1,0:T(8,128)(2,1)} %bitcast.294), custom_call_target="tpu_custom_call" | custom-call | flops 12079595520 | bytes 15728640 | tf_op jit(solution)/shard_map/mid_weight_grad/pallas_call | solution.py:789
  314.7 2.8 convert_add_fusion.1
  321.0 17.3 %attn_backward.2 = (bf16[2048,2304]{1,0:T(8,128)(2,1)}, f32[2,768]{1,0:T(2,128)}) custom-call(s32[3]{0:T(128)} %pad_add_fusion.1.info, bf16[2048,2304]{1,0:T(8,128)(2,1)} %get-tuple-element.130.packed_ref, bf16[2048,768]{1,0:T(8,128)(2,1)} %bitcast.306), custom_call_target="tpu_custom_call" | custom-call | flops 15728640000 | bytes 12582912 | tf_op jit(solution)/shard_map/attn_backward/pallas_call | solution.py:736
  350.4 17.1 %attn_backward.3 = (bf16[2048,2304]{1,0:T(8,128)(2,1)}, f32[2,768]{1,0:T(2,128)}) custom-call(s32[3]{0:T(128)} %pad_add_fusion.1.info, bf16[2048,2304]{1,0:T(8,128)(2,1)} %get-tuple-element.130.packed_ref, bf16[2048,768]{1,0:T(8,128)(2,1)} %bitcast.307, bf16[2048,2304]{1,0:T(8,128)(2,1)} %get-tuple-element.168.rest_0_), custom_call_target="tpu_custom_call", output_to_operand_aliasing={{0}: (3, {})} | custom-call | flops 15728640000 | bytes 12582912 | tf_op jit(solution)/shard_map/attn_backward/pallas_call | solution.py:736
  380.5 2.8 collective-permute-start.51
  383.4 13.2 %qkv_weight_grad.1 = (bf16[4,304,768]{2,1,0:T(8,128)(2,1)}, bf16[4,304,768]{2,1,0:T(8,128)(2,1)}) custom-call(s32[3]{0:T(128)} %pad_add_fusion.1.info, bf16[2048,768]{1,0:T(8,128)(2,1)} %bitcast.291, bf16[2048,2304]{1,0:T(8,128)(2,1)} %get-tuple-element.180.right_ref.packed_grad_ref, bf16[8,16,768]{2,1,0:T(8,128)(2,1)} %copy-done.21), custom_call_target="tpu_custom_call" | custom-call | flops 7247757312 | bytes 9437184 | tf_op jit(solution)/shard_map/qkv_weight_grad/pallas_call | solution.py:772
  412.4 13.7 %token_gradient.1 = bf16[2048,768]{1,0:T(8,128)(2,1)} custom-call(s32[3]{0:T(128)} %pad_add_fusion.1.info, bf16[2048,2304]{1,0:T(8,128)(2,1)} %get-tuple-element.180.right_ref.packed_grad_ref, bf16[2048,768]{1,0:T(8,128)(2,1)} %bitcast.304, bf16[304,768]{1,0:T(8,128)(2,1)} %fusion.17.rest_0_, bf16[304,768]{1,0:T(8,128)(2,1)} %collective-permute-done.8.rest_1_, ...), custom_call_target="tpu_custom_call" | custom-call | flops 9437184000 | bytes 15728640 | tf_op jit(solution)/shard_map/token_gradient/pallas_call | solution.py:751
  426.2 3.0 collective-permute-start.63
  (352 shorter events, 124.5 us)
Async XLA Ops:
  7.2 218.8 %all-gather.2.cloned.1.call-start = ((), (), s32[]{:S(2)}) async-start(), calls=%async_computation | async-start | bytes 14598144 | tf_op jit(solution)/shard_map/all_gather | solution.py:1252
  51.1 28.7 %collective-permute-start.10 = (bf16[480,768]{1,0:T(8,128)(2,1)S(1)}, bf16[480,768]{1,0:T(8,128)(2,1)}, u32[]{:S(2)}, u32[]{:S(2)}) collective-permute-start(bf16[480,768]{1,0:T(8,128)(2,1)S(1)} %bitcast.252), channel_id=1, source_target_pairs={{0,8},{1,9},{2,10},{3,11},{4,12},{5,13},{6,14},{7,15},{8,0},{9,1},... | collective-permute-start | bytes 2211848 | tf_op jit(solution)/shard_map/ppermute | solution.py:1012
  51.6 28.1 %collective-permute-start.11 = (bf16[480,768]{1,0:T(8,128)(2,1)S(1)}, bf16[480,768]{1,0:T(8,128)(2,1)}, u32[]{:S(2)}, u32[]{:S(2)}) collective-permute-start(bf16[480,768]{1,0:T(8,128)(2,1)S(1)} %bitcast.253), channel_id=1, source_target_pairs={{0,16},{1,17},{2,18},{3,19},{4,20},{5,21},{6,22},{7,23},{8,24},{9,... | collective-permute-start | bytes 2211848 | tf_op jit(solution)/shard_map/ppermute | solution.py:1012
  52.9 26.7 %collective-permute-start.24 = (bf16[96,768]{1,0:T(8,128)(2,1)S(1)}, bf16[96,768]{1,0:T(8,128)(2,1)S(1)}, u32[]{:S(2)}, u32[]{:S(2)}) collective-permute-start(bf16[96,768]{1,0:T(8,128)(2,1)S(1)} %copy-done.8), channel_id=1, source_target_pairs={{0,2},{1,3},{2,0},{3,1},{4,6},{5,7},{6,4},{7,5},{8,10},{9,11},{10,... | collective-permute-start | bytes 442376 | tf_op jit(solution)/shard_map/ppermute | solution.py:1020
  100.8 33.2 %collective-permute-start.29 = (bf16[384,768]{1,0:T(8,128)(2,1)S(1)}, bf16[384,768]{1,0:T(8,128)(2,1)S(1)}, u32[]{:S(2)}, u32[]{:S(2)}) collective-permute-start(bf16[384,768]{1,0:T(8,128)(2,1)S(1)} %pad_maximum_fusion.4.rest_0_.rest_10_.rest_19_), channel_id=1, source_target_pairs={{0,24},{1,25},{2,26},{3,27},{4,28},{5,29},{6,30},{7,31},{8,16},{9,... | collective-permute-start | bytes 1769480 | tf_op jit(solution)/shard_map/ppermute | solution.py:1012
  102.3 33.8 %collective-permute-start.28 = (bf16[384,768]{1,0:T(8,128)(2,1)S(1)}, bf16[384,768]{1,0:T(8,128)(2,1)S(1)}, u32[]{:S(2)}, u32[]{:S(2)}) collective-permute-start(bf16[384,768]{1,0:T(8,128)(2,1)S(1)} %pad_maximum_fusion.4.rest_0_.rest_10_.rest_19_), channel_id=1, source_target_pairs={{0,16},{1,17},{2,18},{3,19},{4,20},{5,21},{6,22},{7,23},{8,24},{9,... | collective-permute-start | bytes 1769480 | tf_op jit(solution)/shard_map/ppermute | solution.py:1012
  102.9 38.8 %collective-permute-start.27 = (bf16[384,768]{1,0:T(8,128)(2,1)S(1)}, bf16[384,768]{1,0:T(8,128)(2,1)}, u32[]{:S(2)}, u32[]{:S(2)}) collective-permute-start(bf16[384,768]{1,0:T(8,128)(2,1)S(1)} %pad_maximum_fusion.4.rest_0_.rest_10_.rest_19_), channel_id=1, source_target_pairs={{0,8},{1,9},{2,10},{3,11},{4,12},{5,13},{6,14},{7,15},{8,0},{9,1},... | collective-permute-start | bytes 1769480 | tf_op jit(solution)/shard_map/ppermute | solution.py:1012
  104.4 38.6 %collective-permute-start.30 = (bf16[384,768]{1,0:T(8,128)(2,1)S(1)}, bf16[384,768]{1,0:T(8,128)(2,1)}, u32[]{:S(2)}, u32[]{:S(2)}) collective-permute-start(bf16[384,768]{1,0:T(8,128)(2,1)S(1)} %pad_maximum_fusion.4.rest_0_.rest_10_.rest_19_), channel_id=1, source_target_pairs={{0,4},{1,5},{2,6},{3,7},{4,0},{5,1},{6,2},{7,3},{8,12},{9,13},{10,... | collective-permute-start | bytes 1769480 | tf_op jit(solution)/shard_map/ppermute | solution.py:1012
  164.2 28.5 %collective-permute-start.34 = (bf16[2,16,768]{2,1,0:T(8,128)(2,1)S(1)}, bf16[2,16,768]{2,1,0:T(8,128)(2,1)S(1)}, u32[]{:S(2)}, u32[]{:S(2)}) collective-permute-start(bf16[2,16,768]{2,1,0:T(8,128)(2,1)S(1)} %pad_maximum_fusion.11), channel_id=1, source_target_pairs={{0,2},{1,3},{2,0},{3,1},{4,6},{5,7},{6,4},{7,5},{8,10},{9,11},{10,... | collective-permute-start | bytes 147464 | tf_op jit(solution)/shard_map/ppermute | solution.py:1020
  164.3 28.5 %collective-permute-start.35 = (bf16[2,16,768]{2,1,0:T(8,128)(2,1)S(1)}, bf16[2,16,768]{2,1,0:T(8,128)(2,1)S(1)}, u32[]{:S(2)}, u32[]{:S(2)}) collective-permute-start(bf16[2,16,768]{2,1,0:T(8,128)(2,1)S(1)} %pad_maximum_fusion.11), channel_id=1, source_target_pairs={{0,1},{1,2},{2,3},{3,0},{4,5},{5,6},{6,7},{7,4},{8,9},{9,10},{10,1... | collective-permute-start | bytes 147464 | tf_op jit(solution)/shard_map/ppermute | solution.py:1020
  165.5 27.3 %collective-permute-start.36 = (bf16[2,16,768]{2,1,0:T(8,128)(2,1)S(1)}, bf16[2,16,768]{2,1,0:T(8,128)(2,1)S(1)}, u32[]{:S(2)}, u32[]{:S(2)}) collective-permute-start(bf16[2,16,768]{2,1,0:T(8,128)(2,1)S(1)} %pad_maximum_fusion.11), channel_id=1, source_target_pairs={{0,3},{1,0},{2,1},{3,2},{4,7},{5,4},{6,5},{7,6},{8,11},{9,8},{10,9... | collective-permute-start | bytes 147464 | tf_op jit(solution)/shard_map/ppermute | solution.py:1020
  192.9 27.9 %collective-permute-start.37 = (bf16[4,2,16,768]{3,2,1,0:T(8,128)(2,1)S(1)}, bf16[4,2,16,768]{3,2,1,0:T(8,128)(2,1)S(1)}, u32[]{:S(2)}, u32[]{:S(2)}) collective-permute-start(bf16[4,2,16,768]{3,2,1,0:T(8,128)(2,1)S(1)} %pad_maximum_fusion.9), channel_id=1, source_target_pairs={{0,8},{1,9},{2,10},{3,11},{4,12},{5,13},{6,14},{7,15},{8,0},{9,1},... | collective-permute-start | bytes 589832 | tf_op jit(solution)/shard_map/ppermute | solution.py:1012
  194.7 26.1 %collective-permute-start.38 = (bf16[4,2,16,768]{3,2,1,0:T(8,128)(2,1)S(1)}, bf16[4,2,16,768]{3,2,1,0:T(8,128)(2,1)S(1)}, u32[]{:S(2)}, u32[]{:S(2)}) collective-permute-start(bf16[4,2,16,768]{3,2,1,0:T(8,128)(2,1)S(1)} %pad_maximum_fusion.9), channel_id=1, source_target_pairs={{0,16},{1,17},{2,18},{3,19},{4,20},{5,21},{6,22},{7,23},{8,24},{9,... | collective-permute-start | bytes 589832 | tf_op jit(solution)/shard_map/ppermute | solution.py:1012
  195.6 25.2 %collective-permute-start.39 = (bf16[4,2,16,768]{3,2,1,0:T(8,128)(2,1)S(1)}, bf16[4,2,16,768]{3,2,1,0:T(8,128)(2,1)S(1)}, u32[]{:S(2)}, u32[]{:S(2)}) collective-permute-start(bf16[4,2,16,768]{3,2,1,0:T(8,128)(2,1)S(1)} %pad_maximum_fusion.9), channel_id=1, source_target_pairs={{0,24},{1,25},{2,26},{3,27},{4,28},{5,29},{6,30},{7,31},{8,16},{9,... | collective-permute-start | bytes 589832 | tf_op jit(solution)/shard_map/ppermute | solution.py:1012
  293.7 21.0 %collective-permute-start.41 = (bf16[4,384,768]{2,1,0:T(8,128)(2,1)}, bf16[4,384,768]{2,1,0:T(8,128)(2,1)}, u32[]{:S(2)}, u32[]{:S(2)}) collective-permute-start(bf16[4,384,768]{2,1,0:T(8,128)(2,1)} %get-tuple-element.166), channel_id=1, source_target_pairs={{0,4},{1,5},{2,6},{3,7},{4,0},{5,1},{6,2},{7,3},{8,12},{9,13},{10,... | collective-permute-start | bytes 7077896 | tf_op jit(solution)/shard_map/ppermute | solution.py:1012
  314.1 27.7 %collective-permute-start.44 = (bf16[4,480,768]{2,1,0:T(8,128)(2,1)}, bf16[4,480,768]{2,1,0:T(8,128)(2,1)}, u32[]{:S(2)}, u32[]{:S(2)}) collective-permute-start(bf16[4,480,768]{2,1,0:T(8,128)(2,1)} %get-tuple-element.165), channel_id=1, source_target_pairs={{0,4},{1,5},{2,6},{3,7},{4,0},{5,1},{6,2},{7,3},{8,12},{9,13},{10,... | collective-permute-start | bytes 8847368 | tf_op jit(solution)/shard_map/ppermute | solution.py:1012
  339.4 32.3 %collective-permute-start.46 = (bf16[4,96,768]{2,1,0:T(8,128)(2,1)}, bf16[4,96,768]{2,1,0:T(8,128)(2,1)}, u32[]{:S(2)}, u32[]{:S(2)}) collective-permute-start(bf16[4,96,768]{2,1,0:T(8,128)(2,1)} %pad_maximum_fusion.6), channel_id=1, source_target_pairs={{0,16},{1,17},{2,18},{3,19},{4,20},{5,21},{6,22},{7,23},{8,24},{9,... | collective-permute-start | bytes 1769480 | tf_op jit(solution)/shard_map/ppermute | solution.py:1012
  341.4 30.3 %collective-permute-start.45 = (bf16[4,96,768]{2,1,0:T(8,128)(2,1)}, bf16[4,96,768]{2,1,0:T(8,128)(2,1)}, u32[]{:S(2)}, u32[]{:S(2)}) collective-permute-start(bf16[4,96,768]{2,1,0:T(8,128)(2,1)} %pad_maximum_fusion.5), channel_id=1, source_target_pairs={{0,8},{1,9},{2,10},{3,11},{4,12},{5,13},{6,14},{7,15},{8,0},{9,1},... | collective-permute-start | bytes 1769480 | tf_op jit(solution)/shard_map/ppermute | solution.py:1012
  345.9 27.9 %collective-permute-start.47 = (bf16[2,120,768]{2,1,0:T(8,128)(2,1)}, bf16[2,120,768]{2,1,0:T(8,128)(2,1)}, u32[]{:S(2)}, u32[]{:S(2)}) collective-permute-start(bf16[2,120,768]{2,1,0:T(8,128)(2,1)} %bitcast.75), channel_id=1, source_target_pairs={{0,8},{1,9},{2,10},{3,11},{4,12},{5,13},{6,14},{7,15},{8,0},{9,1},... | collective-permute-start | bytes 1105928 | tf_op jit(solution)/shard_map/ppermute | solution.py:1012
  349.5 27.4 %collective-permute-start.48 = (bf16[2,120,768]{2,1,0:T(8,128)(2,1)}, bf16[2,120,768]{2,1,0:T(8,128)(2,1)}, u32[]{:S(2)}, u32[]{:S(2)}) collective-permute-start(bf16[2,120,768]{2,1,0:T(8,128)(2,1)} %bitcast.77), channel_id=1, source_target_pairs={{0,16},{1,17},{2,18},{3,19},{4,20},{5,21},{6,22},{7,23},{8,24},{9,... | collective-permute-start | bytes 1105928 | tf_op jit(solution)/shard_map/ppermute | solution.py:1012
  402.3 33.5 %collective-permute-start.61 = (bf16[120,768]{1,0:T(8,128)(2,1)}, bf16[120,768]{1,0:T(8,128)(2,1)}, u32[]{:S(2)}, u32[]{:S(2)}) collective-permute-start(bf16[120,768]{1,0:T(8,128)(2,1)} %get-tuple-element.228), channel_id=1, source_target_pairs={{0,1},{1,2},{2,3},{3,0},{4,5},{5,6},{6,7},{7,4},{8,9},{9,10},{10,1... | collective-permute-start | bytes 552968 | tf_op jit(solution)/shard_map/ppermute | solution.py:1020
  402.6 34.6 %collective-permute-start.62 = (bf16[120,768]{1,0:T(8,128)(2,1)}, bf16[120,768]{1,0:T(8,128)(2,1)}, u32[]{:S(2)}, u32[]{:S(2)}) collective-permute-start(bf16[120,768]{1,0:T(8,128)(2,1)} %get-tuple-element.230), channel_id=1, source_target_pairs={{0,2},{1,3},{2,0},{3,1},{4,6},{5,7},{6,4},{7,5},{8,10},{9,11},{10,... | collective-permute-start | bytes 552968 | tf_op jit(solution)/shard_map/ppermute | solution.py:1020
  407.9 23.6 %collective-permute-start.56 = (bf16[4,80,768]{2,1,0:T(8,128)(2,1)S(1)}, bf16[4,80,768]{2,1,0:T(8,128)(2,1)S(1)}, u32[]{:S(2)}, u32[]{:S(2)}) collective-permute-start(bf16[4,80,768]{2,1,0:T(8,128)(2,1)S(1)} %fusion.15), channel_id=1, source_target_pairs={{0,16},{1,17},{2,18},{3,19},{4,20},{5,21},{6,22},{7,23},{8,24},{9,... | collective-permute-start | bytes 1474568 | tf_op jit(solution)/shard_map/ppermute | solution.py:1012
  409.8 21.8 %collective-permute-start.57 = (bf16[4,80,768]{2,1,0:T(8,128)(2,1)}, bf16[4,80,768]{2,1,0:T(8,128)(2,1)S(1)}, u32[]{:S(2)}, u32[]{:S(2)}) collective-permute-start(bf16[4,80,768]{2,1,0:T(8,128)(2,1)} %fusion.16), channel_id=1, source_target_pairs={{0,24},{1,25},{2,26},{3,27},{4,28},{5,29},{6,30},{7,31},{8,16},{9,... | collective-permute-start | bytes 1474568 | tf_op jit(solution)/shard_map/ppermute | solution.py:1012
  (73 other events, 779.4 us)
Sparse Core Ops, SparseCore 0:
  79.9 116.6 all-gather.1

commit v9 on v8

--- a/solution.py
+++ b/solution.py
@@ -226,13 +226,13 @@
     heads_ref[...] = normed * (1.0 + vec_ref[10:11, :]) + vec_ref[11:12, :]
 
 
-def cross_kernel(blocks, segs, seg_count, info, heads_ref, up_ref, live_ref, vec_ref, pos_ref, seg_vec_ref, *rest):
+def cross_kernel(blocks, segs, seg_count, info, both_ref, live_ref, vec_ref, pos_ref, seg_vec_ref, *rest):
     wide, tops_in, sources, mid, more, rest = rest[0], rest[1:6], rest[6:9], rest[9:19], rest[19:27], rest[27:]
     grads_ref, pos_grad_ref, qkv_grad_ref, out_grad_ref, up_grad_ref, down_grad_ref, seg_grads_ref, *tops_out = rest[:12]
     (qkv, out, up, down, sems, result, heads_grad, slope, lefts, act, packed, rights, hidden_grad) = rest[12:25]
     tops, parts, own_hidden, weights, (seg_sems, top_sems) = rest[25:30], rest[30:33], rest[33], rest[34:37], rest[37:]
     step = pl.program_id(0)
-    count = heads_ref.shape[0]
+    count = live_ref.shape[0]
     at = pl.ds(pl.multiple_of(step * count, count), count)
     targets = [qkv.at[j] for j in range(3)] + [out] + [up.at[j] for j in range(4)]
     targets += [down.at[j * 768 : (j + 1) * 768] for j in range(4)]
@@ -249,7 +249,7 @@
             copy.wait()
 
     vec = vec_ref[...]
-    inputs = heads_ref[...].astype(F32).reshape(-1, 8, 768) + pos_ref[...][None]
+    inputs = both_ref[:, 0].reshape(count, 768).astype(F32).reshape(-1, 8, 768) + pos_ref[...][None]
     inputs = inputs.reshape(count, 768)
     low = inputs.astype(LOW)
     lefts[0, at, :] = low
@@ -292,7 +292,7 @@
         total = total + mm(active.astype(LOW), down[cols, :])
     normed, inv_scale = normalize(total)
     result[at, :] = normed * (1.0 + vec[10:11]) + vec[11:12]
-    upstream = up_ref[...].astype(F32)
+    upstream = both_ref[:, 1].reshape(count, 768).astype(F32)
     back_two = normalize_back(upstream * (1.0 + vec[10:11]), normed, inv_scale)
     down_grad = back_two.astype(LOW)
     rights[1, at, :] = down_grad
@@ -333,7 +333,7 @@
     @pl.when(step == blocks - 1)
     def _():
         me = info[1]
-        own = pl.ds(pl.multiple_of(me * 16, 16), 16)
+        own = pl.ds(pl.multiple_of(info[2] * 16, 16), 16)
         groups = opening_groups(info[0], tops_in, sources, mid, more, tops, parts, weights, seg_sems, top_sems)
 
         def wait(*names):
@@ -341,7 +341,7 @@
                 for copy in groups[name]:
                     copy.wait()
 
-        lengths = [info[2 + i] for i in range(segs // seg_count)]
+        lengths = [info[3 + i] for i in range(segs // seg_count)]
         opening_rows(segs, seg_count, lengths, result[own, :], heads_grad[own, :], seg_vec_ref, tops_out,
                      seg_grads_ref, tops, parts, own_hidden, weights, top_sems, wait)
 
@@ -545,7 +545,7 @@
     def _():
         for mask in range(8):
             target = send_ref if mask % 2 else keep_ref
-            target[mask // 2, 288:304, :] = more_ref[mask]
+            target[mask // 2, 288:304, :] = more_ref[info[0] ^ mask]
 
 
 def mid_grad_kernel(info, mixed_ref, proj_ref, low_ref, hidden_ref, keep_ref, send_ref, total):
@@ -660,17 +660,17 @@
     return tops + parts + [pltpu.VMEM((segs, 3072), F32)] + MID + DOWN + sems(72) + sems(8)
 
 
-def cross_whole(info, heads, upstream, live, vec, positions, wide, seg_vec, arrays, sources, mid, more, seg_count):
-    rows = heads.shape[0]
+def cross_whole(info, both, live, vec, positions, wide, seg_vec, arrays, sources, mid, more, seg_count):
+    rows = live.shape[0]
     count = 2 * SEG
+    pair = pl.BlockSpec((count // 16, 2, 16, 768), lambda i: (i, 0, 0, 0))
     arrays, sources = [grouped(a) for a in arrays], [grouped(a) for a in sources]
     segs = arrays[0].shape[0]
     own = [(12, 768), (8, 768), (24, 2304), (24, 768), (24, 3072), (96, 768), (12, 768)]
     *grads, seg_grads, layer, down, hidden, proj, mixed = pl.pallas_call(
         functools.partial(cross_kernel, rows // count, segs, seg_count),
         grid=(rows // count,),
-        in_specs=[SMEM, block_rows(count, 768), block_rows(count, 768), block_rows(count, SEG),
-                  fixed((12, 768)), fixed((8, 768)), fixed((12, 768))] + [ANY] * 27,
+        in_specs=[SMEM, pair, block_rows(count, SEG), fixed((12, 768)), fixed((8, 768)), fixed((12, 768))] + [ANY] * 27,
         out_specs=[fixed(dims) for dims in own] + [ANY] * 5,
         out_shape=[shape_of(dims, F32) for dims in own] + [shape_of(a.shape) for a in arrays],
         scratch_shapes=QKV + MID + DOWN + sems(12) + [
@@ -678,11 +678,11 @@
             pltpu.VMEM((3, rows, 768), LOW), pltpu.VMEM((rows, 3072), LOW), pltpu.VMEM((count, 2304), LOW),
             pltpu.VMEM((5, rows, 768), LOW), pltpu.VMEM((rows, 3072), LOW),
         ] + top_scratch(segs, arrays),
-        input_output_aliases={8 + i: 7 + i for i in range(5)},
+        input_output_aliases={7 + i: 7 + i for i in range(5)},
         compiler_params=params(),
         cost_estimate=cost(2 * rows * 768 * 30000, 2**24),
         name="cross_encoder",
-    )(info, heads, upstream, live, vec, positions, seg_vec, wide, *arrays, *sources, *mid, *more)
+    )(info, both, live, vec, positions, seg_vec, wide, *arrays, *sources, *mid, *more)
     return grads, seg_grads, [a.reshape(-1, a.shape[2]) for a in (layer, down, hidden, proj, mixed)]
 
 
@@ -1052,9 +1052,7 @@
         return jnp.stack([block] + [self.flip(block, m) for m in (2, 4, 6)])
 
     def gather_core(self, plane):
-        other = self.flip(plane, 1)
-        whole = self.in_order([(plane, other)[m % 2][m // 2] for m in range(8)])
-        return whole.reshape((-1,) + plane.shape[2:])
+        return jnp.stack([plane, self.flip(plane, 1)]).reshape((-1,) + plane.shape[2:])
 
 
 class PlainLinks:
@@ -1275,17 +1273,18 @@
         both = links.gather_plane(after(both, first_half[1]))
         *arrays, grads_two = back(after(cot_rows, first_half[1]), *args, half=1, before=first_half[:5])
         both = links.gather_core(after(both, arrays[1]))
-    heads_all, up_all = both[:, 0].reshape(-1, feat_dim), both[:, 1].reshape(-1, feat_dim)
     live_all = seg_starts[None, :] < lengths[:, None]
     if fast:
-        cross_info = jnp.concatenate([jnp.stack([links.place, me]).astype(jnp.int32), my_lengths])
-        live = jnp.broadcast_to(live_all.reshape(-1, 1), (live_all.size, SEG)).astype(F32)
+        cross_info = jnp.concatenate([jnp.stack([links.place, me, links.z]).astype(jnp.int32), my_lengths])
+        live = links.in_order(list(live_all.reshape(outer, -1))).reshape(4, 2, -1).transpose(1, 0, 2)
+        live = jnp.broadcast_to(live.reshape(-1, 1), (live_all.size, SEG)).astype(F32)
         (vec_grad, pos_grad, *cross_grads), grads_more, arrays = cross_whole(
-            cross_info, heads_all, up_all, live, cross_v, pos_table, wide,
+            cross_info, both, live, cross_v, pos_table, wide,
             seg_v, arrays, (second, summed, slope), mid, down, seg_count,
         )
     else:
         weights = (matrix_of(wide[:3]), wide[3], matrix_of(wide[4:8]), wide[8:].reshape(-1, feat_dim), cross_v)
+        heads_all, up_all = both[:, 0].reshape(-1, feat_dim), both[:, 1].reshape(-1, feat_dim)
         heads_in = heads_all.astype(F32).reshape(-1, seg_count, feat_dim) + pos_table[None]
         heads_in = heads_in.reshape(-1, feat_dim)
         cross_result, kept = encode(heads_in, heads_in.astype(LOW), weights, live_all)
@@ -1321,8 +1320,6 @@
     if outer > 8:
         vec_parts = vec_parts.reshape(8, -1, seg_rows * width)
     vec_parts = jnp.pad(vec_parts, ((0, 0), (0, 16 - vec_parts.shape[1]), (0, feat_dim - seg_rows * width)))
-    if fast:
-        vec_parts = links.in_order(list(vec_parts))
     ready = after(packed_grad, *down_sum.near(), *mid_sum.far())
     keep, send = qkv_weight_grad(info, rows_in, ready, vec_parts)
     qkv_sum = summing(links, keep, after(send, *down_sum.turn(), *mid_sum.near()), 3)

time: 463 us -> 470 us (1.015); the launches traced: 458 us -> 470 us
  Pallas kernels: 272 us -> 284 us
    pallas_call x1, Pallas kernels: 50.9 us -> 62.6 us  [cross_whole(): pl.pallas_call(functools.partial(cross_kernel, rows // count, segs, seg_c...]
  transfers between devices with their start and end apart: 65 -> 65, of which waited for: 13 -> 12; matrix products, arithmetic and copies ran while one was open for 13% -> 13% of each run, Pallas kernels for 45% -> 44%
where the time goes in v9:
time: 470 us
  Pallas kernels  284 us (60%)
  starting transfers between devices  75.2 us (16%)
  local copies, waits for them, and re-layouts  37.2 us (8%)
  other arithmetic  31.2 us (7%)
  waiting for transfers between devices  27.3 us (6%)
  between operations  15.6 us (3%)
    pallas_call x1, Pallas kernels, cross_whole(): pl.pallas_call(functools.partial(cross_kernel, rows // count, segs, seg_c...  62.6 us
    pallas_call x2, Pallas kernels, ffn_backward(): pl.pallas_call(functools.partial(ffn_backward_kernel, segs, seg_count, fi...  48.8 us
    ppermute x21, starting transfers between devices, turn(): return lax.ppermute(value, AXES, pairs)  43.9 us
    pallas_call x2, Pallas kernels, attn_backward(): pl.pallas_call(functools.partial(attn_backward_kernel, segs, seg_count, f...  34.4 us
    ppermute x43, starting transfers between devices, flip(): return lax.ppermute(value, AXES, pairs)  31.3 us
    pallas_call x1, Pallas kernels, mid_forward(): pl.pallas_call(mid_forward_kernel, grid=(rows // count,), in_specs=[SMEM,...  29.6 us
    pallas_call x2, Pallas kernels, attn_forward(): pl.pallas_call(functools.partial(attn_forward_kernel, segs, seg_count, fi...  26.1 us
    pallas_call x1, Pallas kernels, mid_weight_grad(): pl.pallas_call(mid_grad_kernel, grid=(5,), in_specs=[SMEM, still, still,...  19.9 us
  transfers between devices with their start and end apart: 65, of which 12 were waited for; matrix products, arithmetic and copies ran while one was open for 13% of the time, Pallas kernels for 44%

profile of v9, /device:TPU:0, one launch (start us, length us, event | category | flops | bytes accessed | tf_op | source)
XLA Modules:
  0.0 470.4 jit_solution(10105339010090698991)
XLA Ops:
  9.0 4.1 collective-permute-start
  17.0 5.6 %collective-permute-done = bf16[80,768]{1,0:T(8,128)(2,1)S(1)} collective-permute-done((bf16[80,768]{1,0:T(8,128)(2,1)S(1)}, bf16[80,768]{1,0:T(8,128)(2,1)S(1)}, u32[]{:S(2)}, u32[]{:S(2)}) %collective-permute-start) | collective-permute-done | bytes 122912 | tf_op jit(solution)/shard_map/ppermute | solution.py:1020
  27.7 3.7 collective-permute-start.3
  31.4 3.8 collective-permute-start.5
  40.7 3.1 collective-permute-done.3
  52.8 6.7 %collective-permute-start.24 = (bf16[96,768]{1,0:T(8,128)(2,1)S(1)}, bf16[96,768]{1,0:T(8,128)(2,1)S(1)}, u32[]{:S(2)}, u32[]{:S(2)}) collective-permute-start(bf16[96,768]{1,0:T(8,128)(2,1)S(1)} %copy-done.13), channel_id=1, source_target_pairs={{0,2},{1,3},{2,0},{3,1},{4,6},{5,7},{6,4},{7,5},{8,10},{9,11},{10,... | collective-permute-start | bytes 442376 | tf_op jit(solution)/shard_map/ppermute | solution.py:1020
  59.5 4.3 collective-permute-start.26
  66.9 13.0 %attn_forward.2 = (bf16[2048,2304]{1,0:T(8,128)(2,1)}, bf16[2048,768]{1,0:T(8,128)(2,1)}) custom-call(s32[3]{0:T(128)} %pad_add_fusion.1.info, bf16[2048,768]{1,0:T(8,128)(2,1)} %bitcast.295, f32[12,768]{1,0:T(8,128)} %slice.349.vec_ref.seg_vec_ref, bf16[304,768]{1,0:T(8,128)(2,1)} %fusion.17.rest_0_, bf16[304,768]{1,0:T(8,128)(2,1)} %collective-permute-done.8.rest_1_, ...), custom_call_target="tpu_custom_call" | custom-call | flops 12582912000 | bytes 12582912 | tf_op jit(solution)/shard_map/attn_forward/pallas_call | solution.py:606
  82.9 13.2 %attn_forward.3 = (bf16[2048,2304]{1,0:T(8,128)(2,1)}, bf16[2048,768]{1,0:T(8,128)(2,1)}) custom-call(s32[3]{0:T(128)} %pad_add_fusion.1.info, bf16[2048,768]{1,0:T(8,128)(2,1)} %bitcast.296, f32[12,768]{1,0:T(8,128)} %slice.349.vec_ref.seg_vec_ref, bf16[304,768]{1,0:T(8,128)(2,1)} %fusion.17.rest_0_, ...), custom_call_target="tpu_custom_call", output_to_operand_aliasing={{0}: (13, {}), {1}: (14, {})} | custom-call | flops 12582912000 | bytes 12582912 | tf_op jit(solution)/shard_map/attn_forward/pallas_call | solution.py:606
  103.5 29.6 %mid_forward.1 = (f32[2048,768]{1,0:T(8,128)}, bf16[2048,768]{1,0:T(8,128)(2,1)}, bf16[2048,3072]{1,0:T(8,128)(2,1)}, bf16[2048,3072]{1,0:T(8,128)(2,1)}) custom-call(s32[3]{0:T(128)} %pad_add_fusion.1.info, bf16[2048,768]{1,0:T(8,128)(2,1)} %bitcast.297, bf16[2048,768]{1,0:T(8,128)(2,1)} %get-tuple-element.126.mixed_ref, ...), custom_call_target="tpu_custom_call" | custom-call | flops 25165824000 | bytes 47185920 | tf_op jit(solution)/shard_map/mid_forward/pallas_call | solution.py:623
  134.9 5.7 %collective-permute-done.27.rest_1_.rest_11_.rest_20_ = bf16[384,768]{1,0:T(8,128)(2,1)} collective-permute-done((bf16[384,768]{1,0:T(8,128)(2,1)S(1)}, bf16[384,768]{1,0:T(8,128)(2,1)}, u32[]{:S(2)}, u32[]{:S(2)}) %collective-permute-start.27) | collective-permute-done | bytes 589856 | tf_op jit(solution)/shard_map/ppermute | solution.py:1012
  143.0 19.6 %down_forward.1 = (f32[2048,768]{1,0:T(8,128)}, f32[8,2,768]{2,1,0:T(2,128)}) custom-call(s32[3]{0:T(128)} %pad_add_fusion.1.info, f32[2048,768]{1,0:T(8,128)} %get-tuple-element.133.sum_ref, bf16[2048,3072]{1,0:T(8,128)(2,1)} %get-tuple-element.134.act_ref.left_ref, f32[12,768]{1,0:T(8,128)} %slice.349.vec_ref.seg_vec_ref, bf16[384,768]{1,0:T(8,128)(2,1)} %copy-done.10, ...), custom_call_target="tpu_custom_call" | custom-call | flops 12582912000 | bytes 25165824 | tf_op jit(solution)/shard_map/down_forward/pallas_call | solution.py:640
  163.8 3.6 collective-permute-start.36
  167.4 24.4 %ffn_backward.2 = (bf16[2048,768]{1,0:T(8,128)(2,1)}, bf16[2048,768]{1,0:T(8,128)(2,1)}, bf16[2048,3072]{1,0:T(8,128)(2,1)}, bf16[2048,768]{1,0:T(8,128)(2,1)}, ...) custom-call(s32[3]{0:T(128)} %pad_add_fusion.1.info, bf16[2048,768]{1,0:T(8,128)(2,1)} %bitcast.293, ...), custom_call_target="tpu_custom_call" | custom-call | flops 22020096000 | bytes 23592960 | tf_op jit(solution)/shard_map/ffn_backward/pallas_call | solution.py:696
  195.4 24.4 %ffn_backward.3 = (bf16[2048,768]{1,0:T(8,128)(2,1)}, bf16[2048,768]{1,0:T(8,128)(2,1)}, bf16[2048,3072]{1,0:T(8,128)(2,1)}, bf16[2048,768]{1,0:T(8,128)(2,1)}, ...) custom-call(s32[3]{0:T(128)} %pad_add_fusion.1.info, ...), custom_call_target="tpu_custom_call", output_to_operand_aliasing={{0}: (24, {}), {1}: (25, {}), {2}: (26, {}), {3}: (27, {}),... | custom-call | flops 22020096000 | bytes 23592960 | tf_op jit(solution)/shard_map/ffn_backward/pallas_call | solution.py:696
  225.2 62.6 %cross_encoder.1 = (f32[12,768]{1,0:T(8,128)}, f32[8,768]{1,0:T(8,128)}, f32[24,2304]{1,0:T(8,128)}, f32[24,768]{1,0:T(8,128)}, f32[24,3072]{1,0:T(8,128)}, /*in...) custom-call(s32[5]{0:T(128)} %pad_add_fusion.info, ...), custom_call_target="tpu_custom_call", output_to_operand_aliasing={{7}: (7, {}), {8}: (8, {}), {9}: (9, {}), {10}: (10, {}), {... | custom-call | flops 23592960000 | bytes 16777216 | tf_op jit(solution)/shard_map/cross_encoder/pallas_call | solution.py:670
  287.8 16.1 %down_weight_grad.1 = (bf16[4,384,768]{2,1,0:T(8,128)(2,1)}, bf16[4,384,768]{2,1,0:T(8,128)(2,1)}) custom-call(s32[3]{0:T(128)} %pad_add_fusion.1.info, bf16[2048,3072]{1,0:T(8,128)(2,1)} %get-tuple-element.134.act_ref.left_ref, bf16[2048,768]{1,0:T(8,128)(2,1)} %bitcast.308), custom_call_target="tpu_custom_call" | custom-call | flops 9663676416 | bytes 12582912 | tf_op jit(solution)/shard_map/down_weight_grad/pallas_call | solution.py:816
  304.4 19.9 %mid_weight_grad.1 = (bf16[4,480,768]{2,1,0:T(8,128)(2,1)}, bf16[4,480,768]{2,1,0:T(8,128)(2,1)}) custom-call(s32[3]{0:T(128)} %pad_add_fusion.1.info, bf16[2048,768]{1,0:T(8,128)(2,1)} %get-tuple-element.126.mixed_ref, bf16[2048,768]{1,0:T(8,128)(2,1)} %bitcast.310, bf16[2048,768]{1,0:T(8,128)(2,1)} %get-tuple-element.160.low_ref, bf16[2048,3072]{1,0:T(8,128)(2,1)} %bitcast.301), custom_call_target="tpu_custom_call" | custom-call | flops 12079595520 | bytes 15728640 | tf_op jit(solution)/shard_map/mid_weight_grad/pallas_call | solution.py:789
  330.9 17.3 %attn_backward.2 = (bf16[2048,2304]{1,0:T(8,128)(2,1)}, f32[2,768]{1,0:T(2,128)}) custom-call(s32[3]{0:T(128)} %pad_add_fusion.1.info, bf16[2048,2304]{1,0:T(8,128)(2,1)} %get-tuple-element.130.packed_ref, bf16[2048,768]{1,0:T(8,128)(2,1)} %bitcast.313), custom_call_target="tpu_custom_call" | custom-call | flops 15728640000 | bytes 12582912 | tf_op jit(solution)/shard_map/attn_backward/pallas_call | solution.py:736
  360.2 17.1 %attn_backward.3 = (bf16[2048,2304]{1,0:T(8,128)(2,1)}, f32[2,768]{1,0:T(2,128)}) custom-call(s32[3]{0:T(128)} %pad_add_fusion.1.info, bf16[2048,2304]{1,0:T(8,128)(2,1)} %get-tuple-element.130.packed_ref, bf16[2048,768]{1,0:T(8,128)(2,1)} %bitcast.314, bf16[2048,2304]{1,0:T(8,128)(2,1)} %get-tuple-element.168.rest_0_), custom_call_target="tpu_custom_call", output_to_operand_aliasing={{0}: (3, {})} | custom-call | flops 15728640000 | bytes 12582912 | tf_op jit(solution)/shard_map/attn_backward/pallas_call | solution.py:736
  391.6 13.2 %qkv_weight_grad.1 = (bf16[4,304,768]{2,1,0:T(8,128)(2,1)}, bf16[4,304,768]{2,1,0:T(8,128)(2,1)}) custom-call(s32[3]{0:T(128)} %pad_add_fusion.1.info, bf16[2048,768]{1,0:T(8,128)(2,1)} %bitcast.298, bf16[2048,2304]{1,0:T(8,128)(2,1)} %get-tuple-element.180.right_ref.packed_grad_ref, bf16[8,16,768]{2,1,0:T(8,128)(2,1)} %pad.34.more_ref), custom_call_target="tpu_custom_call" | custom-call | flops 7247757312 | bytes 9437184 | tf_op jit(solution)/shard_map/qkv_weight_grad/pallas_call | solution.py:772
  422.4 13.6 %token_gradient.1 = bf16[2048,768]{1,0:T(8,128)(2,1)} custom-call(s32[3]{0:T(128)} %pad_add_fusion.1.info, bf16[2048,2304]{1,0:T(8,128)(2,1)} %get-tuple-element.180.right_ref.packed_grad_ref, bf16[2048,768]{1,0:T(8,128)(2,1)} %bitcast.311, bf16[304,768]{1,0:T(8,128)(2,1)} %fusion.17.rest_0_, bf16[304,768]{1,0:T(8,128)(2,1)} %collective-permute-done.8.rest_1_, ...), custom_call_target="tpu_custom_call" | custom-call | flops 9437184000 | bytes 15728640 | tf_op jit(solution)/shard_map/token_gradient/pallas_call | solution.py:751
  436.1 2.9 collective-permute-start.63
  439.0 4.2 collective-permute-done.56
  (368 shorter events, 123.1 us)
Async XLA Ops:
  7.2 217.2 %all-gather.2.cloned.1.call-start = ((), (), s32[]{:S(2)}) async-start(), calls=%async_computation | async-start | bytes 14598144 | tf_op jit(solution)/shard_map/all_gather | solution.py:1250
  51.0 28.9 %collective-permute-start.10 = (bf16[480,768]{1,0:T(8,128)(2,1)S(1)}, bf16[480,768]{1,0:T(8,128)(2,1)}, u32[]{:S(2)}, u32[]{:S(2)}) collective-permute-start(bf16[480,768]{1,0:T(8,128)(2,1)S(1)} %bitcast.257), channel_id=1, source_target_pairs={{0,8},{1,9},{2,10},{3,11},{4,12},{5,13},{6,14},{7,15},{8,0},{9,1},... | collective-permute-start | bytes 2211848 | tf_op jit(solution)/shard_map/ppermute | solution.py:1012
  51.6 28.4 %collective-permute-start.11 = (bf16[480,768]{1,0:T(8,128)(2,1)S(1)}, bf16[480,768]{1,0:T(8,128)(2,1)S(1)}, u32[]{:S(2)}, u32[]{:S(2)}) collective-permute-start(bf16[480,768]{1,0:T(8,128)(2,1)S(1)} %bitcast.258), channel_id=1, source_target_pairs={{0,16},{1,17},{2,18},{3,19},{4,20},{5,21},{6,22},{7,23},{8,24},{9,... | collective-permute-start | bytes 2211848 | tf_op jit(solution)/shard_map/ppermute | solution.py:1012
  52.8 27.0 %collective-permute-start.24 = (bf16[96,768]{1,0:T(8,128)(2,1)S(1)}, bf16[96,768]{1,0:T(8,128)(2,1)S(1)}, u32[]{:S(2)}, u32[]{:S(2)}) collective-permute-start(bf16[96,768]{1,0:T(8,128)(2,1)S(1)} %copy-done.13), channel_id=1, source_target_pairs={{0,2},{1,3},{2,0},{3,1},{4,6},{5,7},{6,4},{7,5},{8,10},{9,11},{10,... | collective-permute-start | bytes 442376 | tf_op jit(solution)/shard_map/ppermute | solution.py:1020
  99.9 33.2 %collective-permute-start.29 = (bf16[384,768]{1,0:T(8,128)(2,1)S(1)}, bf16[384,768]{1,0:T(8,128)(2,1)S(1)}, u32[]{:S(2)}, u32[]{:S(2)}) collective-permute-start(bf16[384,768]{1,0:T(8,128)(2,1)S(1)} %pad_maximum_fusion.5.rest_0_.rest_10_.rest_19_), channel_id=1, source_target_pairs={{0,24},{1,25},{2,26},{3,27},{4,28},{5,29},{6,30},{7,31},{8,16},{9,... | collective-permute-start | bytes 1769480 | tf_op jit(solution)/shard_map/ppermute | solution.py:1012
  100.9 34.0 %collective-permute-start.28 = (bf16[384,768]{1,0:T(8,128)(2,1)S(1)}, bf16[384,768]{1,0:T(8,128)(2,1)S(1)}, u32[]{:S(2)}, u32[]{:S(2)}) collective-permute-start(bf16[384,768]{1,0:T(8,128)(2,1)S(1)} %pad_maximum_fusion.5.rest_0_.rest_10_.rest_19_), channel_id=1, source_target_pairs={{0,16},{1,17},{2,18},{3,19},{4,20},{5,21},{6,22},{7,23},{8,24},{9,... | collective-permute-start | bytes 1769480 | tf_op jit(solution)/shard_map/ppermute | solution.py:1012
  102.0 38.7 %collective-permute-start.27 = (bf16[384,768]{1,0:T(8,128)(2,1)S(1)}, bf16[384,768]{1,0:T(8,128)(2,1)}, u32[]{:S(2)}, u32[]{:S(2)}) collective-permute-start(bf16[384,768]{1,0:T(8,128)(2,1)S(1)} %pad_maximum_fusion.5.rest_0_.rest_10_.rest_19_), channel_id=1, source_target_pairs={{0,8},{1,9},{2,10},{3,11},{4,12},{5,13},{6,14},{7,15},{8,0},{9,1},... | collective-permute-start | bytes 1769480 | tf_op jit(solution)/shard_map/ppermute | solution.py:1012
  103.5 38.4 %collective-permute-start.30 = (bf16[384,768]{1,0:T(8,128)(2,1)S(1)}, bf16[384,768]{1,0:T(8,128)(2,1)}, u32[]{:S(2)}, u32[]{:S(2)}) collective-permute-start(bf16[384,768]{1,0:T(8,128)(2,1)S(1)} %pad_maximum_fusion.5.rest_0_.rest_10_.rest_19_), channel_id=1, source_target_pairs={{0,4},{1,5},{2,6},{3,7},{4,0},{5,1},{6,2},{7,3},{8,12},{9,13},{10,... | collective-permute-start | bytes 1769480 | tf_op jit(solution)/shard_map/ppermute | solution.py:1012
  163.4 28.4 %collective-permute-start.34 = (bf16[2,16,768]{2,1,0:T(8,128)(2,1)S(1)}, bf16[2,16,768]{2,1,0:T(8,128)(2,1)S(1)}, u32[]{:S(2)}, u32[]{:S(2)}) collective-permute-start(bf16[2,16,768]{2,1,0:T(8,128)(2,1)S(1)} %pad_maximum_fusion.12), channel_id=1, source_target_pairs={{0,2},{1,3},{2,0},{3,1},{4,6},{5,7},{6,4},{7,5},{8,10},{9,11},{10,... | collective-permute-start | bytes 147464 | tf_op jit(solution)/shard_map/ppermute | solution.py:1020
  163.5 28.3 %collective-permute-start.35 = (bf16[2,16,768]{2,1,0:T(8,128)(2,1)S(1)}, bf16[2,16,768]{2,1,0:T(8,128)(2,1)S(1)}, u32[]{:S(2)}, u32[]{:S(2)}) collective-permute-start(bf16[2,16,768]{2,1,0:T(8,128)(2,1)S(1)} %pad_maximum_fusion.12), channel_id=1, source_target_pairs={{0,1},{1,2},{2,3},{3,0},{4,5},{5,6},{6,7},{7,4},{8,9},{9,10},{10,1... | collective-permute-start | bytes 147464 | tf_op jit(solution)/shard_map/ppermute | solution.py:1020
  163.8 28.0 %collective-permute-start.36 = (bf16[2,16,768]{2,1,0:T(8,128)(2,1)S(1)}, bf16[2,16,768]{2,1,0:T(8,128)(2,1)S(1)}, u32[]{:S(2)}, u32[]{:S(2)}) collective-permute-start(bf16[2,16,768]{2,1,0:T(8,128)(2,1)S(1)} %pad_maximum_fusion.12), channel_id=1, source_target_pairs={{0,3},{1,0},{2,1},{3,2},{4,7},{5,4},{6,5},{7,6},{8,11},{9,8},{10,9... | collective-permute-start | bytes 147464 | tf_op jit(solution)/shard_map/ppermute | solution.py:1020
  191.9 28.0 %collective-permute-start.37 = (bf16[4,2,16,768]{3,2,1,0:T(8,128)(2,1)S(1)}, bf16[4,2,16,768]{3,2,1,0:T(8,128)(2,1)S(1)}, u32[]{:S(2)}, u32[]{:S(2)}) collective-permute-start(bf16[4,2,16,768]{3,2,1,0:T(8,128)(2,1)S(1)} %pad_maximum_fusion.10), channel_id=1, source_target_pairs={{0,8},{1,9},{2,10},{3,11},{4,12},{5,13},{6,14},{7,15},{8,0},{9,1},... | collective-permute-start | bytes 589832 | tf_op jit(solution)/shard_map/ppermute | solution.py:1012
  193.3 26.7 %collective-permute-start.38 = (bf16[4,2,16,768]{3,2,1,0:T(8,128)(2,1)S(1)}, bf16[4,2,16,768]{3,2,1,0:T(8,128)(2,1)S(1)}, u32[]{:S(2)}, u32[]{:S(2)}) collective-permute-start(bf16[4,2,16,768]{3,2,1,0:T(8,128)(2,1)S(1)} %pad_maximum_fusion.10), channel_id=1, source_target_pairs={{0,16},{1,17},{2,18},{3,19},{4,20},{5,21},{6,22},{7,23},{8,24},{9,... | collective-permute-start | bytes 589832 | tf_op jit(solution)/shard_map/ppermute | solution.py:1012
  194.3 25.6 %collective-permute-start.39 = (bf16[4,2,16,768]{3,2,1,0:T(8,128)(2,1)S(1)}, bf16[4,2,16,768]{3,2,1,0:T(8,128)(2,1)S(1)}, u32[]{:S(2)}, u32[]{:S(2)}) collective-permute-start(bf16[4,2,16,768]{3,2,1,0:T(8,128)(2,1)S(1)} %pad_maximum_fusion.10), channel_id=1, source_target_pairs={{0,24},{1,25},{2,26},{3,27},{4,28},{5,29},{6,30},{7,31},{8,16},{9,... | collective-permute-start | bytes 589832 | tf_op jit(solution)/shard_map/ppermute | solution.py:1012
  303.9 21.0 %collective-permute-start.41 = (bf16[4,384,768]{2,1,0:T(8,128)(2,1)}, bf16[4,384,768]{2,1,0:T(8,128)(2,1)}, u32[]{:S(2)}, u32[]{:S(2)}) collective-permute-start(bf16[4,384,768]{2,1,0:T(8,128)(2,1)} %get-tuple-element.166), channel_id=1, source_target_pairs={{0,4},{1,5},{2,6},{3,7},{4,0},{5,1},{6,2},{7,3},{8,12},{9,13},{10,... | collective-permute-start | bytes 7077896 | tf_op jit(solution)/shard_map/ppermute | solution.py:1012
  324.3 27.6 %collective-permute-start.44 = (bf16[4,480,768]{2,1,0:T(8,128)(2,1)}, bf16[4,480,768]{2,1,0:T(8,128)(2,1)}, u32[]{:S(2)}, u32[]{:S(2)}) collective-permute-start(bf16[4,480,768]{2,1,0:T(8,128)(2,1)} %get-tuple-element.165), channel_id=1, source_target_pairs={{0,4},{1,5},{2,6},{3,7},{4,0},{5,1},{6,2},{7,3},{8,12},{9,13},{10,... | collective-permute-start | bytes 8847368 | tf_op jit(solution)/shard_map/ppermute | solution.py:1012
  349.3 31.6 %collective-permute-start.46 = (bf16[4,96,768]{2,1,0:T(8,128)(2,1)}, bf16[4,96,768]{2,1,0:T(8,128)(2,1)}, u32[]{:S(2)}, u32[]{:S(2)}) collective-permute-start(bf16[4,96,768]{2,1,0:T(8,128)(2,1)} %pad_maximum_fusion.7), channel_id=1, source_target_pairs={{0,16},{1,17},{2,18},{3,19},{4,20},{5,21},{6,22},{7,23},{8,24},{9,... | collective-permute-start | bytes 1769480 | tf_op jit(solution)/shard_map/ppermute | solution.py:1012
  351.1 29.7 %collective-permute-start.45 = (bf16[4,96,768]{2,1,0:T(8,128)(2,1)}, bf16[4,96,768]{2,1,0:T(8,128)(2,1)}, u32[]{:S(2)}, u32[]{:S(2)}) collective-permute-start(bf16[4,96,768]{2,1,0:T(8,128)(2,1)} %pad_maximum_fusion.6), channel_id=1, source_target_pairs={{0,8},{1,9},{2,10},{3,11},{4,12},{5,13},{6,14},{7,15},{8,0},{9,1},... | collective-permute-start | bytes 1769480 | tf_op jit(solution)/shard_map/ppermute | solution.py:1012
  356.2 26.1 %collective-permute-start.47 = (bf16[2,120,768]{2,1,0:T(8,128)(2,1)}, bf16[2,120,768]{2,1,0:T(8,128)(2,1)}, u32[]{:S(2)}, u32[]{:S(2)}) collective-permute-start(bf16[2,120,768]{2,1,0:T(8,128)(2,1)} %bitcast.78), channel_id=1, source_target_pairs={{0,8},{1,9},{2,10},{3,11},{4,12},{5,13},{6,14},{7,15},{8,0},{9,1},... | collective-permute-start | bytes 1105928 | tf_op jit(solution)/shard_map/ppermute | solution.py:1012
  359.1 26.5 %collective-permute-start.48 = (bf16[2,120,768]{2,1,0:T(8,128)(2,1)}, bf16[2,120,768]{2,1,0:T(8,128)(2,1)}, u32[]{:S(2)}, u32[]{:S(2)}) collective-permute-start(bf16[2,120,768]{2,1,0:T(8,128)(2,1)} %bitcast.80), channel_id=1, source_target_pairs={{0,16},{1,17},{2,18},{3,19},{4,20},{5,21},{6,22},{7,23},{8,24},{9,... | collective-permute-start | bytes 1105928 | tf_op jit(solution)/shard_map/ppermute | solution.py:1012
  413.7 35.1 %collective-permute-start.61 = (bf16[120,768]{1,0:T(8,128)(2,1)S(1)}, bf16[120,768]{1,0:T(8,128)(2,1)}, u32[]{:S(2)}, u32[]{:S(2)}) collective-permute-start(bf16[120,768]{1,0:T(8,128)(2,1)S(1)} %get-tuple-element.226), channel_id=1, source_target_pairs={{0,1},{1,2},{2,3},{3,0},{4,5},{5,6},{6,7},{7,4},{8,9},{9,10},{10,1... | collective-permute-start | bytes 552968 | tf_op jit(solution)/shard_map/ppermute | solution.py:1020
  414.1 36.1 %collective-permute-start.62 = (bf16[120,768]{1,0:T(8,128)(2,1)S(1)}, bf16[120,768]{1,0:T(8,128)(2,1)}, u32[]{:S(2)}, u32[]{:S(2)}) collective-permute-start(bf16[120,768]{1,0:T(8,128)(2,1)S(1)} %get-tuple-element.228), channel_id=1, source_target_pairs={{0,2},{1,3},{2,0},{3,1},{4,6},{5,7},{6,4},{7,5},{8,10},{9,11},{10,... | collective-permute-start | bytes 552968 | tf_op jit(solution)/shard_map/ppermute | solution.py:1020
  419.3 23.9 %collective-permute-start.56 = (bf16[4,80,768]{2,1,0:T(8,128)(2,1)}, bf16[4,80,768]{2,1,0:T(8,128)(2,1)}, u32[]{:S(2)}, u32[]{:S(2)}) collective-permute-start(bf16[4,80,768]{2,1,0:T(8,128)(2,1)} %fusion.15), channel_id=1, source_target_pairs={{0,16},{1,17},{2,18},{3,19},{4,20},{5,21},{6,22},{7,23},{8,24},{9,... | collective-permute-start | bytes 1474568 | tf_op jit(solution)/shard_map/ppermute | solution.py:1012
  421.2 22.0 %collective-permute-start.57 = (bf16[4,80,768]{2,1,0:T(8,128)(2,1)}, bf16[4,80,768]{2,1,0:T(8,128)(2,1)}, u32[]{:S(2)}, u32[]{:S(2)}) collective-permute-start(bf16[4,80,768]{2,1,0:T(8,128)(2,1)} %fusion.16), channel_id=1, source_target_pairs={{0,24},{1,25},{2,26},{3,27},{4,28},{5,29},{6,30},{7,31},{8,16},{9,... | collective-permute-start | bytes 1474568 | tf_op jit(solution)/shard_map/ppermute | solution.py:1012
  (82 other events, 803.2 us)
Sparse Core Ops, SparseCore 0:
  80.1 115.8 all-gather.1

commit v10 on v9

--- a/solution.py
+++ b/solution.py
@@ -141,12 +141,20 @@
     return [functools.partial(rows_of, qkv, slab=j) for j in range(3)]
 
 
-def mid_slabs(out, up):
-    return [functools.partial(rows_of, out)] + [functools.partial(rows_of, up, slab=j) for j in range(4)]
-
-
-def down_slabs(down):
-    return [functools.partial(down_rows, down, part=j) for j in range(4)]
+def piece_copies(place, pieces, target, sems, first_sem=0):
+    whole = len(pieces) == 8
+    copies = []
+    for index, piece in enumerate(pieces):
+        side, part = divmod(index, len(pieces) // 2)
+        block = place ^ (min(part, 3) * 2 + side)
+        if whole:
+            where = target.at[pl.ds(pl.multiple_of(block * 384, 384), 384)]
+        else:
+            count, slabs = piece.shape[0], target.shape[0]
+            first = slabs - count if part == 4 else 0
+            where = target.at[first : first + count, pl.ds(pl.multiple_of(block * 96, 96), 96)]
+        copies.append(pltpu.make_async_copy(piece, where, sems.at[first_sem + index]))
+    return copies
 
 
 def segment_mask(length, seg_in_seq):
@@ -183,20 +191,19 @@
 
 
 def mid_forward_kernel(info, x_ref, mixed_ref, vec_ref, *rest):
-    pieces, (sum_ref, low_ref, act_ref, slope_ref, out, up, sems) = rest[:10], rest[10:]
+    pieces, (sum_ref, low_ref, act_ref, slope_ref, weights, sems) = rest[:10], rest[10:]
+    out, up = weights.at[0], weights.at[1:5]
     step = pl.program_id(0)
 
     def body(wait):
-        wait("out")
+        wait("mid")
         summed = x_ref[...].astype(F32) + mm(mixed_ref[...], out[...]) + vec_ref[2:3, :]
         sum_ref[...] = summed
         first_low = norm_one(summed, vec_ref).astype(LOW)
         low_ref[...] = first_low
-        wait("up0")
         hidden = mm(first_low, up[0]) + vec_ref[5:6, :]
         for j in range(4):
             if j < 3:
-                wait(f"up{j + 1}")
                 later = mm(first_low, up[j + 1]) + vec_ref[6 + j : 7 + j, :]
             act, slope = gelu_parts(hidden)
             act_ref[:, j * 768 : (j + 1) * 768] = act.astype(LOW)
@@ -205,7 +212,7 @@
 
     @pl.when(step == 0)
     def _():
-        body(staged(mid_groups(info[0], pieces, out, up, sems)))
+        body(staged({"mid": piece_copies(info[0], pieces, weights, sems)}))
 
     @pl.when(step > 0)
     def _():
@@ -217,7 +224,7 @@
 
     @pl.when(pl.program_id(0) == 0)
     def _():
-        load(slab_copies(info[0], pieces, down_slabs(down), sems))
+        load(piece_copies(info[0], pieces, down, sems))
 
     total = norm_one(sum_ref[...], vec_ref) + vec_ref[9:10, :] + mm(act_ref[...], down[...])
     second_ref[...] = total
@@ -229,12 +236,13 @@
 def cross_kernel(blocks, segs, seg_count, info, both_ref, live_ref, vec_ref, pos_ref, seg_vec_ref, *rest):
     wide, tops_in, sources, mid, more, rest = rest[0], rest[1:6], rest[6:9], rest[9:19], rest[19:27], rest[27:]
     grads_ref, pos_grad_ref, qkv_grad_ref, out_grad_ref, up_grad_ref, down_grad_ref, seg_grads_ref, *tops_out = rest[:12]
-    (qkv, out, up, down, sems, result, heads_grad, slope, lefts, act, packed, rights, hidden_grad) = rest[12:25]
-    tops, parts, own_hidden, weights, (seg_sems, top_sems) = rest[25:30], rest[30:33], rest[33], rest[34:37], rest[37:]
+    (qkv, middle, down, sems, result, heads_grad, slope, lefts, act, packed, rights, hidden_grad) = rest[12:24]
+    out, up = middle.at[0], middle.at[1:5]
+    tops, parts, own_hidden, weights, (seg_sems, top_sems) = rest[24:29], rest[29:32], rest[32], rest[33:35], rest[35:]
     step = pl.program_id(0)
     count = live_ref.shape[0]
     at = pl.ds(pl.multiple_of(step * count, count), count)
-    targets = [qkv.at[j] for j in range(3)] + [out] + [up.at[j] for j in range(4)]
+    targets = [qkv.at[j] for j in range(3)] + [middle.at[j] for j in range(5)]
     targets += [down.at[j * 768 : (j + 1) * 768] for j in range(4)]
     copies = [pltpu.make_async_copy(wide.at[j], t, sems.at[j]) for j, t in enumerate(targets)]
 
@@ -370,7 +378,7 @@
     return jnp.sum(value.astype(F32), axis=0, keepdims=True)
 
 
-def ffn_back_rows(upstream, second, summed, slope, vec, grads_ref, hidden_grad, out, up, down, wait):
+def ffn_back_rows(upstream, second, summed, slope, vec, grads_ref, hidden_grad, weights, down, wait):
     normed, inv_scale = normalize(second)
     back_two = normalize_back(upstream * (1.0 + vec[10:11, :]), normed, inv_scale)
     down_grad = back_two.astype(LOW)
@@ -378,15 +386,14 @@
     grads_ref[10:11, :] += column_sum(upstream * normed)
     grads_ref[11:12, :] += column_sum(upstream)
     total = back_two
-    wait("down")
+    out, up = weights.at[0], weights.at[1:5]
+    wait("down", "mid")
     for j in range(4):
         cols = slice(j * 768, (j + 1) * 768)
         grad = (mm_nt(down_grad, down[cols, :]) * slope(cols).astype(F32)).astype(LOW)
         hidden_grad(cols, grad)
         grads_ref[5 + j : 6 + j, :] += column_sum(grad)
-        wait(f"up{j}")
         total = total + mm_nt(grad, up[j])
-    wait("out")
     normed, inv_scale = normalize(summed)
     back_one = normalize_back(total * (1.0 + vec[3:4, :]), normed, inv_scale)
     proj_grad = back_one.astype(LOW)
@@ -396,21 +403,13 @@
     return down_grad, proj_grad, mm_nt(proj_grad, out[...]).astype(LOW)
 
 
-def mid_groups(place, mid, out, up, sems):
-    copies = slab_copies(place, mid, mid_slabs(out, up), sems, by_slab=True)
-    groups = {f"up{j}": copies[j + 1] for j in range(4)}
-    return {"out": copies[0], **groups}
-
-
-def ffn_groups(place, mid, rest, out, up, down, sems):
-    groups = mid_groups(place, mid, out, up, sems)
-    last = groups.pop("out")
-    return {"down": slab_copies(place, rest, down_slabs(down), sems, 40), **groups, "out": last}
+def ffn_groups(place, mid, rest, weights, down, sems):
+    return {"down": piece_copies(place, rest, down, sems, 10), "mid": piece_copies(place, mid, weights, sems)}
 
 
 def ffn_backward_kernel(segs, seg_count, first_step, info, cot_ref, second_ref, sum_ref, slope_ref, vec_ref, *rest):
-    mid, more, rest = rest[:10], rest[10:18], rest[-10:]
-    out_ref, down_grad_ref, hidden_grad_ref, proj_grad_ref, mixed_grad_ref, grads_ref, out, up, down, sems = rest
+    mid, more, rest = rest[:10], rest[10:18], rest[-9:]
+    out_ref, down_grad_ref, hidden_grad_ref, proj_grad_ref, mixed_grad_ref, grads_ref, weights, down, sems = rest
     step = pl.program_id(0)
 
     def body(wait):
@@ -431,12 +430,12 @@
 
         down_grad_ref[...], proj_grad_ref[...], mixed_grad_ref[...] = ffn_back_rows(
             jnp.concatenate(ups, axis=0), second, sum_ref[...], lambda cols: slope_ref[:, cols], vec_ref, grads_ref,
-            store, out, up, down, wait,
+            store, weights, down, wait,
         )
 
     @pl.when(step == 0)
     def _():
-        wait = staged(ffn_groups(info[0], mid, more, out, up, down, sems))
+        wait = staged(ffn_groups(info[0], mid, more, weights, down, sems))
         grads_ref[...] = jnp.zeros_like(grads_ref)
         body(wait)
 
@@ -585,12 +584,16 @@
 
 
 QKV = [pltpu.VMEM((3, 768, 768), LOW)]
-MID = [pltpu.VMEM((768, 768), LOW), pltpu.VMEM((4, 768, 768), LOW)]
+MID = [pltpu.VMEM((5, 768, 768), LOW)]
 DOWN = [pltpu.VMEM((3072, 768), LOW)]
 
 
 def sems(count):
     return [pltpu.SemaphoreType.DMA((count,))]
+
+
+def tall_pieces(pieces):
+    return [p.reshape(-1, 96, 768) for p in pieces]
 
 
 def shifted(count, width, first):
@@ -630,7 +633,7 @@
         compiler_params=params(),
         cost_estimate=cost(2 * rows * 768 * 8000, rows * 768 * 30),
         name="mid_forward",
-    )(info, rows_in, mixed, vec, *pieces)
+    )(info, rows_in, mixed, vec, *tall_pieces(pieces))
 
 
 def down_forward(info, summed, act, vec, pieces, segs=2):
@@ -682,7 +685,7 @@
         compiler_params=params(),
         cost_estimate=cost(2 * rows * 768 * 30000, 2**24),
         name="cross_encoder",
-    )(info, both, live, vec, positions, seg_vec, wide, *arrays, *sources, *mid, *more)
+    )(info, both, live, vec, positions, seg_vec, wide, *arrays, *sources, *tall_pieces(mid), *more)
     return grads, seg_grads, [a.reshape(-1, a.shape[2]) for a in (layer, down, hidden, proj, mixed)]
 
 
@@ -705,7 +708,7 @@
         compiler_params=params(),
         cost_estimate=cost(rows * 768 * 14000, rows * 768 * 15),
         name="ffn_backward",
-    )(info, cotangent, second, summed, slope, vec, *mid, *down, *before)
+    )(info, cotangent, second, summed, slope, vec, *tall_pieces(mid), *down, *before)
 
 
 def opening_backward(info, heads, heads_grad, vec, arrays, sources, mid, down, seg_count):
@@ -723,7 +726,7 @@
         compiler_params=params(),
         cost_estimate=cost(2**33, 2**24),
         name="opening_backward",
-    )(info, heads, heads_grad, vec, *arrays, *sources, *mid, *down)
+    )(info, heads, heads_grad, vec, *arrays, *sources, *tall_pieces(mid), *down)
     return [a.reshape(-1, a.shape[2]) for a in done], grads
 
 

time: 470 us -> 476 us (1.013)
  waiting for transfers between devices: 27.3 us -> 33.1 us
    ppermute x21, waiting for transfers between devices: 10.4 us -> 17.8 us  [turn(): return lax.ppermute(value, AXES, pairs)]
  transfers between devices with their start and end apart: 65 -> 65, of which waited for: 12 -> 11; matrix products, arithmetic and copies ran while one was open for 13% -> 13% of each run, Pallas kernels for 44% -> 43%
where the time goes in v10:
time: 476 us
  Pallas kernels  284 us (60%)
  starting transfers between devices  74.4 us (16%)
  local copies, waits for them, and re-layouts  37.5 us (8%)
  waiting for transfers between devices  33.1 us (7%)
  other arithmetic  31.5 us (7%)
  between operations  15.7 us (3%)
    pallas_call x1, Pallas kernels, cross_whole(): pl.pallas_call(functools.partial(cross_kernel, rows // count, segs, seg_c...  61.5 us
    pallas_call x2, Pallas kernels, ffn_backward(): pl.pallas_call(functools.partial(ffn_backward_kernel, segs, seg_count, fi...  49.6 us
    ppermute x21, starting transfers between devices, turn(): return lax.ppermute(value, AXES, pairs)  41.8 us
    pallas_call x2, Pallas kernels, attn_backward(): pl.pallas_call(functools.partial(attn_backward_kernel, segs, seg_count, f...  34.4 us
    ppermute x43, starting transfers between devices, flip(): return lax.ppermute(value, AXES, pairs)  32.6 us
    pallas_call x1, Pallas kernels, mid_forward(): pl.pallas_call(mid_forward_kernel, grid=(rows // count,), in_specs=[SMEM,...  29.7 us
    pallas_call x2, Pallas kernels, attn_forward(): pl.pallas_call(functools.partial(attn_forward_kernel, segs, seg_count, fi...  26.1 us
    pallas_call x1, Pallas kernels, down_forward(): pl.pallas_call(functools.partial(down_forward_kernel, segs), grid=(rows /...  19.9 us
  transfers between devices with their start and end apart: 65, of which 11 were waited for; matrix products, arithmetic and copies ran while one was open for 13% of the time, Pallas kernels for 43%

profile of v10, /device:TPU:0, one launch (start us, length us, event | category | flops | bytes accessed | tf_op | source)
XLA Modules:
  0.0 476.3 jit_solution(9565330319753070926)
XLA Ops:
  9.0 4.1 collective-permute-start
  17.0 5.6 %collective-permute-done = bf16[80,768]{1,0:T(8,128)(2,1)S(1)} collective-permute-done((bf16[80,768]{1,0:T(8,128)(2,1)S(1)}, bf16[80,768]{1,0:T(8,128)(2,1)S(1)}, u32[]{:S(2)}, u32[]{:S(2)}) %collective-permute-start) | collective-permute-done | bytes 122912 | tf_op jit(solution)/shard_map/ppermute | solution.py:1023
  27.9 3.7 collective-permute-start.3
  31.6 3.8 collective-permute-start.5
  40.7 10.5 %collective-permute-done.3 = bf16[5,24,768]{2,0,1:T(8,128)(2,1)S(1)} collective-permute-done((bf16[5,24,768]{2,0,1:T(8,128)(2,1)S(1)}, bf16[5,24,768]{2,0,1:T(8,128)(2,1)S(1)}, u32[]{:S(2)}, u32[]{:S(2)}) %collective-permute-start.3) | collective-permute-done | bytes 184352 | tf_op jit(solution)/shard_map/ppermute | solution.py:1023
  59.5 4.8 %collective-permute-start.24 = (bf16[96,768]{1,0:T(8,128)(2,1)S(1)}, bf16[96,768]{1,0:T(8,128)(2,1)S(1)}, u32[]{:S(2)}, u32[]{:S(2)}) collective-permute-start(bf16[96,768]{1,0:T(8,128)(2,1)S(1)} %copy-done.13), channel_id=1, source_target_pairs={{0,2},{1,3},{2,0},{3,1},{4,6},{5,7},{6,4},{7,5},{8,10},{9,11},{10,... | collective-permute-start | bytes 442376 | tf_op jit(solution)/shard_map/ppermute | solution.py:1023
  65.4 3.2 collective-permute-start.26
  71.7 13.0 %attn_forward.2 = (bf16[2048,2304]{1,0:T(8,128)(2,1)}, bf16[2048,768]{1,0:T(8,128)(2,1)}) custom-call(s32[3]{0:T(128)} %pad_add_fusion.1.info, bf16[2048,768]{1,0:T(8,128)(2,1)} %bitcast.296, f32[12,768]{1,0:T(8,128)} %slice.349.vec_ref.seg_vec_ref, bf16[304,768]{1,0:T(8,128)(2,1)} %fusion.17.rest_0_, bf16[304,768]{1,0:T(8,128)(2,1)} %collective-permute-done.8.rest_1_, ...), custom_call_target="tpu_custom_call" | custom-call | flops 12582912000 | bytes 12582912 | tf_op jit(solution)/shard_map/attn_forward/pallas_call | solution.py:609
  89.6 13.2 %attn_forward.3 = (bf16[2048,2304]{1,0:T(8,128)(2,1)}, bf16[2048,768]{1,0:T(8,128)(2,1)}) custom-call(s32[3]{0:T(128)} %pad_add_fusion.1.info, bf16[2048,768]{1,0:T(8,128)(2,1)} %bitcast.297, f32[12,768]{1,0:T(8,128)} %slice.349.vec_ref.seg_vec_ref, bf16[304,768]{1,0:T(8,128)(2,1)} %fusion.17.rest_0_, ...), custom_call_target="tpu_custom_call", output_to_operand_aliasing={{0}: (13, {}), {1}: (14, {})} | custom-call | flops 12582912000 | bytes 12582912 | tf_op jit(solution)/shard_map/attn_forward/pallas_call | solution.py:609
  108.8 29.7 %mid_forward.1 = (f32[2048,768]{1,0:T(8,128)}, bf16[2048,768]{1,0:T(8,128)(2,1)}, bf16[2048,3072]{1,0:T(8,128)(2,1)}, bf16[2048,3072]{1,0:T(8,128)(2,1)}) custom-call(s32[3]{0:T(128)} %pad_add_fusion.1.info, bf16[2048,768]{1,0:T(8,128)(2,1)} %bitcast.298, bf16[2048,768]{1,0:T(8,128)(2,1)} %get-tuple-element.126.mixed_ref, ...), custom_call_target="tpu_custom_call" | custom-call | flops 25165824000 | bytes 47185920 | tf_op jit(solution)/shard_map/mid_forward/pallas_call | solution.py:626
  140.5 5.9 %collective-permute-done.27.rest_1_.rest_11_.rest_20_ = bf16[384,768]{1,0:T(8,128)(2,1)} collective-permute-done((bf16[384,768]{1,0:T(8,128)(2,1)S(1)}, bf16[384,768]{1,0:T(8,128)(2,1)}, u32[]{:S(2)}, u32[]{:S(2)}) %collective-permute-start.27) | collective-permute-done | bytes 589856 | tf_op jit(solution)/shard_map/ppermute | solution.py:1015
  148.8 19.9 %down_forward.1 = (f32[2048,768]{1,0:T(8,128)}, f32[8,2,768]{2,1,0:T(2,128)}) custom-call(s32[3]{0:T(128)} %pad_add_fusion.1.info, f32[2048,768]{1,0:T(8,128)} %get-tuple-element.133.sum_ref, bf16[2048,3072]{1,0:T(8,128)(2,1)} %get-tuple-element.134.act_ref.left_ref, f32[12,768]{1,0:T(8,128)} %slice.349.vec_ref.seg_vec_ref, bf16[384,768]{1,0:T(8,128)(2,1)} %copy-done.10, ...), custom_call_target="tpu_custom_call" | custom-call | flops 12582912000 | bytes 25165824 | tf_op jit(solution)/shard_map/down_forward/pallas_call | solution.py:643
  173.6 24.7 %ffn_backward.2 = (bf16[2048,768]{1,0:T(8,128)(2,1)}, bf16[2048,768]{1,0:T(8,128)(2,1)}, bf16[2048,3072]{1,0:T(8,128)(2,1)}, bf16[2048,768]{1,0:T(8,128)(2,1)}, ...) custom-call(s32[3]{0:T(128)} %pad_add_fusion.1.info, bf16[2048,768]{1,0:T(8,128)(2,1)} %bitcast.294, ...), custom_call_target="tpu_custom_call" | custom-call | flops 22020096000 | bytes 23592960 | tf_op jit(solution)/shard_map/ffn_backward/pallas_call | solution.py:699
  202.0 24.9 %ffn_backward.3 = (bf16[2048,768]{1,0:T(8,128)(2,1)}, bf16[2048,768]{1,0:T(8,128)(2,1)}, bf16[2048,3072]{1,0:T(8,128)(2,1)}, bf16[2048,768]{1,0:T(8,128)(2,1)}, ...) custom-call(s32[3]{0:T(128)} %pad_add_fusion.1.info, ...), custom_call_target="tpu_custom_call", output_to_operand_aliasing={{0}: (24, {}), {1}: (25, {}), {2}: (26, {}), {3}: (27, {}),... | custom-call | flops 22020096000 | bytes 23592960 | tf_op jit(solution)/shard_map/ffn_backward/pallas_call | solution.py:699
  232.2 61.5 %cross_encoder.1 = (f32[12,768]{1,0:T(8,128)}, f32[8,768]{1,0:T(8,128)}, f32[24,2304]{1,0:T(8,128)}, f32[24,768]{1,0:T(8,128)}, f32[24,3072]{1,0:T(8,128)}, /*in...) custom-call(s32[5]{0:T(128)} %pad_add_fusion.info, ...), custom_call_target="tpu_custom_call", output_to_operand_aliasing={{7}: (7, {}), {8}: (8, {}), {9}: (9, {}), {10}: (10, {}), {... | custom-call | flops 23592960000 | bytes 16777216 | tf_op jit(solution)/shard_map/cross_encoder/pallas_call | solution.py:673
  293.7 16.1 %down_weight_grad.1 = (bf16[4,384,768]{2,1,0:T(8,128)(2,1)}, bf16[4,384,768]{2,1,0:T(8,128)(2,1)}) custom-call(s32[3]{0:T(128)} %pad_add_fusion.1.info, bf16[2048,3072]{1,0:T(8,128)(2,1)} %get-tuple-element.134.act_ref.left_ref, bf16[2048,768]{1,0:T(8,128)(2,1)} %bitcast.321), custom_call_target="tpu_custom_call" | custom-call | flops 9663676416 | bytes 12582912 | tf_op jit(solution)/shard_map/down_weight_grad/pallas_call | solution.py:819
  310.3 19.9 %mid_weight_grad.1 = (bf16[4,480,768]{2,1,0:T(8,128)(2,1)}, bf16[4,480,768]{2,1,0:T(8,128)(2,1)}) custom-call(s32[3]{0:T(128)} %pad_add_fusion.1.info, bf16[2048,768]{1,0:T(8,128)(2,1)} %get-tuple-element.126.mixed_ref, bf16[2048,768]{1,0:T(8,128)(2,1)} %bitcast.323, bf16[2048,768]{1,0:T(8,128)(2,1)} %get-tuple-element.160.low_ref, bf16[2048,3072]{1,0:T(8,128)(2,1)} %bitcast.314), custom_call_target="tpu_custom_call" | custom-call | flops 12079595520 | bytes 15728640 | tf_op jit(solution)/shard_map/mid_weight_grad/pallas_call | solution.py:792
  330.8 2.8 convert_add_fusion.1
  336.6 17.3 %attn_backward.2 = (bf16[2048,2304]{1,0:T(8,128)(2,1)}, f32[2,768]{1,0:T(2,128)}) custom-call(s32[3]{0:T(128)} %pad_add_fusion.1.info, bf16[2048,2304]{1,0:T(8,128)(2,1)} %get-tuple-element.130.packed_ref, bf16[2048,768]{1,0:T(8,128)(2,1)} %bitcast.326), custom_call_target="tpu_custom_call" | custom-call | flops 15728640000 | bytes 12582912 | tf_op jit(solution)/shard_map/attn_backward/pallas_call | solution.py:739
  365.8 17.1 %attn_backward.3 = (bf16[2048,2304]{1,0:T(8,128)(2,1)}, f32[2,768]{1,0:T(2,128)}) custom-call(s32[3]{0:T(128)} %pad_add_fusion.1.info, bf16[2048,2304]{1,0:T(8,128)(2,1)} %get-tuple-element.130.packed_ref, bf16[2048,768]{1,0:T(8,128)(2,1)} %bitcast.327, bf16[2048,2304]{1,0:T(8,128)(2,1)} %get-tuple-element.168.rest_0_), custom_call_target="tpu_custom_call", output_to_operand_aliasing={{0}: (3, {})} | custom-call | flops 15728640000 | bytes 12582912 | tf_op jit(solution)/shard_map/attn_backward/pallas_call | solution.py:739
  397.3 13.2 %qkv_weight_grad.1 = (bf16[4,304,768]{2,1,0:T(8,128)(2,1)}, bf16[4,304,768]{2,1,0:T(8,128)(2,1)}) custom-call(s32[3]{0:T(128)} %pad_add_fusion.1.info, bf16[2048,768]{1,0:T(8,128)(2,1)} %bitcast.299, bf16[2048,2304]{1,0:T(8,128)(2,1)} %get-tuple-element.180.right_ref.packed_grad_ref, bf16[8,16,768]{2,1,0:T(8,128)(2,1)} %pad.34.more_ref), custom_call_target="tpu_custom_call" | custom-call | flops 7247757312 | bytes 9437184 | tf_op jit(solution)/shard_map/qkv_weight_grad/pallas_call | solution.py:775
  428.3 13.6 %token_gradient.1 = bf16[2048,768]{1,0:T(8,128)(2,1)} custom-call(s32[3]{0:T(128)} %pad_add_fusion.1.info, bf16[2048,2304]{1,0:T(8,128)(2,1)} %get-tuple-element.180.right_ref.packed_grad_ref, bf16[2048,768]{1,0:T(8,128)(2,1)} %bitcast.324, bf16[304,768]{1,0:T(8,128)(2,1)} %fusion.17.rest_0_, bf16[304,768]{1,0:T(8,128)(2,1)} %collective-permute-done.8.rest_1_, ...), custom_call_target="tpu_custom_call" | custom-call | flops 9437184000 | bytes 15728640 | tf_op jit(solution)/shard_map/token_gradient/pallas_call | solution.py:754
  442.0 2.9 collective-permute-start.63
  444.9 4.4 collective-permute-done.56
  (370 shorter events, 124.7 us)
Async XLA Ops:
  7.2 224.1 %all-gather.2.cloned.1.call-start = ((), (), s32[]{:S(2)}) async-start(), calls=%async_computation | async-start | bytes 14598144 | tf_op jit(solution)/shard_map/all_gather | solution.py:1253
  27.9 23.3 %collective-permute-start.3 = (bf16[5,24,768]{2,0,1:T(8,128)(2,1)S(1)}, bf16[5,24,768]{2,0,1:T(8,128)(2,1)S(1)}, u32[]{:S(2)}, u32[]{:S(2)}) collective-permute-start(bf16[5,24,768]{2,0,1:T(8,128)(2,1)S(1)} %pad_maximum_fusion.10), channel_id=1, source_target_pairs={{0,2},{1,3},{2,0},{3,1},{4,6},{5,7},{6,4},{7,5},{8,10},{9,11},{10,... | collective-permute-start | bytes 552968 | tf_op jit(solution)/shard_map/ppermute | solution.py:1023
  58.5 26.3 %collective-permute-start.10 = (bf16[480,768]{1,0:T(8,128)(2,1)S(1)}, bf16[480,768]{1,0:T(8,128)(2,1)}, u32[]{:S(2)}, u32[]{:S(2)}) collective-permute-start(bf16[480,768]{1,0:T(8,128)(2,1)S(1)} %bitcast.259), channel_id=1, source_target_pairs={{0,8},{1,9},{2,10},{3,11},{4,12},{5,13},{6,14},{7,15},{8,0},{9,1},... | collective-permute-start | bytes 2211848 | tf_op jit(solution)/shard_map/ppermute | solution.py:1015
  59.0 25.8 %collective-permute-start.11 = (bf16[480,768]{1,0:T(8,128)(2,1)S(1)}, bf16[480,768]{1,0:T(8,128)(2,1)S(1)}, u32[]{:S(2)}, u32[]{:S(2)}) collective-permute-start(bf16[480,768]{1,0:T(8,128)(2,1)S(1)} %bitcast.260), channel_id=1, source_target_pairs={{0,16},{1,17},{2,18},{3,19},{4,20},{5,21},{6,22},{7,23},{8,24},{9,... | collective-permute-start | bytes 2211848 | tf_op jit(solution)/shard_map/ppermute | solution.py:1015
  59.5 25.1 %collective-permute-start.24 = (bf16[96,768]{1,0:T(8,128)(2,1)S(1)}, bf16[96,768]{1,0:T(8,128)(2,1)S(1)}, u32[]{:S(2)}, u32[]{:S(2)}) collective-permute-start(bf16[96,768]{1,0:T(8,128)(2,1)S(1)} %copy-done.13), channel_id=1, source_target_pairs={{0,2},{1,3},{2,0},{3,1},{4,6},{5,7},{6,4},{7,5},{8,10},{9,11},{10,... | collective-permute-start | bytes 442376 | tf_op jit(solution)/shard_map/ppermute | solution.py:1023
  105.2 33.3 %collective-permute-start.29 = (bf16[384,768]{1,0:T(8,128)(2,1)S(1)}, bf16[384,768]{1,0:T(8,128)(2,1)S(1)}, u32[]{:S(2)}, u32[]{:S(2)}) collective-permute-start(bf16[384,768]{1,0:T(8,128)(2,1)S(1)} %pad_maximum_fusion.5.rest_0_.rest_10_.rest_19_), channel_id=1, source_target_pairs={{0,24},{1,25},{2,26},{3,27},{4,28},{5,29},{6,30},{7,31},{8,16},{9,... | collective-permute-start | bytes 1769480 | tf_op jit(solution)/shard_map/ppermute | solution.py:1015
  107.2 33.2 %collective-permute-start.28 = (bf16[384,768]{1,0:T(8,128)(2,1)S(1)}, bf16[384,768]{1,0:T(8,128)(2,1)S(1)}, u32[]{:S(2)}, u32[]{:S(2)}) collective-permute-start(bf16[384,768]{1,0:T(8,128)(2,1)S(1)} %pad_maximum_fusion.5.rest_0_.rest_10_.rest_19_), channel_id=1, source_target_pairs={{0,16},{1,17},{2,18},{3,19},{4,20},{5,21},{6,22},{7,23},{8,24},{9,... | collective-permute-start | bytes 1769480 | tf_op jit(solution)/shard_map/ppermute | solution.py:1015
  107.7 38.7 %collective-permute-start.27 = (bf16[384,768]{1,0:T(8,128)(2,1)S(1)}, bf16[384,768]{1,0:T(8,128)(2,1)}, u32[]{:S(2)}, u32[]{:S(2)}) collective-permute-start(bf16[384,768]{1,0:T(8,128)(2,1)S(1)} %pad_maximum_fusion.5.rest_0_.rest_10_.rest_19_), channel_id=1, source_target_pairs={{0,8},{1,9},{2,10},{3,11},{4,12},{5,13},{6,14},{7,15},{8,0},{9,1},... | collective-permute-start | bytes 1769480 | tf_op jit(solution)/shard_map/ppermute | solution.py:1015
  108.7 38.9 %collective-permute-start.30 = (bf16[384,768]{1,0:T(8,128)(2,1)S(1)}, bf16[384,768]{1,0:T(8,128)(2,1)}, u32[]{:S(2)}, u32[]{:S(2)}) collective-permute-start(bf16[384,768]{1,0:T(8,128)(2,1)S(1)} %pad_maximum_fusion.5.rest_0_.rest_10_.rest_19_), channel_id=1, source_target_pairs={{0,4},{1,5},{2,6},{3,7},{4,0},{5,1},{6,2},{7,3},{8,12},{9,13},{10,... | collective-permute-start | bytes 1769480 | tf_op jit(solution)/shard_map/ppermute | solution.py:1015
  169.6 28.7 %collective-permute-start.34 = (bf16[2,16,768]{2,1,0:T(8,128)(2,1)S(1)}, bf16[2,16,768]{2,1,0:T(8,128)(2,1)S(1)}, u32[]{:S(2)}, u32[]{:S(2)}) collective-permute-start(bf16[2,16,768]{2,1,0:T(8,128)(2,1)S(1)} %pad_maximum_fusion.12), channel_id=1, source_target_pairs={{0,2},{1,3},{2,0},{3,1},{4,6},{5,7},{6,4},{7,5},{8,10},{9,11},{10,... | collective-permute-start | bytes 147464 | tf_op jit(solution)/shard_map/ppermute | solution.py:1023
  169.7 28.6 %collective-permute-start.35 = (bf16[2,16,768]{2,1,0:T(8,128)(2,1)S(1)}, bf16[2,16,768]{2,1,0:T(8,128)(2,1)S(1)}, u32[]{:S(2)}, u32[]{:S(2)}) collective-permute-start(bf16[2,16,768]{2,1,0:T(8,128)(2,1)S(1)} %pad_maximum_fusion.12), channel_id=1, source_target_pairs={{0,1},{1,2},{2,3},{3,0},{4,5},{5,6},{6,7},{7,4},{8,9},{9,10},{10,1... | collective-permute-start | bytes 147464 | tf_op jit(solution)/shard_map/ppermute | solution.py:1023
  171.2 27.1 %collective-permute-start.36 = (bf16[2,16,768]{2,1,0:T(8,128)(2,1)S(1)}, bf16[2,16,768]{2,1,0:T(8,128)(2,1)S(1)}, u32[]{:S(2)}, u32[]{:S(2)}) collective-permute-start(bf16[2,16,768]{2,1,0:T(8,128)(2,1)S(1)} %pad_maximum_fusion.12), channel_id=1, source_target_pairs={{0,3},{1,0},{2,1},{3,2},{4,7},{5,4},{6,5},{7,6},{8,11},{9,8},{10,9... | collective-permute-start | bytes 147464 | tf_op jit(solution)/shard_map/ppermute | solution.py:1023
  198.4 28.4 %collective-permute-start.37 = (bf16[4,2,16,768]{3,2,1,0:T(8,128)(2,1)S(1)}, bf16[4,2,16,768]{3,2,1,0:T(8,128)(2,1)S(1)}, u32[]{:S(2)}, u32[]{:S(2)}) collective-permute-start(bf16[4,2,16,768]{3,2,1,0:T(8,128)(2,1)S(1)} %pad_maximum_fusion.11), channel_id=1, source_target_pairs={{0,8},{1,9},{2,10},{3,11},{4,12},{5,13},{6,14},{7,15},{8,0},{9,1},... | collective-permute-start | bytes 589832 | tf_op jit(solution)/shard_map/ppermute | solution.py:1015
  200.0 26.9 %collective-permute-start.38 = (bf16[4,2,16,768]{3,2,1,0:T(8,128)(2,1)S(1)}, bf16[4,2,16,768]{3,2,1,0:T(8,128)(2,1)S(1)}, u32[]{:S(2)}, u32[]{:S(2)}) collective-permute-start(bf16[4,2,16,768]{3,2,1,0:T(8,128)(2,1)S(1)} %pad_maximum_fusion.11), channel_id=1, source_target_pairs={{0,16},{1,17},{2,18},{3,19},{4,20},{5,21},{6,22},{7,23},{8,24},{9,... | collective-permute-start | bytes 589832 | tf_op jit(solution)/shard_map/ppermute | solution.py:1015
  200.6 26.3 %collective-permute-start.39 = (bf16[4,2,16,768]{3,2,1,0:T(8,128)(2,1)S(1)}, bf16[4,2,16,768]{3,2,1,0:T(8,128)(2,1)S(1)}, u32[]{:S(2)}, u32[]{:S(2)}) collective-permute-start(bf16[4,2,16,768]{3,2,1,0:T(8,128)(2,1)S(1)} %pad_maximum_fusion.11), channel_id=1, source_target_pairs={{0,24},{1,25},{2,26},{3,27},{4,28},{5,29},{6,30},{7,31},{8,16},{9,... | collective-permute-start | bytes 589832 | tf_op jit(solution)/shard_map/ppermute | solution.py:1015
  330.1 27.6 %collective-permute-start.44 = (bf16[4,480,768]{2,1,0:T(8,128)(2,1)}, bf16[4,480,768]{2,1,0:T(8,128)(2,1)}, u32[]{:S(2)}, u32[]{:S(2)}) collective-permute-start(bf16[4,480,768]{2,1,0:T(8,128)(2,1)} %get-tuple-element.165), channel_id=1, source_target_pairs={{0,4},{1,5},{2,6},{3,7},{4,0},{5,1},{6,2},{7,3},{8,12},{9,13},{10,... | collective-permute-start | bytes 8847368 | tf_op jit(solution)/shard_map/ppermute | solution.py:1015
  354.9 31.6 %collective-permute-start.46 = (bf16[4,96,768]{2,1,0:T(8,128)(2,1)}, bf16[4,96,768]{2,1,0:T(8,128)(2,1)}, u32[]{:S(2)}, u32[]{:S(2)}) collective-permute-start(bf16[4,96,768]{2,1,0:T(8,128)(2,1)} %pad_maximum_fusion.7), channel_id=1, source_target_pairs={{0,16},{1,17},{2,18},{3,19},{4,20},{5,21},{6,22},{7,23},{8,24},{9,... | collective-permute-start | bytes 1769480 | tf_op jit(solution)/shard_map/ppermute | solution.py:1015
  357.2 29.3 %collective-permute-start.45 = (bf16[4,96,768]{2,1,0:T(8,128)(2,1)}, bf16[4,96,768]{2,1,0:T(8,128)(2,1)}, u32[]{:S(2)}, u32[]{:S(2)}) collective-permute-start(bf16[4,96,768]{2,1,0:T(8,128)(2,1)} %pad_maximum_fusion.6), channel_id=1, source_target_pairs={{0,8},{1,9},{2,10},{3,11},{4,12},{5,13},{6,14},{7,15},{8,0},{9,1},... | collective-permute-start | bytes 1769480 | tf_op jit(solution)/shard_map/ppermute | solution.py:1015
  362.1 25.9 %collective-permute-start.47 = (bf16[2,120,768]{2,1,0:T(8,128)(2,1)}, bf16[2,120,768]{2,1,0:T(8,128)(2,1)}, u32[]{:S(2)}, u32[]{:S(2)}) collective-permute-start(bf16[2,120,768]{2,1,0:T(8,128)(2,1)} %bitcast.85), channel_id=1, source_target_pairs={{0,8},{1,9},{2,10},{3,11},{4,12},{5,13},{6,14},{7,15},{8,0},{9,1},... | collective-permute-start | bytes 1105928 | tf_op jit(solution)/shard_map/ppermute | solution.py:1015
  365.1 26.5 %collective-permute-start.48 = (bf16[2,120,768]{2,1,0:T(8,128)(2,1)}, bf16[2,120,768]{2,1,0:T(8,128)(2,1)}, u32[]{:S(2)}, u32[]{:S(2)}) collective-permute-start(bf16[2,120,768]{2,1,0:T(8,128)(2,1)} %bitcast.87), channel_id=1, source_target_pairs={{0,16},{1,17},{2,18},{3,19},{4,20},{5,21},{6,22},{7,23},{8,24},{9,... | collective-permute-start | bytes 1105928 | tf_op jit(solution)/shard_map/ppermute | solution.py:1015
  419.3 35.5 %collective-permute-start.61 = (bf16[120,768]{1,0:T(8,128)(2,1)S(1)}, bf16[120,768]{1,0:T(8,128)(2,1)}, u32[]{:S(2)}, u32[]{:S(2)}) collective-permute-start(bf16[120,768]{1,0:T(8,128)(2,1)S(1)} %get-tuple-element.230), channel_id=1, source_target_pairs={{0,1},{1,2},{2,3},{3,0},{4,5},{5,6},{6,7},{7,4},{8,9},{9,10},{10,1... | collective-permute-start | bytes 552968 | tf_op jit(solution)/shard_map/ppermute | solution.py:1023
  419.9 36.1 %collective-permute-start.62 = (bf16[120,768]{1,0:T(8,128)(2,1)S(1)}, bf16[120,768]{1,0:T(8,128)(2,1)}, u32[]{:S(2)}, u32[]{:S(2)}) collective-permute-start(bf16[120,768]{1,0:T(8,128)(2,1)S(1)} %get-tuple-element.232), channel_id=1, source_target_pairs={{0,2},{1,3},{2,0},{3,1},{4,6},{5,7},{6,4},{7,5},{8,10},{9,11},{10,... | collective-permute-start | bytes 552968 | tf_op jit(solution)/shard_map/ppermute | solution.py:1023
  425.3 23.9 %collective-permute-start.56 = (bf16[4,80,768]{2,1,0:T(8,128)(2,1)}, bf16[4,80,768]{2,1,0:T(8,128)(2,1)}, u32[]{:S(2)}, u32[]{:S(2)}) collective-permute-start(bf16[4,80,768]{2,1,0:T(8,128)(2,1)} %fusion.15), channel_id=1, source_target_pairs={{0,16},{1,17},{2,18},{3,19},{4,20},{5,21},{6,22},{7,23},{8,24},{9,... | collective-permute-start | bytes 1474568 | tf_op jit(solution)/shard_map/ppermute | solution.py:1015
  426.9 22.4 %collective-permute-start.57 = (bf16[4,80,768]{2,1,0:T(8,128)(2,1)}, bf16[4,80,768]{2,1,0:T(8,128)(2,1)}, u32[]{:S(2)}, u32[]{:S(2)}) collective-permute-start(bf16[4,80,768]{2,1,0:T(8,128)(2,1)} %fusion.16), channel_id=1, source_target_pairs={{0,24},{1,25},{2,26},{3,27},{4,28},{5,29},{6,30},{7,31},{8,16},{9,... | collective-permute-start | bytes 1474568 | tf_op jit(solution)/shard_map/ppermute | solution.py:1015
  (82 other events, 833.8 us)
Sparse Core Ops, SparseCore 0:
  84.9 119.2 all-gather.1
